TPU v7x, 256 devices: a whole 4x4x8 slice. The times are simulated.
256 devices in a mesh: beam: 32 (over z, x), tm: 8 (over y, core).
Axes of the slice: x: 4, y: 4, z: 8, core: 2. Of those that a mesh axis runs over, the one named last changes fastest.
Arguments:
- voltages: float32 [32, 2, 2, 128, 8192], P('beam', None, None, 'tm'), may hold values from -20 to 20
- filter_taps: float32 [8, 8192], replicated, may hold values from -2 to 2
Outputs:
- cleaned: float32 [32, 2, 128, 8192], P('beam', None, 'tm')
All inputs are finite; a program needn't handle non-finite values.
Results may differ from a plain program's by a relative error of at most 0.000058.
Values sent between devices are 32-bit elements; how exact they have to be, the bound alone decides.
No kernel may reach another device: no remote copies, remote signals or barrier semaphores. Data moves between devices by JAX's collectives and lax.ppermute only.
A program may use at most 64 MiB of HBM per device.

v0:
```python
import math

import jax
import jax.numpy as jnp
from jax import lax
from jax.sharding import PartitionSpec as P

RADIX = 128


def passed_along(x, axis, by):
    devices = lax.axis_size(axis)
    pairs = [(i, i + by) for i in range(devices) if 0 <= i + by < devices]
    return lax.ppermute(x, axis, pairs)


def total_of_pieces(x, axis):
    blocks = lax.all_gather(x, axis)
    return blocks.sum(axis=0)


def split_up(x, dim, devices):
    lengths = x.shape
    blocks = x.reshape(*lengths[:dim], devices, lengths[dim] // devices, *lengths[dim + 1 :])
    return jnp.moveaxis(blocks, dim, 0)


def summed_on_arrival(x, axis, dim):
    blocks = split_up(x, dim, lax.axis_size(axis))
    arrived = lax.all_to_all(blocks, axis, split_axis=0, concat_axis=0, tiled=True)
    return arrived.sum(axis=0)


def laid_out(blocks, dim):
    blocks = jnp.moveaxis(blocks, 0, dim)
    lengths = blocks.shape
    return blocks.reshape(*lengths[:dim], lengths[dim] * lengths[dim + 1], *lengths[dim + 2 :])


def sent_to_all(x, axis):
    devices = lax.axis_size(axis)
    return lax.all_to_all(jnp.broadcast_to(x[None], (devices, *x.shape)), axis, 0, 0, tiled=True)


def gathered_copies(x, axis, dim):
    return laid_out(sent_to_all(x, axis), dim)


def twiddles(rows_count, cols_count, modulus):
    product = (
        jnp.arange(rows_count, dtype=jnp.int32)[:, None]
        * jnp.arange(cols_count, dtype=jnp.int32)[None, :]
        % modulus
    )
    angles = product.astype(jnp.float32) * (-2.0 * math.pi / modulus)
    return (jnp.cos(angles), jnp.sin(angles))


def complex_apply(form, table_cos, table_sin, real_part, imag_part):

    def apply(table, values):
        return jnp.einsum(form, table, values, precision=lax.Precision.HIGHEST)

    return (
        apply(table_cos, real_part) - apply(table_sin, imag_part),
        apply(table_cos, imag_part) + apply(table_sin, real_part),
    )


def tap_sum(filter_taps, source, count):
    result = filter_taps[0] * source[:, :, 0:count]
    for tap_index in range(1, filter_taps.shape[0]):
        result = result + filter_taps[tap_index] * source[:, :, tap_index : tap_index + count]
    return result


def body(voltages, filter_taps):
    segment = voltages[0]
    frames = segment.shape[2]
    channels = segment.shape[3]
    rim_frames = filter_taps.shape[0] - 1
    zero_rim = jnp.zeros((2, 2, rim_frames, channels), jnp.float32)
    padded = jnp.concatenate([segment, zero_rim], axis=2)
    filtered = tap_sum(filter_taps, padded, frames)
    leading_rows = jnp.concatenate([zero_rim, segment[:, :, :rim_frames]], axis=2)
    partial_value = tap_sum(filter_taps, leading_rows, rim_frames)
    incoming = passed_along(partial_value, "tm", -1)
    filtered = filtered.at[:, :, frames - rim_frames :].add(incoming)
    stride = channels // RADIX
    grid_real = filtered[:, 0].reshape(2, frames, RADIX, stride)
    grid_imag = filtered[:, 1].reshape(2, frames, RADIX, stride)
    cos_first, sin_first = twiddles(RADIX, RADIX, RADIX)
    section_real, section_imag = complex_apply(
        "kn,pfnm->pfmk", cos_first, sin_first, grid_real, grid_imag
    )
    twist_cos, twist_sin = twiddles(stride, RADIX, channels)
    twisted_real = section_real * twist_cos - section_imag * twist_sin
    twisted_imag = section_real * twist_sin + section_imag * twist_cos
    cos_second, sin_second = twiddles(stride, stride, stride)
    spec_real, spec_imag = complex_apply(
        "jm,pfmk->pfjk", cos_second, sin_second, twisted_real, twisted_imag
    )
    powers = ((spec_real * spec_real + spec_imag * spec_imag) / channels).reshape(
        2, frames, channels
    )
    totals = jnp.sum(powers, axis=1)
    time_sums = total_of_pieces(totals, "tm")
    shares = summed_on_arrival(time_sums, "beam", 1)
    channel_sum = gathered_copies(shares, "beam", 1)
    all_frames = frames * lax.axis_size("tm")
    all_beams = voltages.shape[0] * lax.axis_size("beam")
    baseline = channel_sum / all_frames / all_beams
    return (powers - baseline[:, None, :])[None]


def solution(mesh):
    placed = (P("beam", None, None, "tm", None), P())
    return jax.shard_map(
        body, mesh=mesh, in_specs=placed, out_specs=P("beam", None, "tm", None), check_vma=False
    )
```

profile of v0, /device:TPU:1, one launch (start us, length us, event | category | flops | bytes accessed | tf_op | source)
XLA Modules:
  0.0 103.8 jit_solution(10426323434390127581)
XLA Ops:
  0.0 2.5 %fusion.100 = (f32[1,8192]{1,0:T(1,128)S(1)}, f32[1,8192]{1,0:T(1,128)S(1)}, f32[1,8192]{1,0:T(1,128)S(1)}, f32[1,8192]{1,0:T(1,128)S(1)}, f32[1,8192]{1,0:T(1,1...) fusion(f32[8,8192]{1,0:T(8,128)} %param.5), kind=kLoop, calls=%fused_computation.125 | loop fusion | bytes 524288 | tf_op jit(solution)/shard_map/slice | solution.py:71
  2.6 3.2 %copy.21 = f32[1,2,2,16,8192]{4,2,3,1,0:T(2,128)S(1)} copy(f32[1,2,2,16,8192]{4,3,2,1,0:T(8,128)} %param.4) | data formatting | bytes 4194304 | tf_op args[0]
  5.8 0.1 slice.135
  5.8 1.6 %multiply_add_fusion.2 = f32[2,2,7,8192]{3,1,2,0:T(2,128)S(1)} fusion(f32[2,2,7,8192]{3,1,2,0:T(2,128)S(1)} %slice.135, f32[8192]{0:T(1024)S(1)} %bitcast.67, f32[8192]{0:T(1024)S(1)} %bitcast.69, f32[8192]{0:T(1024)S(1)} %bitcast.57, f32[8192]{0:T(1024)S(1)} %bitcast.59, f32[8192]{0:T(1024)S(1)} %bitcast.61, f32[8192]{0:T(1024)S(1)} %bitcast.63, ...), kind=kLoop, calls=%fused_computation.44 | loop fusion | flops 3211264 | bytes 2097152 | tf_op jit(solution)/shard_map/add | solution.py:73
  7.4 5.1 %collective-permute-start = (f32[2,2,7,8192]{3,1,2,0:T(2,128)S(1)}, f32[2,2,7,8192]{3,1,2,0:T(2,128)S(1)}, u32[]{:S(2)}, u32[]{:S(2)}) collective-permute-start(f32[2,2,7,8192]{3,1,2,0:T(2,128)S(1)} %multiply_add_fusion.2), channel_id=1, source_target_pairs={{1,0},{2,1},{3,2},{4,3},{5,4},{6,5},{7,6},{9,8},{10,9},{11,10},{12... | collective-permute-start | bytes 2752520 | tf_op jit(solution)/shard_map/ppermute | solution.py:14
  12.6 7.2 %multiply_add_fusion = f32[2,2,16,8192]{3,1,2,0:T(2,128)S(1)} fusion(f32[2,2,16,8192]{3,1,2,0:T(2,128)S(1)} %bitcast.56, f32[8192]{0:T(1024)S(1)} %bitcast.68, f32[8192]{0:T(1024)S(1)} %bitcast.70, f32[8192]{0:T(1024)S(1)} %bitcast.58, f32[8192]{0:T(1024)S(1)} %bitcast.60, f32[8192]{0:T(1024)S(1)} %bitcast.62, f32[8192]{0:T(1024)S(1)} %bitcast.64, ...), kind=kLoop, calls=%fused_computation.1 | loop fusion | flops 7864320 | bytes 4456448 | tf_op jit(solution)/shard_map/add | solution.py:73
  19.8 0.1 fusion.66
  19.9 3.2 %collective-permute-done = f32[2,2,7,8192]{3,1,2,0:T(2,128)S(1)} collective-permute-done((f32[2,2,7,8192]{3,1,2,0:T(2,128)S(1)}, f32[2,2,7,8192]{3,1,2,0:T(2,128)S(1)}, u32[]{:S(2)}, u32[]{:S(2)}) %collective-permute-start) | collective-permute-done | bytes 917536 | tf_op jit(solution)/shard_map/ppermute | solution.py:14
  23.1 0.5 fusion.23
  23.6 6.6 %slice_reduce_fusion.1 = (f32[2,16,8192]{2,1,0:T(8,128)}, f32[2,16,8192]{2,1,0:T(8,128)S(1)}) fusion(f32[2,2,16,8192]{3,1,2,0:T(2,128)S(1)} %fusion.23), kind=kLoop, calls=%fused_computation.27 | loop fusion | bytes 4194304 | tf_op jit(solution)/shard_map/slice | solution.py:90
  30.2 2.2 %reshape_squeeze.6 = f32[2,16,128,64]{3,2,1,0:T(8,128)S(1)} reshape(f32[2,16,8192]{2,1,0:T(8,128)} %get-tuple-element.17) | data formatting | bytes 2097152 | tf_op jit(solution)/shard_map/reshape;squeeze | solution.py:90
  32.4 4.4 %fusion.33 = f32[2,16,64,128]{3,2,1,0:T(8,128)} fusion(f32[2,16,128,64]{3,2,1,0:T(8,128)S(1)} %reshape_squeeze.6), kind=kOutput, calls=%fused_computation.58 | convolution fusion | flops 402882560 | bytes 2097152 | tf_op jit(solution)/shard_map/kn,pfnm->pfmk/dot_general | solution.py:62
  36.8 2.2 %reshape_squeeze.7 = f32[2,16,128,64]{3,2,1,0:T(8,128)} reshape(f32[2,16,8192]{2,1,0:T(8,128)S(1)} %get-tuple-element.18) | data formatting | bytes 2097152 | tf_op jit(solution)/shard_map/reshape;squeeze | solution.py:91
  39.0 0.0 copy-start
  39.0 0.0 copy-start.1
  39.0 5.2 %fusion.31 = f32[2,16,64,128]{3,2,1,0:T(8,128)S(1)} fusion(f32[2,16,128,64]{3,2,1,0:T(8,128)} %reshape_squeeze.7), kind=kOutput, calls=%fused_computation.56 | convolution fusion | flops 402882560 | bytes 2097152 | tf_op jit(solution)/shard_map/kn,pfnm->pfmk/dot_general | solution.py:62
  44.3 0.0 copy-done
  44.3 0.0 copy-done.1
  44.3 3.5 %convolution_subtract_fusion.1 = f32[2,16,64,128]{3,2,1,0:T(8,128)S(1)} fusion(f32[2,16,64,128]{3,2,1,0:T(8,128)S(1)} %copy-done.1, f32[2,16,128,64]{3,2,1,0:T(8,128)S(1)} %copy-done), kind=kOutput, calls=%fused_computation.23 | convolution fusion | flops 403144704 | bytes 3145728 | tf_op jit(solution)/shard_map/kn,pfnm->pfmk/dot_general | solution.py:62
  47.7 3.7 %convolution_add_fusion.1 = f32[2,16,64,128]{3,2,1,0:T(8,128)S(1)} fusion(f32[2,16,64,128]{3,2,1,0:T(8,128)S(1)} %fusion.31, f32[2,16,128,64]{3,2,1,0:T(8,128)S(1)} %reshape_squeeze.6), kind=kOutput, calls=%fused_computation.22 | convolution fusion | flops 403144704 | bytes 3145728 | tf_op jit(solution)/shard_map/kn,pfnm->pfmk/dot_general | solution.py:62
  51.5 1.3 %fusion.25 = f32[2,16,128,64]{2,3,1,0:T(8,128)S(1)} fusion(f32[2,16,64,128]{3,2,1,0:T(8,128)S(1)} %convolution_add_fusion.1, f32[2,16,64,128]{3,2,1,0:T(8,128)S(1)} %convolution_subtract_fusion.1, f32[64,128]{1,0:T(8,128)S(1)} %get-tuple-element.29, f32[64,128]{1,0:T(8,128)S(1)} %get-tuple-element.30), kind=kOutput, calls=%fused_computation.47 | convolution fusion | flops 202170368 | bytes 3211264 | tf_op jit(solution)/shard_map/jm,pfmk->pfjk/dot_general | solution.py:62
  52.8 1.3 %fusion.24 = f32[2,16,128,64]{2,3,1,0:T(8,128)S(1)} fusion(f32[2,16,64,128]{3,2,1,0:T(8,128)S(1)} %convolution_add_fusion.1, f32[2,16,64,128]{3,2,1,0:T(8,128)S(1)} %convolution_subtract_fusion.1, f32[64,128]{1,0:T(8,128)S(1)} %get-tuple-element.29, f32[64,128]{1,0:T(8,128)S(1)} %get-tuple-element.30), kind=kOutput, calls=%fused_computation.46 | convolution fusion | flops 202170368 | bytes 3211264 | tf_op jit(solution)/shard_map/jm,pfmk->pfjk/dot_general | solution.py:62
  54.1 1.4 %fusion.8 = f32[2,16,128,64]{2,3,1,0:T(8,128)S(1)} fusion(f32[2,16,128,64]{2,3,1,0:T(8,128)S(1)} %fusion.24, f32[2,16,64,128]{3,2,1,0:T(8,128)S(1)} %convolution_add_fusion.1, f32[2,16,64,128]{3,2,1,0:T(8,128)S(1)} %convolution_subtract_fusion.1, f32[64,128]{1,0:T(8,128)S(1)} %get-tuple-element.29, f32[64,128]{1,0:T(8,128)S(1)} %get-tuple-element.30), kind=kOutput, calls=%fused_computation.21 | convolution fusion | flops 202694656 | bytes 4259840 | tf_op jit(solution)/shard_map/jm,pfmk->pfjk/dot_general | solution.py:62
  55.5 1.5 %fusion.101 = (f32[2,64,128]{2,1,0:T(8,128)S(1)}, f32[2,16,64,128]{3,2,1,0:T(8,128)S(1)}) fusion(f32[2,16,128,64]{2,3,1,0:T(8,128)S(1)} %fusion.8, f32[2,16,128,64]{2,3,1,0:T(8,128)S(1)} %fusion.25, f32[2,16,64,128]{3,2,1,0:T(8,128)S(1)} %convolution_add_fusion.1, f32[2,16,64,128]{3,2,1,0:T(8,128)S(1)} %convolution_subtract_fusion.1, ...), kind=kOutput, calls=%fused_computation.126 | convolution fusion | flops 203464704 | bytes 5373952 | tf_op jit(solution)/shard_map/jm,pfmk->pfjk/dot_general | solution.py:62
  57.0 12.4 %all_gather.7 = f32[8,2,8192]{2,1,0:T(2,128)S(1)} all-gather(f32[1,2,8192]{2,1,0:T(2,128)S(1)} %all_gather.6), channel_id=1, replica_groups=mesh['beam'=32,'tm'=8] {'tm'}, dimensions={0}, use_global_device_ids=true | all-gather | bytes 589824 | tf_op jit(solution)/shard_map/all_gather | solution.py:18
  69.4 0.2 reduce_sum.28
  69.6 19.7 %all_to_all.10 = f32[32,2,256]{2,1,0:T(2,128)S(1)} all-to-all(f32[32,2,256]{2,1,0:T(2,128)S(1)} %bitcast.74), channel_id=1, replica_groups=mesh['beam'=32,'tm'=8] {'beam'}, dimensions={0} | all-to-all | bytes 131072 | tf_op jit(solution)/shard_map/all_to_all | solution.py:30
  89.3 0.7 broadcast_in_dim.5
  90.0 3.9 %all-to-all-start.1 = ((f32[32,2,256]{2,1,0:T(2,128)}), f32[32,2,256]{2,1,0:T(2,128)S(1)}, u32[]{:S(2)}, u32[]{:S(2)}) async-start(f32[32,2,256]{2,1,0:T(2,128)} %broadcast_in_dim.5), calls=%async_computation.1 | async-start | bytes 131072 | tf_op jit(solution)/shard_map/all_to_all | solution.py:42
  93.8 0.2 reshape.107
  94.0 8.7 %all-to-all-done.1 = f32[32,2,256]{2,1,0:T(2,128)S(1)} async-done(((f32[32,2,256]{2,1,0:T(2,128)}), f32[32,2,256]{2,1,0:T(2,128)S(1)}, u32[]{:S(2)}, u32[]{:S(2)}) %all-to-all-start.1) | async-done | bytes 65568 | tf_op jit(solution)/shard_map/all_to_all | solution.py:42
  102.7 1.1 %broadcast_subtract_fusion = f32[1,2,16,8192]{3,2,1,0:T(8,128)} fusion(f32[1,2,16,8192]{3,2,1,0:T(8,128)S(1)} %reshape.107, f32[2,8192]{1,0:T(2,128)S(1)} %bitcast.73), kind=kLoop, calls=%fused_computation.45 | loop fusion | flops 262144 | bytes 2162688 | tf_op jit(solution)/shard_map/sub | solution.py:113
  (4 shorter events, 0.1 us)
Async XLA Ops:
  7.4 15.7 %collective-permute-start = (f32[2,2,7,8192]{3,1,2,0:T(2,128)S(1)}, f32[2,2,7,8192]{3,1,2,0:T(2,128)S(1)}, u32[]{:S(2)}, u32[]{:S(2)}) collective-permute-start(f32[2,2,7,8192]{3,1,2,0:T(2,128)S(1)} %multiply_add_fusion.2), channel_id=1, source_target_pairs={{1,0},{2,1},{3,2},{4,3},{5,4},{6,5},{7,6},{9,8},{10,9},{11,10},{12... | collective-permute-start | bytes 2752520 | tf_op jit(solution)/shard_map/ppermute | solution.py:14
  39.0 5.2 %copy-start = (f32[2,16,128,64]{3,2,1,0:T(8,128)S(1)}, f32[2,16,128,64]{3,2,1,0:T(8,128)}, u32[]{:S(2)}) copy-start(f32[2,16,128,64]{3,2,1,0:T(8,128)} %reshape_squeeze.7) | copy-start | bytes 3145732
  39.0 5.2 %copy-start.1 = (f32[2,16,64,128]{3,2,1,0:T(8,128)S(1)}, f32[2,16,64,128]{3,2,1,0:T(8,128)}, u32[]{:S(2)}) copy-start(f32[2,16,64,128]{3,2,1,0:T(8,128)} %fusion.33) | copy-start | bytes 3145732
  90.0 12.7 %all-to-all-start.1 = ((f32[32,2,256]{2,1,0:T(2,128)}), f32[32,2,256]{2,1,0:T(2,128)S(1)}, u32[]{:S(2)}, u32[]{:S(2)}) async-start(f32[32,2,256]{2,1,0:T(2,128)} %broadcast_in_dim.5), calls=%async_computation.1 | async-start | bytes 131072 | tf_op jit(solution)/shard_map/all_to_all | solution.py:42
where the time goes:
time: 105 us; the launch traced here: 104 us
  blocking collectives  32.1 us (31%)
  matrix products  22.3 us (21%)
  local copies, waits for them, and re-layouts  17.6 us (17%)
  waiting for transfers between devices  11.8 us (11%)
  other arithmetic  10.8 us (10%)
  starting transfers between devices  9 us (9%)
    dot_general x8, matrix products, apply(): return jnp.einsum(form, table, values, precision=lax.Precision.HIGHEST)  22.3 us
    all_to_all x1, blocking collectives, summed_on_arrival(): lax.all_to_all(blocks, axis, split_axis=0, concat_axis=0, tiled=True)  19.7 us
    all_gather x1, blocking collectives, total_of_pieces(): blocks = lax.all_gather(x, axis)  12.4 us
    add x2, other arithmetic, tap_sum(): result + filter_taps[tap_index] * source[:, :, tap_index:tap_index + count]  8.78 us
    all_to_all x1, waiting for transfers between devices, sent_to_all(): lax.all_to_all(jnp.broadcast_to(x[None], (devices, *x.shape)), axis, 0, 0...  8.67 us
    slice x1, local copies, waits for them, and re-layouts, body(): grid_real = filtered[:, 0].reshape(2, frames, RADIX, stride)  6.58 us
    ppermute x1, starting transfers between devices, passed_along(): return lax.ppermute(x, axis, pairs)  5.15 us
    all_to_all x1, starting transfers between devices, sent_to_all(): lax.all_to_all(jnp.broadcast_to(x[None], (devices, *x.shape)), axis, 0, 0...  3.86 us
  transfers between devices with their start and end apart: 2, of which 2 were waited for; matrix products, arithmetic and copies ran while one was open for 7% of the time, Pallas kernels for 0%

commit v1 on v0

v1 whole, which is shorter than its diff:
```python
import functools
import math

import jax
import jax.numpy as jnp
import ml_dtypes
import numpy as np
from jax import lax
from jax.experimental import pallas as pl
from jax.experimental.pallas import tpu as pltpu
from jax.sharding import PartitionSpec as P

LANES = 128
ROWS = 64
CHANNELS = ROWS * LANES
TAPS = 8
FRAMES = 16
HELD = 9
AHEAD = 4
BACK = 3
BOTH = ("beam", "tm")
X, Y, Z = 4, 4, 8

RING4 = ((1, 0, 3, 2), (3, 2, 1, 0))
RING8 = ((1, 0, 3, 2, 5, 4, 7, 6), (7, 2, 1, 4, 3, 6, 5, 0), (3, 6, 5, 0, 7, 2, 1, 4))


def place(z, x, y, core):
    return ((z * X + x) * Y + y) * 2 + core


def swap_pairs(axis, partner):
    pairs = []
    for z in range(Z):
        for x in range(X):
            for y in range(Y):
                there = {
                    "z": lambda: (partner[z], x, y),
                    "x": lambda: (z, partner[x], y),
                    "y": lambda: (z, x, partner[y]),
                }[axis]()
                pairs.append((place(z, x, y, 1), place(*there, 1)))
    return pairs


def in_two(table):
    high = table.astype(ml_dtypes.bfloat16)
    low = (table - high.astype(np.float64)).astype(ml_dtypes.bfloat16)
    return high, low


def dft_tables():
    q = np.arange(ROWS)
    angle = 2.0 * np.pi * (np.outer(q, q) % ROWS) / ROWS
    cos, sin = np.cos(angle), np.sin(angle)
    first = np.block([[cos, sin], [-sin, cos]])
    high, low = in_two(first)
    first = np.block([[high, high], [low, low]])
    lane = np.arange(LANES)
    order = np.concatenate([np.arange(0, LANES, 2), np.arange(1, LANES, 2)])
    angle = 2.0 * np.pi * (np.outer(order, lane) % LANES) / LANES
    cos, sin = np.cos(angle), np.sin(angle)
    second = np.block([[cos, sin], [-sin, cos]])
    second = np.concatenate(in_two(second), axis=0)
    angle = 2.0 * np.pi * np.outer(q, lane) / CHANNELS
    twist = np.stack([np.cos(angle), np.sin(angle)]).astype(np.float32)
    return first, second, twist


def halves(values):
    high = values.astype(jnp.bfloat16)
    low = (values - high.astype(jnp.float32)).astype(jnp.bfloat16)
    return high, low


def power_rows(frames, first_ref, second_ref, twist_ref):
    count = len(frames)
    cols = [jnp.concatenate([re, im], axis=0) for re, im in frames]
    high, low = halves(jnp.concatenate(cols, axis=1))
    both = jnp.dot(
        first_ref[...],
        jnp.concatenate([high, low], axis=0),
        preferred_element_type=jnp.float32,
    )
    section = both[: 2 * ROWS] + both[2 * ROWS :]
    cos, sin = twist_ref[0], twist_ref[1]
    rows = []
    for g in range(count):
        re = section[:ROWS, g * LANES : (g + 1) * LANES]
        im = section[ROWS:, g * LANES : (g + 1) * LANES]
        rows.append(jnp.concatenate([re * cos + im * sin, im * cos - re * sin], axis=1))
    high, low = halves(jnp.concatenate(rows, axis=0))
    across = (((1,), (1,)), ((), ()))
    table = second_ref[...]
    both = lax.dot_general(table, high, across, preferred_element_type=jnp.float32)
    both += lax.dot_general(table, low, across, preferred_element_type=jnp.float32)
    spec = both[: 2 * LANES] + both[2 * LANES :]
    re, im = spec[:LANES], spec[LANES:]
    powers = (re * re + im * im) * (1.0 / CHANNELS)
    left = lax.broadcasted_iota(jnp.int32, (ROWS, LANES), 1) < ROWS
    out = []
    for g in range(0, count, 2):
        even = powers[:ROWS, g * ROWS : (g + 2) * ROWS]
        odd = powers[ROWS:, g * ROWS : (g + 2) * ROWS]
        out.append(jnp.where(left, even, pltpu.roll(odd, ROWS, 1)))
        out.append(jnp.where(left, pltpu.roll(even, ROWS, 1), odd))
    return out


def held_kernel(volt_ref, taps_ref, first_ref, second_ref, twist_ref, pow_ref, part_ref, sum_ref, filt_ref):
    keep = lax.axis_index("tm") > 0

    def strip(s, _):
        at = pl.multiple_of(s * 64, 64)
        rows = pl.ds(pl.multiple_of(s * 8, 8), 8)
        taps = [taps_ref[pl.ds(at + t, 8, stride=8), :] for t in range(TAPS)]
        for p in range(2):
            for c in range(2):
                x = [volt_ref[p, c, f // 8, pl.ds(at + f % 8, 8, stride=8), :] for f in range(FRAMES)]
                for f in range(HELD + AHEAD):
                    total = taps[0] * x[f]
                    for t in range(1, min(TAPS, FRAMES - f)):
                        total = total + taps[t] * x[f + t]
                    if f < HELD:
                        filt_ref[p, c, f, rows, :] = total
                    else:
                        part_ref[p, c, f - HELD, rows, :] = total
                for j in range(BACK):
                    total = taps[BACK - j] * x[0]
                    for t in range(BACK - j + 1, TAPS):
                        total = total + taps[t] * x[t - BACK + j]
                    part_ref[p, c, AHEAD + j, rows, :] = jnp.where(keep, total, 0.0)
        return 0

    lax.fori_loop(0, ROWS // 8, strip, 0)
    sums = [None, None]
    for start in range(0, HELD, 2):
        which = [(p, f) for f in range(start, min(start + 2, HELD)) for p in range(2)]
        frames = [(filt_ref[p, 0, f], filt_ref[p, 1, f]) for p, f in which]
        for (p, f), power in zip(which, power_rows(frames, first_ref, second_ref, twist_ref)):
            pow_ref[p, f] = power
            sums[p] = power if sums[p] is None else sums[p] + power
    for p in range(2):
        sum_ref[p] = sums[p]


def rim_kernel(part_ref, later_ref, earlier_ref, taps_ref, first_ref, second_ref, twist_ref, had_ref, pow_ref, back_ref, sum_ref):
    taps = [taps_ref[pl.ds(t, ROWS, stride=8), :] for t in range(TAPS)]

    def finished(p, j):
        out = []
        for c in range(2):
            total = part_ref[p, c, j]
            if j < AHEAD:
                for i in range(j + 1):
                    t = FRAMES + i - HELD - j
                    total = total + taps[t] * later_ref[p, c, pl.ds(i, ROWS, stride=AHEAD), :]
            else:
                for t in range(BACK - (j - AHEAD)):
                    i = 4 - BACK + (j - AHEAD) + t
                    total = total + taps[t] * earlier_ref[p, c, pl.ds(i, ROWS, stride=4), :]
            out.append(total)
        return tuple(out)

    sums = [had_ref[0], had_ref[1]]
    for start in range(0, AHEAD + BACK, 2):
        which = [(p, j) for j in range(start, min(start + 2, AHEAD + BACK)) for p in range(2)]
        frames = [finished(p, j) for p, j in which]
        for (p, j), power in zip(which, power_rows(frames, first_ref, second_ref, twist_ref)):
            if j < AHEAD:
                pow_ref[p, j] = power
            else:
                back_ref[p, j - AHEAD] = power
            sums[p] = sums[p] + power
    for p in range(2):
        sum_ref[p * ROWS : (p + 1) * ROWS, :] = sums[p]


def clean_kernel(scale, held_ref, ahead_ref, back_ref, sum_ref, out_ref):
    for p in range(2):
        base = sum_ref[p * ROWS : (p + 1) * ROWS, :] * scale
        for f in range(FRAMES):
            if f < HELD:
                power = held_ref[p, f]
            elif f < HELD + AHEAD:
                power = ahead_ref[p, f - HELD]
            else:
                power = back_ref[p, f - HELD - AHEAD]
            out_ref[p, f // 8, pl.ds(f % 8, ROWS, stride=8), :] = power - base


def on_core(kernel, out_shape, scratch=(), cost=None):
    return lambda *args: pl.pallas_call(
        kernel,
        out_shape=[jax.ShapeDtypeStruct(s, jnp.float32) for s in out_shape],
        in_specs=[pl.BlockSpec(memory_space=pltpu.VMEM)] * len(args),
        out_specs=[pl.BlockSpec(memory_space=pltpu.VMEM)] * len(out_shape),
        scratch_shapes=[pltpu.VMEM(s, jnp.float32) for s in scratch],
        compiler_params=pltpu.CompilerParams(vmem_limit_bytes=16 << 20),
        cost_estimate=cost,
    )(*args)


def by_rows(x):
    lead, frames = x.shape[:-2], x.shape[-2]
    x = x.reshape(*lead, frames, ROWS, LANES)
    return jnp.swapaxes(x, -3, -2).reshape(*lead, ROWS * frames, LANES)


def total_over_all(sums):
    up = [(i, i + 1) for i in range(0, 2 * X * Y * Z, 2)]
    sums = sums + lax.ppermute(sums, BOTH, up)
    for axis, ring in (("y", RING4), ("x", RING4), ("z", RING8)):
        for partner in ring:
            sums = sums + lax.ppermute(sums, BOTH, swap_pairs(axis, partner))
    other = lax.ppermute(sums, BOTH, [(b, a) for a, b in up])
    return jnp.where(lax.axis_index("tm") % 2 == 1, sums, other)


def body(voltages, filter_taps):
    volts = voltages[0]
    first, second, twist = (jnp.asarray(t) for t in dft_tables())
    devices = lax.axis_size("tm")
    later = lax.ppermute(volts[:, :, :AHEAD], "tm", [(i, i - 1) for i in range(1, devices)])
    earlier = lax.ppermute(volts[:, :, FRAMES - 4 :], "tm", [(i, (i + 1) % devices) for i in range(devices)])
    tiles = by_rows(volts.reshape(2, 2, 2, 8, CHANNELS))
    taps = by_rows(filter_taps)
    held, part, had = on_core(
        held_kernel,
        [(2, HELD, ROWS, LANES), (2, 2, AHEAD + BACK, ROWS, LANES), (2, ROWS, LANES)],
        scratch=[(2, 2, HELD, ROWS, LANES)],
        cost=pl.CostEstimate(flops=2 * 10**9, bytes_accessed=6 << 20, transcendentals=0),
    )(tiles, taps, first, second, twist)
    ahead, back, sums = on_core(
        rim_kernel,
        [(2, AHEAD, ROWS, LANES), (2, BACK, ROWS, LANES), (2 * ROWS, LANES)],
    )(part, by_rows(later), by_rows(earlier), taps, first, second, twist, had)
    back = lax.ppermute(back, "tm", [(i, (i - 1) % devices) for i in range(devices)])
    total = total_over_all(sums)
    scale = 1.0 / (FRAMES * devices * lax.axis_size("beam"))
    (out,) = on_core(functools.partial(clean_kernel, scale), [(2, 2, 8 * ROWS, LANES)])(held, ahead, back, total)
    out = jnp.swapaxes(out.reshape(2, 2, ROWS, 8, LANES), 2, 3)
    return out.reshape(1, 2, FRAMES, CHANNELS)


def solution(mesh):
    placed = (P("beam", None, None, "tm", None), P())
    return jax.shard_map(
        body, mesh=mesh, in_specs=placed, out_specs=P("beam", None, "tm", None), check_vma=False
    )
```

time: 105 us -> 72.3 us (0.69)
  blocking collectives: 32.1 us -> 0 us
  starting transfers between devices: 9 us -> 36.2 us
  matrix products: 22.3 us -> 0 us
  waiting for transfers between devices: 11.8 us -> 24 us
  local copies, waits for them, and re-layouts: 17.6 us -> 5.52 us
  other arithmetic: 10.8 us -> 0.08 us
  Pallas kernels: 0 us -> 5.82 us
    ppermute x1 -> x12, starting transfers between devices: 5.15 us -> 36.2 us  [the longest x7 28.4 us: total_over_all(): sums = sums + lax.ppermute(sums, BOTH, swap_pairs(axis, partner))]
    dot_general x8 -> x0, matrix products: 22.3 us -> none  [apply(): return jnp.einsum(form, table, values, precision=lax.Precision.HIGHEST)]
    ppermute x1 -> x12, waiting for transfers between devices: 3.16 us -> 24 us  [the longest x7 15.6 us: total_over_all(): sums = sums + lax.ppermute(sums, BOTH, swap_pairs(axis, partner))]
    all_to_all x1 -> x0, blocking collectives: 19.7 us -> none  [summed_on_arrival(): lax.all_to_all(blocks, axis, split_axis=0, concat_axis=0, tiled=True)]
    all_gather x1 -> x0, blocking collectives: 12.4 us -> none  [total_of_pieces(): blocks = lax.all_gather(x, axis)]
    add x2 -> x8, other arithmetic: 8.78 us -> 0.07 us  [the longest x7 0.06 us: total_over_all(): sums = sums + lax.ppermute(sums, BOTH, swap_pairs(axis, partner))]
    all_to_all x1 -> x0, waiting for transfers between devices: 8.67 us -> none  [sent_to_all(): lax.all_to_all(jnp.broadcast_to(x[None], (devices, *x.shape)), axis, 0, 0...]
    slice x3 -> x1, local copies, waits for them, and re-layouts: 9.18 us -> 1.87 us  [body(): volts[:, :, FRAMES - 4:]]
  transfers between devices with their start and end apart: 2 -> 12, of which waited for: 2 -> 11; matrix products, arithmetic and copies ran while one was open for 7% -> 0% of each run, Pallas kernels for 0% -> 4%
where the time goes in v1:
time: 72.3 us; the launch traced here: 71.9 us
  starting transfers between devices  36.2 us (50%)
  waiting for transfers between devices  24 us (33%)
  Pallas kernels  5.82 us (8%)
  local copies, waits for them, and re-layouts  5.52 us (8%)
    ppermute x7, starting transfers between devices, total_over_all(): sums = sums + lax.ppermute(sums, BOTH, swap_pairs(axis, partner))  28.4 us
    ppermute x7, waiting for transfers between devices, total_over_all(): sums = sums + lax.ppermute(sums, BOTH, swap_pairs(axis, partner))  15.6 us
    pallas_call x3, Pallas kernels, on_core(): pl.pallas_call(kernel, out_shape=[jax.ShapeDtypeStruct(s, jnp.float32) fo...  5.82 us
    ppermute x1, waiting for transfers between devices, body(): lax.ppermute(back, 'tm', [(i, (i - 1) % devices) for i in range(devices)])  4.23 us
    unnamed x14, local copies, waits for them, and re-layouts  3.65 us
    ppermute x1, starting transfers between devices, body(): lax.ppermute(volts[:, :, FRAMES - 4:], 'tm', [(i, (i + 1) % devices) for...  2.7 us
    ppermute x1, starting transfers between devices, body(): lax.ppermute(volts[:, :, :AHEAD], 'tm', [(i, i - 1) for i in range(1, dev...  2.48 us
    slice x1, local copies, waits for them, and re-layouts, body(): volts[:, :, FRAMES - 4:]  1.87 us
  transfers between devices with their start and end apart: 12, of which 11 were waited for; matrix products, arithmetic and copies ran while one was open for 0% of the time, Pallas kernels for 4%

profile of v1, /device:TPU:1, one launch (start us, length us, event | category | flops | bytes accessed | tf_op | source)
XLA Modules:
  0.0 71.9 jit_solution(9806346542827929270)
XLA Ops:
  0.0 0.0 copy-start
  0.0 1.9 %fusion = (f32[2,2,4,8192]{3,2,1,0:T(4,128)S(1)}, f32[2,2,4,8192]{3,2,1,0:T(4,128)S(1)}) fusion(f32[2,2,16,8192]{3,2,1,0:T(8,128)} %bitcast.26), kind=kLoop, calls=%fused_computation.1 | loop fusion | bytes 2097152 | tf_op jit(solution)/shard_map/slice | solution.py:225
  1.9 2.7 %collective-permute-start.1 = (f32[2,2,4,8192]{3,2,1,0:T(4,128)S(1)}, f32[2,2,4,8192]{3,2,1,0:T(4,128)S(1)}, u32[]{:S(2)}, u32[]{:S(2)}) collective-permute-start(f32[2,2,4,8192]{3,2,1,0:T(4,128)S(1)} %get-tuple-element.17), channel_id=1, source_target_pairs={{0,1},{1,2},{2,3},{3,4},{4,5},{5,6},{6,7},{7,0},{8,9},{9,10},{10,1... | collective-permute-start | bytes 1572872 | tf_op jit(solution)/shard_map/ppermute | solution.py:225
  4.6 2.5 %collective-permute-start = (f32[2,2,4,8192]{3,2,1,0:T(4,128)S(1)}, f32[2,2,4,8192]{3,2,1,0:T(4,128)S(1)}, u32[]{:S(2)}, u32[]{:S(2)}) collective-permute-start(f32[2,2,4,8192]{3,2,1,0:T(4,128)S(1)} %get-tuple-element.18), channel_id=1, source_target_pairs={{1,0},{2,1},{3,2},{4,3},{5,4},{6,5},{7,6},{9,8},{10,9},{11,10},{12... | collective-permute-start | bytes 1572872 | tf_op jit(solution)/shard_map/ppermute | solution.py:224
  7.1 0.0 copy-done
  7.1 0.0 copy-start.1
  7.1 0.9 %copy-done.1 = f32[8,8192]{1,0:T(8,128)S(1)} copy-done((f32[8,8192]{1,0:T(8,128)S(1)}, f32[8,8192]{1,0:T(8,128)}, u32[]{:S(2)}) %copy-start.1) | copy-done | bytes 262168
  8.0 0.0 copy-start.3
  8.0 0.9 %copy-done.3 = bf16[512,256]{1,0:T(8,128)(2,1)S(1)} copy-done((bf16[512,256]{1,0:T(8,128)(2,1)S(1)}, bf16[512,256]{1,0:T(8,128)(2,1)}, u32[]{:S(2)}) %copy-start.3) | copy-done | bytes 262168
  9.0 0.0 copy-start.4
  9.0 0.9 %copy-done.4 = bf16[256,256]{1,0:T(8,128)(2,1)S(1)} copy-done((bf16[256,256]{1,0:T(8,128)(2,1)S(1)}, bf16[256,256]{1,0:T(8,128)(2,1)}, u32[]{:S(2)}) %copy-start.4) | copy-done | bytes 131096
  9.9 0.0 copy-start.6
  9.9 0.8 %copy-done.6 = f32[2,64,128]{2,1,0:T(8,128)S(1)} copy-done((f32[2,64,128]{2,1,0:T(8,128)S(1)}, f32[2,64,128]{2,1,0:T(8,128)}, u32[]{:S(2)}) %copy-start.6) | copy-done | bytes 65560
  10.7 0.0 copy-start.2
  10.7 0.0 copy-start.5
  10.7 2.8 %shard_map.55 = (f32[2,9,64,128]{3,2,1,0:T(8,128)S(1)}, f32[2,2,7,64,128]{4,3,2,1,0:T(8,128)S(1)}, f32[2,64,128]{2,1,0:T(8,128)S(1)}) custom-call(f32[2,2,2,512,128]{4,3,2,1,0:T(8,128)S(1)} %bitcast.27, f32[512,128]{1,0:T(8,128)S(1)} %bitcast.30, bf16[256,256]{1,0:T(8,128)(2,1)S(1)} %copy-done.4, bf16[512,256]{1,0:T(8,128)(2,1)S(1)} %copy-done.3, ...), custom_call_target="tpu_custom_call" | custom-call | flops 2000000000 | bytes 6291456 | tf_op jit(solution)/shard_map/pallas_call | solution.py:193
  13.5 0.0 collective-permute-done.1
  13.6 1.5 %collective-permute-done = f32[2,2,4,8192]{3,2,1,0:T(4,128)S(1)} collective-permute-done((f32[2,2,4,8192]{3,2,1,0:T(4,128)S(1)}, f32[2,2,4,8192]{3,2,1,0:T(4,128)S(1)}, u32[]{:S(2)}, u32[]{:S(2)}) %collective-permute-start) | collective-permute-done | bytes 524320 | tf_op jit(solution)/shard_map/ppermute | solution.py:224
  15.1 0.0 copy-done.2
  15.1 0.0 copy-done.5
  15.1 1.8 %shard_map.56 = (f32[2,4,64,128]{3,2,1,0:T(8,128)S(1)}, f32[2,3,64,128]{3,2,1,0:T(8,128)S(1)}, f32[128,128]{1,0:T(8,128)S(1)}) custom-call(f32[2,2,7,64,128]{4,3,2,1,0:T(8,128)S(1)} %get-tuple-element.12.part_ref, f32[2,2,256,128]{3,2,1,0:T(8,128)S(1)} %bitcast.29, f32[2,2,256,128]{3,2,1,0:T(8,128)S(1)} %bitcast.28, f32[512,128]{1,0:T(8,128)S(1)} %bitcast.31, ...), custom_call_target="tpu_custom_call" | custom-call | tf_op jit(solution)/shard_map/pallas_call | solution.py:193
  16.9 1.3 %collective-permute-start.3 = (f32[128,128]{1,0:T(8,128)S(1)}, f32[128,128]{1,0:T(8,128)S(1)}, u32[]{:S(2)}, u32[]{:S(2)}) collective-permute-start(f32[128,128]{1,0:T(8,128)S(1)} %get-tuple-element.16), channel_id=1, source_target_pairs={{0,1},{2,3},{4,5},{6,7},{8,9},{10,11},{12,13},{14,15},{16,17},{18,... | collective-permute-start | bytes 196616 | tf_op jit(solution)/shard_map/ppermute | solution.py:212
  18.2 1.8 %collective-permute-done.3 = f32[128,128]{1,0:T(8,128)S(1)} collective-permute-done((f32[128,128]{1,0:T(8,128)S(1)}, f32[128,128]{1,0:T(8,128)S(1)}, u32[]{:S(2)}, u32[]{:S(2)}) %collective-permute-start.3) | collective-permute-done | bytes 65568 | tf_op jit(solution)/shard_map/ppermute | solution.py:212
  20.0 3.2 %collective-permute-start.4 = (f32[128,128]{1,0:T(8,128)S(1)}, f32[128,128]{1,0:T(8,128)S(1)}, u32[]{:S(2)}, u32[]{:S(2)}) collective-permute-start(f32[128,128]{1,0:T(8,128)S(1)} %add.29), channel_id=1, source_target_pairs={{1,3},{3,1},{5,7},{7,5},{9,11},{11,9},{13,15},{15,13},{17,19},{19,... | collective-permute-start | bytes 196616 | tf_op jit(solution)/shard_map/ppermute | solution.py:215
  23.2 1.8 %collective-permute-done.4 = f32[128,128]{1,0:T(8,128)S(1)} collective-permute-done((f32[128,128]{1,0:T(8,128)S(1)}, f32[128,128]{1,0:T(8,128)S(1)}, u32[]{:S(2)}, u32[]{:S(2)}) %collective-permute-start.4) | collective-permute-done | bytes 65568 | tf_op jit(solution)/shard_map/ppermute | solution.py:215
  25.1 3.4 %collective-permute-start.5 = (f32[128,128]{1,0:T(8,128)S(1)}, f32[128,128]{1,0:T(8,128)S(1)}, u32[]{:S(2)}, u32[]{:S(2)}) collective-permute-start(f32[128,128]{1,0:T(8,128)S(1)} %add.30), channel_id=1, source_target_pairs={{1,7},{3,5},{5,3},{7,1},{9,15},{11,13},{13,11},{15,9},{17,23},{19,... | collective-permute-start | bytes 196616 | tf_op jit(solution)/shard_map/ppermute | solution.py:215
  28.4 2.9 %collective-permute-done.5 = f32[128,128]{1,0:T(8,128)S(1)} collective-permute-done((f32[128,128]{1,0:T(8,128)S(1)}, f32[128,128]{1,0:T(8,128)S(1)}, u32[]{:S(2)}, u32[]{:S(2)}) %collective-permute-start.5) | collective-permute-done | bytes 65568 | tf_op jit(solution)/shard_map/ppermute | solution.py:215
  31.3 3.1 %collective-permute-start.6 = (f32[128,128]{1,0:T(8,128)S(1)}, f32[128,128]{1,0:T(8,128)S(1)}, u32[]{:S(2)}, u32[]{:S(2)}) collective-permute-start(f32[128,128]{1,0:T(8,128)S(1)} %add.31), channel_id=1, source_target_pairs={{1,9},{3,11},{5,13},{7,15},{9,1},{11,3},{13,5},{15,7},{17,25},{19,... | collective-permute-start | bytes 196616 | tf_op jit(solution)/shard_map/ppermute | solution.py:215
  34.4 1.9 %collective-permute-done.6 = f32[128,128]{1,0:T(8,128)S(1)} collective-permute-done((f32[128,128]{1,0:T(8,128)S(1)}, f32[128,128]{1,0:T(8,128)S(1)}, u32[]{:S(2)}, u32[]{:S(2)}) %collective-permute-start.6) | collective-permute-done | bytes 65568 | tf_op jit(solution)/shard_map/ppermute | solution.py:215
  36.3 4.4 %collective-permute-start.7 = (f32[128,128]{1,0:T(8,128)S(1)}, f32[128,128]{1,0:T(8,128)S(1)}, u32[]{:S(2)}, u32[]{:S(2)}) collective-permute-start(f32[128,128]{1,0:T(8,128)S(1)} %add.32), channel_id=1, source_target_pairs={{1,25},{3,27},{5,29},{7,31},{9,17},{11,19},{13,21},{15,23},{17,9},... | collective-permute-start | bytes 196616 | tf_op jit(solution)/shard_map/ppermute | solution.py:215
  40.7 1.8 %collective-permute-done.7 = f32[128,128]{1,0:T(8,128)S(1)} collective-permute-done((f32[128,128]{1,0:T(8,128)S(1)}, f32[128,128]{1,0:T(8,128)S(1)}, u32[]{:S(2)}, u32[]{:S(2)}) %collective-permute-start.7) | collective-permute-done | bytes 65568 | tf_op jit(solution)/shard_map/ppermute | solution.py:215
  42.5 3.5 %collective-permute-start.8 = (f32[128,128]{1,0:T(8,128)S(1)}, f32[128,128]{1,0:T(8,128)S(1)}, u32[]{:S(2)}, u32[]{:S(2)}) collective-permute-start(f32[128,128]{1,0:T(8,128)S(1)} %add.33), channel_id=1, source_target_pairs={{1,33},{3,35},{5,37},{7,39},{9,41},{11,43},{13,45},{15,47},{17,49}... | collective-permute-start | bytes 196616 | tf_op jit(solution)/shard_map/ppermute | solution.py:215
  46.1 1.6 %collective-permute-done.8 = f32[128,128]{1,0:T(8,128)S(1)} collective-permute-done((f32[128,128]{1,0:T(8,128)S(1)}, f32[128,128]{1,0:T(8,128)S(1)}, u32[]{:S(2)}, u32[]{:S(2)}) %collective-permute-start.8) | collective-permute-done | bytes 65568 | tf_op jit(solution)/shard_map/ppermute | solution.py:215
  47.8 7.3 %collective-permute-start.9 = (f32[128,128]{1,0:T(8,128)S(1)}, f32[128,128]{1,0:T(8,128)S(1)}, u32[]{:S(2)}, u32[]{:S(2)}) collective-permute-start(f32[128,128]{1,0:T(8,128)S(1)} %add.34), channel_id=1, source_target_pairs={{1,225},{3,227},{5,229},{7,231},{9,233},{11,235},{13,237},{15,239}... | collective-permute-start | bytes 196616 | tf_op jit(solution)/shard_map/ppermute | solution.py:215
  55.1 1.6 %collective-permute-done.9 = f32[128,128]{1,0:T(8,128)S(1)} collective-permute-done((f32[128,128]{1,0:T(8,128)S(1)}, f32[128,128]{1,0:T(8,128)S(1)}, u32[]{:S(2)}, u32[]{:S(2)}) %collective-permute-start.9) | collective-permute-done | bytes 65568 | tf_op jit(solution)/shard_map/ppermute | solution.py:215
  56.7 3.5 %collective-permute-start.10 = (f32[128,128]{1,0:T(8,128)S(1)}, f32[128,128]{1,0:T(8,128)S(1)}, u32[]{:S(2)}, u32[]{:S(2)}) collective-permute-start(f32[128,128]{1,0:T(8,128)S(1)} %add.35), channel_id=1, source_target_pairs={{1,97},{3,99},{5,101},{7,103},{9,105},{11,107},{13,109},{15,111},{... | collective-permute-start | bytes 196616 | tf_op jit(solution)/shard_map/ppermute | solution.py:215
  60.2 4.0 %collective-permute-done.10 = f32[128,128]{1,0:T(8,128)S(1)} collective-permute-done((f32[128,128]{1,0:T(8,128)S(1)}, f32[128,128]{1,0:T(8,128)S(1)}, u32[]{:S(2)}, u32[]{:S(2)}) %collective-permute-start.10) | collective-permute-done | bytes 65568 | tf_op jit(solution)/shard_map/ppermute | solution.py:215
  64.2 1.3 %collective-permute-start.11 = (f32[128,128]{1,0:T(8,128)S(1)}, f32[128,128]{1,0:T(8,128)S(1)}, u32[]{:S(2)}, u32[]{:S(2)}) collective-permute-start(f32[128,128]{1,0:T(8,128)S(1)} %add.36), channel_id=1, source_target_pairs={{1,0},{3,2},{5,4},{7,6},{9,8},{11,10},{13,12},{15,14},{17,16},{19,... | collective-permute-start | bytes 196616 | tf_op jit(solution)/shard_map/ppermute | solution.py:216
  65.5 0.0 collective-permute-start.2
  65.6 0.8 %collective-permute-done.11 = f32[128,128]{1,0:T(8,128)S(1)} collective-permute-done((f32[128,128]{1,0:T(8,128)S(1)}, f32[128,128]{1,0:T(8,128)S(1)}, u32[]{:S(2)}, u32[]{:S(2)}) %collective-permute-start.11) | collective-permute-done | bytes 65568 | tf_op jit(solution)/shard_map/ppermute | solution.py:216
  66.4 4.2 %collective-permute-done.2.back_ref = f32[2,3,64,128]{3,2,1,0:T(8,128)S(1)} collective-permute-done((f32[2,3,64,128]{3,2,1,0:T(8,128)S(1)}, f32[2,3,64,128]{3,2,1,0:T(8,128)S(1)}, u32[]{:S(2)}, u32[]{:S(2)}) %collective-permute-start.2) | collective-permute-done | bytes 196640 | tf_op jit(solution)/shard_map/ppermute | solution.py:238
  70.6 1.2 %shard_map.57 = f32[2,2,512,128]{3,2,1,0:T(8,128)} custom-call(f32[2,9,64,128]{3,2,1,0:T(8,128)S(1)} %get-tuple-element.11.held_ref, f32[2,4,64,128]{3,2,1,0:T(8,128)S(1)} %get-tuple-element.14.ahead_ref, f32[2,3,64,128]{3,2,1,0:T(8,128)S(1)} %collective-permute-done.2.back_ref, f32[128,128]{1,0:T(8,128)S(1)} %broadcast_select_fusion.sum_ref), custom_call_target="tpu_custom_call" | custom-call | tf_op jit(solution)/shard_map/pallas_call | solution.py:193
  (9 shorter events, 0.1 us)
Async XLA Ops:
  0.0 7.1 %copy-start = (f32[1,2,2,16,8192]{4,3,2,1,0:T(8,128)S(1)}, f32[1,2,2,16,8192]{4,3,2,1,0:T(8,128)}, u32[]{:S(2)}) copy-start(f32[1,2,2,16,8192]{4,3,2,1,0:T(8,128)} %param.5) | copy-start | bytes 6291460
  1.9 11.7 %collective-permute-start.1 = (f32[2,2,4,8192]{3,2,1,0:T(4,128)S(1)}, f32[2,2,4,8192]{3,2,1,0:T(4,128)S(1)}, u32[]{:S(2)}, u32[]{:S(2)}) collective-permute-start(f32[2,2,4,8192]{3,2,1,0:T(4,128)S(1)} %get-tuple-element.17), channel_id=1, source_target_pairs={{0,1},{1,2},{2,3},{3,4},{4,5},{5,6},{6,7},{7,0},{8,9},{9,10},{10,1... | collective-permute-start | bytes 1572872 | tf_op jit(solution)/shard_map/ppermute | solution.py:225
  4.6 10.5 %collective-permute-start = (f32[2,2,4,8192]{3,2,1,0:T(4,128)S(1)}, f32[2,2,4,8192]{3,2,1,0:T(4,128)S(1)}, u32[]{:S(2)}, u32[]{:S(2)}) collective-permute-start(f32[2,2,4,8192]{3,2,1,0:T(4,128)S(1)} %get-tuple-element.18), channel_id=1, source_target_pairs={{1,0},{2,1},{3,2},{4,3},{5,4},{6,5},{7,6},{9,8},{10,9},{11,10},{12... | collective-permute-start | bytes 1572872 | tf_op jit(solution)/shard_map/ppermute | solution.py:224
  7.1 1.0 %copy-start.1 = (f32[8,8192]{1,0:T(8,128)S(1)}, f32[8,8192]{1,0:T(8,128)}, u32[]{:S(2)}) copy-start(f32[8,8192]{1,0:T(8,128)} %param.6) | copy-start | bytes 786436
  8.0 0.9 %copy-start.3 = (bf16[512,256]{1,0:T(8,128)(2,1)S(1)}, bf16[512,256]{1,0:T(8,128)(2,1)}, u32[]{:S(2)}) copy-start(bf16[512,256]{1,0:T(8,128)(2,1)} %constant.25.clone.second_ref) | copy-start | bytes 786436
  9.0 0.9 %copy-start.4 = (bf16[256,256]{1,0:T(8,128)(2,1)S(1)}, bf16[256,256]{1,0:T(8,128)(2,1)}, u32[]{:S(2)}) copy-start(bf16[256,256]{1,0:T(8,128)(2,1)} %constant.24.clone.first_ref) | copy-start | bytes 393220
  9.9 0.8 %copy-start.6 = (f32[2,64,128]{2,1,0:T(8,128)S(1)}, f32[2,64,128]{2,1,0:T(8,128)}, u32[]{:S(2)}) copy-start(f32[2,64,128]{2,1,0:T(8,128)} %constant.26.clone.twist_ref) | copy-start | bytes 196612
  10.7 4.3 %copy-start.2 = (f32[8,8192]{1,0:T(8,128)S(1)}, f32[8,8192]{1,0:T(8,128)}, u32[]{:S(2)}) copy-start(f32[8,8192]{1,0:T(8,128)} %param.6) | copy-start | bytes 786436
  10.7 4.3 %copy-start.5 = (bf16[256,256]{1,0:T(8,128)(2,1)S(1)}, bf16[256,256]{1,0:T(8,128)(2,1)}, u32[]{:S(2)}) copy-start(bf16[256,256]{1,0:T(8,128)(2,1)} %constant.24.clone.first_ref) | copy-start | bytes 393220
  16.9 3.1 %collective-permute-start.3 = (f32[128,128]{1,0:T(8,128)S(1)}, f32[128,128]{1,0:T(8,128)S(1)}, u32[]{:S(2)}, u32[]{:S(2)}) collective-permute-start(f32[128,128]{1,0:T(8,128)S(1)} %get-tuple-element.16), channel_id=1, source_target_pairs={{0,1},{2,3},{4,5},{6,7},{8,9},{10,11},{12,13},{14,15},{16,17},{18,... | collective-permute-start | bytes 196616 | tf_op jit(solution)/shard_map/ppermute | solution.py:212
  20.0 5.0 %collective-permute-start.4 = (f32[128,128]{1,0:T(8,128)S(1)}, f32[128,128]{1,0:T(8,128)S(1)}, u32[]{:S(2)}, u32[]{:S(2)}) collective-permute-start(f32[128,128]{1,0:T(8,128)S(1)} %add.29), channel_id=1, source_target_pairs={{1,3},{3,1},{5,7},{7,5},{9,11},{11,9},{13,15},{15,13},{17,19},{19,... | collective-permute-start | bytes 196616 | tf_op jit(solution)/shard_map/ppermute | solution.py:215
  25.1 6.2 %collective-permute-start.5 = (f32[128,128]{1,0:T(8,128)S(1)}, f32[128,128]{1,0:T(8,128)S(1)}, u32[]{:S(2)}, u32[]{:S(2)}) collective-permute-start(f32[128,128]{1,0:T(8,128)S(1)} %add.30), channel_id=1, source_target_pairs={{1,7},{3,5},{5,3},{7,1},{9,15},{11,13},{13,11},{15,9},{17,23},{19,... | collective-permute-start | bytes 196616 | tf_op jit(solution)/shard_map/ppermute | solution.py:215
  31.3 5.0 %collective-permute-start.6 = (f32[128,128]{1,0:T(8,128)S(1)}, f32[128,128]{1,0:T(8,128)S(1)}, u32[]{:S(2)}, u32[]{:S(2)}) collective-permute-start(f32[128,128]{1,0:T(8,128)S(1)} %add.31), channel_id=1, source_target_pairs={{1,9},{3,11},{5,13},{7,15},{9,1},{11,3},{13,5},{15,7},{17,25},{19,... | collective-permute-start | bytes 196616 | tf_op jit(solution)/shard_map/ppermute | solution.py:215
  36.3 6.2 %collective-permute-start.7 = (f32[128,128]{1,0:T(8,128)S(1)}, f32[128,128]{1,0:T(8,128)S(1)}, u32[]{:S(2)}, u32[]{:S(2)}) collective-permute-start(f32[128,128]{1,0:T(8,128)S(1)} %add.32), channel_id=1, source_target_pairs={{1,25},{3,27},{5,29},{7,31},{9,17},{11,19},{13,21},{15,23},{17,9},... | collective-permute-start | bytes 196616 | tf_op jit(solution)/shard_map/ppermute | solution.py:215
  42.5 5.2 %collective-permute-start.8 = (f32[128,128]{1,0:T(8,128)S(1)}, f32[128,128]{1,0:T(8,128)S(1)}, u32[]{:S(2)}, u32[]{:S(2)}) collective-permute-start(f32[128,128]{1,0:T(8,128)S(1)} %add.33), channel_id=1, source_target_pairs={{1,33},{3,35},{5,37},{7,39},{9,41},{11,43},{13,45},{15,47},{17,49}... | collective-permute-start | bytes 196616 | tf_op jit(solution)/shard_map/ppermute | solution.py:215
  47.8 8.9 %collective-permute-start.9 = (f32[128,128]{1,0:T(8,128)S(1)}, f32[128,128]{1,0:T(8,128)S(1)}, u32[]{:S(2)}, u32[]{:S(2)}) collective-permute-start(f32[128,128]{1,0:T(8,128)S(1)} %add.34), channel_id=1, source_target_pairs={{1,225},{3,227},{5,229},{7,231},{9,233},{11,235},{13,237},{15,239}... | collective-permute-start | bytes 196616 | tf_op jit(solution)/shard_map/ppermute | solution.py:215
  56.7 7.5 %collective-permute-start.10 = (f32[128,128]{1,0:T(8,128)S(1)}, f32[128,128]{1,0:T(8,128)S(1)}, u32[]{:S(2)}, u32[]{:S(2)}) collective-permute-start(f32[128,128]{1,0:T(8,128)S(1)} %add.35), channel_id=1, source_target_pairs={{1,97},{3,99},{5,101},{7,103},{9,105},{11,107},{13,109},{15,111},{... | collective-permute-start | bytes 196616 | tf_op jit(solution)/shard_map/ppermute | solution.py:215
  64.2 2.2 %collective-permute-start.11 = (f32[128,128]{1,0:T(8,128)S(1)}, f32[128,128]{1,0:T(8,128)S(1)}, u32[]{:S(2)}, u32[]{:S(2)}) collective-permute-start(f32[128,128]{1,0:T(8,128)S(1)} %add.36), channel_id=1, source_target_pairs={{1,0},{3,2},{5,4},{7,6},{9,8},{11,10},{13,12},{15,14},{17,16},{19,... | collective-permute-start | bytes 196616 | tf_op jit(solution)/shard_map/ppermute | solution.py:216
  65.5 5.1 %collective-permute-start.2 = (f32[2,3,64,128]{3,2,1,0:T(8,128)S(1)}, f32[2,3,64,128]{3,2,1,0:T(8,128)S(1)}, u32[]{:S(2)}, u32[]{:S(2)}) collective-permute-start(f32[2,3,64,128]{3,2,1,0:T(8,128)S(1)} %get-tuple-element.15), channel_id=1, source_target_pairs={{0,7},{1,0},{2,1},{3,2},{4,3},{5,4},{6,5},{7,6},{8,15},{9,8},{10,9... | collective-permute-start | bytes 589832 | tf_op jit(solution)/shard_map/ppermute | solution.py:238

commit v2 on v1

--- a/solution.py
+++ b/solution.py
@@ -39,8 +39,13 @@
                     "x": lambda: (z, partner[x], y),
                     "y": lambda: (z, x, partner[y]),
                 }[axis]()
-                pairs.append((place(z, x, y, 1), place(*there, 1)))
+                pairs += [(place(z, x, y, c), place(*there, 1 - c)) for c in range(2)]
     return pairs
+
+
+def kept_half():
+    tm, beam = lax.axis_index("tm"), lax.axis_index("beam")
+    return (tm % 2 + tm // 2 + beam % X + beam // X) % 2
 
 
 def in_two(table):
@@ -144,7 +149,7 @@
         sum_ref[p] = sums[p]
 
 
-def rim_kernel(part_ref, later_ref, earlier_ref, taps_ref, first_ref, second_ref, twist_ref, had_ref, pow_ref, back_ref, sum_ref):
+def rim_kernel(part_ref, later_ref, earlier_ref, taps_ref, first_ref, second_ref, twist_ref, had_ref, pow_ref, back_ref, mine_ref, send_ref):
     taps = [taps_ref[pl.ds(t, ROWS, stride=8), :] for t in range(TAPS)]
 
     def finished(p, j):
@@ -172,13 +177,16 @@
             else:
                 back_ref[p, j - AHEAD] = power
             sums[p] = sums[p] + power
+    keeps_second = kept_half() == 1
+    mine_ref[...] = jnp.where(keeps_second, sums[1], sums[0])
+    send_ref[...] = jnp.where(keeps_second, sums[0], sums[1])
+
+
+def clean_kernel(scale, held_ref, ahead_ref, back_ref, mine_ref, other_ref, out_ref):
+    keeps_second = kept_half() == 1
+    mine, other = mine_ref[...] * scale, other_ref[...] * scale
     for p in range(2):
-        sum_ref[p * ROWS : (p + 1) * ROWS, :] = sums[p]
-
-
-def clean_kernel(scale, held_ref, ahead_ref, back_ref, sum_ref, out_ref):
-    for p in range(2):
-        base = sum_ref[p * ROWS : (p + 1) * ROWS, :] * scale
+        base = jnp.where(keeps_second, mine, other) if p else jnp.where(keeps_second, other, mine)
         for f in range(FRAMES):
             if f < HELD:
                 power = held_ref[p, f]
@@ -207,14 +215,19 @@
     return jnp.swapaxes(x, -3, -2).reshape(*lead, ROWS * frames, LANES)
 
 
-def total_over_all(sums):
-    up = [(i, i + 1) for i in range(0, 2 * X * Y * Z, 2)]
-    sums = sums + lax.ppermute(sums, BOTH, up)
-    for axis, ring in (("y", RING4), ("x", RING4), ("z", RING8)):
-        for partner in ring:
-            sums = sums + lax.ppermute(sums, BOTH, swap_pairs(axis, partner))
-    other = lax.ppermute(sums, BOTH, [(b, a) for a, b in up])
-    return jnp.where(lax.axis_index("tm") % 2 == 1, sums, other)
+def total_over_all(mine, send, back):
+    cores = [(i, i ^ 1) for i in range(2 * X * Y * Z)]
+    left = [(i, (i - 1) % (2 * Y)) for i in range(2 * Y)]
+    sums = mine + lax.ppermute(send, BOTH, cores)
+    steps = [("y", r) for r in RING4] + [("x", r) for r in RING4] + [("z", r) for r in RING8]
+    for n, (axis, partner) in enumerate(steps):
+        if n == 1:
+            sums, back = lax.optimization_barrier((sums, back))
+            back = lax.ppermute(back, "tm", left)
+        sums = sums + lax.ppermute(sums, BOTH, swap_pairs(axis, partner))
+        if n == 4:
+            sums, back = lax.optimization_barrier((sums, back))
+    return sums, lax.ppermute(sums, BOTH, cores), back
 
 
 def body(voltages, filter_taps):
@@ -231,14 +244,13 @@
         scratch=[(2, 2, HELD, ROWS, LANES)],
         cost=pl.CostEstimate(flops=2 * 10**9, bytes_accessed=6 << 20, transcendentals=0),
     )(tiles, taps, first, second, twist)
-    ahead, back, sums = on_core(
+    ahead, back, mine, send = on_core(
         rim_kernel,
-        [(2, AHEAD, ROWS, LANES), (2, BACK, ROWS, LANES), (2 * ROWS, LANES)],
+        [(2, AHEAD, ROWS, LANES), (2, BACK, ROWS, LANES), (ROWS, LANES), (ROWS, LANES)],
     )(part, by_rows(later), by_rows(earlier), taps, first, second, twist, had)
-    back = lax.ppermute(back, "tm", [(i, (i - 1) % devices) for i in range(devices)])
-    total = total_over_all(sums)
+    mine, other, back = total_over_all(mine, send, back)
     scale = 1.0 / (FRAMES * devices * lax.axis_size("beam"))
-    (out,) = on_core(functools.partial(clean_kernel, scale), [(2, 2, 8 * ROWS, LANES)])(held, ahead, back, total)
+    (out,) = on_core(functools.partial(clean_kernel, scale), [(2, 2, 8 * ROWS, LANES)])(held, ahead, back, mine, other)
     out = jnp.swapaxes(out.reshape(2, 2, ROWS, 8, LANES), 2, 3)
     return out.reshape(1, 2, FRAMES, CHANNELS)
 

time: 72.3 us -> 55 us (0.76)
  starting transfers between devices: 36.2 us -> 24.6 us
  waiting for transfers between devices: 24 us -> 18.7 us
    ppermute x7, starting transfers between devices: 28.4 us -> 18.7 us  [total_over_all(): sums = sums + lax.ppermute(sums, BOTH, swap_pairs(axis, partner))]
    ppermute x3, waiting for transfers between devices: 6.92 us -> 2.06 us  [the longest x1 1.19 us: total_over_all(): sums = mine + lax.ppermute(send, BOTH, cores)]
    ppermute x3, starting transfers between devices: 2.6 us -> 0.65 us  [the longest x1 0.39 us: total_over_all(): return (sums, lax.ppermute(sums, BOTH, cores), back)]
  transfers between devices with their start and end apart: 12 -> 12, of which waited for: 11 -> 10; matrix products, arithmetic and copies ran while one was open for 0% -> 0% of each run, Pallas kernels for 4% -> 5%
where the time goes in v2:
time: 55 us; the launch traced here: 54.7 us
  starting transfers between devices  24.6 us (45%)
  waiting for transfers between devices  18.7 us (34%)
  Pallas kernels  5.83 us (11%)
  local copies, waits for them, and re-layouts  5.52 us (10%)
    ppermute x7, starting transfers between devices, total_over_all(): sums = sums + lax.ppermute(sums, BOTH, swap_pairs(axis, partner))  18.7 us
    ppermute x7, waiting for transfers between devices, total_over_all(): sums = sums + lax.ppermute(sums, BOTH, swap_pairs(axis, partner))  15.1 us
    pallas_call x3, Pallas kernels, on_core(): pl.pallas_call(kernel, out_shape=[jax.ShapeDtypeStruct(s, jnp.float32) fo...  5.83 us
    unnamed x14, local copies, waits for them, and re-layouts  3.65 us
    ppermute x1, starting transfers between devices, body(): lax.ppermute(volts[:, :, FRAMES - 4:], 'tm', [(i, (i + 1) % devices) for...  2.7 us
    ppermute x1, starting transfers between devices, body(): lax.ppermute(volts[:, :, :AHEAD], 'tm', [(i, i - 1) for i in range(1, dev...  2.48 us
    slice x1, local copies, waits for them, and re-layouts, body(): volts[:, :, FRAMES - 4:]  1.87 us
    ppermute x1, waiting for transfers between devices, body(): lax.ppermute(volts[:, :, :AHEAD], 'tm', [(i, i - 1) for i in range(1, dev...  1.51 us
  transfers between devices with their start and end apart: 12, of which 10 were waited for; matrix products, arithmetic and copies ran while one was open for 0% of the time, Pallas kernels for 5%

profile of v2, /device:TPU:1, one launch (start us, length us, event | category | flops | bytes accessed | tf_op | source)
XLA Modules:
  0.0 54.7 jit_solution(9314590118727428442)
XLA Ops:
  0.0 0.0 copy-start
  0.0 1.9 %fusion = (f32[2,2,4,8192]{3,2,1,0:T(4,128)S(1)}, f32[2,2,4,8192]{3,2,1,0:T(4,128)S(1)}) fusion(f32[2,2,16,8192]{3,2,1,0:T(8,128)} %bitcast.26), kind=kLoop, calls=%fused_computation | loop fusion | bytes 2097152 | tf_op jit(solution)/shard_map/slice | solution.py:238
  1.9 2.7 %collective-permute-start.1 = (f32[2,2,4,8192]{3,2,1,0:T(4,128)S(1)}, f32[2,2,4,8192]{3,2,1,0:T(4,128)S(1)}, u32[]{:S(2)}, u32[]{:S(2)}) collective-permute-start(f32[2,2,4,8192]{3,2,1,0:T(4,128)S(1)} %get-tuple-element.27), channel_id=1, source_target_pairs={{0,1},{1,2},{2,3},{3,4},{4,5},{5,6},{6,7},{7,0},{8,9},{9,10},{10,1... | collective-permute-start | bytes 1572872 | tf_op jit(solution)/shard_map/ppermute | solution.py:238
  4.6 2.5 %collective-permute-start = (f32[2,2,4,8192]{3,2,1,0:T(4,128)S(1)}, f32[2,2,4,8192]{3,2,1,0:T(4,128)S(1)}, u32[]{:S(2)}, u32[]{:S(2)}) collective-permute-start(f32[2,2,4,8192]{3,2,1,0:T(4,128)S(1)} %get-tuple-element.28), channel_id=1, source_target_pairs={{1,0},{2,1},{3,2},{4,3},{5,4},{6,5},{7,6},{9,8},{10,9},{11,10},{12... | collective-permute-start | bytes 1572872 | tf_op jit(solution)/shard_map/ppermute | solution.py:237
  7.1 0.0 copy-done
  7.1 0.0 copy-start.1
  7.1 0.9 %copy-done.1 = f32[8,8192]{1,0:T(8,128)S(1)} copy-done((f32[8,8192]{1,0:T(8,128)S(1)}, f32[8,8192]{1,0:T(8,128)}, u32[]{:S(2)}) %copy-start.1) | copy-done | bytes 262168
  8.0 0.0 copy-start.3
  8.0 0.9 %copy-done.3 = bf16[512,256]{1,0:T(8,128)(2,1)S(1)} copy-done((bf16[512,256]{1,0:T(8,128)(2,1)S(1)}, bf16[512,256]{1,0:T(8,128)(2,1)}, u32[]{:S(2)}) %copy-start.3) | copy-done | bytes 262168
  9.0 0.0 copy-start.4
  9.0 0.9 %copy-done.4 = bf16[256,256]{1,0:T(8,128)(2,1)S(1)} copy-done((bf16[256,256]{1,0:T(8,128)(2,1)S(1)}, bf16[256,256]{1,0:T(8,128)(2,1)}, u32[]{:S(2)}) %copy-start.4) | copy-done | bytes 131096
  9.9 0.0 copy-start.6
  9.9 0.8 %copy-done.6 = f32[2,64,128]{2,1,0:T(8,128)S(1)} copy-done((f32[2,64,128]{2,1,0:T(8,128)S(1)}, f32[2,64,128]{2,1,0:T(8,128)}, u32[]{:S(2)}) %copy-start.6) | copy-done | bytes 65560
  10.7 0.0 copy-start.2
  10.7 0.0 copy-start.5
  10.7 2.8 %shard_map.55 = (f32[2,9,64,128]{3,2,1,0:T(8,128)S(1)}, f32[2,2,7,64,128]{4,3,2,1,0:T(8,128)S(1)}, f32[2,64,128]{2,1,0:T(8,128)S(1)}) custom-call(f32[2,2,2,512,128]{4,3,2,1,0:T(8,128)S(1)} %bitcast.27, f32[512,128]{1,0:T(8,128)S(1)} %bitcast.30, bf16[256,256]{1,0:T(8,128)(2,1)S(1)} %copy-done.4, bf16[512,256]{1,0:T(8,128)(2,1)S(1)} %copy-done.3, ...), custom_call_target="tpu_custom_call" | custom-call | flops 2000000000 | bytes 6291456 | tf_op jit(solution)/shard_map/pallas_call | solution.py:201
  13.5 0.0 collective-permute-done.1
  13.6 1.5 %collective-permute-done = f32[2,2,4,8192]{3,2,1,0:T(4,128)S(1)} collective-permute-done((f32[2,2,4,8192]{3,2,1,0:T(4,128)S(1)}, f32[2,2,4,8192]{3,2,1,0:T(4,128)S(1)}, u32[]{:S(2)}, u32[]{:S(2)}) %collective-permute-start) | collective-permute-done | bytes 524320 | tf_op jit(solution)/shard_map/ppermute | solution.py:237
  15.1 0.0 copy-done.2
  15.1 0.0 copy-done.5
  15.1 1.8 %shard_map.56 = (f32[2,4,64,128]{3,2,1,0:T(8,128)S(1)}, f32[2,3,64,128]{3,2,1,0:T(8,128)S(1)}, f32[64,128]{1,0:T(8,128)S(1)}, f32[64,128]{1,0:T(8,128)S(1)}) custom-call(f32[2,2,7,64,128]{4,3,2,1,0:T(8,128)S(1)} %get-tuple-element.17.part_ref, f32[2,2,256,128]{3,2,1,0:T(8,128)S(1)} %bitcast.29, f32[2,2,256,128]{3,2,1,0:T(8,128)S(1)} %bitcast.28, ...), custom_call_target="tpu_custom_call" | custom-call | tf_op jit(solution)/shard_map/pallas_call | solution.py:201
  16.9 0.1 collective-permute-start.2
  17.0 1.2 %collective-permute-done.2 = f32[64,128]{1,0:T(8,128)S(1)} collective-permute-done((f32[64,128]{1,0:T(8,128)S(1)}, f32[64,128]{1,0:T(8,128)S(1)}, u32[]{:S(2)}, u32[]{:S(2)}) %collective-permute-start.2) | collective-permute-done | bytes 32800 | tf_op jit(solution)/shard_map/ppermute | solution.py:221
  18.2 1.3 %collective-permute-start.3 = (f32[64,128]{1,0:T(8,128)S(1)}, f32[64,128]{1,0:T(8,128)S(1)}, u32[]{:S(2)}, u32[]{:S(2)}) collective-permute-start(f32[64,128]{1,0:T(8,128)S(1)} %add.24), channel_id=1, source_target_pairs={{0,3},{1,2},{2,1},{3,0},{4,7},{5,6},{6,5},{7,4},{8,11},{9,10},{10,... | collective-permute-start | bytes 98312 | tf_op jit(solution)/shard_map/ppermute | solution.py:227
  19.5 2.0 %collective-permute-done.3 = f32[64,128]{1,0:T(8,128)S(1)} collective-permute-done((f32[64,128]{1,0:T(8,128)S(1)}, f32[64,128]{1,0:T(8,128)S(1)}, u32[]{:S(2)}, u32[]{:S(2)}) %collective-permute-start.3) | collective-permute-done | bytes 32800 | tf_op jit(solution)/shard_map/ppermute | solution.py:227
  21.5 0.2 collective-permute-start.8
  21.7 3.0 %collective-permute-start.4 = (f32[64,128]{1,0:T(8,128)S(1)}, f32[64,128]{1,0:T(8,128)S(1)}, u32[]{:S(2)}, u32[]{:S(2)}) collective-permute-start(f32[64,128]{1,0:T(8,128)S(1)} %add.25), channel_id=1, source_target_pairs={{0,7},{1,6},{2,5},{3,4},{4,3},{5,2},{6,1},{7,0},{8,15},{9,14},{10,... | collective-permute-start | bytes 98312 | tf_op jit(solution)/shard_map/ppermute | solution.py:227
  24.7 1.6 %collective-permute-done.4 = f32[64,128]{1,0:T(8,128)S(1)} collective-permute-done((f32[64,128]{1,0:T(8,128)S(1)}, f32[64,128]{1,0:T(8,128)S(1)}, u32[]{:S(2)}, u32[]{:S(2)}) %collective-permute-start.4) | collective-permute-done | bytes 32800 | tf_op jit(solution)/shard_map/ppermute | solution.py:227
  26.3 2.5 %collective-permute-start.5 = (f32[64,128]{1,0:T(8,128)S(1)}, f32[64,128]{1,0:T(8,128)S(1)}, u32[]{:S(2)}, u32[]{:S(2)}) collective-permute-start(f32[64,128]{1,0:T(8,128)S(1)} %add.26), channel_id=1, source_target_pairs={{0,9},{1,8},{2,11},{3,10},{4,13},{5,12},{6,15},{7,14},{8,1},{9,0},... | collective-permute-start | bytes 98312 | tf_op jit(solution)/shard_map/ppermute | solution.py:227
  28.8 2.2 %collective-permute-done.5 = f32[64,128]{1,0:T(8,128)S(1)} collective-permute-done((f32[64,128]{1,0:T(8,128)S(1)}, f32[64,128]{1,0:T(8,128)S(1)}, u32[]{:S(2)}, u32[]{:S(2)}) %collective-permute-start.5) | collective-permute-done | bytes 32800 | tf_op jit(solution)/shard_map/ppermute | solution.py:227
  31.0 2.5 %collective-permute-start.6 = (f32[64,128]{1,0:T(8,128)S(1)}, f32[64,128]{1,0:T(8,128)S(1)}, u32[]{:S(2)}, u32[]{:S(2)}) collective-permute-start(f32[64,128]{1,0:T(8,128)S(1)} %add.27), channel_id=1, source_target_pairs={{0,25},{1,24},{2,27},{3,26},{4,29},{5,28},{6,31},{7,30},{8,17},{9,... | collective-permute-start | bytes 98312 | tf_op jit(solution)/shard_map/ppermute | solution.py:227
  33.4 2.2 %collective-permute-done.6 = f32[64,128]{1,0:T(8,128)S(1)} collective-permute-done((f32[64,128]{1,0:T(8,128)S(1)}, f32[64,128]{1,0:T(8,128)S(1)}, u32[]{:S(2)}, u32[]{:S(2)}) %collective-permute-start.6) | collective-permute-done | bytes 32800 | tf_op jit(solution)/shard_map/ppermute | solution.py:227
  35.6 1.9 %collective-permute-start.7 = (f32[64,128]{1,0:T(8,128)S(1)}, f32[64,128]{1,0:T(8,128)S(1)}, u32[]{:S(2)}, u32[]{:S(2)}) collective-permute-start(f32[64,128]{1,0:T(8,128)S(1)} %add.28), channel_id=1, source_target_pairs={{0,33},{1,32},{2,35},{3,34},{4,37},{5,36},{6,39},{7,38},{8,41},{9,... | collective-permute-start | bytes 98312 | tf_op jit(solution)/shard_map/ppermute | solution.py:227
  37.5 1.6 %collective-permute-done.7 = f32[64,128]{1,0:T(8,128)S(1)} collective-permute-done((f32[64,128]{1,0:T(8,128)S(1)}, f32[64,128]{1,0:T(8,128)S(1)}, u32[]{:S(2)}, u32[]{:S(2)}) %collective-permute-start.7) | collective-permute-done | bytes 32800 | tf_op jit(solution)/shard_map/ppermute | solution.py:227
  39.1 0.0 collective-permute-done.8.back_ref
  39.1 5.8 %collective-permute-start.9 = (f32[64,128]{1,0:T(8,128)S(1)}, f32[64,128]{1,0:T(8,128)S(1)}, u32[]{:S(2)}, u32[]{:S(2)}) collective-permute-start(f32[64,128]{1,0:T(8,128)S(1)} %add.29), channel_id=1, source_target_pairs={{0,225},{1,224},{2,227},{3,226},{4,229},{5,228},{6,231},{7,230},{8... | collective-permute-start | bytes 98312 | tf_op jit(solution)/shard_map/ppermute | solution.py:227
  44.9 1.6 %collective-permute-done.9 = f32[64,128]{1,0:T(8,128)S(1)} collective-permute-done((f32[64,128]{1,0:T(8,128)S(1)}, f32[64,128]{1,0:T(8,128)S(1)}, u32[]{:S(2)}, u32[]{:S(2)}) %collective-permute-start.9) | collective-permute-done | bytes 32800 | tf_op jit(solution)/shard_map/ppermute | solution.py:227
  46.5 1.7 %collective-permute-start.10 = (f32[64,128]{1,0:T(8,128)S(1)}, f32[64,128]{1,0:T(8,128)S(1)}, u32[]{:S(2)}, u32[]{:S(2)}) collective-permute-start(f32[64,128]{1,0:T(8,128)S(1)} %add.30), channel_id=1, source_target_pairs={{0,97},{1,96},{2,99},{3,98},{4,101},{5,100},{6,103},{7,102},{8,105... | collective-permute-start | bytes 98312 | tf_op jit(solution)/shard_map/ppermute | solution.py:227
  48.2 4.0 %collective-permute-done.10 = f32[64,128]{1,0:T(8,128)S(1)} collective-permute-done((f32[64,128]{1,0:T(8,128)S(1)}, f32[64,128]{1,0:T(8,128)S(1)}, u32[]{:S(2)}, u32[]{:S(2)}) %collective-permute-start.10) | collective-permute-done | bytes 32800 | tf_op jit(solution)/shard_map/ppermute | solution.py:227
  52.3 0.4 collective-permute-start.11
  52.7 0.9 %collective-permute-done.11.other_ref = f32[64,128]{1,0:T(8,128)S(1)} collective-permute-done((f32[64,128]{1,0:T(8,128)S(1)}, f32[64,128]{1,0:T(8,128)S(1)}, u32[]{:S(2)}, u32[]{:S(2)}) %collective-permute-start.11) | collective-permute-done | bytes 32800 | tf_op jit(solution)/shard_map/ppermute | solution.py:230
  53.5 1.2 %shard_map.57 = f32[2,2,512,128]{3,2,1,0:T(8,128)} custom-call(f32[2,9,64,128]{3,2,1,0:T(8,128)S(1)} %get-tuple-element.16.held_ref, f32[2,4,64,128]{3,2,1,0:T(8,128)S(1)} %get-tuple-element.19.ahead_ref, f32[2,3,64,128]{3,2,1,0:T(8,128)S(1)} %collective-permute-done.8.back_ref, f32[64,128]{1,0:T(8,128)S(1)} %add.31.mine_ref, ...), custom_call_target="tpu_custom_call" | custom-call | tf_op jit(solution)/shard_map/pallas_call | solution.py:201
  (8 shorter events, 0.0 us)
Async XLA Ops:
  0.0 7.1 %copy-start = (f32[1,2,2,16,8192]{4,3,2,1,0:T(8,128)S(1)}, f32[1,2,2,16,8192]{4,3,2,1,0:T(8,128)}, u32[]{:S(2)}) copy-start(f32[1,2,2,16,8192]{4,3,2,1,0:T(8,128)} %param.5) | copy-start | bytes 6291460
  1.9 11.7 %collective-permute-start.1 = (f32[2,2,4,8192]{3,2,1,0:T(4,128)S(1)}, f32[2,2,4,8192]{3,2,1,0:T(4,128)S(1)}, u32[]{:S(2)}, u32[]{:S(2)}) collective-permute-start(f32[2,2,4,8192]{3,2,1,0:T(4,128)S(1)} %get-tuple-element.27), channel_id=1, source_target_pairs={{0,1},{1,2},{2,3},{3,4},{4,5},{5,6},{6,7},{7,0},{8,9},{9,10},{10,1... | collective-permute-start | bytes 1572872 | tf_op jit(solution)/shard_map/ppermute | solution.py:238
  4.6 10.5 %collective-permute-start = (f32[2,2,4,8192]{3,2,1,0:T(4,128)S(1)}, f32[2,2,4,8192]{3,2,1,0:T(4,128)S(1)}, u32[]{:S(2)}, u32[]{:S(2)}) collective-permute-start(f32[2,2,4,8192]{3,2,1,0:T(4,128)S(1)} %get-tuple-element.28), channel_id=1, source_target_pairs={{1,0},{2,1},{3,2},{4,3},{5,4},{6,5},{7,6},{9,8},{10,9},{11,10},{12... | collective-permute-start | bytes 1572872 | tf_op jit(solution)/shard_map/ppermute | solution.py:237
  7.1 1.0 %copy-start.1 = (f32[8,8192]{1,0:T(8,128)S(1)}, f32[8,8192]{1,0:T(8,128)}, u32[]{:S(2)}) copy-start(f32[8,8192]{1,0:T(8,128)} %param.6) | copy-start | bytes 786436
  8.0 0.9 %copy-start.3 = (bf16[512,256]{1,0:T(8,128)(2,1)S(1)}, bf16[512,256]{1,0:T(8,128)(2,1)}, u32[]{:S(2)}) copy-start(bf16[512,256]{1,0:T(8,128)(2,1)} %constant.7.clone.second_ref) | copy-start | bytes 786436
  9.0 0.9 %copy-start.4 = (bf16[256,256]{1,0:T(8,128)(2,1)S(1)}, bf16[256,256]{1,0:T(8,128)(2,1)}, u32[]{:S(2)}) copy-start(bf16[256,256]{1,0:T(8,128)(2,1)} %constant.6.clone.first_ref) | copy-start | bytes 393220
  9.9 0.8 %copy-start.6 = (f32[2,64,128]{2,1,0:T(8,128)S(1)}, f32[2,64,128]{2,1,0:T(8,128)}, u32[]{:S(2)}) copy-start(f32[2,64,128]{2,1,0:T(8,128)} %constant.8.clone.twist_ref) | copy-start | bytes 196612
  10.7 4.3 %copy-start.2 = (f32[8,8192]{1,0:T(8,128)S(1)}, f32[8,8192]{1,0:T(8,128)}, u32[]{:S(2)}) copy-start(f32[8,8192]{1,0:T(8,128)} %param.6) | copy-start | bytes 786436
  10.7 4.3 %copy-start.5 = (bf16[256,256]{1,0:T(8,128)(2,1)S(1)}, bf16[256,256]{1,0:T(8,128)(2,1)}, u32[]{:S(2)}) copy-start(bf16[256,256]{1,0:T(8,128)(2,1)} %constant.6.clone.first_ref) | copy-start | bytes 393220
  16.9 1.3 %collective-permute-start.2 = (f32[64,128]{1,0:T(8,128)S(1)}, f32[64,128]{1,0:T(8,128)S(1)}, u32[]{:S(2)}, u32[]{:S(2)}) collective-permute-start(f32[64,128]{1,0:T(8,128)S(1)} %get-tuple-element.21), channel_id=1, source_target_pairs={{0,1},{1,0},{2,3},{3,2},{4,5},{5,4},{6,7},{7,6},{8,9},{9,8},{10,11... | collective-permute-start | bytes 98312 | tf_op jit(solution)/shard_map/ppermute | solution.py:221
  18.2 3.3 %collective-permute-start.3 = (f32[64,128]{1,0:T(8,128)S(1)}, f32[64,128]{1,0:T(8,128)S(1)}, u32[]{:S(2)}, u32[]{:S(2)}) collective-permute-start(f32[64,128]{1,0:T(8,128)S(1)} %add.24), channel_id=1, source_target_pairs={{0,3},{1,2},{2,1},{3,0},{4,7},{5,6},{6,5},{7,4},{8,11},{9,10},{10,... | collective-permute-start | bytes 98312 | tf_op jit(solution)/shard_map/ppermute | solution.py:227
  21.5 17.6 %collective-permute-start.8 = (f32[2,3,64,128]{3,2,1,0:T(8,128)S(1)}, f32[2,3,64,128]{3,2,1,0:T(8,128)S(1)}, u32[]{:S(2)}, u32[]{:S(2)}) collective-permute-start(f32[2,3,64,128]{3,2,1,0:T(8,128)S(1)} %get-tuple-element.24), channel_id=1, source_target_pairs={{0,7},{1,0},{2,1},{3,2},{4,3},{5,4},{6,5},{7,6},{8,15},{9,8},{10,9... | collective-permute-start | bytes 589832 | tf_op jit(solution)/shard_map/ppermute | solution.py:226
  21.7 4.6 %collective-permute-start.4 = (f32[64,128]{1,0:T(8,128)S(1)}, f32[64,128]{1,0:T(8,128)S(1)}, u32[]{:S(2)}, u32[]{:S(2)}) collective-permute-start(f32[64,128]{1,0:T(8,128)S(1)} %add.25), channel_id=1, source_target_pairs={{0,7},{1,6},{2,5},{3,4},{4,3},{5,2},{6,1},{7,0},{8,15},{9,14},{10,... | collective-permute-start | bytes 98312 | tf_op jit(solution)/shard_map/ppermute | solution.py:227
  26.3 4.6 %collective-permute-start.5 = (f32[64,128]{1,0:T(8,128)S(1)}, f32[64,128]{1,0:T(8,128)S(1)}, u32[]{:S(2)}, u32[]{:S(2)}) collective-permute-start(f32[64,128]{1,0:T(8,128)S(1)} %add.26), channel_id=1, source_target_pairs={{0,9},{1,8},{2,11},{3,10},{4,13},{5,12},{6,15},{7,14},{8,1},{9,0},... | collective-permute-start | bytes 98312 | tf_op jit(solution)/shard_map/ppermute | solution.py:227
  31.0 4.6 %collective-permute-start.6 = (f32[64,128]{1,0:T(8,128)S(1)}, f32[64,128]{1,0:T(8,128)S(1)}, u32[]{:S(2)}, u32[]{:S(2)}) collective-permute-start(f32[64,128]{1,0:T(8,128)S(1)} %add.27), channel_id=1, source_target_pairs={{0,25},{1,24},{2,27},{3,26},{4,29},{5,28},{6,31},{7,30},{8,17},{9,... | collective-permute-start | bytes 98312 | tf_op jit(solution)/shard_map/ppermute | solution.py:227
  35.6 3.5 %collective-permute-start.7 = (f32[64,128]{1,0:T(8,128)S(1)}, f32[64,128]{1,0:T(8,128)S(1)}, u32[]{:S(2)}, u32[]{:S(2)}) collective-permute-start(f32[64,128]{1,0:T(8,128)S(1)} %add.28), channel_id=1, source_target_pairs={{0,33},{1,32},{2,35},{3,34},{4,37},{5,36},{6,39},{7,38},{8,41},{9,... | collective-permute-start | bytes 98312 | tf_op jit(solution)/shard_map/ppermute | solution.py:227
  39.1 7.4 %collective-permute-start.9 = (f32[64,128]{1,0:T(8,128)S(1)}, f32[64,128]{1,0:T(8,128)S(1)}, u32[]{:S(2)}, u32[]{:S(2)}) collective-permute-start(f32[64,128]{1,0:T(8,128)S(1)} %add.29), channel_id=1, source_target_pairs={{0,225},{1,224},{2,227},{3,226},{4,229},{5,228},{6,231},{7,230},{8... | collective-permute-start | bytes 98312 | tf_op jit(solution)/shard_map/ppermute | solution.py:227
  46.5 5.8 %collective-permute-start.10 = (f32[64,128]{1,0:T(8,128)S(1)}, f32[64,128]{1,0:T(8,128)S(1)}, u32[]{:S(2)}, u32[]{:S(2)}) collective-permute-start(f32[64,128]{1,0:T(8,128)S(1)} %add.30), channel_id=1, source_target_pairs={{0,97},{1,96},{2,99},{3,98},{4,101},{5,100},{6,103},{7,102},{8,105... | collective-permute-start | bytes 98312 | tf_op jit(solution)/shard_map/ppermute | solution.py:227
  52.3 1.3 %collective-permute-start.11 = (f32[64,128]{1,0:T(8,128)S(1)}, f32[64,128]{1,0:T(8,128)S(1)}, u32[]{:S(2)}, u32[]{:S(2)}) collective-permute-start(f32[64,128]{1,0:T(8,128)S(1)} %add.31.mine_ref), channel_id=1, source_target_pairs={{0,1},{1,0},{2,3},{3,2},{4,5},{5,4},{6,7},{7,6},{8,9},{9,8},{10,11... | collective-permute-start | bytes 98312 | tf_op jit(solution)/shard_map/ppermute | solution.py:230

commit v3 on v2

--- a/solution.py
+++ b/solution.py
@@ -18,6 +18,7 @@
 HELD = 9
 AHEAD = 4
 BACK = 3
+SHORT = pl.CostEstimate(flops=1000, bytes_accessed=1000, transcendentals=0)
 BOTH = ("beam", "tm")
 X, Y, Z = 4, 4, 8
 
@@ -69,7 +70,7 @@
     second = np.concatenate(in_two(second), axis=0)
     angle = 2.0 * np.pi * np.outer(q, lane) / CHANNELS
     twist = np.stack([np.cos(angle), np.sin(angle)]).astype(np.float32)
-    return first, second, twist
+    return np.concatenate([first, second], axis=0), twist
 
 
 def halves(values):
@@ -78,12 +79,12 @@
     return high, low
 
 
-def power_rows(frames, first_ref, second_ref, twist_ref):
+def power_rows(frames, table_ref, twist_ref):
     count = len(frames)
     cols = [jnp.concatenate([re, im], axis=0) for re, im in frames]
     high, low = halves(jnp.concatenate(cols, axis=1))
     both = jnp.dot(
-        first_ref[...],
+        table_ref[: 4 * ROWS],
         jnp.concatenate([high, low], axis=0),
         preferred_element_type=jnp.float32,
     )
@@ -96,7 +97,7 @@
         rows.append(jnp.concatenate([re * cos + im * sin, im * cos - re * sin], axis=1))
     high, low = halves(jnp.concatenate(rows, axis=0))
     across = (((1,), (1,)), ((), ()))
-    table = second_ref[...]
+    table = table_ref[4 * ROWS :]
     both = lax.dot_general(table, high, across, preferred_element_type=jnp.float32)
     both += lax.dot_general(table, low, across, preferred_element_type=jnp.float32)
     spec = both[: 2 * LANES] + both[2 * LANES :]
@@ -112,10 +113,50 @@
     return out
 
 
-def held_kernel(volt_ref, taps_ref, first_ref, second_ref, twist_ref, pow_ref, part_ref, sum_ref, filt_ref):
+def rim_copies(volt_ref, out_ref, sems, last):
+    half, at = (1, 8 - AHEAD) if last else (0, 0)
+    return [
+        pltpu.make_async_copy(volt_ref.at[p, c, half, :, at : at + AHEAD, :], out_ref.at[p, c], sems.at[2 * p + c])
+        for p in range(2)
+        for c in range(2)
+    ]
+
+
+def rim_kernel(volt_ref, cross_ref, near_ref, sems):
+    for core in range(2):
+
+        @pl.when(lax.axis_index("tm") % 2 == core)
+        def _():
+            copies = rim_copies(volt_ref, near_ref, sems.at[0], core == 0)
+            copies += rim_copies(volt_ref, cross_ref, sems.at[1], core == 1)
+            for copy in copies:
+                copy.start()
+            for copy in copies:
+                copy.wait()
+
+
+def held_kernel(
+    volt_in, taps_in, table_in, twist_in,
+    pow_ref, part_ref, sum_ref, taps_ref, table_ref, twist_ref,
+    volt_ref, filt_ref, strip_sems, table_sems,
+):
+    def strip_copy(s):
+        rows = pl.ds(pl.multiple_of(s * 64, 64), 64)
+        return pltpu.make_async_copy(volt_in.at[:, :, :, rows, :], volt_ref.at[:, :, :, rows, :], strip_sems.at[s])
+
+    taps_copy = pltpu.make_async_copy(taps_in, taps_ref, table_sems.at[0])
+    table_copy = pltpu.make_async_copy(table_in, table_ref, table_sems.at[1])
+    twist_copy = pltpu.make_async_copy(twist_in, twist_ref, table_sems.at[2])
+    taps_copy.start()
+    for s in range(ROWS // 8):
+        strip_copy(s).start()
+    table_copy.start()
+    twist_copy.start()
+    taps_copy.wait()
     keep = lax.axis_index("tm") > 0
 
     def strip(s, _):
+        strip_copy(s).wait()
         at = pl.multiple_of(s * 64, 64)
         rows = pl.ds(pl.multiple_of(s * 8, 8), 8)
         taps = [taps_ref[pl.ds(at + t, 8, stride=8), :] for t in range(TAPS)]
@@ -138,48 +179,75 @@
         return 0
 
     lax.fori_loop(0, ROWS // 8, strip, 0)
+    table_copy.wait()
+    twist_copy.wait()
     sums = [None, None]
     for start in range(0, HELD, 2):
         which = [(p, f) for f in range(start, min(start + 2, HELD)) for p in range(2)]
         frames = [(filt_ref[p, 0, f], filt_ref[p, 1, f]) for p, f in which]
-        for (p, f), power in zip(which, power_rows(frames, first_ref, second_ref, twist_ref)):
+        for (p, f), power in zip(which, power_rows(frames, table_ref, twist_ref)):
             pow_ref[p, f] = power
             sums[p] = power if sums[p] is None else sums[p] + power
     for p in range(2):
         sum_ref[p] = sums[p]
 
 
-def rim_kernel(part_ref, later_ref, earlier_ref, taps_ref, first_ref, second_ref, twist_ref, had_ref, pow_ref, back_ref, mine_ref, send_ref):
+def rim_powers(role, part_ref, came_ref, taps_ref, table_ref, twist_ref, sums, keep, store):
+    slots = AHEAD if role == "ahead" else BACK
     taps = [taps_ref[pl.ds(t, ROWS, stride=8), :] for t in range(TAPS)]
 
     def finished(p, j):
         out = []
         for c in range(2):
-            total = part_ref[p, c, j]
-            if j < AHEAD:
-                for i in range(j + 1):
-                    t = FRAMES + i - HELD - j
-                    total = total + taps[t] * later_ref[p, c, pl.ds(i, ROWS, stride=AHEAD), :]
+            if role == "ahead":
+                terms = [(FRAMES + i - HELD - j, i) for i in range(j + 1)]
+                total = part_ref[p, c, j]
             else:
-                for t in range(BACK - (j - AHEAD)):
-                    i = 4 - BACK + (j - AHEAD) + t
-                    total = total + taps[t] * earlier_ref[p, c, pl.ds(i, ROWS, stride=4), :]
-            out.append(total)
+                terms = [(t, AHEAD - BACK + j + t) for t in range(BACK - j)]
+                total = part_ref[p, c, AHEAD + j]
+            rest = None
+            for t, i in terms:
+                term = taps[t] * came_ref[p, c, pl.ds(i, ROWS, stride=AHEAD), :]
+                rest = term if rest is None else rest + term
+            out.append(total + (rest if keep is None else jnp.where(keep, rest, 0.0)))
         return tuple(out)
 
-    sums = [had_ref[0], had_ref[1]]
-    for start in range(0, AHEAD + BACK, 2):
-        which = [(p, j) for j in range(start, min(start + 2, AHEAD + BACK)) for p in range(2)]
+    for start in range(0, slots, 2):
+        which = [(p, j) for j in range(start, min(start + 2, slots)) for p in range(2)]
         frames = [finished(p, j) for p, j in which]
-        for (p, j), power in zip(which, power_rows(frames, first_ref, second_ref, twist_ref)):
-            if j < AHEAD:
-                pow_ref[p, j] = power
-            else:
-                back_ref[p, j - AHEAD] = power
+        for (p, j), power in zip(which, power_rows(frames, table_ref, twist_ref)):
+            store[p, j] = power
             sums[p] = sums[p] + power
-    keeps_second = kept_half() == 1
-    mine_ref[...] = jnp.where(keeps_second, sums[1], sums[0])
-    send_ref[...] = jnp.where(keeps_second, sums[0], sums[1])
+    return sums
+
+
+def near_kernel(part_ref, near_ref, taps_ref, table_ref, twist_ref, had_ref, early_ref, sum_ref):
+    for core, role in enumerate(("ahead", "back")):
+
+        @pl.when(lax.axis_index("tm") % 2 == core)
+        def _():
+            sums = [had_ref[0], had_ref[1]]
+            sums = rim_powers(role, part_ref, near_ref, taps_ref, table_ref, twist_ref, sums, None, early_ref)
+            sum_ref[0], sum_ref[1] = sums
+
+
+def cross_kernel(last, part_ref, cross_ref, taps_ref, table_ref, twist_ref, had_ref, early_ref, ahead_ref, back_ref, mine_ref, send_ref):
+    tm = lax.axis_index("tm")
+    for core, role in enumerate(("back", "ahead")):
+
+        @pl.when(tm % 2 == core)
+        def _():
+            sums = [had_ref[0], had_ref[1]]
+            store, keep = (back_ref, None) if core == 0 else (ahead_ref, tm < last)
+            sums = rim_powers(role, part_ref, cross_ref, taps_ref, table_ref, twist_ref, sums, keep, store)
+            for p in range(2):
+                if core == 0:
+                    ahead_ref[p] = early_ref[p]
+                else:
+                    back_ref[p] = early_ref[p, :BACK]
+            keeps_second = kept_half() == 1
+            mine_ref[...] = jnp.where(keeps_second, sums[1], sums[0])
+            send_ref[...] = jnp.where(keeps_second, sums[0], sums[1])
 
 
 def clean_kernel(scale, held_ref, ahead_ref, back_ref, mine_ref, other_ref, out_ref):
@@ -197,16 +265,23 @@
             out_ref[p, f // 8, pl.ds(f % 8, ROWS, stride=8), :] = power - base
 
 
-def on_core(kernel, out_shape, scratch=(), cost=None):
+def on_core(kernel, out_shape, scratch=(), far=False, vmem=16 << 20, cost=None):
+    space = pl.ANY if far else pltpu.VMEM
+    where = pltpu.VMEM if far else jax.ShapeDtypeStruct
+    shapes = [s if not isinstance(s, tuple) else where(s, jnp.float32) for s in out_shape]
     return lambda *args: pl.pallas_call(
         kernel,
-        out_shape=[jax.ShapeDtypeStruct(s, jnp.float32) for s in out_shape],
-        in_specs=[pl.BlockSpec(memory_space=pltpu.VMEM)] * len(args),
+        out_shape=shapes,
+        in_specs=[pl.BlockSpec(memory_space=space)] * len(args),
         out_specs=[pl.BlockSpec(memory_space=pltpu.VMEM)] * len(out_shape),
-        scratch_shapes=[pltpu.VMEM(s, jnp.float32) for s in scratch],
-        compiler_params=pltpu.CompilerParams(vmem_limit_bytes=16 << 20),
+        scratch_shapes=[pltpu.VMEM(s, jnp.float32) if isinstance(s, tuple) else s for s in scratch],
+        compiler_params=pltpu.CompilerParams(vmem_limit_bytes=vmem),
         cost_estimate=cost,
     )(*args)
+
+
+def in_hbm(x):
+    return pltpu.with_memory_space_constraint(x, pltpu.HBM)
 
 
 def by_rows(x):
@@ -231,23 +306,49 @@
 
 
 def body(voltages, filter_taps):
-    volts = voltages[0]
-    first, second, twist = (jnp.asarray(t) for t in dft_tables())
     devices = lax.axis_size("tm")
-    later = lax.ppermute(volts[:, :, :AHEAD], "tm", [(i, i - 1) for i in range(1, devices)])
-    earlier = lax.ppermute(volts[:, :, FRAMES - 4 :], "tm", [(i, (i + 1) % devices) for i in range(devices)])
-    tiles = by_rows(volts.reshape(2, 2, 2, 8, CHANNELS))
-    taps = by_rows(filter_taps)
-    held, part, had = on_core(
+    table, twist = (jnp.asarray(t) for t in dft_tables())
+    tiles = jnp.swapaxes(voltages[0].reshape(2, 2, 2, 8, ROWS, LANES), 3, 4)
+    rim = (2, 2, ROWS, AHEAD, LANES)
+    rows = (2, 2, ROWS * AHEAD, LANES)
+    cross, near = on_core(
+        rim_kernel,
+        [rim, rim],
+        scratch=[pltpu.SemaphoreType.DMA((2, 4))],
+        far=True,
+        cost=SHORT,
+    )(in_hbm(tiles))
+    near = lax.ppermute(near.reshape(rows), "tm", [(i, i ^ 1) for i in range(devices)])
+    cross = lax.ppermute(cross.reshape(rows), "tm", [(i, (i + 1 if i % 2 else i - 1) % devices) for i in range(devices)])
+    strips = (2, 2, 2, ROWS * 8, LANES)
+    held, part, had, taps, table, twist = on_core(
         held_kernel,
-        [(2, HELD, ROWS, LANES), (2, 2, AHEAD + BACK, ROWS, LANES), (2, ROWS, LANES)],
-        scratch=[(2, 2, HELD, ROWS, LANES)],
+        [
+            (2, HELD, ROWS, LANES),
+            (2, 2, AHEAD + BACK, ROWS, LANES),
+            (2, ROWS, LANES),
+            (ROWS * TAPS, LANES),
+            pltpu.VMEM(table.shape, table.dtype),
+            twist.shape,
+        ],
+        scratch=[
+            strips,
+            (2, 2, HELD, ROWS, LANES),
+            pltpu.SemaphoreType.DMA((ROWS // 8,)),
+            pltpu.SemaphoreType.DMA((3,)),
+        ],
+        far=True,
         cost=pl.CostEstimate(flops=2 * 10**9, bytes_accessed=6 << 20, transcendentals=0),
-    )(tiles, taps, first, second, twist)
+    )(in_hbm(tiles.reshape(strips)), in_hbm(by_rows(filter_taps)), in_hbm(table), in_hbm(twist))
+    early, had = on_core(
+        near_kernel,
+        [(2, AHEAD, ROWS, LANES), (2, ROWS, LANES)],
+        cost=pl.CostEstimate(flops=10**9, bytes_accessed=3 << 20, transcendentals=0),
+    )(part, near, taps, table, twist, had)
     ahead, back, mine, send = on_core(
-        rim_kernel,
+        functools.partial(cross_kernel, devices - 1),
         [(2, AHEAD, ROWS, LANES), (2, BACK, ROWS, LANES), (ROWS, LANES), (ROWS, LANES)],
-    )(part, by_rows(later), by_rows(earlier), taps, first, second, twist, had)
+    )(part, cross, taps, table, twist, had, early)
     mine, other, back = total_over_all(mine, send, back)
     scale = 1.0 / (FRAMES * devices * lax.axis_size("beam"))
     (out,) = on_core(functools.partial(clean_kernel, scale), [(2, 2, 8 * ROWS, LANES)])(held, ahead, back, mine, other)

time: 55 us -> 53.2 us (0.967)
  waiting for transfers between devices: 18.7 us -> 24.3 us
  local copies, waits for them, and re-layouts: 5.52 us -> 0 us
  starting transfers between devices: 24.6 us -> 19.6 us
  Pallas kernels: 5.83 us -> 9.06 us
    ppermute x7, starting transfers between devices: 18.7 us -> 14.1 us  [total_over_all(): sums = sums + lax.ppermute(sums, BOTH, swap_pairs(axis, partner))]
    ppermute x7, waiting for transfers between devices: 15.1 us -> 19.3 us  [total_over_all(): sums = sums + lax.ppermute(sums, BOTH, swap_pairs(axis, partner))]
    unnamed x14 -> x0, local copies, waits for them, and re-layouts: 3.65 us -> none
    pallas_call x3 -> x5, Pallas kernels: 5.83 us -> 9.06 us  [on_core(): pl.pallas_call(kernel, out_shape=shapes, in_specs=[pl.BlockSpec(memory_sp...]
    slice x1 -> x0, local copies, waits for them, and re-layouts: 1.87 us -> none  [body(): volts[:, :, FRAMES - 4:]]
    ppermute x2, starting transfers between devices: 5.17 us -> 3.33 us  [the longest x1 3.33 us: body(): lax.ppermute(near.reshape(rows), 'tm', [(i, i ^ 1) for i in range(devices)])]
    ppermute x2, waiting for transfers between devices: 1.51 us -> 3.31 us  [the longest x1 3.31 us: body(): lax.ppermute(cross.reshape(rows), 'tm', [(i, (i + 1 if i % 2 else i - 1)...]
    ppermute x1, starting transfers between devices: 0.09 us -> 1.43 us  [total_over_all(): sums = mine + lax.ppermute(send, BOTH, cores)]
  transfers between devices with their start and end apart: 12 -> 12, of which waited for: 10 -> 10; matrix products, arithmetic and copies ran while one was open for 0% -> 0% of each run, Pallas kernels for 5% -> 10%
where the time goes in v3:
time: 53.2 us; the launch traced here: 53.1 us
  waiting for transfers between devices  24.3 us (46%)
  starting transfers between devices  19.6 us (37%)
  Pallas kernels  9.06 us (17%)
    ppermute x7, waiting for transfers between devices, total_over_all(): sums = sums + lax.ppermute(sums, BOTH, swap_pairs(axis, partner))  19.3 us
    ppermute x7, starting transfers between devices, total_over_all(): sums = sums + lax.ppermute(sums, BOTH, swap_pairs(axis, partner))  14.1 us
    pallas_call x5, Pallas kernels, on_core(): pl.pallas_call(kernel, out_shape=shapes, in_specs=[pl.BlockSpec(memory_sp...  9.06 us
    ppermute x1, starting transfers between devices, body(): lax.ppermute(near.reshape(rows), 'tm', [(i, i ^ 1) for i in range(devices)])  3.33 us
    ppermute x1, waiting for transfers between devices, body(): lax.ppermute(cross.reshape(rows), 'tm', [(i, (i + 1 if i % 2 else i - 1)...  3.31 us
    ppermute x1, starting transfers between devices, total_over_all(): sums = mine + lax.ppermute(send, BOTH, cores)  1.43 us
  transfers between devices with their start and end apart: 12, of which 10 were waited for; matrix products, arithmetic and copies ran while one was open for 0% of the time, Pallas kernels for 10%

profile of v3, /device:TPU:1, one launch (start us, length us, event | category | flops | bytes accessed | tf_op | source)
XLA Modules:
  0.0 53.1 jit_solution(5421840541864540713)
XLA Ops:
  0.0 1.3 %shard_map.47 = (f32[2,2,64,4,128]{4,3,2,1,0:T(4,128)S(1)}, f32[2,2,64,4,128]{4,3,2,1,0:T(4,128)S(1)}) custom-call(f32[2,2,2,64,8,128]{5,4,3,2,1,0:T(8,128)} %bitcast.19), custom_call_target="tpu_custom_call" | custom-call | flops 1000 | bytes 1000 | tf_op jit(solution)/shard_map/pallas_call | solution.py:272
  1.4 3.3 %collective-permute-start.1 = (f32[2,2,256,128]{3,2,1,0:T(8,128)S(1)}, f32[2,2,256,128]{3,2,1,0:T(8,128)S(1)}, u32[]{:S(2)}, u32[]{:S(2)}) collective-permute-start(f32[2,2,256,128]{3,2,1,0:T(8,128)S(1)} %bitcast.18), channel_id=1, source_target_pairs={{0,1},{1,0},{2,3},{3,2},{4,5},{5,4},{6,7},{7,6},{8,9},{9,8},{10,11... | collective-permute-start | bytes 1572872 | tf_op jit(solution)/shard_map/ppermute | solution.py:321
  4.7 0.0 collective-permute-start
  4.7 4.3 %shard_map.46 = (f32[2,9,64,128]{3,2,1,0:T(8,128)S(1)}, f32[2,2,7,64,128]{4,3,2,1,0:T(8,128)S(1)}, f32[2,64,128]{2,1,0:T(8,128)S(1)}, f32[512,128]{1,0:T(8,128)S...) custom-call(f32[2,2,2,512,128]{4,3,2,1,0:T(8,128)} %bitcast.20, f32[512,128]{1,0:T(8,128)} %bitcast.21, ...), custom_call_target="tpu_custom_call" | custom-call | flops 2000000000 | bytes 6291456 | tf_op jit(solution)/shard_map/pallas_call | solution.py:272
  9.0 0.0 collective-permute-done.1.near_ref
  9.0 1.3 %shard_map.48 = (f32[2,4,64,128]{3,2,1,0:T(8,128)S(1)}, f32[2,64,128]{2,1,0:T(8,128)S(1)}) custom-call(f32[2,2,7,64,128]{4,3,2,1,0:T(8,128)S(1)} %get-tuple-element.24.part_ref, f32[2,2,256,128]{3,2,1,0:T(8,128)S(1)} %collective-permute-done.1.near_ref, f32[512,128]{1,0:T(8,128)S(1)} %get-tuple-element.26.taps_ref, ...), custom_call_target="tpu_custom_call" | custom-call | flops 1000000000 | bytes 3145728 | tf_op jit(solution)/shard_map/pallas_call | solution.py:272
  10.3 3.3 %collective-permute-done.cross_ref = f32[2,2,256,128]{3,2,1,0:T(8,128)S(1)} collective-permute-done((f32[2,2,256,128]{3,2,1,0:T(8,128)S(1)}, f32[2,2,256,128]{3,2,1,0:T(8,128)S(1)}, u32[]{:S(2)}, u32[]{:S(2)}) %collective-permute-start) | collective-permute-done | bytes 524320 | tf_op jit(solution)/shard_map/ppermute | solution.py:322
  13.6 0.9 %shard_map.49 = (f32[2,4,64,128]{3,2,1,0:T(8,128)S(1)}, f32[2,3,64,128]{3,2,1,0:T(8,128)S(1)}, f32[64,128]{1,0:T(8,128)S(1)}, f32[64,128]{1,0:T(8,128)S(1)}) custom-call(f32[2,2,7,64,128]{4,3,2,1,0:T(8,128)S(1)} %get-tuple-element.24.part_ref, f32[2,2,256,128]{3,2,1,0:T(8,128)S(1)} %collective-permute-done.cross_ref, ...), custom_call_target="tpu_custom_call" | custom-call | tf_op jit(solution)/shard_map/pallas_call | solution.py:272
  14.5 1.4 %collective-permute-start.2 = (f32[64,128]{1,0:T(8,128)S(1)}, f32[64,128]{1,0:T(8,128)S(1)}, u32[]{:S(2)}, u32[]{:S(2)}) collective-permute-start(f32[64,128]{1,0:T(8,128)S(1)} %get-tuple-element.35), channel_id=1, source_target_pairs={{0,1},{1,0},{2,3},{3,2},{4,5},{5,4},{6,7},{7,6},{8,9},{9,8},{10,11... | collective-permute-start | bytes 98312 | tf_op jit(solution)/shard_map/ppermute | solution.py:296
  16.0 0.9 %collective-permute-done.2 = f32[64,128]{1,0:T(8,128)S(1)} collective-permute-done((f32[64,128]{1,0:T(8,128)S(1)}, f32[64,128]{1,0:T(8,128)S(1)}, u32[]{:S(2)}, u32[]{:S(2)}) %collective-permute-start.2) | collective-permute-done | bytes 32800 | tf_op jit(solution)/shard_map/ppermute | solution.py:296
  16.8 0.0 collective-permute-start.3
  16.8 3.3 %collective-permute-done.3 = f32[64,128]{1,0:T(8,128)S(1)} collective-permute-done((f32[64,128]{1,0:T(8,128)S(1)}, f32[64,128]{1,0:T(8,128)S(1)}, u32[]{:S(2)}, u32[]{:S(2)}) %collective-permute-start.3) | collective-permute-done | bytes 32800 | tf_op jit(solution)/shard_map/ppermute | solution.py:302
  20.2 0.3 collective-permute-start.8
  20.5 0.7 %collective-permute-start.4 = (f32[64,128]{1,0:T(8,128)S(1)}, f32[64,128]{1,0:T(8,128)S(1)}, u32[]{:S(2)}, u32[]{:S(2)}) collective-permute-start(f32[64,128]{1,0:T(8,128)S(1)} %add.25), channel_id=1, source_target_pairs={{0,7},{1,6},{2,5},{3,4},{4,3},{5,2},{6,1},{7,0},{8,15},{9,14},{10,... | collective-permute-start | bytes 98312 | tf_op jit(solution)/shard_map/ppermute | solution.py:302
  21.2 4.2 %collective-permute-done.4 = f32[64,128]{1,0:T(8,128)S(1)} collective-permute-done((f32[64,128]{1,0:T(8,128)S(1)}, f32[64,128]{1,0:T(8,128)S(1)}, u32[]{:S(2)}, u32[]{:S(2)}) %collective-permute-start.4) | collective-permute-done | bytes 32800 | tf_op jit(solution)/shard_map/ppermute | solution.py:302
  25.5 1.7 %collective-permute-start.5 = (f32[64,128]{1,0:T(8,128)S(1)}, f32[64,128]{1,0:T(8,128)S(1)}, u32[]{:S(2)}, u32[]{:S(2)}) collective-permute-start(f32[64,128]{1,0:T(8,128)S(1)} %add.26), channel_id=1, source_target_pairs={{0,9},{1,8},{2,11},{3,10},{4,13},{5,12},{6,15},{7,14},{8,1},{9,0},... | collective-permute-start | bytes 98312 | tf_op jit(solution)/shard_map/ppermute | solution.py:302
  27.1 2.3 %collective-permute-done.5 = f32[64,128]{1,0:T(8,128)S(1)} collective-permute-done((f32[64,128]{1,0:T(8,128)S(1)}, f32[64,128]{1,0:T(8,128)S(1)}, u32[]{:S(2)}, u32[]{:S(2)}) %collective-permute-start.5) | collective-permute-done | bytes 32800 | tf_op jit(solution)/shard_map/ppermute | solution.py:302
  29.4 2.4 %collective-permute-start.6 = (f32[64,128]{1,0:T(8,128)S(1)}, f32[64,128]{1,0:T(8,128)S(1)}, u32[]{:S(2)}, u32[]{:S(2)}) collective-permute-start(f32[64,128]{1,0:T(8,128)S(1)} %add.27), channel_id=1, source_target_pairs={{0,25},{1,24},{2,27},{3,26},{4,29},{5,28},{6,31},{7,30},{8,17},{9,... | collective-permute-start | bytes 98312 | tf_op jit(solution)/shard_map/ppermute | solution.py:302
  31.8 2.3 %collective-permute-done.6 = f32[64,128]{1,0:T(8,128)S(1)} collective-permute-done((f32[64,128]{1,0:T(8,128)S(1)}, f32[64,128]{1,0:T(8,128)S(1)}, u32[]{:S(2)}, u32[]{:S(2)}) %collective-permute-start.6) | collective-permute-done | bytes 32800 | tf_op jit(solution)/shard_map/ppermute | solution.py:302
  34.0 1.8 %collective-permute-start.7 = (f32[64,128]{1,0:T(8,128)S(1)}, f32[64,128]{1,0:T(8,128)S(1)}, u32[]{:S(2)}, u32[]{:S(2)}) collective-permute-start(f32[64,128]{1,0:T(8,128)S(1)} %add.28), channel_id=1, source_target_pairs={{0,33},{1,32},{2,35},{3,34},{4,37},{5,36},{6,39},{7,38},{8,41},{9,... | collective-permute-start | bytes 98312 | tf_op jit(solution)/shard_map/ppermute | solution.py:302
  35.8 1.6 %collective-permute-done.7 = f32[64,128]{1,0:T(8,128)S(1)} collective-permute-done((f32[64,128]{1,0:T(8,128)S(1)}, f32[64,128]{1,0:T(8,128)S(1)}, u32[]{:S(2)}, u32[]{:S(2)}) %collective-permute-start.7) | collective-permute-done | bytes 32800 | tf_op jit(solution)/shard_map/ppermute | solution.py:302
  37.4 0.0 collective-permute-done.8.back_ref
  37.4 5.8 %collective-permute-start.9 = (f32[64,128]{1,0:T(8,128)S(1)}, f32[64,128]{1,0:T(8,128)S(1)}, u32[]{:S(2)}, u32[]{:S(2)}) collective-permute-start(f32[64,128]{1,0:T(8,128)S(1)} %add.29), channel_id=1, source_target_pairs={{0,225},{1,224},{2,227},{3,226},{4,229},{5,228},{6,231},{7,230},{8... | collective-permute-start | bytes 98312 | tf_op jit(solution)/shard_map/ppermute | solution.py:302
  43.3 1.6 %collective-permute-done.9 = f32[64,128]{1,0:T(8,128)S(1)} collective-permute-done((f32[64,128]{1,0:T(8,128)S(1)}, f32[64,128]{1,0:T(8,128)S(1)}, u32[]{:S(2)}, u32[]{:S(2)}) %collective-permute-start.9) | collective-permute-done | bytes 32800 | tf_op jit(solution)/shard_map/ppermute | solution.py:302
  44.9 1.7 %collective-permute-start.10 = (f32[64,128]{1,0:T(8,128)S(1)}, f32[64,128]{1,0:T(8,128)S(1)}, u32[]{:S(2)}, u32[]{:S(2)}) collective-permute-start(f32[64,128]{1,0:T(8,128)S(1)} %add.30), channel_id=1, source_target_pairs={{0,97},{1,96},{2,99},{3,98},{4,101},{5,100},{6,103},{7,102},{8,105... | collective-permute-start | bytes 98312 | tf_op jit(solution)/shard_map/ppermute | solution.py:302
  46.6 4.0 %collective-permute-done.10 = f32[64,128]{1,0:T(8,128)S(1)} collective-permute-done((f32[64,128]{1,0:T(8,128)S(1)}, f32[64,128]{1,0:T(8,128)S(1)}, u32[]{:S(2)}, u32[]{:S(2)}) %collective-permute-start.10) | collective-permute-done | bytes 32800 | tf_op jit(solution)/shard_map/ppermute | solution.py:302
  50.6 0.4 collective-permute-start.11
  51.0 0.9 %collective-permute-done.11.other_ref = f32[64,128]{1,0:T(8,128)S(1)} collective-permute-done((f32[64,128]{1,0:T(8,128)S(1)}, f32[64,128]{1,0:T(8,128)S(1)}, u32[]{:S(2)}, u32[]{:S(2)}) %collective-permute-start.11) | collective-permute-done | bytes 32800 | tf_op jit(solution)/shard_map/ppermute | solution.py:305
  51.9 1.2 %shard_map.50 = f32[2,2,512,128]{3,2,1,0:T(8,128)} custom-call(f32[2,9,64,128]{3,2,1,0:T(8,128)S(1)} %get-tuple-element.23.held_ref, f32[2,4,64,128]{3,2,1,0:T(8,128)S(1)} %get-tuple-element.33.ahead_ref, f32[2,3,64,128]{3,2,1,0:T(8,128)S(1)} %collective-permute-done.8.back_ref, f32[64,128]{1,0:T(8,128)S(1)} %add.31.mine_ref, ...), custom_call_target="tpu_custom_call" | custom-call | tf_op jit(solution)/shard_map/pallas_call | solution.py:272
  (8 shorter events, 0.0 us)
Async XLA Ops:
  1.4 7.6 %collective-permute-start.1 = (f32[2,2,256,128]{3,2,1,0:T(8,128)S(1)}, f32[2,2,256,128]{3,2,1,0:T(8,128)S(1)}, u32[]{:S(2)}, u32[]{:S(2)}) collective-permute-start(f32[2,2,256,128]{3,2,1,0:T(8,128)S(1)} %bitcast.18), channel_id=1, source_target_pairs={{0,1},{1,0},{2,3},{3,2},{4,5},{5,4},{6,7},{7,6},{8,9},{9,8},{10,11... | collective-permute-start | bytes 1572872 | tf_op jit(solution)/shard_map/ppermute | solution.py:321
  4.7 8.9 %collective-permute-start = (f32[2,2,256,128]{3,2,1,0:T(8,128)S(1)}, f32[2,2,256,128]{3,2,1,0:T(8,128)S(1)}, u32[]{:S(2)}, u32[]{:S(2)}) collective-permute-start(f32[2,2,256,128]{3,2,1,0:T(8,128)S(1)} %bitcast.17), channel_id=1, source_target_pairs={{0,7},{1,2},{2,1},{3,4},{4,3},{5,6},{6,5},{7,0},{8,15},{9,10},{10,... | collective-permute-start | bytes 1572872 | tf_op jit(solution)/shard_map/ppermute | solution.py:322
  14.5 2.3 %collective-permute-start.2 = (f32[64,128]{1,0:T(8,128)S(1)}, f32[64,128]{1,0:T(8,128)S(1)}, u32[]{:S(2)}, u32[]{:S(2)}) collective-permute-start(f32[64,128]{1,0:T(8,128)S(1)} %get-tuple-element.35), channel_id=1, source_target_pairs={{0,1},{1,0},{2,3},{3,2},{4,5},{5,4},{6,7},{7,6},{8,9},{9,8},{10,11... | collective-permute-start | bytes 98312 | tf_op jit(solution)/shard_map/ppermute | solution.py:296
  16.8 3.3 %collective-permute-start.3 = (f32[64,128]{1,0:T(8,128)S(1)}, f32[64,128]{1,0:T(8,128)S(1)}, u32[]{:S(2)}, u32[]{:S(2)}) collective-permute-start(f32[64,128]{1,0:T(8,128)S(1)} %add.24), channel_id=1, source_target_pairs={{0,3},{1,2},{2,1},{3,0},{4,7},{5,6},{6,5},{7,4},{8,11},{9,10},{10,... | collective-permute-start | bytes 98312 | tf_op jit(solution)/shard_map/ppermute | solution.py:302
  20.2 17.3 %collective-permute-start.8 = (f32[2,3,64,128]{3,2,1,0:T(8,128)S(1)}, f32[2,3,64,128]{3,2,1,0:T(8,128)S(1)}, u32[]{:S(2)}, u32[]{:S(2)}) collective-permute-start(f32[2,3,64,128]{3,2,1,0:T(8,128)S(1)} %get-tuple-element.38), channel_id=1, source_target_pairs={{0,7},{1,0},{2,1},{3,2},{4,3},{5,4},{6,5},{7,6},{8,15},{9,8},{10,9... | collective-permute-start | bytes 589832 | tf_op jit(solution)/shard_map/ppermute | solution.py:301
  20.5 4.9 %collective-permute-start.4 = (f32[64,128]{1,0:T(8,128)S(1)}, f32[64,128]{1,0:T(8,128)S(1)}, u32[]{:S(2)}, u32[]{:S(2)}) collective-permute-start(f32[64,128]{1,0:T(8,128)S(1)} %add.25), channel_id=1, source_target_pairs={{0,7},{1,6},{2,5},{3,4},{4,3},{5,2},{6,1},{7,0},{8,15},{9,14},{10,... | collective-permute-start | bytes 98312 | tf_op jit(solution)/shard_map/ppermute | solution.py:302
  25.5 3.9 %collective-permute-start.5 = (f32[64,128]{1,0:T(8,128)S(1)}, f32[64,128]{1,0:T(8,128)S(1)}, u32[]{:S(2)}, u32[]{:S(2)}) collective-permute-start(f32[64,128]{1,0:T(8,128)S(1)} %add.26), channel_id=1, source_target_pairs={{0,9},{1,8},{2,11},{3,10},{4,13},{5,12},{6,15},{7,14},{8,1},{9,0},... | collective-permute-start | bytes 98312 | tf_op jit(solution)/shard_map/ppermute | solution.py:302
  29.4 4.6 %collective-permute-start.6 = (f32[64,128]{1,0:T(8,128)S(1)}, f32[64,128]{1,0:T(8,128)S(1)}, u32[]{:S(2)}, u32[]{:S(2)}) collective-permute-start(f32[64,128]{1,0:T(8,128)S(1)} %add.27), channel_id=1, source_target_pairs={{0,25},{1,24},{2,27},{3,26},{4,29},{5,28},{6,31},{7,30},{8,17},{9,... | collective-permute-start | bytes 98312 | tf_op jit(solution)/shard_map/ppermute | solution.py:302
  34.0 3.4 %collective-permute-start.7 = (f32[64,128]{1,0:T(8,128)S(1)}, f32[64,128]{1,0:T(8,128)S(1)}, u32[]{:S(2)}, u32[]{:S(2)}) collective-permute-start(f32[64,128]{1,0:T(8,128)S(1)} %add.28), channel_id=1, source_target_pairs={{0,33},{1,32},{2,35},{3,34},{4,37},{5,36},{6,39},{7,38},{8,41},{9,... | collective-permute-start | bytes 98312 | tf_op jit(solution)/shard_map/ppermute | solution.py:302
  37.4 7.4 %collective-permute-start.9 = (f32[64,128]{1,0:T(8,128)S(1)}, f32[64,128]{1,0:T(8,128)S(1)}, u32[]{:S(2)}, u32[]{:S(2)}) collective-permute-start(f32[64,128]{1,0:T(8,128)S(1)} %add.29), channel_id=1, source_target_pairs={{0,225},{1,224},{2,227},{3,226},{4,229},{5,228},{6,231},{7,230},{8... | collective-permute-start | bytes 98312 | tf_op jit(solution)/shard_map/ppermute | solution.py:302
  44.9 5.8 %collective-permute-start.10 = (f32[64,128]{1,0:T(8,128)S(1)}, f32[64,128]{1,0:T(8,128)S(1)}, u32[]{:S(2)}, u32[]{:S(2)}) collective-permute-start(f32[64,128]{1,0:T(8,128)S(1)} %add.30), channel_id=1, source_target_pairs={{0,97},{1,96},{2,99},{3,98},{4,101},{5,100},{6,103},{7,102},{8,105... | collective-permute-start | bytes 98312 | tf_op jit(solution)/shard_map/ppermute | solution.py:302
  50.6 1.3 %collective-permute-start.11 = (f32[64,128]{1,0:T(8,128)S(1)}, f32[64,128]{1,0:T(8,128)S(1)}, u32[]{:S(2)}, u32[]{:S(2)}) collective-permute-start(f32[64,128]{1,0:T(8,128)S(1)} %add.31.mine_ref), channel_id=1, source_target_pairs={{0,1},{1,0},{2,3},{3,2},{4,5},{5,4},{6,7},{7,6},{8,9},{9,8},{10,11... | collective-permute-start | bytes 98312 | tf_op jit(solution)/shard_map/ppermute | solution.py:305

commit v4 on v3

--- a/solution.py
+++ b/solution.py
@@ -250,19 +250,38 @@
             send_ref[...] = jnp.where(keeps_second, sums[0], sums[1])
 
 
-def clean_kernel(scale, held_ref, ahead_ref, back_ref, mine_ref, other_ref, out_ref):
-    keeps_second = kept_half() == 1
-    mine, other = mine_ref[...] * scale, other_ref[...] * scale
-    for p in range(2):
-        base = jnp.where(keeps_second, mine, other) if p else jnp.where(keeps_second, other, mine)
-        for f in range(FRAMES):
+def clean_kernel(scale, own, held_ref, ahead_ref, back_ref, sum_ref, *refs):
+    out_ref, tile_ref, sems = refs[-3:]
+    p = kept_half() if own else 1 - kept_half()
+    base = sum_ref[...] * scale
+    copies = []
+    for half in range(2):
+        for f in range(8 * half, 8 * half + 8):
             if f < HELD:
                 power = held_ref[p, f]
             elif f < HELD + AHEAD:
                 power = ahead_ref[p, f - HELD]
             else:
                 power = back_ref[p, f - HELD - AHEAD]
-            out_ref[p, f // 8, pl.ds(f % 8, ROWS, stride=8), :] = power - base
+            tile_ref[half, pl.ds(f % 8, ROWS, stride=8), :] = power - base
+        copies.append(pltpu.make_async_copy(tile_ref.at[half], out_ref.at[p, half], sems.at[half]))
+        copies[-1].start()
+    for copy in copies:
+        copy.wait()
+
+
+def clean(scale, own, *args):
+    far = [pl.BlockSpec(memory_space=pl.ANY)]
+    return pl.pallas_call(
+        functools.partial(clean_kernel, scale, own),
+        out_shape=pltpu.HBM((2, 2, 8 * ROWS, LANES), jnp.float32),
+        in_specs=[pl.BlockSpec(memory_space=pltpu.VMEM)] * 4 + far * (len(args) - 4),
+        out_specs=far[0],
+        scratch_shapes=[pltpu.VMEM((2, 8 * ROWS, LANES), jnp.float32), pltpu.SemaphoreType.DMA((2,))],
+        input_output_aliases={} if own else {4: 0},
+        compiler_params=pltpu.CompilerParams(vmem_limit_bytes=16 << 20),
+        cost_estimate=pl.CostEstimate(flops=10**6, bytes_accessed=2 << 20, transcendentals=0),
+    )(*args)
 
 
 def on_core(kernel, out_shape, scratch=(), far=False, vmem=16 << 20, cost=None):
@@ -296,11 +315,11 @@
     sums = mine + lax.ppermute(send, BOTH, cores)
     steps = [("y", r) for r in RING4] + [("x", r) for r in RING4] + [("z", r) for r in RING8]
     for n, (axis, partner) in enumerate(steps):
-        if n == 1:
+        if n == 2:
             sums, back = lax.optimization_barrier((sums, back))
             back = lax.ppermute(back, "tm", left)
         sums = sums + lax.ppermute(sums, BOTH, swap_pairs(axis, partner))
-        if n == 4:
+        if n == 5:
             sums, back = lax.optimization_barrier((sums, back))
     return sums, lax.ppermute(sums, BOTH, cores), back
 
@@ -351,7 +370,8 @@
     )(part, cross, taps, table, twist, had, early)
     mine, other, back = total_over_all(mine, send, back)
     scale = 1.0 / (FRAMES * devices * lax.axis_size("beam"))
-    (out,) = on_core(functools.partial(clean_kernel, scale), [(2, 2, 8 * ROWS, LANES)])(held, ahead, back, mine, other)
+    out = clean(scale, True, held, ahead, back, mine)
+    out = clean(scale, False, held, ahead, back, other, out)
     out = jnp.swapaxes(out.reshape(2, 2, ROWS, 8, LANES), 2, 3)
     return out.reshape(1, 2, FRAMES, CHANNELS)
 

time: 53.2 us -> 52.9 us (level)
  waiting for transfers between devices: 24.3 us -> 22.7 us
  starting transfers between devices: 19.6 us -> 20.4 us
  Pallas kernels: 9.06 us -> 9.61 us
    pallas_call x0 -> x2, Pallas kernels: none -> 1.77 us  [clean(): pl.pallas_call(functools.partial(clean_kernel, scale, own), out_shape=plt...]
    pallas_call x5 -> x4, Pallas kernels: 9.06 us -> 7.84 us  [on_core(): pl.pallas_call(kernel, out_shape=shapes, in_specs=[pl.BlockSpec(memory_sp...]
    ppermute x1, waiting for transfers between devices: 0.86 us -> 0.01 us  [total_over_all(): return (sums, lax.ppermute(sums, BOTH, cores), back)]
    ppermute x7, starting transfers between devices: 14.1 us -> 14.9 us  [total_over_all(): sums = sums + lax.ppermute(sums, BOTH, swap_pairs(axis, partner))]
    ppermute x7, waiting for transfers between devices: 19.3 us -> 18.5 us  [total_over_all(): sums = sums + lax.ppermute(sums, BOTH, swap_pairs(axis, partner))]
  transfers between devices with their start and end apart: 12 -> 12, of which waited for: 10 -> 9; matrix products, arithmetic and copies ran while one was open for 0% -> 0% of each run, Pallas kernels for 10% -> 12%
where the time goes in v4:
time: 52.9 us; the launch traced here: 52.8 us
  waiting for transfers between devices  22.7 us (43%)
  starting transfers between devices  20.4 us (39%)
  Pallas kernels  9.61 us (18%)
    ppermute x7, waiting for transfers between devices, total_over_all(): sums = sums + lax.ppermute(sums, BOTH, swap_pairs(axis, partner))  18.5 us
    ppermute x7, starting transfers between devices, total_over_all(): sums = sums + lax.ppermute(sums, BOTH, swap_pairs(axis, partner))  14.9 us
    pallas_call x4, Pallas kernels, on_core(): pl.pallas_call(kernel, out_shape=shapes, in_specs=[pl.BlockSpec(memory_sp...  7.84 us
    ppermute x1, starting transfers between devices, body(): lax.ppermute(near.reshape(rows), 'tm', [(i, i ^ 1) for i in range(devices)])  3.33 us
    ppermute x1, waiting for transfers between devices, body(): lax.ppermute(cross.reshape(rows), 'tm', [(i, (i + 1 if i % 2 else i - 1)...  3.31 us
    pallas_call x2, Pallas kernels, clean(): pl.pallas_call(functools.partial(clean_kernel, scale, own), out_shape=plt...  1.77 us
    ppermute x1, starting transfers between devices, total_over_all(): sums = mine + lax.ppermute(send, BOTH, cores)  1.43 us
  transfers between devices with their start and end apart: 12, of which 9 were waited for; matrix products, arithmetic and copies ran while one was open for 0% of the time, Pallas kernels for 12%

profile of v4, /device:TPU:1, one launch (start us, length us, event | category | flops | bytes accessed | tf_op | source)
XLA Modules:
  0.0 52.8 jit_solution(10541933926270089895)
XLA Ops:
  0.0 1.3 %shard_map.47 = (f32[2,2,64,4,128]{4,3,2,1,0:T(4,128)S(1)}, f32[2,2,64,4,128]{4,3,2,1,0:T(4,128)S(1)}) custom-call(f32[2,2,2,64,8,128]{5,4,3,2,1,0:T(8,128)} %bitcast.19), custom_call_target="tpu_custom_call" | custom-call | flops 1000 | bytes 1000 | tf_op jit(solution)/shard_map/pallas_call | solution.py:291
  1.4 3.3 %collective-permute-start.1 = (f32[2,2,256,128]{3,2,1,0:T(8,128)S(1)}, f32[2,2,256,128]{3,2,1,0:T(8,128)S(1)}, u32[]{:S(2)}, u32[]{:S(2)}) collective-permute-start(f32[2,2,256,128]{3,2,1,0:T(8,128)S(1)} %bitcast.18), channel_id=1, source_target_pairs={{0,1},{1,0},{2,3},{3,2},{4,5},{5,4},{6,7},{7,6},{8,9},{9,8},{10,11... | collective-permute-start | bytes 1572872 | tf_op jit(solution)/shard_map/ppermute | solution.py:340
  4.7 0.0 collective-permute-start
  4.7 4.3 %shard_map.46 = (f32[2,9,64,128]{3,2,1,0:T(8,128)S(1)}, f32[2,2,7,64,128]{4,3,2,1,0:T(8,128)S(1)}, f32[2,64,128]{2,1,0:T(8,128)S(1)}, f32[512,128]{1,0:T(8,128)S...) custom-call(f32[2,2,2,512,128]{4,3,2,1,0:T(8,128)} %bitcast.20, f32[512,128]{1,0:T(8,128)} %bitcast.21, ...), custom_call_target="tpu_custom_call" | custom-call | flops 2000000000 | bytes 6291456 | tf_op jit(solution)/shard_map/pallas_call | solution.py:291
  9.0 0.0 collective-permute-done.1.near_ref
  9.0 1.3 %shard_map.48 = (f32[2,4,64,128]{3,2,1,0:T(8,128)S(1)}, f32[2,64,128]{2,1,0:T(8,128)S(1)}) custom-call(f32[2,2,7,64,128]{4,3,2,1,0:T(8,128)S(1)} %get-tuple-element.24.part_ref, f32[2,2,256,128]{3,2,1,0:T(8,128)S(1)} %collective-permute-done.1.near_ref, f32[512,128]{1,0:T(8,128)S(1)} %get-tuple-element.26.taps_ref, ...), custom_call_target="tpu_custom_call" | custom-call | flops 1000000000 | bytes 3145728 | tf_op jit(solution)/shard_map/pallas_call | solution.py:291
  10.3 3.3 %collective-permute-done.cross_ref = f32[2,2,256,128]{3,2,1,0:T(8,128)S(1)} collective-permute-done((f32[2,2,256,128]{3,2,1,0:T(8,128)S(1)}, f32[2,2,256,128]{3,2,1,0:T(8,128)S(1)}, u32[]{:S(2)}, u32[]{:S(2)}) %collective-permute-start) | collective-permute-done | bytes 524320 | tf_op jit(solution)/shard_map/ppermute | solution.py:341
  13.6 0.9 %shard_map.49 = (f32[2,4,64,128]{3,2,1,0:T(8,128)S(1)}, f32[2,3,64,128]{3,2,1,0:T(8,128)S(1)}, f32[64,128]{1,0:T(8,128)S(1)}, f32[64,128]{1,0:T(8,128)S(1)}) custom-call(f32[2,2,7,64,128]{4,3,2,1,0:T(8,128)S(1)} %get-tuple-element.24.part_ref, f32[2,2,256,128]{3,2,1,0:T(8,128)S(1)} %collective-permute-done.cross_ref, ...), custom_call_target="tpu_custom_call" | custom-call | tf_op jit(solution)/shard_map/pallas_call | solution.py:291
  14.5 1.4 %collective-permute-start.2 = (f32[64,128]{1,0:T(8,128)S(1)}, f32[64,128]{1,0:T(8,128)S(1)}, u32[]{:S(2)}, u32[]{:S(2)}) collective-permute-start(f32[64,128]{1,0:T(8,128)S(1)} %get-tuple-element.35), channel_id=1, source_target_pairs={{0,1},{1,0},{2,3},{3,2},{4,5},{5,4},{6,7},{7,6},{8,9},{9,8},{10,11... | collective-permute-start | bytes 98312 | tf_op jit(solution)/shard_map/ppermute | solution.py:315
  16.0 0.9 %collective-permute-done.2 = f32[64,128]{1,0:T(8,128)S(1)} collective-permute-done((f32[64,128]{1,0:T(8,128)S(1)}, f32[64,128]{1,0:T(8,128)S(1)}, u32[]{:S(2)}, u32[]{:S(2)}) %collective-permute-start.2) | collective-permute-done | bytes 32800 | tf_op jit(solution)/shard_map/ppermute | solution.py:315
  16.8 0.0 collective-permute-start.3
  16.8 3.3 %collective-permute-done.3 = f32[64,128]{1,0:T(8,128)S(1)} collective-permute-done((f32[64,128]{1,0:T(8,128)S(1)}, f32[64,128]{1,0:T(8,128)S(1)}, u32[]{:S(2)}, u32[]{:S(2)}) %collective-permute-start.3) | collective-permute-done | bytes 32800 | tf_op jit(solution)/shard_map/ppermute | solution.py:321
  20.2 1.0 %collective-permute-start.4 = (f32[64,128]{1,0:T(8,128)S(1)}, f32[64,128]{1,0:T(8,128)S(1)}, u32[]{:S(2)}, u32[]{:S(2)}) collective-permute-start(f32[64,128]{1,0:T(8,128)S(1)} %add.25), channel_id=1, source_target_pairs={{0,7},{1,6},{2,5},{3,4},{4,3},{5,2},{6,1},{7,0},{8,15},{9,14},{10,... | collective-permute-start | bytes 98312 | tf_op jit(solution)/shard_map/ppermute | solution.py:321
  21.1 3.6 %collective-permute-done.4 = f32[64,128]{1,0:T(8,128)S(1)} collective-permute-done((f32[64,128]{1,0:T(8,128)S(1)}, f32[64,128]{1,0:T(8,128)S(1)}, u32[]{:S(2)}, u32[]{:S(2)}) %collective-permute-start.4) | collective-permute-done | bytes 32800 | tf_op jit(solution)/shard_map/ppermute | solution.py:321
  24.7 0.3 collective-permute-start.9
  25.1 2.1 %collective-permute-start.5 = (f32[64,128]{1,0:T(8,128)S(1)}, f32[64,128]{1,0:T(8,128)S(1)}, u32[]{:S(2)}, u32[]{:S(2)}) collective-permute-start(f32[64,128]{1,0:T(8,128)S(1)} %add.26), channel_id=1, source_target_pairs={{0,9},{1,8},{2,11},{3,10},{4,13},{5,12},{6,15},{7,14},{8,1},{9,0},... | collective-permute-start | bytes 98312 | tf_op jit(solution)/shard_map/ppermute | solution.py:321
  27.1 2.2 %collective-permute-done.5 = f32[64,128]{1,0:T(8,128)S(1)} collective-permute-done((f32[64,128]{1,0:T(8,128)S(1)}, f32[64,128]{1,0:T(8,128)S(1)}, u32[]{:S(2)}, u32[]{:S(2)}) %collective-permute-start.5) | collective-permute-done | bytes 32800 | tf_op jit(solution)/shard_map/ppermute | solution.py:321
  29.3 2.5 %collective-permute-start.6 = (f32[64,128]{1,0:T(8,128)S(1)}, f32[64,128]{1,0:T(8,128)S(1)}, u32[]{:S(2)}, u32[]{:S(2)}) collective-permute-start(f32[64,128]{1,0:T(8,128)S(1)} %add.27), channel_id=1, source_target_pairs={{0,25},{1,24},{2,27},{3,26},{4,29},{5,28},{6,31},{7,30},{8,17},{9,... | collective-permute-start | bytes 98312 | tf_op jit(solution)/shard_map/ppermute | solution.py:321
  31.8 2.2 %collective-permute-done.6 = f32[64,128]{1,0:T(8,128)S(1)} collective-permute-done((f32[64,128]{1,0:T(8,128)S(1)}, f32[64,128]{1,0:T(8,128)S(1)}, u32[]{:S(2)}, u32[]{:S(2)}) %collective-permute-start.6) | collective-permute-done | bytes 32800 | tf_op jit(solution)/shard_map/ppermute | solution.py:321
  33.9 1.9 %collective-permute-start.7 = (f32[64,128]{1,0:T(8,128)S(1)}, f32[64,128]{1,0:T(8,128)S(1)}, u32[]{:S(2)}, u32[]{:S(2)}) collective-permute-start(f32[64,128]{1,0:T(8,128)S(1)} %add.28), channel_id=1, source_target_pairs={{0,33},{1,32},{2,35},{3,34},{4,37},{5,36},{6,39},{7,38},{8,41},{9,... | collective-permute-start | bytes 98312 | tf_op jit(solution)/shard_map/ppermute | solution.py:321
  35.8 1.6 %collective-permute-done.7 = f32[64,128]{1,0:T(8,128)S(1)} collective-permute-done((f32[64,128]{1,0:T(8,128)S(1)}, f32[64,128]{1,0:T(8,128)S(1)}, u32[]{:S(2)}, u32[]{:S(2)}) %collective-permute-start.7) | collective-permute-done | bytes 32800 | tf_op jit(solution)/shard_map/ppermute | solution.py:321
  37.4 5.7 %collective-permute-start.8 = (f32[64,128]{1,0:T(8,128)S(1)}, f32[64,128]{1,0:T(8,128)S(1)}, u32[]{:S(2)}, u32[]{:S(2)}) collective-permute-start(f32[64,128]{1,0:T(8,128)S(1)} %add.29), channel_id=1, source_target_pairs={{0,225},{1,224},{2,227},{3,226},{4,229},{5,228},{6,231},{7,230},{8... | collective-permute-start | bytes 98312 | tf_op jit(solution)/shard_map/ppermute | solution.py:321
  43.2 1.6 %collective-permute-done.8 = f32[64,128]{1,0:T(8,128)S(1)} collective-permute-done((f32[64,128]{1,0:T(8,128)S(1)}, f32[64,128]{1,0:T(8,128)S(1)}, u32[]{:S(2)}, u32[]{:S(2)}) %collective-permute-start.8) | collective-permute-done | bytes 32800 | tf_op jit(solution)/shard_map/ppermute | solution.py:321
  44.8 0.0 collective-permute-done.9.back_ref
  44.8 1.8 %collective-permute-start.10 = (f32[64,128]{1,0:T(8,128)S(1)}, f32[64,128]{1,0:T(8,128)S(1)}, u32[]{:S(2)}, u32[]{:S(2)}) collective-permute-start(f32[64,128]{1,0:T(8,128)S(1)} %add.30), channel_id=1, source_target_pairs={{0,97},{1,96},{2,99},{3,98},{4,101},{5,100},{6,103},{7,102},{8,105... | collective-permute-start | bytes 98312 | tf_op jit(solution)/shard_map/ppermute | solution.py:321
  46.6 4.0 %collective-permute-done.10 = f32[64,128]{1,0:T(8,128)S(1)} collective-permute-done((f32[64,128]{1,0:T(8,128)S(1)}, f32[64,128]{1,0:T(8,128)S(1)}, u32[]{:S(2)}, u32[]{:S(2)}) %collective-permute-start.10) | collective-permute-done | bytes 32800 | tf_op jit(solution)/shard_map/ppermute | solution.py:321
  50.6 0.4 collective-permute-start.11
  51.0 0.9 %shard_map.50.refs_0_ = f32[2,2,512,128]{3,2,1,0:T(8,128)} custom-call(f32[2,9,64,128]{3,2,1,0:T(8,128)S(1)} %get-tuple-element.23.held_ref, f32[2,4,64,128]{3,2,1,0:T(8,128)S(1)} %get-tuple-element.33.ahead_ref, f32[2,3,64,128]{3,2,1,0:T(8,128)S(1)} %collective-permute-done.9.back_ref, f32[64,128]{1,0:T(8,128)S(1)} %add.31.sum_ref), custom_call_target="tpu_custom_call" | custom-call | flops 1000000 | bytes 2097152 | tf_op jit(solution)/shard_map/pallas_call | solution.py:275
  51.9 0.0 collective-permute-done.11.sum_ref
  51.9 0.9 %shard_map.51 = f32[2,2,512,128]{3,2,1,0:T(8,128)} custom-call(f32[2,9,64,128]{3,2,1,0:T(8,128)S(1)} %get-tuple-element.23.held_ref, f32[2,4,64,128]{3,2,1,0:T(8,128)S(1)} %get-tuple-element.33.ahead_ref, f32[2,3,64,128]{3,2,1,0:T(8,128)S(1)} %collective-permute-done.9.back_ref, ...), custom_call_target="tpu_custom_call", output_to_operand_aliasing={{}: (4, {})} | custom-call | flops 1000000 | bytes 2097152 | tf_op jit(solution)/shard_map/pallas_call | solution.py:275
  (8 shorter events, 0.0 us)
Async XLA Ops:
  1.4 7.6 %collective-permute-start.1 = (f32[2,2,256,128]{3,2,1,0:T(8,128)S(1)}, f32[2,2,256,128]{3,2,1,0:T(8,128)S(1)}, u32[]{:S(2)}, u32[]{:S(2)}) collective-permute-start(f32[2,2,256,128]{3,2,1,0:T(8,128)S(1)} %bitcast.18), channel_id=1, source_target_pairs={{0,1},{1,0},{2,3},{3,2},{4,5},{5,4},{6,7},{7,6},{8,9},{9,8},{10,11... | collective-permute-start | bytes 1572872 | tf_op jit(solution)/shard_map/ppermute | solution.py:340
  4.7 8.9 %collective-permute-start = (f32[2,2,256,128]{3,2,1,0:T(8,128)S(1)}, f32[2,2,256,128]{3,2,1,0:T(8,128)S(1)}, u32[]{:S(2)}, u32[]{:S(2)}) collective-permute-start(f32[2,2,256,128]{3,2,1,0:T(8,128)S(1)} %bitcast.17), channel_id=1, source_target_pairs={{0,7},{1,2},{2,1},{3,4},{4,3},{5,6},{6,5},{7,0},{8,15},{9,10},{10,... | collective-permute-start | bytes 1572872 | tf_op jit(solution)/shard_map/ppermute | solution.py:341
  14.5 2.3 %collective-permute-start.2 = (f32[64,128]{1,0:T(8,128)S(1)}, f32[64,128]{1,0:T(8,128)S(1)}, u32[]{:S(2)}, u32[]{:S(2)}) collective-permute-start(f32[64,128]{1,0:T(8,128)S(1)} %get-tuple-element.35), channel_id=1, source_target_pairs={{0,1},{1,0},{2,3},{3,2},{4,5},{5,4},{6,7},{7,6},{8,9},{9,8},{10,11... | collective-permute-start | bytes 98312 | tf_op jit(solution)/shard_map/ppermute | solution.py:315
  16.8 3.3 %collective-permute-start.3 = (f32[64,128]{1,0:T(8,128)S(1)}, f32[64,128]{1,0:T(8,128)S(1)}, u32[]{:S(2)}, u32[]{:S(2)}) collective-permute-start(f32[64,128]{1,0:T(8,128)S(1)} %add.24), channel_id=1, source_target_pairs={{0,3},{1,2},{2,1},{3,0},{4,7},{5,6},{6,5},{7,4},{8,11},{9,10},{10,... | collective-permute-start | bytes 98312 | tf_op jit(solution)/shard_map/ppermute | solution.py:321
  20.2 4.6 %collective-permute-start.4 = (f32[64,128]{1,0:T(8,128)S(1)}, f32[64,128]{1,0:T(8,128)S(1)}, u32[]{:S(2)}, u32[]{:S(2)}) collective-permute-start(f32[64,128]{1,0:T(8,128)S(1)} %add.25), channel_id=1, source_target_pairs={{0,7},{1,6},{2,5},{3,4},{4,3},{5,2},{6,1},{7,0},{8,15},{9,14},{10,... | collective-permute-start | bytes 98312 | tf_op jit(solution)/shard_map/ppermute | solution.py:321
  24.7 20.0 %collective-permute-start.9 = (f32[2,3,64,128]{3,2,1,0:T(8,128)S(1)}, f32[2,3,64,128]{3,2,1,0:T(8,128)S(1)}, u32[]{:S(2)}, u32[]{:S(2)}) collective-permute-start(f32[2,3,64,128]{3,2,1,0:T(8,128)S(1)} %get-tuple-element.38), channel_id=1, source_target_pairs={{0,7},{1,0},{2,1},{3,2},{4,3},{5,4},{6,5},{7,6},{8,15},{9,8},{10,9... | collective-permute-start | bytes 589832 | tf_op jit(solution)/shard_map/ppermute | solution.py:320
  25.1 4.2 %collective-permute-start.5 = (f32[64,128]{1,0:T(8,128)S(1)}, f32[64,128]{1,0:T(8,128)S(1)}, u32[]{:S(2)}, u32[]{:S(2)}) collective-permute-start(f32[64,128]{1,0:T(8,128)S(1)} %add.26), channel_id=1, source_target_pairs={{0,9},{1,8},{2,11},{3,10},{4,13},{5,12},{6,15},{7,14},{8,1},{9,0},... | collective-permute-start | bytes 98312 | tf_op jit(solution)/shard_map/ppermute | solution.py:321
  29.3 4.6 %collective-permute-start.6 = (f32[64,128]{1,0:T(8,128)S(1)}, f32[64,128]{1,0:T(8,128)S(1)}, u32[]{:S(2)}, u32[]{:S(2)}) collective-permute-start(f32[64,128]{1,0:T(8,128)S(1)} %add.27), channel_id=1, source_target_pairs={{0,25},{1,24},{2,27},{3,26},{4,29},{5,28},{6,31},{7,30},{8,17},{9,... | collective-permute-start | bytes 98312 | tf_op jit(solution)/shard_map/ppermute | solution.py:321
  33.9 3.5 %collective-permute-start.7 = (f32[64,128]{1,0:T(8,128)S(1)}, f32[64,128]{1,0:T(8,128)S(1)}, u32[]{:S(2)}, u32[]{:S(2)}) collective-permute-start(f32[64,128]{1,0:T(8,128)S(1)} %add.28), channel_id=1, source_target_pairs={{0,33},{1,32},{2,35},{3,34},{4,37},{5,36},{6,39},{7,38},{8,41},{9,... | collective-permute-start | bytes 98312 | tf_op jit(solution)/shard_map/ppermute | solution.py:321
  37.4 7.3 %collective-permute-start.8 = (f32[64,128]{1,0:T(8,128)S(1)}, f32[64,128]{1,0:T(8,128)S(1)}, u32[]{:S(2)}, u32[]{:S(2)}) collective-permute-start(f32[64,128]{1,0:T(8,128)S(1)} %add.29), channel_id=1, source_target_pairs={{0,225},{1,224},{2,227},{3,226},{4,229},{5,228},{6,231},{7,230},{8... | collective-permute-start | bytes 98312 | tf_op jit(solution)/shard_map/ppermute | solution.py:321
  44.8 5.8 %collective-permute-start.10 = (f32[64,128]{1,0:T(8,128)S(1)}, f32[64,128]{1,0:T(8,128)S(1)}, u32[]{:S(2)}, u32[]{:S(2)}) collective-permute-start(f32[64,128]{1,0:T(8,128)S(1)} %add.30), channel_id=1, source_target_pairs={{0,97},{1,96},{2,99},{3,98},{4,101},{5,100},{6,103},{7,102},{8,105... | collective-permute-start | bytes 98312 | tf_op jit(solution)/shard_map/ppermute | solution.py:321
  50.6 1.3 %collective-permute-start.11 = (f32[64,128]{1,0:T(8,128)S(1)}, f32[64,128]{1,0:T(8,128)S(1)}, u32[]{:S(2)}, u32[]{:S(2)}) collective-permute-start(f32[64,128]{1,0:T(8,128)S(1)} %add.31.sum_ref), channel_id=1, source_target_pairs={{0,1},{1,0},{2,3},{3,2},{4,5},{5,4},{6,7},{7,6},{8,9},{9,8},{10,11... | collective-permute-start | bytes 98312 | tf_op jit(solution)/shard_map/ppermute | solution.py:324

commit v5 on v4

--- a/solution.py
+++ b/solution.py
@@ -250,12 +250,17 @@
             send_ref[...] = jnp.where(keeps_second, sums[0], sums[1])
 
 
-def clean_kernel(scale, own, held_ref, ahead_ref, back_ref, sum_ref, *refs):
-    out_ref, tile_ref, sems = refs[-3:]
-    p = kept_half() if own else 1 - kept_half()
-    base = sum_ref[...] * scale
+def clean_kernel(scale, *refs):
+    held_ref, mine_ref, out_ref, tile_ref, sems = refs[0], refs[1], refs[-3], refs[-2], refs[-1]
+    own = kept_half()
+    if len(refs) == 5:
+        parts = [(own, 0, mine_ref)]
+    else:
+        ahead_ref, back_ref, other_ref = refs[2:5]
+        parts = [(own, 1, mine_ref), (1 - own, 0, other_ref), (1 - own, 1, other_ref)]
     copies = []
-    for half in range(2):
+    for n, (p, half, sum_ref) in enumerate(parts):
+        base = sum_ref[...] * scale
         for f in range(8 * half, 8 * half + 8):
             if f < HELD:
                 power = held_ref[p, f]
@@ -263,22 +268,25 @@
                 power = ahead_ref[p, f - HELD]
             else:
                 power = back_ref[p, f - HELD - AHEAD]
-            tile_ref[half, pl.ds(f % 8, ROWS, stride=8), :] = power - base
-        copies.append(pltpu.make_async_copy(tile_ref.at[half], out_ref.at[p, half], sems.at[half]))
+            tile_ref[n, pl.ds(f % 8, ROWS, stride=8), :] = power - base
+        copies.append(pltpu.make_async_copy(tile_ref.at[n], out_ref.at[p, half], sems.at[n]))
         copies[-1].start()
     for copy in copies:
         copy.wait()
 
 
-def clean(scale, own, *args):
+def clean(scale, *args):
+    first = len(args) == 2
     far = [pl.BlockSpec(memory_space=pl.ANY)]
+    near = [pl.BlockSpec(memory_space=pltpu.VMEM)]
+    parts = 1 if first else 3
     return pl.pallas_call(
-        functools.partial(clean_kernel, scale, own),
+        functools.partial(clean_kernel, scale),
         out_shape=pltpu.HBM((2, 2, 8 * ROWS, LANES), jnp.float32),
-        in_specs=[pl.BlockSpec(memory_space=pltpu.VMEM)] * 4 + far * (len(args) - 4),
+        in_specs=near * 2 if first else near * 5 + far,
         out_specs=far[0],
-        scratch_shapes=[pltpu.VMEM((2, 8 * ROWS, LANES), jnp.float32), pltpu.SemaphoreType.DMA((2,))],
-        input_output_aliases={} if own else {4: 0},
+        scratch_shapes=[pltpu.VMEM((parts, 8 * ROWS, LANES), jnp.float32), pltpu.SemaphoreType.DMA((parts,))],
+        input_output_aliases={} if first else {5: 0},
         compiler_params=pltpu.CompilerParams(vmem_limit_bytes=16 << 20),
         cost_estimate=pl.CostEstimate(flops=10**6, bytes_accessed=2 << 20, transcendentals=0),
     )(*args)
@@ -319,8 +327,6 @@
             sums, back = lax.optimization_barrier((sums, back))
             back = lax.ppermute(back, "tm", left)
         sums = sums + lax.ppermute(sums, BOTH, swap_pairs(axis, partner))
-        if n == 5:
-            sums, back = lax.optimization_barrier((sums, back))
     return sums, lax.ppermute(sums, BOTH, cores), back
 
 
@@ -370,8 +376,8 @@
     )(part, cross, taps, table, twist, had, early)
     mine, other, back = total_over_all(mine, send, back)
     scale = 1.0 / (FRAMES * devices * lax.axis_size("beam"))
-    out = clean(scale, True, held, ahead, back, mine)
-    out = clean(scale, False, held, ahead, back, other, out)
+    out = clean(scale, held, mine)
+    out = clean(scale, held, mine, ahead, back, other, out)
     out = jnp.swapaxes(out.reshape(2, 2, ROWS, 8, LANES), 2, 3)
     return out.reshape(1, 2, FRAMES, CHANNELS)
 

time: 52.9 us -> 50.9 us (0.962)
  starting transfers between devices: 20.4 us -> 15.3 us
  waiting for transfers between devices: 22.7 us -> 25.7 us
    ppermute x7, starting transfers between devices: 14.9 us -> 9.81 us  [total_over_all(): sums = sums + lax.ppermute(sums, BOTH, swap_pairs(axis, partner))]
    ppermute x7, waiting for transfers between devices: 18.5 us -> 21.5 us  [total_over_all(): sums = sums + lax.ppermute(sums, BOTH, swap_pairs(axis, partner))]
  transfers between devices with their start and end apart: 12 -> 12, of which waited for: 9 -> 10; matrix products, arithmetic and copies ran while one was open for 0% -> 0% of each run, Pallas kernels for 12% -> 12%
where the time goes in v5:
time: 50.9 us; the launch traced here: 50.8 us
  waiting for transfers between devices  25.7 us (50%)
  starting transfers between devices  15.3 us (30%)
  Pallas kernels  9.58 us (19%)
    ppermute x7, waiting for transfers between devices, total_over_all(): sums = sums + lax.ppermute(sums, BOTH, swap_pairs(axis, partner))  21.5 us
    ppermute x7, starting transfers between devices, total_over_all(): sums = sums + lax.ppermute(sums, BOTH, swap_pairs(axis, partner))  9.81 us
    pallas_call x4, Pallas kernels, on_core(): pl.pallas_call(kernel, out_shape=shapes, in_specs=[pl.BlockSpec(memory_sp...  7.84 us
    ppermute x1, starting transfers between devices, body(): lax.ppermute(near.reshape(rows), 'tm', [(i, i ^ 1) for i in range(devices)])  3.33 us
    ppermute x1, waiting for transfers between devices, body(): lax.ppermute(cross.reshape(rows), 'tm', [(i, (i + 1 if i % 2 else i - 1)...  3.31 us
    pallas_call x2, Pallas kernels, clean(): pl.pallas_call(functools.partial(clean_kernel, scale), out_shape=pltpu.HB...  1.74 us
    ppermute x1, starting transfers between devices, total_over_all(): sums = mine + lax.ppermute(send, BOTH, cores)  1.43 us
  transfers between devices with their start and end apart: 12, of which 10 were waited for; matrix products, arithmetic and copies ran while one was open for 0% of the time, Pallas kernels for 12%

profile of v5, /device:TPU:1, one launch (start us, length us, event | category | flops | bytes accessed | tf_op | source)
XLA Modules:
  0.0 50.8 jit_solution(8256839961826690820)
XLA Ops:
  0.0 1.3 %shard_map.47 = (f32[2,2,64,4,128]{4,3,2,1,0:T(4,128)S(1)}, f32[2,2,64,4,128]{4,3,2,1,0:T(4,128)S(1)}) custom-call(f32[2,2,2,64,8,128]{5,4,3,2,1,0:T(8,128)} %bitcast.19), custom_call_target="tpu_custom_call" | custom-call | flops 1000 | bytes 1000 | tf_op jit(solution)/shard_map/pallas_call | solution.py:299
  1.4 3.3 %collective-permute-start.1 = (f32[2,2,256,128]{3,2,1,0:T(8,128)S(1)}, f32[2,2,256,128]{3,2,1,0:T(8,128)S(1)}, u32[]{:S(2)}, u32[]{:S(2)}) collective-permute-start(f32[2,2,256,128]{3,2,1,0:T(8,128)S(1)} %bitcast.18), channel_id=1, source_target_pairs={{0,1},{1,0},{2,3},{3,2},{4,5},{5,4},{6,7},{7,6},{8,9},{9,8},{10,11... | collective-permute-start | bytes 1572872 | tf_op jit(solution)/shard_map/ppermute | solution.py:346
  4.7 0.0 collective-permute-start
  4.7 4.3 %shard_map.46 = (f32[2,9,64,128]{3,2,1,0:T(8,128)S(1)}, f32[2,2,7,64,128]{4,3,2,1,0:T(8,128)S(1)}, f32[2,64,128]{2,1,0:T(8,128)S(1)}, f32[512,128]{1,0:T(8,128)S...) custom-call(f32[2,2,2,512,128]{4,3,2,1,0:T(8,128)} %bitcast.20, f32[512,128]{1,0:T(8,128)} %bitcast.21, ...), custom_call_target="tpu_custom_call" | custom-call | flops 2000000000 | bytes 6291456 | tf_op jit(solution)/shard_map/pallas_call | solution.py:299
  9.0 0.0 collective-permute-done.1.near_ref
  9.0 1.3 %shard_map.48 = (f32[2,4,64,128]{3,2,1,0:T(8,128)S(1)}, f32[2,64,128]{2,1,0:T(8,128)S(1)}) custom-call(f32[2,2,7,64,128]{4,3,2,1,0:T(8,128)S(1)} %get-tuple-element.22.part_ref, f32[2,2,256,128]{3,2,1,0:T(8,128)S(1)} %collective-permute-done.1.near_ref, f32[512,128]{1,0:T(8,128)S(1)} %get-tuple-element.24.taps_ref, ...), custom_call_target="tpu_custom_call" | custom-call | flops 1000000000 | bytes 3145728 | tf_op jit(solution)/shard_map/pallas_call | solution.py:299
  10.3 3.3 %collective-permute-done.cross_ref = f32[2,2,256,128]{3,2,1,0:T(8,128)S(1)} collective-permute-done((f32[2,2,256,128]{3,2,1,0:T(8,128)S(1)}, f32[2,2,256,128]{3,2,1,0:T(8,128)S(1)}, u32[]{:S(2)}, u32[]{:S(2)}) %collective-permute-start) | collective-permute-done | bytes 524320 | tf_op jit(solution)/shard_map/ppermute | solution.py:347
  13.6 0.9 %shard_map.49 = (f32[2,4,64,128]{3,2,1,0:T(8,128)S(1)}, f32[2,3,64,128]{3,2,1,0:T(8,128)S(1)}, f32[64,128]{1,0:T(8,128)S(1)}, f32[64,128]{1,0:T(8,128)S(1)}) custom-call(f32[2,2,7,64,128]{4,3,2,1,0:T(8,128)S(1)} %get-tuple-element.22.part_ref, f32[2,2,256,128]{3,2,1,0:T(8,128)S(1)} %collective-permute-done.cross_ref, ...), custom_call_target="tpu_custom_call" | custom-call | tf_op jit(solution)/shard_map/pallas_call | solution.py:299
  14.5 1.4 %collective-permute-start.2 = (f32[64,128]{1,0:T(8,128)S(1)}, f32[64,128]{1,0:T(8,128)S(1)}, u32[]{:S(2)}, u32[]{:S(2)}) collective-permute-start(f32[64,128]{1,0:T(8,128)S(1)} %get-tuple-element.32), channel_id=1, source_target_pairs={{0,1},{1,0},{2,3},{3,2},{4,5},{5,4},{6,7},{7,6},{8,9},{9,8},{10,11... | collective-permute-start | bytes 98312 | tf_op jit(solution)/shard_map/ppermute | solution.py:323
  16.0 0.9 %collective-permute-done.2 = f32[64,128]{1,0:T(8,128)S(1)} collective-permute-done((f32[64,128]{1,0:T(8,128)S(1)}, f32[64,128]{1,0:T(8,128)S(1)}, u32[]{:S(2)}, u32[]{:S(2)}) %collective-permute-start.2) | collective-permute-done | bytes 32800 | tf_op jit(solution)/shard_map/ppermute | solution.py:323
  16.8 0.0 collective-permute-start.3
  16.8 3.3 %collective-permute-done.3 = f32[64,128]{1,0:T(8,128)S(1)} collective-permute-done((f32[64,128]{1,0:T(8,128)S(1)}, f32[64,128]{1,0:T(8,128)S(1)}, u32[]{:S(2)}, u32[]{:S(2)}) %collective-permute-start.3) | collective-permute-done | bytes 32800 | tf_op jit(solution)/shard_map/ppermute | solution.py:329
  20.2 1.0 %collective-permute-start.4 = (f32[64,128]{1,0:T(8,128)S(1)}, f32[64,128]{1,0:T(8,128)S(1)}, u32[]{:S(2)}, u32[]{:S(2)}) collective-permute-start(f32[64,128]{1,0:T(8,128)S(1)} %add.25), channel_id=1, source_target_pairs={{0,7},{1,6},{2,5},{3,4},{4,3},{5,2},{6,1},{7,0},{8,15},{9,14},{10,... | collective-permute-start | bytes 98312 | tf_op jit(solution)/shard_map/ppermute | solution.py:329
  21.1 3.6 %collective-permute-done.4 = f32[64,128]{1,0:T(8,128)S(1)} collective-permute-done((f32[64,128]{1,0:T(8,128)S(1)}, f32[64,128]{1,0:T(8,128)S(1)}, u32[]{:S(2)}, u32[]{:S(2)}) %collective-permute-start.4) | collective-permute-done | bytes 32800 | tf_op jit(solution)/shard_map/ppermute | solution.py:329
  24.7 0.0 collective-permute-start.5
  24.8 0.4 collective-permute-start.10
  25.1 3.0 %collective-permute-done.5 = f32[64,128]{1,0:T(8,128)S(1)} collective-permute-done((f32[64,128]{1,0:T(8,128)S(1)}, f32[64,128]{1,0:T(8,128)S(1)}, u32[]{:S(2)}, u32[]{:S(2)}) %collective-permute-start.5) | collective-permute-done | bytes 32800 | tf_op jit(solution)/shard_map/ppermute | solution.py:329
  28.1 1.0 %collective-permute-start.6 = (f32[64,128]{1,0:T(8,128)S(1)}, f32[64,128]{1,0:T(8,128)S(1)}, u32[]{:S(2)}, u32[]{:S(2)}) collective-permute-start(f32[64,128]{1,0:T(8,128)S(1)} %add.27), channel_id=1, source_target_pairs={{0,25},{1,24},{2,27},{3,26},{4,29},{5,28},{6,31},{7,30},{8,17},{9,... | collective-permute-start | bytes 98312 | tf_op jit(solution)/shard_map/ppermute | solution.py:329
  29.1 3.5 %collective-permute-done.6 = f32[64,128]{1,0:T(8,128)S(1)} collective-permute-done((f32[64,128]{1,0:T(8,128)S(1)}, f32[64,128]{1,0:T(8,128)S(1)}, u32[]{:S(2)}, u32[]{:S(2)}) %collective-permute-start.6) | collective-permute-done | bytes 32800 | tf_op jit(solution)/shard_map/ppermute | solution.py:329
  32.7 0.9 %collective-permute-start.7 = (f32[64,128]{1,0:T(8,128)S(1)}, f32[64,128]{1,0:T(8,128)S(1)}, u32[]{:S(2)}, u32[]{:S(2)}) collective-permute-start(f32[64,128]{1,0:T(8,128)S(1)} %add.28), channel_id=1, source_target_pairs={{0,33},{1,32},{2,35},{3,34},{4,37},{5,36},{6,39},{7,38},{8,41},{9,... | collective-permute-start | bytes 98312 | tf_op jit(solution)/shard_map/ppermute | solution.py:329
  33.6 2.4 %collective-permute-done.7 = f32[64,128]{1,0:T(8,128)S(1)} collective-permute-done((f32[64,128]{1,0:T(8,128)S(1)}, f32[64,128]{1,0:T(8,128)S(1)}, u32[]{:S(2)}, u32[]{:S(2)}) %collective-permute-start.7) | collective-permute-done | bytes 32800 | tf_op jit(solution)/shard_map/ppermute | solution.py:329
  36.0 5.2 %collective-permute-start.8 = (f32[64,128]{1,0:T(8,128)S(1)}, f32[64,128]{1,0:T(8,128)S(1)}, u32[]{:S(2)}, u32[]{:S(2)}) collective-permute-start(f32[64,128]{1,0:T(8,128)S(1)} %add.29), channel_id=1, source_target_pairs={{0,225},{1,224},{2,227},{3,226},{4,229},{5,228},{6,231},{7,230},{8... | collective-permute-start | bytes 98312 | tf_op jit(solution)/shard_map/ppermute | solution.py:329
  41.2 1.6 %collective-permute-done.8 = f32[64,128]{1,0:T(8,128)S(1)} collective-permute-done((f32[64,128]{1,0:T(8,128)S(1)}, f32[64,128]{1,0:T(8,128)S(1)}, u32[]{:S(2)}, u32[]{:S(2)}) %collective-permute-start.8) | collective-permute-done | bytes 32800 | tf_op jit(solution)/shard_map/ppermute | solution.py:329
  42.8 1.7 %collective-permute-start.9 = (f32[64,128]{1,0:T(8,128)S(1)}, f32[64,128]{1,0:T(8,128)S(1)}, u32[]{:S(2)}, u32[]{:S(2)}) collective-permute-start(f32[64,128]{1,0:T(8,128)S(1)} %add.30), channel_id=1, source_target_pairs={{0,97},{1,96},{2,99},{3,98},{4,101},{5,100},{6,103},{7,102},{8,105... | collective-permute-start | bytes 98312 | tf_op jit(solution)/shard_map/ppermute | solution.py:329
  44.5 4.0 %collective-permute-done.9 = f32[64,128]{1,0:T(8,128)S(1)} collective-permute-done((f32[64,128]{1,0:T(8,128)S(1)}, f32[64,128]{1,0:T(8,128)S(1)}, u32[]{:S(2)}, u32[]{:S(2)}) %collective-permute-start.9) | collective-permute-done | bytes 32800 | tf_op jit(solution)/shard_map/ppermute | solution.py:329
  48.5 0.4 collective-permute-start.11
  48.9 0.8 %shard_map.50.refs_5_ = f32[2,2,512,128]{3,2,1,0:T(8,128)} custom-call(f32[2,9,64,128]{3,2,1,0:T(8,128)S(1)} %get-tuple-element.21.refs_0_, f32[64,128]{1,0:T(8,128)S(1)} %add.31.refs_1_), custom_call_target="tpu_custom_call" | custom-call | flops 1000000 | bytes 2097152 | tf_op jit(solution)/shard_map/pallas_call | solution.py:283
  49.7 0.1 collective-permute-done.11.refs_4_
  49.8 0.0 collective-permute-done.10.refs_3_
  49.8 1.0 %shard_map.51 = f32[2,2,512,128]{3,2,1,0:T(8,128)} custom-call(f32[2,9,64,128]{3,2,1,0:T(8,128)S(1)} %get-tuple-element.21.refs_0_, f32[64,128]{1,0:T(8,128)S(1)} %add.31.refs_1_, f32[2,4,64,128]{3,2,1,0:T(8,128)S(1)} %get-tuple-element.35.refs_2_, f32[2,3,64,128]{3,2,1,0:T(8,128)S(1)} %collective-permute-done.10.refs_3_, ...), custom_call_target="tpu_custom_call", output_to_operand_aliasing={{}: (5, {})} | custom-call | flops 1000000 | bytes 2097152 | tf_op jit(solution)/shard_map/pallas_call | solution.py:283
  (8 shorter events, 0.0 us)
Async XLA Ops:
  1.4 7.6 %collective-permute-start.1 = (f32[2,2,256,128]{3,2,1,0:T(8,128)S(1)}, f32[2,2,256,128]{3,2,1,0:T(8,128)S(1)}, u32[]{:S(2)}, u32[]{:S(2)}) collective-permute-start(f32[2,2,256,128]{3,2,1,0:T(8,128)S(1)} %bitcast.18), channel_id=1, source_target_pairs={{0,1},{1,0},{2,3},{3,2},{4,5},{5,4},{6,7},{7,6},{8,9},{9,8},{10,11... | collective-permute-start | bytes 1572872 | tf_op jit(solution)/shard_map/ppermute | solution.py:346
  4.7 8.9 %collective-permute-start = (f32[2,2,256,128]{3,2,1,0:T(8,128)S(1)}, f32[2,2,256,128]{3,2,1,0:T(8,128)S(1)}, u32[]{:S(2)}, u32[]{:S(2)}) collective-permute-start(f32[2,2,256,128]{3,2,1,0:T(8,128)S(1)} %bitcast.17), channel_id=1, source_target_pairs={{0,7},{1,2},{2,1},{3,4},{4,3},{5,6},{6,5},{7,0},{8,15},{9,10},{10,... | collective-permute-start | bytes 1572872 | tf_op jit(solution)/shard_map/ppermute | solution.py:347
  14.5 2.3 %collective-permute-start.2 = (f32[64,128]{1,0:T(8,128)S(1)}, f32[64,128]{1,0:T(8,128)S(1)}, u32[]{:S(2)}, u32[]{:S(2)}) collective-permute-start(f32[64,128]{1,0:T(8,128)S(1)} %get-tuple-element.32), channel_id=1, source_target_pairs={{0,1},{1,0},{2,3},{3,2},{4,5},{5,4},{6,7},{7,6},{8,9},{9,8},{10,11... | collective-permute-start | bytes 98312 | tf_op jit(solution)/shard_map/ppermute | solution.py:323
  16.8 3.3 %collective-permute-start.3 = (f32[64,128]{1,0:T(8,128)S(1)}, f32[64,128]{1,0:T(8,128)S(1)}, u32[]{:S(2)}, u32[]{:S(2)}) collective-permute-start(f32[64,128]{1,0:T(8,128)S(1)} %add.24), channel_id=1, source_target_pairs={{0,3},{1,2},{2,1},{3,0},{4,7},{5,6},{6,5},{7,4},{8,11},{9,10},{10,... | collective-permute-start | bytes 98312 | tf_op jit(solution)/shard_map/ppermute | solution.py:329
  20.2 4.6 %collective-permute-start.4 = (f32[64,128]{1,0:T(8,128)S(1)}, f32[64,128]{1,0:T(8,128)S(1)}, u32[]{:S(2)}, u32[]{:S(2)}) collective-permute-start(f32[64,128]{1,0:T(8,128)S(1)} %add.25), channel_id=1, source_target_pairs={{0,7},{1,6},{2,5},{3,4},{4,3},{5,2},{6,1},{7,0},{8,15},{9,14},{10,... | collective-permute-start | bytes 98312 | tf_op jit(solution)/shard_map/ppermute | solution.py:329
  24.7 3.3 %collective-permute-start.5 = (f32[64,128]{1,0:T(8,128)S(1)}, f32[64,128]{1,0:T(8,128)S(1)}, u32[]{:S(2)}, u32[]{:S(2)}) collective-permute-start(f32[64,128]{1,0:T(8,128)S(1)} %add.26), channel_id=1, source_target_pairs={{0,9},{1,8},{2,11},{3,10},{4,13},{5,12},{6,15},{7,14},{8,1},{9,0},... | collective-permute-start | bytes 98312 | tf_op jit(solution)/shard_map/ppermute | solution.py:329
  24.8 25.0 %collective-permute-start.10 = (f32[2,3,64,128]{3,2,1,0:T(8,128)S(1)}, f32[2,3,64,128]{3,2,1,0:T(8,128)S(1)}, u32[]{:S(2)}, u32[]{:S(2)}) collective-permute-start(f32[2,3,64,128]{3,2,1,0:T(8,128)S(1)} %get-tuple-element.36), channel_id=1, source_target_pairs={{0,7},{1,0},{2,1},{3,2},{4,3},{5,4},{6,5},{7,6},{8,15},{9,8},{10,9... | collective-permute-start | bytes 589832 | tf_op jit(solution)/shard_map/ppermute | solution.py:328
  28.1 4.6 %collective-permute-start.6 = (f32[64,128]{1,0:T(8,128)S(1)}, f32[64,128]{1,0:T(8,128)S(1)}, u32[]{:S(2)}, u32[]{:S(2)}) collective-permute-start(f32[64,128]{1,0:T(8,128)S(1)} %add.27), channel_id=1, source_target_pairs={{0,25},{1,24},{2,27},{3,26},{4,29},{5,28},{6,31},{7,30},{8,17},{9,... | collective-permute-start | bytes 98312 | tf_op jit(solution)/shard_map/ppermute | solution.py:329
  32.7 3.3 %collective-permute-start.7 = (f32[64,128]{1,0:T(8,128)S(1)}, f32[64,128]{1,0:T(8,128)S(1)}, u32[]{:S(2)}, u32[]{:S(2)}) collective-permute-start(f32[64,128]{1,0:T(8,128)S(1)} %add.28), channel_id=1, source_target_pairs={{0,33},{1,32},{2,35},{3,34},{4,37},{5,36},{6,39},{7,38},{8,41},{9,... | collective-permute-start | bytes 98312 | tf_op jit(solution)/shard_map/ppermute | solution.py:329
  36.0 6.8 %collective-permute-start.8 = (f32[64,128]{1,0:T(8,128)S(1)}, f32[64,128]{1,0:T(8,128)S(1)}, u32[]{:S(2)}, u32[]{:S(2)}) collective-permute-start(f32[64,128]{1,0:T(8,128)S(1)} %add.29), channel_id=1, source_target_pairs={{0,225},{1,224},{2,227},{3,226},{4,229},{5,228},{6,231},{7,230},{8... | collective-permute-start | bytes 98312 | tf_op jit(solution)/shard_map/ppermute | solution.py:329
  42.8 5.8 %collective-permute-start.9 = (f32[64,128]{1,0:T(8,128)S(1)}, f32[64,128]{1,0:T(8,128)S(1)}, u32[]{:S(2)}, u32[]{:S(2)}) collective-permute-start(f32[64,128]{1,0:T(8,128)S(1)} %add.30), channel_id=1, source_target_pairs={{0,97},{1,96},{2,99},{3,98},{4,101},{5,100},{6,103},{7,102},{8,105... | collective-permute-start | bytes 98312 | tf_op jit(solution)/shard_map/ppermute | solution.py:329
  48.5 1.3 %collective-permute-start.11 = (f32[64,128]{1,0:T(8,128)S(1)}, f32[64,128]{1,0:T(8,128)S(1)}, u32[]{:S(2)}, u32[]{:S(2)}) collective-permute-start(f32[64,128]{1,0:T(8,128)S(1)} %add.31.refs_1_), channel_id=1, source_target_pairs={{0,1},{1,0},{2,3},{3,2},{4,5},{5,4},{6,7},{7,6},{8,9},{9,8},{10,11... | collective-permute-start | bytes 98312 | tf_op jit(solution)/shard_map/ppermute | solution.py:330

commit v6 on v5

--- a/solution.py
+++ b/solution.py
@@ -16,8 +16,11 @@
 TAPS = 8
 FRAMES = 16
 HELD = 9
-AHEAD = 4
-BACK = 3
+RIM = FRAMES - HELD
+AHEAD = (4, 3)
+BACK = (3, 4)
+AHEAD_AT = (0, AHEAD[0])
+BACK_AT = (0, BACK[0])
 SHORT = pl.CostEstimate(flops=1000, bytes_accessed=1000, transcendentals=0)
 BOTH = ("beam", "tm")
 X, Y, Z = 4, 4, 8
@@ -106,6 +109,9 @@
     left = lax.broadcasted_iota(jnp.int32, (ROWS, LANES), 1) < ROWS
     out = []
     for g in range(0, count, 2):
+        if g + 1 == count:
+            out.append(jnp.concatenate([powers[:ROWS, g * ROWS :], powers[ROWS:, g * ROWS :]], axis=1))
+            break
         even = powers[:ROWS, g * ROWS : (g + 2) * ROWS]
         odd = powers[ROWS:, g * ROWS : (g + 2) * ROWS]
         out.append(jnp.where(left, even, pltpu.roll(odd, ROWS, 1)))
@@ -114,12 +120,14 @@
 
 
 def rim_copies(volt_ref, out_ref, sems, last):
-    half, at = (1, 8 - AHEAD) if last else (0, 0)
-    return [
-        pltpu.make_async_copy(volt_ref.at[p, c, half, :, at : at + AHEAD, :], out_ref.at[p, c], sems.at[2 * p + c])
-        for p in range(2)
-        for c in range(2)
-    ]
+    copies = []
+    for p in range(2):
+        for n in range(BACK[p] if last else AHEAD[p]):
+            f, slot = (FRAMES - BACK[p] + n, BACK_AT[p] + n) if last else (n, AHEAD_AT[p] + n)
+            for c in range(2):
+                frame = volt_ref.at[p, c, f // 8, :, f % 8, :]
+                copies.append(pltpu.make_async_copy(frame, out_ref.at[c, slot], sems.at[c, slot]))
+    return copies
 
 
 def rim_kernel(volt_ref, cross_ref, near_ref, sems):
@@ -127,8 +135,8 @@
 
         @pl.when(lax.axis_index("tm") % 2 == core)
         def _():
-            copies = rim_copies(volt_ref, near_ref, sems.at[0], core == 0)
-            copies += rim_copies(volt_ref, cross_ref, sems.at[1], core == 1)
+            copies = rim_copies(volt_ref, cross_ref, sems.at[1], core == 1)
+            copies += rim_copies(volt_ref, near_ref, sems.at[0], core == 0)
             for copy in copies:
                 copy.start()
             for copy in copies:
@@ -163,7 +171,7 @@
         for p in range(2):
             for c in range(2):
                 x = [volt_ref[p, c, f // 8, pl.ds(at + f % 8, 8, stride=8), :] for f in range(FRAMES)]
-                for f in range(HELD + AHEAD):
+                for f in range(HELD + AHEAD[p]):
                     total = taps[0] * x[f]
                     for t in range(1, min(TAPS, FRAMES - f)):
                         total = total + taps[t] * x[f + t]
@@ -171,11 +179,12 @@
                         filt_ref[p, c, f, rows, :] = total
                     else:
                         part_ref[p, c, f - HELD, rows, :] = total
-                for j in range(BACK):
-                    total = taps[BACK - j] * x[0]
-                    for t in range(BACK - j + 1, TAPS):
-                        total = total + taps[t] * x[t - BACK + j]
-                    part_ref[p, c, AHEAD + j, rows, :] = jnp.where(keep, total, 0.0)
+                for j in range(BACK[p]):
+                    reach = BACK[p] - j
+                    total = taps[reach] * x[0]
+                    for t in range(reach + 1, TAPS):
+                        total = total + taps[t] * x[t - reach]
+                    part_ref[p, c, AHEAD[p] + j, rows, :] = jnp.where(keep, total, 0.0)
         return 0
 
     lax.fori_loop(0, ROWS // 8, strip, 0)
@@ -193,30 +202,31 @@
 
 
 def rim_powers(role, part_ref, came_ref, taps_ref, table_ref, twist_ref, sums, keep, store):
-    slots = AHEAD if role == "ahead" else BACK
+    slots, at = (AHEAD, AHEAD_AT) if role == "ahead" else (BACK, BACK_AT)
     taps = [taps_ref[pl.ds(t, ROWS, stride=8), :] for t in range(TAPS)]
 
     def finished(p, j):
         out = []
         for c in range(2):
             if role == "ahead":
-                terms = [(FRAMES + i - HELD - j, i) for i in range(j + 1)]
+                terms = [(RIM + i - j, i) for i in range(j + 1)]
                 total = part_ref[p, c, j]
             else:
-                terms = [(t, AHEAD - BACK + j + t) for t in range(BACK - j)]
-                total = part_ref[p, c, AHEAD + j]
+                terms = [(t, j + t) for t in range(BACK[p] - j)]
+                total = part_ref[p, c, AHEAD[p] + j]
             rest = None
             for t, i in terms:
-                term = taps[t] * came_ref[p, c, pl.ds(i, ROWS, stride=AHEAD), :]
+                term = taps[t] * came_ref[c, at[p] + i]
                 rest = term if rest is None else rest + term
             out.append(total + (rest if keep is None else jnp.where(keep, rest, 0.0)))
         return tuple(out)
 
-    for start in range(0, slots, 2):
-        which = [(p, j) for j in range(start, min(start + 2, slots)) for p in range(2)]
+    every = [(p, j) for j in range(max(slots)) for p in range(2) if j < slots[p]]
+    for start in range(0, RIM, 4):
+        which = every[start : start + 4]
         frames = [finished(p, j) for p, j in which]
         for (p, j), power in zip(which, power_rows(frames, table_ref, twist_ref)):
-            store[p, j] = power
+            store[at[p] + j] = power
             sums[p] = sums[p] + power
     return sums
 
@@ -240,11 +250,8 @@
             sums = [had_ref[0], had_ref[1]]
             store, keep = (back_ref, None) if core == 0 else (ahead_ref, tm < last)
             sums = rim_powers(role, part_ref, cross_ref, taps_ref, table_ref, twist_ref, sums, keep, store)
-            for p in range(2):
-                if core == 0:
-                    ahead_ref[p] = early_ref[p]
-                else:
-                    back_ref[p] = early_ref[p, :BACK]
+            kept_ref = ahead_ref if core == 0 else back_ref
+            kept_ref[...] = early_ref[...]
             keeps_second = kept_half() == 1
             mine_ref[...] = jnp.where(keeps_second, sums[1], sums[0])
             send_ref[...] = jnp.where(keeps_second, sums[0], sums[1])
@@ -264,10 +271,12 @@
         for f in range(8 * half, 8 * half + 8):
             if f < HELD:
                 power = held_ref[p, f]
-            elif f < HELD + AHEAD:
-                power = ahead_ref[p, f - HELD]
+            elif f < HELD + min(AHEAD):
+                power = ahead_ref[jnp.where(p == 0, AHEAD_AT[0], AHEAD_AT[1]) + f - HELD]
+            elif f >= FRAMES - min(BACK):
+                power = back_ref[jnp.where(p == 0, BACK_AT[0] + BACK[0], BACK_AT[1] + BACK[1]) + f - FRAMES]
             else:
-                power = back_ref[p, f - HELD - AHEAD]
+                power = jnp.where(p == 0, ahead_ref[AHEAD_AT[0] + f - HELD], back_ref[BACK_AT[1] + f - FRAMES + BACK[1]])
             tile_ref[n, pl.ds(f % 8, ROWS, stride=8), :] = power - base
         copies.append(pltpu.make_async_copy(tile_ref.at[n], out_ref.at[p, half], sems.at[n]))
         copies[-1].start()
@@ -321,9 +330,9 @@
     cores = [(i, i ^ 1) for i in range(2 * X * Y * Z)]
     left = [(i, (i - 1) % (2 * Y)) for i in range(2 * Y)]
     sums = mine + lax.ppermute(send, BOTH, cores)
-    steps = [("y", r) for r in RING4] + [("x", r) for r in RING4] + [("z", r) for r in RING8]
+    steps = [("x", r) for r in RING4] + [("y", r) for r in RING4] + [("z", r) for r in RING8]
     for n, (axis, partner) in enumerate(steps):
-        if n == 2:
+        if n == 1:
             sums, back = lax.optimization_barrier((sums, back))
             back = lax.ppermute(back, "tm", left)
         sums = sums + lax.ppermute(sums, BOTH, swap_pairs(axis, partner))
@@ -334,23 +343,22 @@
     devices = lax.axis_size("tm")
     table, twist = (jnp.asarray(t) for t in dft_tables())
     tiles = jnp.swapaxes(voltages[0].reshape(2, 2, 2, 8, ROWS, LANES), 3, 4)
-    rim = (2, 2, ROWS, AHEAD, LANES)
-    rows = (2, 2, ROWS * AHEAD, LANES)
+    rim = (2, RIM, ROWS, LANES)
     cross, near = on_core(
         rim_kernel,
         [rim, rim],
-        scratch=[pltpu.SemaphoreType.DMA((2, 4))],
+        scratch=[pltpu.SemaphoreType.DMA((2, 2, RIM))],
         far=True,
         cost=SHORT,
     )(in_hbm(tiles))
-    near = lax.ppermute(near.reshape(rows), "tm", [(i, i ^ 1) for i in range(devices)])
-    cross = lax.ppermute(cross.reshape(rows), "tm", [(i, (i + 1 if i % 2 else i - 1) % devices) for i in range(devices)])
+    near = lax.ppermute(near, "tm", [(i, i ^ 1) for i in range(devices)])
+    cross = lax.ppermute(cross, "tm", [(i, (i + 1 if i % 2 else i - 1) % devices) for i in range(devices)])
     strips = (2, 2, 2, ROWS * 8, LANES)
     held, part, had, taps, table, twist = on_core(
         held_kernel,
         [
             (2, HELD, ROWS, LANES),
-            (2, 2, AHEAD + BACK, ROWS, LANES),
+            (2, 2, RIM, ROWS, LANES),
             (2, ROWS, LANES),
             (ROWS * TAPS, LANES),
             pltpu.VMEM(table.shape, table.dtype),
@@ -367,12 +375,12 @@
     )(in_hbm(tiles.reshape(strips)), in_hbm(by_rows(filter_taps)), in_hbm(table), in_hbm(twist))
     early, had = on_core(
         near_kernel,
-        [(2, AHEAD, ROWS, LANES), (2, ROWS, LANES)],
+        [(RIM, ROWS, LANES), (2, ROWS, LANES)],
         cost=pl.CostEstimate(flops=10**9, bytes_accessed=3 << 20, transcendentals=0),
     )(part, near, taps, table, twist, had)
     ahead, back, mine, send = on_core(
         functools.partial(cross_kernel, devices - 1),
-        [(2, AHEAD, ROWS, LANES), (2, BACK, ROWS, LANES), (ROWS, LANES), (ROWS, LANES)],
+        [(RIM, ROWS, LANES), (RIM, ROWS, LANES), (ROWS, LANES), (ROWS, LANES)],
     )(part, cross, taps, table, twist, had, early)
     mine, other, back = total_over_all(mine, send, back)
     scale = 1.0 / (FRAMES * devices * lax.axis_size("beam"))

time: 50.9 us -> 50.4 us (level)
  waiting for transfers between devices: 25.7 us -> 24.5 us
  starting transfers between devices: 15.3 us -> 16.4 us
    ppermute x7, starting transfers between devices: 9.81 us -> 11.4 us  [total_over_all(): sums = sums + lax.ppermute(sums, BOTH, swap_pairs(axis, partner))]
    ppermute x7, waiting for transfers between devices: 21.5 us -> 20.6 us  [total_over_all(): sums = sums + lax.ppermute(sums, BOTH, swap_pairs(axis, partner))]
where the time goes in v6:
time: 50.4 us; the launch traced here: 50.2 us
  waiting for transfers between devices  24.5 us (49%)
  starting transfers between devices  16.4 us (33%)
  Pallas kernels  9.18 us (18%)
    ppermute x7, waiting for transfers between devices, total_over_all(): sums = sums + lax.ppermute(sums, BOTH, swap_pairs(axis, partner))  20.6 us
    ppermute x7, starting transfers between devices, total_over_all(): sums = sums + lax.ppermute(sums, BOTH, swap_pairs(axis, partner))  11.4 us
    pallas_call x4, Pallas kernels, on_core(): pl.pallas_call(kernel, out_shape=shapes, in_specs=[pl.BlockSpec(memory_sp...  7.45 us
    ppermute x1, starting transfers between devices, body(): near = lax.ppermute(near, 'tm', [(i, i ^ 1) for i in range(devices)])  3.33 us
    ppermute x1, waiting for transfers between devices, body(): lax.ppermute(cross, 'tm', [(i, (i + 1 if i % 2 else i - 1) % devices) for...  2.99 us
    pallas_call x2, Pallas kernels, clean(): pl.pallas_call(functools.partial(clean_kernel, scale), out_shape=pltpu.HB...  1.74 us
    ppermute x1, starting transfers between devices, total_over_all(): sums = mine + lax.ppermute(send, BOTH, cores)  1.09 us
  transfers between devices with their start and end apart: 12, of which 10 were waited for; matrix products, arithmetic and copies ran while one was open for 0% of the time, Pallas kernels for 12%

profile of v6, /device:TPU:1, one launch (start us, length us, event | category | flops | bytes accessed | tf_op | source)
XLA Modules:
  0.0 50.2 jit_solution(16007143156696338089)
XLA Ops:
  0.0 1.4 %shard_map.47 = (f32[2,7,64,128]{3,2,1,0:T(8,128)S(1)}, f32[2,7,64,128]{3,2,1,0:T(8,128)S(1)}) custom-call(f32[2,2,2,64,8,128]{5,4,3,2,1,0:T(8,128)} %bitcast.15), custom_call_target="tpu_custom_call" | custom-call | flops 1000 | bytes 1000 | tf_op jit(solution)/shard_map/pallas_call | solution.py:308
  1.4 3.3 %collective-permute-start.1 = (f32[2,7,64,128]{3,2,1,0:T(8,128)S(1)}, f32[2,7,64,128]{3,2,1,0:T(8,128)S(1)}, u32[]{:S(2)}, u32[]{:S(2)}) collective-permute-start(f32[2,7,64,128]{3,2,1,0:T(8,128)S(1)} %get-tuple-element.27), channel_id=1, source_target_pairs={{0,1},{1,0},{2,3},{3,2},{4,5},{5,4},{6,7},{7,6},{8,9},{9,8},{10,11... | collective-permute-start | bytes 1376264 | tf_op jit(solution)/shard_map/ppermute | solution.py:354
  4.7 0.0 collective-permute-start
  4.7 4.3 %shard_map.46 = (f32[2,9,64,128]{3,2,1,0:T(8,128)S(1)}, f32[2,2,7,64,128]{4,3,2,1,0:T(8,128)S(1)}, f32[2,64,128]{2,1,0:T(8,128)S(1)}, f32[512,128]{1,0:T(8,128)S...) custom-call(f32[2,2,2,512,128]{4,3,2,1,0:T(8,128)} %bitcast.16, f32[512,128]{1,0:T(8,128)} %bitcast.17, ...), custom_call_target="tpu_custom_call" | custom-call | flops 2000000000 | bytes 6291456 | tf_op jit(solution)/shard_map/pallas_call | solution.py:308
  9.0 0.0 collective-permute-done.1.near_ref
  9.0 0.9 %shard_map.48 = (f32[7,64,128]{2,1,0:T(8,128)S(1)}, f32[2,64,128]{2,1,0:T(8,128)S(1)}) custom-call(f32[2,2,7,64,128]{4,3,2,1,0:T(8,128)S(1)} %get-tuple-element.22.part_ref, f32[2,7,64,128]{3,2,1,0:T(8,128)S(1)} %collective-permute-done.1.near_ref, f32[512,128]{1,0:T(8,128)S(1)} %get-tuple-element.24.taps_ref, ...), custom_call_target="tpu_custom_call" | custom-call | flops 1000000000 | bytes 3145728 | tf_op jit(solution)/shard_map/pallas_call | solution.py:308
  9.9 3.0 %collective-permute-done.cross_ref = f32[2,7,64,128]{3,2,1,0:T(8,128)S(1)} collective-permute-done((f32[2,7,64,128]{3,2,1,0:T(8,128)S(1)}, f32[2,7,64,128]{3,2,1,0:T(8,128)S(1)}, u32[]{:S(2)}, u32[]{:S(2)}) %collective-permute-start) | collective-permute-done | bytes 458784 | tf_op jit(solution)/shard_map/ppermute | solution.py:355
  12.9 0.9 %shard_map.49 = (f32[7,64,128]{2,1,0:T(8,128)S(1)}, f32[7,64,128]{2,1,0:T(8,128)S(1)}, f32[64,128]{1,0:T(8,128)S(1)}, f32[64,128]{1,0:T(8,128)S(1)}) custom-call(f32[2,2,7,64,128]{4,3,2,1,0:T(8,128)S(1)} %get-tuple-element.22.part_ref, f32[2,7,64,128]{3,2,1,0:T(8,128)S(1)} %collective-permute-done.cross_ref, f32[512,128]{1,0:T(8,128)S(1)} %get-tuple-element.24.taps_ref, ...), custom_call_target="tpu_custom_call" | custom-call | tf_op jit(solution)/shard_map/pallas_call | solution.py:308
  13.8 1.1 %collective-permute-start.2 = (f32[64,128]{1,0:T(8,128)S(1)}, f32[64,128]{1,0:T(8,128)S(1)}, u32[]{:S(2)}, u32[]{:S(2)}) collective-permute-start(f32[64,128]{1,0:T(8,128)S(1)} %get-tuple-element.32), channel_id=1, source_target_pairs={{0,1},{1,0},{2,3},{3,2},{4,5},{5,4},{6,7},{7,6},{8,9},{9,8},{10,11... | collective-permute-start | bytes 98312 | tf_op jit(solution)/shard_map/ppermute | solution.py:332
  14.9 0.9 %collective-permute-done.2 = f32[64,128]{1,0:T(8,128)S(1)} collective-permute-done((f32[64,128]{1,0:T(8,128)S(1)}, f32[64,128]{1,0:T(8,128)S(1)}, u32[]{:S(2)}, u32[]{:S(2)}) %collective-permute-start.2) | collective-permute-done | bytes 32800 | tf_op jit(solution)/shard_map/ppermute | solution.py:332
  15.8 0.0 collective-permute-start.3
  15.8 3.3 %collective-permute-done.3 = f32[64,128]{1,0:T(8,128)S(1)} collective-permute-done((f32[64,128]{1,0:T(8,128)S(1)}, f32[64,128]{1,0:T(8,128)S(1)}, u32[]{:S(2)}, u32[]{:S(2)}) %collective-permute-start.3) | collective-permute-done | bytes 32800 | tf_op jit(solution)/shard_map/ppermute | solution.py:338
  19.1 1.0 %collective-permute-start.4 = (f32[64,128]{1,0:T(8,128)S(1)}, f32[64,128]{1,0:T(8,128)S(1)}, u32[]{:S(2)}, u32[]{:S(2)}) collective-permute-start(f32[64,128]{1,0:T(8,128)S(1)} %add.25), channel_id=1, source_target_pairs={{0,25},{1,24},{2,27},{3,26},{4,29},{5,28},{6,31},{7,30},{8,17},{9,... | collective-permute-start | bytes 98312 | tf_op jit(solution)/shard_map/ppermute | solution.py:338
  20.2 0.2 collective-permute-start.10
  20.3 3.3 %collective-permute-done.4 = f32[64,128]{1,0:T(8,128)S(1)} collective-permute-done((f32[64,128]{1,0:T(8,128)S(1)}, f32[64,128]{1,0:T(8,128)S(1)}, u32[]{:S(2)}, u32[]{:S(2)}) %collective-permute-start.4) | collective-permute-done | bytes 32800 | tf_op jit(solution)/shard_map/ppermute | solution.py:338
  23.7 0.0 collective-permute-start.5
  23.7 3.3 %collective-permute-done.5 = f32[64,128]{1,0:T(8,128)S(1)} collective-permute-done((f32[64,128]{1,0:T(8,128)S(1)}, f32[64,128]{1,0:T(8,128)S(1)}, u32[]{:S(2)}, u32[]{:S(2)}) %collective-permute-start.5) | collective-permute-done | bytes 32800 | tf_op jit(solution)/shard_map/ppermute | solution.py:338
  27.0 1.3 %collective-permute-start.6 = (f32[64,128]{1,0:T(8,128)S(1)}, f32[64,128]{1,0:T(8,128)S(1)}, u32[]{:S(2)}, u32[]{:S(2)}) collective-permute-start(f32[64,128]{1,0:T(8,128)S(1)} %add.27), channel_id=1, source_target_pairs={{0,7},{1,6},{2,5},{3,4},{4,3},{5,2},{6,1},{7,0},{8,15},{9,14},{10,... | collective-permute-start | bytes 98312 | tf_op jit(solution)/shard_map/ppermute | solution.py:338
  28.3 3.3 %collective-permute-done.6 = f32[64,128]{1,0:T(8,128)S(1)} collective-permute-done((f32[64,128]{1,0:T(8,128)S(1)}, f32[64,128]{1,0:T(8,128)S(1)}, u32[]{:S(2)}, u32[]{:S(2)}) %collective-permute-start.6) | collective-permute-done | bytes 32800 | tf_op jit(solution)/shard_map/ppermute | solution.py:338
  31.6 1.7 %collective-permute-start.7 = (f32[64,128]{1,0:T(8,128)S(1)}, f32[64,128]{1,0:T(8,128)S(1)}, u32[]{:S(2)}, u32[]{:S(2)}) collective-permute-start(f32[64,128]{1,0:T(8,128)S(1)} %add.28), channel_id=1, source_target_pairs={{0,33},{1,32},{2,35},{3,34},{4,37},{5,36},{6,39},{7,38},{8,41},{9,... | collective-permute-start | bytes 98312 | tf_op jit(solution)/shard_map/ppermute | solution.py:338
  33.3 1.6 %collective-permute-done.7 = f32[64,128]{1,0:T(8,128)S(1)} collective-permute-done((f32[64,128]{1,0:T(8,128)S(1)}, f32[64,128]{1,0:T(8,128)S(1)}, u32[]{:S(2)}, u32[]{:S(2)}) %collective-permute-start.7) | collective-permute-done | bytes 32800 | tf_op jit(solution)/shard_map/ppermute | solution.py:338
  34.9 5.7 %collective-permute-start.8 = (f32[64,128]{1,0:T(8,128)S(1)}, f32[64,128]{1,0:T(8,128)S(1)}, u32[]{:S(2)}, u32[]{:S(2)}) collective-permute-start(f32[64,128]{1,0:T(8,128)S(1)} %add.29), channel_id=1, source_target_pairs={{0,225},{1,224},{2,227},{3,226},{4,229},{5,228},{6,231},{7,230},{8... | collective-permute-start | bytes 98312 | tf_op jit(solution)/shard_map/ppermute | solution.py:338
  40.6 1.6 %collective-permute-done.8 = f32[64,128]{1,0:T(8,128)S(1)} collective-permute-done((f32[64,128]{1,0:T(8,128)S(1)}, f32[64,128]{1,0:T(8,128)S(1)}, u32[]{:S(2)}, u32[]{:S(2)}) %collective-permute-start.8) | collective-permute-done | bytes 32800 | tf_op jit(solution)/shard_map/ppermute | solution.py:338
  42.2 1.7 %collective-permute-start.9 = (f32[64,128]{1,0:T(8,128)S(1)}, f32[64,128]{1,0:T(8,128)S(1)}, u32[]{:S(2)}, u32[]{:S(2)}) collective-permute-start(f32[64,128]{1,0:T(8,128)S(1)} %add.30), channel_id=1, source_target_pairs={{0,97},{1,96},{2,99},{3,98},{4,101},{5,100},{6,103},{7,102},{8,105... | collective-permute-start | bytes 98312 | tf_op jit(solution)/shard_map/ppermute | solution.py:338
  43.9 4.0 %collective-permute-done.9 = f32[64,128]{1,0:T(8,128)S(1)} collective-permute-done((f32[64,128]{1,0:T(8,128)S(1)}, f32[64,128]{1,0:T(8,128)S(1)}, u32[]{:S(2)}, u32[]{:S(2)}) %collective-permute-start.9) | collective-permute-done | bytes 32800 | tf_op jit(solution)/shard_map/ppermute | solution.py:338
  48.0 0.4 collective-permute-start.11
  48.4 0.8 %shard_map.50.refs_5_ = f32[2,2,512,128]{3,2,1,0:T(8,128)} custom-call(f32[2,9,64,128]{3,2,1,0:T(8,128)S(1)} %get-tuple-element.21.refs_0_, f32[64,128]{1,0:T(8,128)S(1)} %add.31.refs_1_), custom_call_target="tpu_custom_call" | custom-call | flops 1000000 | bytes 2097152 | tf_op jit(solution)/shard_map/pallas_call | solution.py:292
  49.2 0.0 collective-permute-done.10.refs_3_
  49.2 0.1 collective-permute-done.11.refs_4_
  49.2 1.0 %shard_map.51 = f32[2,2,512,128]{3,2,1,0:T(8,128)} custom-call(f32[2,9,64,128]{3,2,1,0:T(8,128)S(1)} %get-tuple-element.21.refs_0_, f32[64,128]{1,0:T(8,128)S(1)} %add.31.refs_1_, f32[7,64,128]{2,1,0:T(8,128)S(1)} %get-tuple-element.35.refs_2_, f32[7,64,128]{2,1,0:T(8,128)S(1)} %collective-permute-done.10.refs_3_, ...), custom_call_target="tpu_custom_call", output_to_operand_aliasing={{}: (5, {})} | custom-call | flops 1000000 | bytes 2097152 | tf_op jit(solution)/shard_map/pallas_call | solution.py:292
  (8 shorter events, 0.0 us)
Async XLA Ops:
  1.4 7.6 %collective-permute-start.1 = (f32[2,7,64,128]{3,2,1,0:T(8,128)S(1)}, f32[2,7,64,128]{3,2,1,0:T(8,128)S(1)}, u32[]{:S(2)}, u32[]{:S(2)}) collective-permute-start(f32[2,7,64,128]{3,2,1,0:T(8,128)S(1)} %get-tuple-element.27), channel_id=1, source_target_pairs={{0,1},{1,0},{2,3},{3,2},{4,5},{5,4},{6,7},{7,6},{8,9},{9,8},{10,11... | collective-permute-start | bytes 1376264 | tf_op jit(solution)/shard_map/ppermute | solution.py:354
  4.7 8.2 %collective-permute-start = (f32[2,7,64,128]{3,2,1,0:T(8,128)S(1)}, f32[2,7,64,128]{3,2,1,0:T(8,128)S(1)}, u32[]{:S(2)}, u32[]{:S(2)}) collective-permute-start(f32[2,7,64,128]{3,2,1,0:T(8,128)S(1)} %get-tuple-element.23), channel_id=1, source_target_pairs={{0,7},{1,2},{2,1},{3,4},{4,3},{5,6},{6,5},{7,0},{8,15},{9,10},{10,... | collective-permute-start | bytes 1376264 | tf_op jit(solution)/shard_map/ppermute | solution.py:355
  13.8 2.0 %collective-permute-start.2 = (f32[64,128]{1,0:T(8,128)S(1)}, f32[64,128]{1,0:T(8,128)S(1)}, u32[]{:S(2)}, u32[]{:S(2)}) collective-permute-start(f32[64,128]{1,0:T(8,128)S(1)} %get-tuple-element.32), channel_id=1, source_target_pairs={{0,1},{1,0},{2,3},{3,2},{4,5},{5,4},{6,7},{7,6},{8,9},{9,8},{10,11... | collective-permute-start | bytes 98312 | tf_op jit(solution)/shard_map/ppermute | solution.py:332
  15.8 3.3 %collective-permute-start.3 = (f32[64,128]{1,0:T(8,128)S(1)}, f32[64,128]{1,0:T(8,128)S(1)}, u32[]{:S(2)}, u32[]{:S(2)}) collective-permute-start(f32[64,128]{1,0:T(8,128)S(1)} %add.24), channel_id=1, source_target_pairs={{0,9},{1,8},{2,11},{3,10},{4,13},{5,12},{6,15},{7,14},{8,1},{9,0},... | collective-permute-start | bytes 98312 | tf_op jit(solution)/shard_map/ppermute | solution.py:338
  19.1 4.6 %collective-permute-start.4 = (f32[64,128]{1,0:T(8,128)S(1)}, f32[64,128]{1,0:T(8,128)S(1)}, u32[]{:S(2)}, u32[]{:S(2)}) collective-permute-start(f32[64,128]{1,0:T(8,128)S(1)} %add.25), channel_id=1, source_target_pairs={{0,25},{1,24},{2,27},{3,26},{4,29},{5,28},{6,31},{7,30},{8,17},{9,... | collective-permute-start | bytes 98312 | tf_op jit(solution)/shard_map/ppermute | solution.py:338
  20.2 29.0 %collective-permute-start.10 = (f32[7,64,128]{2,1,0:T(8,128)S(1)}, f32[7,64,128]{2,1,0:T(8,128)S(1)}, u32[]{:S(2)}, u32[]{:S(2)}) collective-permute-start(f32[7,64,128]{2,1,0:T(8,128)S(1)} %get-tuple-element.36), channel_id=1, source_target_pairs={{0,7},{1,0},{2,1},{3,2},{4,3},{5,4},{6,5},{7,6},{8,15},{9,8},{10,9... | collective-permute-start | bytes 688136 | tf_op jit(solution)/shard_map/ppermute | solution.py:337
  23.7 3.3 %collective-permute-start.5 = (f32[64,128]{1,0:T(8,128)S(1)}, f32[64,128]{1,0:T(8,128)S(1)}, u32[]{:S(2)}, u32[]{:S(2)}) collective-permute-start(f32[64,128]{1,0:T(8,128)S(1)} %add.26), channel_id=1, source_target_pairs={{0,3},{1,2},{2,1},{3,0},{4,7},{5,6},{6,5},{7,4},{8,11},{9,10},{10,... | collective-permute-start | bytes 98312 | tf_op jit(solution)/shard_map/ppermute | solution.py:338
  27.0 4.6 %collective-permute-start.6 = (f32[64,128]{1,0:T(8,128)S(1)}, f32[64,128]{1,0:T(8,128)S(1)}, u32[]{:S(2)}, u32[]{:S(2)}) collective-permute-start(f32[64,128]{1,0:T(8,128)S(1)} %add.27), channel_id=1, source_target_pairs={{0,7},{1,6},{2,5},{3,4},{4,3},{5,2},{6,1},{7,0},{8,15},{9,14},{10,... | collective-permute-start | bytes 98312 | tf_op jit(solution)/shard_map/ppermute | solution.py:338
  31.6 3.3 %collective-permute-start.7 = (f32[64,128]{1,0:T(8,128)S(1)}, f32[64,128]{1,0:T(8,128)S(1)}, u32[]{:S(2)}, u32[]{:S(2)}) collective-permute-start(f32[64,128]{1,0:T(8,128)S(1)} %add.28), channel_id=1, source_target_pairs={{0,33},{1,32},{2,35},{3,34},{4,37},{5,36},{6,39},{7,38},{8,41},{9,... | collective-permute-start | bytes 98312 | tf_op jit(solution)/shard_map/ppermute | solution.py:338
  34.9 7.3 %collective-permute-start.8 = (f32[64,128]{1,0:T(8,128)S(1)}, f32[64,128]{1,0:T(8,128)S(1)}, u32[]{:S(2)}, u32[]{:S(2)}) collective-permute-start(f32[64,128]{1,0:T(8,128)S(1)} %add.29), channel_id=1, source_target_pairs={{0,225},{1,224},{2,227},{3,226},{4,229},{5,228},{6,231},{7,230},{8... | collective-permute-start | bytes 98312 | tf_op jit(solution)/shard_map/ppermute | solution.py:338
  42.2 5.8 %collective-permute-start.9 = (f32[64,128]{1,0:T(8,128)S(1)}, f32[64,128]{1,0:T(8,128)S(1)}, u32[]{:S(2)}, u32[]{:S(2)}) collective-permute-start(f32[64,128]{1,0:T(8,128)S(1)} %add.30), channel_id=1, source_target_pairs={{0,97},{1,96},{2,99},{3,98},{4,101},{5,100},{6,103},{7,102},{8,105... | collective-permute-start | bytes 98312 | tf_op jit(solution)/shard_map/ppermute | solution.py:338
  48.0 1.3 %collective-permute-start.11 = (f32[64,128]{1,0:T(8,128)S(1)}, f32[64,128]{1,0:T(8,128)S(1)}, u32[]{:S(2)}, u32[]{:S(2)}) collective-permute-start(f32[64,128]{1,0:T(8,128)S(1)} %add.31.refs_1_), channel_id=1, source_target_pairs={{0,1},{1,0},{2,3},{3,2},{4,5},{5,4},{6,7},{7,6},{8,9},{9,8},{10,11... | collective-permute-start | bytes 98312 | tf_op jit(solution)/shard_map/ppermute | solution.py:339

commit v7 on v6

--- a/solution.py
+++ b/solution.py
@@ -26,7 +26,7 @@
 X, Y, Z = 4, 4, 8
 
 RING4 = ((1, 0, 3, 2), (3, 2, 1, 0))
-RING8 = ((1, 0, 3, 2, 5, 4, 7, 6), (7, 2, 1, 4, 3, 6, 5, 0), (3, 6, 5, 0, 7, 2, 1, 4))
+RING8 = ((1, 0, 3, 2, 5, 4, 7, 6), (2, 3, 0, 1, 6, 7, 4, 5), (7, 6, 5, 4, 3, 2, 1, 0))
 
 
 def place(z, x, y, core):
@@ -49,7 +49,8 @@
 
 def kept_half():
     tm, beam = lax.axis_index("tm"), lax.axis_index("beam")
-    return (tm % 2 + tm // 2 + beam % X + beam // X) % 2
+    z = beam // X
+    return (tm % 2 + tm // 2 + beam % X + z + z // 2 + z // 4) % 2
 
 
 def in_two(table):

time: 50.4 us -> 50.3 us (level)
  waiting for transfers between devices: 24.5 us -> 23.4 us
  starting transfers between devices: 16.4 us -> 17.4 us
    ppermute x7, waiting for transfers between devices: 20.6 us -> 19.5 us  [total_over_all(): sums = sums + lax.ppermute(sums, BOTH, swap_pairs(axis, partner))]
    ppermute x7, starting transfers between devices: 11.4 us -> 12.4 us  [total_over_all(): sums = sums + lax.ppermute(sums, BOTH, swap_pairs(axis, partner))]
where the time goes in v7:
time: 50.3 us; the launch traced here: 50.1 us
  waiting for transfers between devices  23.4 us (47%)
  starting transfers between devices  17.4 us (35%)
  Pallas kernels  9.18 us (18%)
    ppermute x7, waiting for transfers between devices, total_over_all(): sums = sums + lax.ppermute(sums, BOTH, swap_pairs(axis, partner))  19.5 us
    ppermute x7, starting transfers between devices, total_over_all(): sums = sums + lax.ppermute(sums, BOTH, swap_pairs(axis, partner))  12.4 us
    pallas_call x4, Pallas kernels, on_core(): pl.pallas_call(kernel, out_shape=shapes, in_specs=[pl.BlockSpec(memory_sp...  7.45 us
    ppermute x1, starting transfers between devices, body(): near = lax.ppermute(near, 'tm', [(i, i ^ 1) for i in range(devices)])  3.33 us
    ppermute x1, waiting for transfers between devices, body(): lax.ppermute(cross, 'tm', [(i, (i + 1 if i % 2 else i - 1) % devices) for...  2.99 us
    pallas_call x2, Pallas kernels, clean(): pl.pallas_call(functools.partial(clean_kernel, scale), out_shape=pltpu.HB...  1.74 us
    ppermute x1, starting transfers between devices, total_over_all(): sums = mine + lax.ppermute(send, BOTH, cores)  1.09 us
  transfers between devices with their start and end apart: 12, of which 10 were waited for; matrix products, arithmetic and copies ran while one was open for 0% of the time, Pallas kernels for 12%

profile of v7, /device:TPU:1, one launch (start us, length us, event | category | flops | bytes accessed | tf_op | source)
XLA Modules:
  0.0 50.1 jit_solution(17635958004787143992)
XLA Ops:
  0.0 1.4 %shard_map.47 = (f32[2,7,64,128]{3,2,1,0:T(8,128)S(1)}, f32[2,7,64,128]{3,2,1,0:T(8,128)S(1)}) custom-call(f32[2,2,2,64,8,128]{5,4,3,2,1,0:T(8,128)} %bitcast.15), custom_call_target="tpu_custom_call" | custom-call | flops 1000 | bytes 1000 | tf_op jit(solution)/shard_map/pallas_call | solution.py:309
  1.4 3.3 %collective-permute-start.1 = (f32[2,7,64,128]{3,2,1,0:T(8,128)S(1)}, f32[2,7,64,128]{3,2,1,0:T(8,128)S(1)}, u32[]{:S(2)}, u32[]{:S(2)}) collective-permute-start(f32[2,7,64,128]{3,2,1,0:T(8,128)S(1)} %get-tuple-element.27), channel_id=1, source_target_pairs={{0,1},{1,0},{2,3},{3,2},{4,5},{5,4},{6,7},{7,6},{8,9},{9,8},{10,11... | collective-permute-start | bytes 1376264 | tf_op jit(solution)/shard_map/ppermute | solution.py:355
  4.7 0.0 collective-permute-start
  4.7 4.3 %shard_map.46 = (f32[2,9,64,128]{3,2,1,0:T(8,128)S(1)}, f32[2,2,7,64,128]{4,3,2,1,0:T(8,128)S(1)}, f32[2,64,128]{2,1,0:T(8,128)S(1)}, f32[512,128]{1,0:T(8,128)S...) custom-call(f32[2,2,2,512,128]{4,3,2,1,0:T(8,128)} %bitcast.16, f32[512,128]{1,0:T(8,128)} %bitcast.17, ...), custom_call_target="tpu_custom_call" | custom-call | flops 2000000000 | bytes 6291456 | tf_op jit(solution)/shard_map/pallas_call | solution.py:309
  9.0 0.0 collective-permute-done.1.near_ref
  9.0 0.9 %shard_map.48 = (f32[7,64,128]{2,1,0:T(8,128)S(1)}, f32[2,64,128]{2,1,0:T(8,128)S(1)}) custom-call(f32[2,2,7,64,128]{4,3,2,1,0:T(8,128)S(1)} %get-tuple-element.22.part_ref, f32[2,7,64,128]{3,2,1,0:T(8,128)S(1)} %collective-permute-done.1.near_ref, f32[512,128]{1,0:T(8,128)S(1)} %get-tuple-element.24.taps_ref, ...), custom_call_target="tpu_custom_call" | custom-call | flops 1000000000 | bytes 3145728 | tf_op jit(solution)/shard_map/pallas_call | solution.py:309
  9.9 3.0 %collective-permute-done.cross_ref = f32[2,7,64,128]{3,2,1,0:T(8,128)S(1)} collective-permute-done((f32[2,7,64,128]{3,2,1,0:T(8,128)S(1)}, f32[2,7,64,128]{3,2,1,0:T(8,128)S(1)}, u32[]{:S(2)}, u32[]{:S(2)}) %collective-permute-start) | collective-permute-done | bytes 458784 | tf_op jit(solution)/shard_map/ppermute | solution.py:356
  12.9 0.9 %shard_map.49 = (f32[7,64,128]{2,1,0:T(8,128)S(1)}, f32[7,64,128]{2,1,0:T(8,128)S(1)}, f32[64,128]{1,0:T(8,128)S(1)}, f32[64,128]{1,0:T(8,128)S(1)}) custom-call(f32[2,2,7,64,128]{4,3,2,1,0:T(8,128)S(1)} %get-tuple-element.22.part_ref, f32[2,7,64,128]{3,2,1,0:T(8,128)S(1)} %collective-permute-done.cross_ref, f32[512,128]{1,0:T(8,128)S(1)} %get-tuple-element.24.taps_ref, ...), custom_call_target="tpu_custom_call" | custom-call | tf_op jit(solution)/shard_map/pallas_call | solution.py:309
  13.8 1.1 %collective-permute-start.2 = (f32[64,128]{1,0:T(8,128)S(1)}, f32[64,128]{1,0:T(8,128)S(1)}, u32[]{:S(2)}, u32[]{:S(2)}) collective-permute-start(f32[64,128]{1,0:T(8,128)S(1)} %get-tuple-element.32), channel_id=1, source_target_pairs={{0,1},{1,0},{2,3},{3,2},{4,5},{5,4},{6,7},{7,6},{8,9},{9,8},{10,11... | collective-permute-start | bytes 98312 | tf_op jit(solution)/shard_map/ppermute | solution.py:333
  14.9 0.9 %collective-permute-done.2 = f32[64,128]{1,0:T(8,128)S(1)} collective-permute-done((f32[64,128]{1,0:T(8,128)S(1)}, f32[64,128]{1,0:T(8,128)S(1)}, u32[]{:S(2)}, u32[]{:S(2)}) %collective-permute-start.2) | collective-permute-done | bytes 32800 | tf_op jit(solution)/shard_map/ppermute | solution.py:333
  15.8 0.0 collective-permute-start.3
  15.8 3.3 %collective-permute-done.3 = f32[64,128]{1,0:T(8,128)S(1)} collective-permute-done((f32[64,128]{1,0:T(8,128)S(1)}, f32[64,128]{1,0:T(8,128)S(1)}, u32[]{:S(2)}, u32[]{:S(2)}) %collective-permute-start.3) | collective-permute-done | bytes 32800 | tf_op jit(solution)/shard_map/ppermute | solution.py:339
  19.1 1.0 %collective-permute-start.4 = (f32[64,128]{1,0:T(8,128)S(1)}, f32[64,128]{1,0:T(8,128)S(1)}, u32[]{:S(2)}, u32[]{:S(2)}) collective-permute-start(f32[64,128]{1,0:T(8,128)S(1)} %add.25), channel_id=1, source_target_pairs={{0,25},{1,24},{2,27},{3,26},{4,29},{5,28},{6,31},{7,30},{8,17},{9,... | collective-permute-start | bytes 98312 | tf_op jit(solution)/shard_map/ppermute | solution.py:339
  20.2 0.2 collective-permute-start.10
  20.3 3.3 %collective-permute-done.4 = f32[64,128]{1,0:T(8,128)S(1)} collective-permute-done((f32[64,128]{1,0:T(8,128)S(1)}, f32[64,128]{1,0:T(8,128)S(1)}, u32[]{:S(2)}, u32[]{:S(2)}) %collective-permute-start.4) | collective-permute-done | bytes 32800 | tf_op jit(solution)/shard_map/ppermute | solution.py:339
  23.7 0.0 collective-permute-start.5
  23.7 3.3 %collective-permute-done.5 = f32[64,128]{1,0:T(8,128)S(1)} collective-permute-done((f32[64,128]{1,0:T(8,128)S(1)}, f32[64,128]{1,0:T(8,128)S(1)}, u32[]{:S(2)}, u32[]{:S(2)}) %collective-permute-start.5) | collective-permute-done | bytes 32800 | tf_op jit(solution)/shard_map/ppermute | solution.py:339
  27.0 1.3 %collective-permute-start.6 = (f32[64,128]{1,0:T(8,128)S(1)}, f32[64,128]{1,0:T(8,128)S(1)}, u32[]{:S(2)}, u32[]{:S(2)}) collective-permute-start(f32[64,128]{1,0:T(8,128)S(1)} %add.27), channel_id=1, source_target_pairs={{0,7},{1,6},{2,5},{3,4},{4,3},{5,2},{6,1},{7,0},{8,15},{9,14},{10,... | collective-permute-start | bytes 98312 | tf_op jit(solution)/shard_map/ppermute | solution.py:339
  28.3 3.3 %collective-permute-done.6 = f32[64,128]{1,0:T(8,128)S(1)} collective-permute-done((f32[64,128]{1,0:T(8,128)S(1)}, f32[64,128]{1,0:T(8,128)S(1)}, u32[]{:S(2)}, u32[]{:S(2)}) %collective-permute-start.6) | collective-permute-done | bytes 32800 | tf_op jit(solution)/shard_map/ppermute | solution.py:339
  31.6 1.7 %collective-permute-start.7 = (f32[64,128]{1,0:T(8,128)S(1)}, f32[64,128]{1,0:T(8,128)S(1)}, u32[]{:S(2)}, u32[]{:S(2)}) collective-permute-start(f32[64,128]{1,0:T(8,128)S(1)} %add.28), channel_id=1, source_target_pairs={{0,33},{1,32},{2,35},{3,34},{4,37},{5,36},{6,39},{7,38},{8,41},{9,... | collective-permute-start | bytes 98312 | tf_op jit(solution)/shard_map/ppermute | solution.py:339
  33.3 1.6 %collective-permute-done.7 = f32[64,128]{1,0:T(8,128)S(1)} collective-permute-done((f32[64,128]{1,0:T(8,128)S(1)}, f32[64,128]{1,0:T(8,128)S(1)}, u32[]{:S(2)}, u32[]{:S(2)}) %collective-permute-start.7) | collective-permute-done | bytes 32800 | tf_op jit(solution)/shard_map/ppermute | solution.py:339
  34.9 3.1 %collective-permute-start.8 = (f32[64,128]{1,0:T(8,128)S(1)}, f32[64,128]{1,0:T(8,128)S(1)}, u32[]{:S(2)}, u32[]{:S(2)}) collective-permute-start(f32[64,128]{1,0:T(8,128)S(1)} %add.29), channel_id=1, source_target_pairs={{0,65},{1,64},{2,67},{3,66},{4,69},{5,68},{6,71},{7,70},{8,73},{9,... | collective-permute-start | bytes 98312 | tf_op jit(solution)/shard_map/ppermute | solution.py:339
  38.0 1.6 %collective-permute-done.8 = f32[64,128]{1,0:T(8,128)S(1)} collective-permute-done((f32[64,128]{1,0:T(8,128)S(1)}, f32[64,128]{1,0:T(8,128)S(1)}, u32[]{:S(2)}, u32[]{:S(2)}) %collective-permute-start.8) | collective-permute-done | bytes 32800 | tf_op jit(solution)/shard_map/ppermute | solution.py:339
  39.6 5.3 %collective-permute-start.9 = (f32[64,128]{1,0:T(8,128)S(1)}, f32[64,128]{1,0:T(8,128)S(1)}, u32[]{:S(2)}, u32[]{:S(2)}) collective-permute-start(f32[64,128]{1,0:T(8,128)S(1)} %add.30), channel_id=1, source_target_pairs={{0,225},{1,224},{2,227},{3,226},{4,229},{5,228},{6,231},{7,230},{8... | collective-permute-start | bytes 98312 | tf_op jit(solution)/shard_map/ppermute | solution.py:339
  44.9 2.9 %collective-permute-done.9 = f32[64,128]{1,0:T(8,128)S(1)} collective-permute-done((f32[64,128]{1,0:T(8,128)S(1)}, f32[64,128]{1,0:T(8,128)S(1)}, u32[]{:S(2)}, u32[]{:S(2)}) %collective-permute-start.9) | collective-permute-done | bytes 32800 | tf_op jit(solution)/shard_map/ppermute | solution.py:339
  47.8 0.4 collective-permute-start.11
  48.3 0.8 %shard_map.50.refs_5_ = f32[2,2,512,128]{3,2,1,0:T(8,128)} custom-call(f32[2,9,64,128]{3,2,1,0:T(8,128)S(1)} %get-tuple-element.21.refs_0_, f32[64,128]{1,0:T(8,128)S(1)} %add.31.refs_1_), custom_call_target="tpu_custom_call" | custom-call | flops 1000000 | bytes 2097152 | tf_op jit(solution)/shard_map/pallas_call | solution.py:293
  49.0 0.0 collective-permute-done.10.refs_3_
  49.0 0.1 collective-permute-done.11.refs_4_
  49.1 1.0 %shard_map.51 = f32[2,2,512,128]{3,2,1,0:T(8,128)} custom-call(f32[2,9,64,128]{3,2,1,0:T(8,128)S(1)} %get-tuple-element.21.refs_0_, f32[64,128]{1,0:T(8,128)S(1)} %add.31.refs_1_, f32[7,64,128]{2,1,0:T(8,128)S(1)} %get-tuple-element.35.refs_2_, f32[7,64,128]{2,1,0:T(8,128)S(1)} %collective-permute-done.10.refs_3_, ...), custom_call_target="tpu_custom_call", output_to_operand_aliasing={{}: (5, {})} | custom-call | flops 1000000 | bytes 2097152 | tf_op jit(solution)/shard_map/pallas_call | solution.py:293
  (8 shorter events, 0.0 us)
Async XLA Ops:
  1.4 7.6 %collective-permute-start.1 = (f32[2,7,64,128]{3,2,1,0:T(8,128)S(1)}, f32[2,7,64,128]{3,2,1,0:T(8,128)S(1)}, u32[]{:S(2)}, u32[]{:S(2)}) collective-permute-start(f32[2,7,64,128]{3,2,1,0:T(8,128)S(1)} %get-tuple-element.27), channel_id=1, source_target_pairs={{0,1},{1,0},{2,3},{3,2},{4,5},{5,4},{6,7},{7,6},{8,9},{9,8},{10,11... | collective-permute-start | bytes 1376264 | tf_op jit(solution)/shard_map/ppermute | solution.py:355
  4.7 8.2 %collective-permute-start = (f32[2,7,64,128]{3,2,1,0:T(8,128)S(1)}, f32[2,7,64,128]{3,2,1,0:T(8,128)S(1)}, u32[]{:S(2)}, u32[]{:S(2)}) collective-permute-start(f32[2,7,64,128]{3,2,1,0:T(8,128)S(1)} %get-tuple-element.23), channel_id=1, source_target_pairs={{0,7},{1,2},{2,1},{3,4},{4,3},{5,6},{6,5},{7,0},{8,15},{9,10},{10,... | collective-permute-start | bytes 1376264 | tf_op jit(solution)/shard_map/ppermute | solution.py:356
  13.8 2.0 %collective-permute-start.2 = (f32[64,128]{1,0:T(8,128)S(1)}, f32[64,128]{1,0:T(8,128)S(1)}, u32[]{:S(2)}, u32[]{:S(2)}) collective-permute-start(f32[64,128]{1,0:T(8,128)S(1)} %get-tuple-element.32), channel_id=1, source_target_pairs={{0,1},{1,0},{2,3},{3,2},{4,5},{5,4},{6,7},{7,6},{8,9},{9,8},{10,11... | collective-permute-start | bytes 98312 | tf_op jit(solution)/shard_map/ppermute | solution.py:333
  15.8 3.3 %collective-permute-start.3 = (f32[64,128]{1,0:T(8,128)S(1)}, f32[64,128]{1,0:T(8,128)S(1)}, u32[]{:S(2)}, u32[]{:S(2)}) collective-permute-start(f32[64,128]{1,0:T(8,128)S(1)} %add.24), channel_id=1, source_target_pairs={{0,9},{1,8},{2,11},{3,10},{4,13},{5,12},{6,15},{7,14},{8,1},{9,0},... | collective-permute-start | bytes 98312 | tf_op jit(solution)/shard_map/ppermute | solution.py:339
  19.1 4.6 %collective-permute-start.4 = (f32[64,128]{1,0:T(8,128)S(1)}, f32[64,128]{1,0:T(8,128)S(1)}, u32[]{:S(2)}, u32[]{:S(2)}) collective-permute-start(f32[64,128]{1,0:T(8,128)S(1)} %add.25), channel_id=1, source_target_pairs={{0,25},{1,24},{2,27},{3,26},{4,29},{5,28},{6,31},{7,30},{8,17},{9,... | collective-permute-start | bytes 98312 | tf_op jit(solution)/shard_map/ppermute | solution.py:339
  20.2 28.9 %collective-permute-start.10 = (f32[7,64,128]{2,1,0:T(8,128)S(1)}, f32[7,64,128]{2,1,0:T(8,128)S(1)}, u32[]{:S(2)}, u32[]{:S(2)}) collective-permute-start(f32[7,64,128]{2,1,0:T(8,128)S(1)} %get-tuple-element.36), channel_id=1, source_target_pairs={{0,7},{1,0},{2,1},{3,2},{4,3},{5,4},{6,5},{7,6},{8,15},{9,8},{10,9... | collective-permute-start | bytes 688136 | tf_op jit(solution)/shard_map/ppermute | solution.py:338
  23.7 3.3 %collective-permute-start.5 = (f32[64,128]{1,0:T(8,128)S(1)}, f32[64,128]{1,0:T(8,128)S(1)}, u32[]{:S(2)}, u32[]{:S(2)}) collective-permute-start(f32[64,128]{1,0:T(8,128)S(1)} %add.26), channel_id=1, source_target_pairs={{0,3},{1,2},{2,1},{3,0},{4,7},{5,6},{6,5},{7,4},{8,11},{9,10},{10,... | collective-permute-start | bytes 98312 | tf_op jit(solution)/shard_map/ppermute | solution.py:339
  27.0 4.6 %collective-permute-start.6 = (f32[64,128]{1,0:T(8,128)S(1)}, f32[64,128]{1,0:T(8,128)S(1)}, u32[]{:S(2)}, u32[]{:S(2)}) collective-permute-start(f32[64,128]{1,0:T(8,128)S(1)} %add.27), channel_id=1, source_target_pairs={{0,7},{1,6},{2,5},{3,4},{4,3},{5,2},{6,1},{7,0},{8,15},{9,14},{10,... | collective-permute-start | bytes 98312 | tf_op jit(solution)/shard_map/ppermute | solution.py:339
  31.6 3.3 %collective-permute-start.7 = (f32[64,128]{1,0:T(8,128)S(1)}, f32[64,128]{1,0:T(8,128)S(1)}, u32[]{:S(2)}, u32[]{:S(2)}) collective-permute-start(f32[64,128]{1,0:T(8,128)S(1)} %add.28), channel_id=1, source_target_pairs={{0,33},{1,32},{2,35},{3,34},{4,37},{5,36},{6,39},{7,38},{8,41},{9,... | collective-permute-start | bytes 98312 | tf_op jit(solution)/shard_map/ppermute | solution.py:339
  34.9 4.7 %collective-permute-start.8 = (f32[64,128]{1,0:T(8,128)S(1)}, f32[64,128]{1,0:T(8,128)S(1)}, u32[]{:S(2)}, u32[]{:S(2)}) collective-permute-start(f32[64,128]{1,0:T(8,128)S(1)} %add.29), channel_id=1, source_target_pairs={{0,65},{1,64},{2,67},{3,66},{4,69},{5,68},{6,71},{7,70},{8,73},{9,... | collective-permute-start | bytes 98312 | tf_op jit(solution)/shard_map/ppermute | solution.py:339
  39.6 8.2 %collective-permute-start.9 = (f32[64,128]{1,0:T(8,128)S(1)}, f32[64,128]{1,0:T(8,128)S(1)}, u32[]{:S(2)}, u32[]{:S(2)}) collective-permute-start(f32[64,128]{1,0:T(8,128)S(1)} %add.30), channel_id=1, source_target_pairs={{0,225},{1,224},{2,227},{3,226},{4,229},{5,228},{6,231},{7,230},{8... | collective-permute-start | bytes 98312 | tf_op jit(solution)/shard_map/ppermute | solution.py:339
  47.8 1.3 %collective-permute-start.11 = (f32[64,128]{1,0:T(8,128)S(1)}, f32[64,128]{1,0:T(8,128)S(1)}, u32[]{:S(2)}, u32[]{:S(2)}) collective-permute-start(f32[64,128]{1,0:T(8,128)S(1)} %add.31.refs_1_), channel_id=1, source_target_pairs={{0,1},{1,0},{2,3},{3,2},{4,5},{5,4},{6,7},{7,6},{8,9},{9,8},{10,11... | collective-permute-start | bytes 98312 | tf_op jit(solution)/shard_map/ppermute | solution.py:340

commit v8 on v7

--- a/solution.py
+++ b/solution.py
@@ -17,10 +17,6 @@
 FRAMES = 16
 HELD = 9
 RIM = FRAMES - HELD
-AHEAD = (4, 3)
-BACK = (3, 4)
-AHEAD_AT = (0, AHEAD[0])
-BACK_AT = (0, BACK[0])
 SHORT = pl.CostEstimate(flops=1000, bytes_accessed=1000, transcendentals=0)
 BOTH = ("beam", "tm")
 X, Y, Z = 4, 4, 8
@@ -43,14 +39,14 @@
                     "x": lambda: (z, partner[x], y),
                     "y": lambda: (z, x, partner[y]),
                 }[axis]()
-                pairs += [(place(z, x, y, c), place(*there, 1 - c)) for c in range(2)]
+                pairs += [(place(z, x, y, c), place(*there, c if axis == "y" else 1 - c)) for c in range(2)]
     return pairs
 
 
 def kept_half():
     tm, beam = lax.axis_index("tm"), lax.axis_index("beam")
     z = beam // X
-    return (tm % 2 + tm // 2 + beam % X + z + z // 2 + z // 4) % 2
+    return (tm + beam % X + z + z // 2 + z // 4) % 2
 
 
 def in_two(table):
@@ -121,13 +117,13 @@
 
 
 def rim_copies(volt_ref, out_ref, sems, last):
+    p = 1 - kept_half()
     copies = []
-    for p in range(2):
-        for n in range(BACK[p] if last else AHEAD[p]):
-            f, slot = (FRAMES - BACK[p] + n, BACK_AT[p] + n) if last else (n, AHEAD_AT[p] + n)
-            for c in range(2):
-                frame = volt_ref.at[p, c, f // 8, :, f % 8, :]
-                copies.append(pltpu.make_async_copy(frame, out_ref.at[c, slot], sems.at[c, slot]))
+    for n in range(RIM):
+        f = HELD + n if last else n
+        for c in range(2):
+            frame = volt_ref.at[p, c, f // 8, :, f % 8, :]
+            copies.append(pltpu.make_async_copy(frame, out_ref.at[c, n], sems.at[c, n]))
     return copies
 
 
@@ -146,7 +142,7 @@
 
 def held_kernel(
     volt_in, taps_in, table_in, twist_in,
-    pow_ref, part_ref, sum_ref, taps_ref, table_ref, twist_ref,
+    pow_ref, part_ref, mine_ref, send_ref, taps_ref, table_ref, twist_ref,
     volt_ref, filt_ref, strip_sems, table_sems,
 ):
     def strip_copy(s):
@@ -163,6 +159,7 @@
     twist_copy.start()
     taps_copy.wait()
     keep = lax.axis_index("tm") > 0
+    own = kept_half()
 
     def strip(s, _):
         strip_copy(s).wait()
@@ -172,20 +169,23 @@
         for p in range(2):
             for c in range(2):
                 x = [volt_ref[p, c, f // 8, pl.ds(at + f % 8, 8, stride=8), :] for f in range(FRAMES)]
-                for f in range(HELD + AHEAD[p]):
+                for f in range(HELD):
                     total = taps[0] * x[f]
-                    for t in range(1, min(TAPS, FRAMES - f)):
+                    for t in range(1, TAPS):
                         total = total + taps[t] * x[f + t]
-                    if f < HELD:
-                        filt_ref[p, c, f, rows, :] = total
-                    else:
-                        part_ref[p, c, f - HELD, rows, :] = total
-                for j in range(BACK[p]):
-                    reach = BACK[p] - j
-                    total = taps[reach] * x[0]
-                    for t in range(reach + 1, TAPS):
-                        total = total + taps[t] * x[t - reach]
-                    part_ref[p, c, AHEAD[p] + j, rows, :] = jnp.where(keep, total, 0.0)
+                    filt_ref[p, c, f, rows, :] = total
+        for c in range(2):
+            x = [volt_ref[own, c, f // 8, pl.ds(at + f % 8, 8, stride=8), :] for f in range(FRAMES)]
+            for j in range(RIM):
+                total = taps[0] * x[HELD + j]
+                for t in range(1, RIM - j):
+                    total = total + taps[t] * x[HELD + j + t]
+                part_ref[c, j, rows, :] = total
+                reach = RIM - j
+                total = taps[reach] * x[0]
+                for t in range(reach + 1, TAPS):
+                    total = total + taps[t] * x[t - reach]
+                part_ref[c, RIM + j, rows, :] = jnp.where(keep, total, 0.0)
         return 0
 
     lax.fori_loop(0, ROWS // 8, strip, 0)
@@ -198,38 +198,35 @@
         for (p, f), power in zip(which, power_rows(frames, table_ref, twist_ref)):
             pow_ref[p, f] = power
             sums[p] = power if sums[p] is None else sums[p] + power
-    for p in range(2):
-        sum_ref[p] = sums[p]
-
-
-def rim_powers(role, part_ref, came_ref, taps_ref, table_ref, twist_ref, sums, keep, store):
-    slots, at = (AHEAD, AHEAD_AT) if role == "ahead" else (BACK, BACK_AT)
+    mine_ref[...] = jnp.where(own == 1, sums[1], sums[0])
+    send_ref[...] = jnp.where(own == 1, sums[0], sums[1])
+
+
+def rim_powers(role, part_ref, came_ref, taps_ref, table_ref, twist_ref, total_sum, keep, store):
     taps = [taps_ref[pl.ds(t, ROWS, stride=8), :] for t in range(TAPS)]
 
-    def finished(p, j):
+    def finished(j):
         out = []
         for c in range(2):
             if role == "ahead":
                 terms = [(RIM + i - j, i) for i in range(j + 1)]
-                total = part_ref[p, c, j]
+                total = part_ref[c, j]
             else:
-                terms = [(t, j + t) for t in range(BACK[p] - j)]
-                total = part_ref[p, c, AHEAD[p] + j]
+                terms = [(t, j + t) for t in range(RIM - j)]
+                total = part_ref[c, RIM + j]
             rest = None
             for t, i in terms:
-                term = taps[t] * came_ref[c, at[p] + i]
+                term = taps[t] * came_ref[c, i]
                 rest = term if rest is None else rest + term
             out.append(total + (rest if keep is None else jnp.where(keep, rest, 0.0)))
         return tuple(out)
 
-    every = [(p, j) for j in range(max(slots)) for p in range(2) if j < slots[p]]
     for start in range(0, RIM, 4):
-        which = every[start : start + 4]
-        frames = [finished(p, j) for p, j in which]
-        for (p, j), power in zip(which, power_rows(frames, table_ref, twist_ref)):
-            store[at[p] + j] = power
-            sums[p] = sums[p] + power
-    return sums
+        which = range(start, min(start + 4, RIM))
+        for j, power in zip(which, power_rows([finished(j) for j in which], table_ref, twist_ref)):
+            store[j] = power
+            total_sum = total_sum + power
+    return total_sum
 
 
 def near_kernel(part_ref, near_ref, taps_ref, table_ref, twist_ref, had_ref, early_ref, sum_ref):
@@ -237,66 +234,50 @@
 
         @pl.when(lax.axis_index("tm") % 2 == core)
         def _():
-            sums = [had_ref[0], had_ref[1]]
-            sums = rim_powers(role, part_ref, near_ref, taps_ref, table_ref, twist_ref, sums, None, early_ref)
-            sum_ref[0], sum_ref[1] = sums
-
-
-def cross_kernel(last, part_ref, cross_ref, taps_ref, table_ref, twist_ref, had_ref, early_ref, ahead_ref, back_ref, mine_ref, send_ref):
+            sum_ref[...] = rim_powers(
+                role, part_ref, near_ref, taps_ref, table_ref, twist_ref, had_ref[...], None, early_ref
+            )
+
+
+def cross_kernel(last, part_ref, cross_ref, taps_ref, table_ref, twist_ref, had_ref, other_ref, early_ref, ahead_ref, back_ref, sum_ref):
     tm = lax.axis_index("tm")
     for core, role in enumerate(("back", "ahead")):
 
         @pl.when(tm % 2 == core)
         def _():
-            sums = [had_ref[0], had_ref[1]]
             store, keep = (back_ref, None) if core == 0 else (ahead_ref, tm < last)
-            sums = rim_powers(role, part_ref, cross_ref, taps_ref, table_ref, twist_ref, sums, keep, store)
+            had = had_ref[...] + other_ref[...]
+            sum_ref[...] = rim_powers(
+                role, part_ref, cross_ref, taps_ref, table_ref, twist_ref, had, keep, store
+            )
             kept_ref = ahead_ref if core == 0 else back_ref
             kept_ref[...] = early_ref[...]
-            keeps_second = kept_half() == 1
-            mine_ref[...] = jnp.where(keeps_second, sums[1], sums[0])
-            send_ref[...] = jnp.where(keeps_second, sums[0], sums[1])
-
-
-def clean_kernel(scale, *refs):
-    held_ref, mine_ref, out_ref, tile_ref, sems = refs[0], refs[1], refs[-3], refs[-2], refs[-1]
-    own = kept_half()
-    if len(refs) == 5:
-        parts = [(own, 0, mine_ref)]
-    else:
-        ahead_ref, back_ref, other_ref = refs[2:5]
-        parts = [(own, 1, mine_ref), (1 - own, 0, other_ref), (1 - own, 1, other_ref)]
+
+
+def clean_kernel(scale, held_ref, rim_ref, sum_ref, *refs):
+    out_ref, tile_ref, sems = refs[-3:]
+    p = kept_half() if len(refs) == 3 else 1 - kept_half()
+    base = sum_ref[...] * scale
     copies = []
-    for n, (p, half, sum_ref) in enumerate(parts):
-        base = sum_ref[...] * scale
+    for half in range(2):
         for f in range(8 * half, 8 * half + 8):
-            if f < HELD:
-                power = held_ref[p, f]
-            elif f < HELD + min(AHEAD):
-                power = ahead_ref[jnp.where(p == 0, AHEAD_AT[0], AHEAD_AT[1]) + f - HELD]
-            elif f >= FRAMES - min(BACK):
-                power = back_ref[jnp.where(p == 0, BACK_AT[0] + BACK[0], BACK_AT[1] + BACK[1]) + f - FRAMES]
-            else:
-                power = jnp.where(p == 0, ahead_ref[AHEAD_AT[0] + f - HELD], back_ref[BACK_AT[1] + f - FRAMES + BACK[1]])
-            tile_ref[n, pl.ds(f % 8, ROWS, stride=8), :] = power - base
-        copies.append(pltpu.make_async_copy(tile_ref.at[n], out_ref.at[p, half], sems.at[n]))
+            power = held_ref[p, f] if f < HELD else rim_ref[f - HELD]
+            tile_ref[half, pl.ds(f % 8, ROWS, stride=8), :] = power - base
+        copies.append(pltpu.make_async_copy(tile_ref.at[half], out_ref.at[p, half], sems.at[half]))
         copies[-1].start()
     for copy in copies:
         copy.wait()
 
 
 def clean(scale, *args):
-    first = len(args) == 2
     far = [pl.BlockSpec(memory_space=pl.ANY)]
-    near = [pl.BlockSpec(memory_space=pltpu.VMEM)]
-    parts = 1 if first else 3
     return pl.pallas_call(
         functools.partial(clean_kernel, scale),
         out_shape=pltpu.HBM((2, 2, 8 * ROWS, LANES), jnp.float32),
-        in_specs=near * 2 if first else near * 5 + far,
+        in_specs=[pl.BlockSpec(memory_space=pltpu.VMEM)] * 3 + far * (len(args) - 3),
         out_specs=far[0],
-        scratch_shapes=[pltpu.VMEM((parts, 8 * ROWS, LANES), jnp.float32), pltpu.SemaphoreType.DMA((parts,))],
-        input_output_aliases={} if first else {5: 0},
+        scratch_shapes=[pltpu.VMEM((2, 8 * ROWS, LANES), jnp.float32), pltpu.SemaphoreType.DMA((2,))],
+        input_output_aliases={3: 0} if len(args) == 4 else {},
         compiler_params=pltpu.CompilerParams(vmem_limit_bytes=16 << 20),
         cost_estimate=pl.CostEstimate(flops=10**6, bytes_accessed=2 << 20, transcendentals=0),
     )(*args)
@@ -327,17 +308,18 @@
     return jnp.swapaxes(x, -3, -2).reshape(*lead, ROWS * frames, LANES)
 
 
-def total_over_all(mine, send, back):
-    cores = [(i, i ^ 1) for i in range(2 * X * Y * Z)]
+CORES = [(i, i ^ 1) for i in range(2 * X * Y * Z)]
+
+
+def total_over_all(sums, back):
     left = [(i, (i - 1) % (2 * Y)) for i in range(2 * Y)]
-    sums = mine + lax.ppermute(send, BOTH, cores)
     steps = [("x", r) for r in RING4] + [("y", r) for r in RING4] + [("z", r) for r in RING8]
     for n, (axis, partner) in enumerate(steps):
         if n == 1:
             sums, back = lax.optimization_barrier((sums, back))
             back = lax.ppermute(back, "tm", left)
         sums = sums + lax.ppermute(sums, BOTH, swap_pairs(axis, partner))
-    return sums, lax.ppermute(sums, BOTH, cores), back
+    return sums, lax.ppermute(sums, BOTH, CORES), back
 
 
 def body(voltages, filter_taps):
@@ -355,12 +337,13 @@
     near = lax.ppermute(near, "tm", [(i, i ^ 1) for i in range(devices)])
     cross = lax.ppermute(cross, "tm", [(i, (i + 1 if i % 2 else i - 1) % devices) for i in range(devices)])
     strips = (2, 2, 2, ROWS * 8, LANES)
-    held, part, had, taps, table, twist = on_core(
+    held, part, had, send, taps, table, twist = on_core(
         held_kernel,
         [
             (2, HELD, ROWS, LANES),
-            (2, 2, RIM, ROWS, LANES),
-            (2, ROWS, LANES),
+            (2, 2 * RIM, ROWS, LANES),
+            (ROWS, LANES),
+            (ROWS, LANES),
             (ROWS * TAPS, LANES),
             pltpu.VMEM(table.shape, table.dtype),
             twist.shape,
@@ -374,19 +357,20 @@
         far=True,
         cost=pl.CostEstimate(flops=2 * 10**9, bytes_accessed=6 << 20, transcendentals=0),
     )(in_hbm(tiles.reshape(strips)), in_hbm(by_rows(filter_taps)), in_hbm(table), in_hbm(twist))
+    other = lax.ppermute(send, BOTH, CORES)
     early, had = on_core(
         near_kernel,
-        [(RIM, ROWS, LANES), (2, ROWS, LANES)],
+        [(RIM, ROWS, LANES), (ROWS, LANES)],
         cost=pl.CostEstimate(flops=10**9, bytes_accessed=3 << 20, transcendentals=0),
     )(part, near, taps, table, twist, had)
-    ahead, back, mine, send = on_core(
+    ahead, back, sums = on_core(
         functools.partial(cross_kernel, devices - 1),
-        [(RIM, ROWS, LANES), (RIM, ROWS, LANES), (ROWS, LANES), (ROWS, LANES)],
-    )(part, cross, taps, table, twist, had, early)
-    mine, other, back = total_over_all(mine, send, back)
+        [(RIM, ROWS, LANES), (RIM, ROWS, LANES), (ROWS, LANES)],
+    )(part, cross, taps, table, twist, had, other, early)
+    mine, other, back = total_over_all(sums, back)
     scale = 1.0 / (FRAMES * devices * lax.axis_size("beam"))
-    out = clean(scale, held, mine)
-    out = clean(scale, held, mine, ahead, back, other, out)
+    out = clean(scale, held, ahead, mine)
+    out = clean(scale, held, back, other, out)
     out = jnp.swapaxes(out.reshape(2, 2, ROWS, 8, LANES), 2, 3)
     return out.reshape(1, 2, FRAMES, CHANNELS)
 

time: 50.3 us -> 48.9 us (0.972)
  waiting for transfers between devices: 23.4 us -> 19.8 us
  starting transfers between devices: 17.4 us -> 19.5 us
    ppermute x7, starting transfers between devices: 12.4 us -> 14.7 us  [total_over_all(): sums = sums + lax.ppermute(sums, BOTH, swap_pairs(axis, partner))]
    ppermute x7, waiting for transfers between devices: 19.5 us -> 18 us  [total_over_all(): sums = sums + lax.ppermute(sums, BOTH, swap_pairs(axis, partner))]
    ppermute x1, waiting for transfers between devices: 2.99 us -> 1.55 us  [body(): lax.ppermute(cross, 'tm', [(i, (i + 1 if i % 2 else i - 1) % devices) for...]
    ppermute x2, waiting for transfers between devices: 0.93 us -> 0.27 us  [the longest x1 0.27 us: total_over_all(): return (sums, lax.ppermute(sums, BOTH, CORES), back)]
  transfers between devices with their start and end apart: 12 -> 12, of which waited for: 10 -> 9; matrix products, arithmetic and copies ran while one was open for 0% -> 0% of each run, Pallas kernels for 12% -> 12%
where the time goes in v8:
time: 48.9 us; the launch traced here: 48.7 us
  waiting for transfers between devices  19.8 us (40%)
  starting transfers between devices  19.5 us (40%)
  Pallas kernels  9.26 us (19%)
    ppermute x7, waiting for transfers between devices, total_over_all(): sums = sums + lax.ppermute(sums, BOTH, swap_pairs(axis, partner))  18 us
    ppermute x7, starting transfers between devices, total_over_all(): sums = sums + lax.ppermute(sums, BOTH, swap_pairs(axis, partner))  14.7 us
    pallas_call x4, Pallas kernels, on_core(): pl.pallas_call(kernel, out_shape=shapes, in_specs=[pl.BlockSpec(memory_sp...  7.45 us
    ppermute x1, starting transfers between devices, body(): near = lax.ppermute(near, 'tm', [(i, i ^ 1) for i in range(devices)])  3.33 us
    pallas_call x2, Pallas kernels, clean(): pl.pallas_call(functools.partial(clean_kernel, scale), out_shape=pltpu.HB...  1.81 us
    ppermute x1, waiting for transfers between devices, body(): lax.ppermute(cross, 'tm', [(i, (i + 1 if i % 2 else i - 1) % devices) for...  1.55 us
    ppermute x1, starting transfers between devices, body(): other = lax.ppermute(send, BOTH, CORES)  1.47 us
  transfers between devices with their start and end apart: 12, of which 9 were waited for; matrix products, arithmetic and copies ran while one was open for 0% of the time, Pallas kernels for 12%

profile of v8, /device:TPU:1, one launch (start us, length us, event | category | flops | bytes accessed | tf_op | source)
XLA Modules:
  0.0 48.7 jit_solution(1205708720235415729)
XLA Ops:
  0.0 1.4 %shard_map.47 = (f32[2,7,64,128]{3,2,1,0:T(8,128)S(1)}, f32[2,7,64,128]{3,2,1,0:T(8,128)S(1)}) custom-call(f32[2,2,2,64,8,128]{5,4,3,2,1,0:T(8,128)} %bitcast.15), custom_call_target="tpu_custom_call" | custom-call | flops 1000 | bytes 1000 | tf_op jit(solution)/shard_map/pallas_call | solution.py:290
  1.4 3.3 %collective-permute-start.1 = (f32[2,7,64,128]{3,2,1,0:T(8,128)S(1)}, f32[2,7,64,128]{3,2,1,0:T(8,128)S(1)}, u32[]{:S(2)}, u32[]{:S(2)}) collective-permute-start(f32[2,7,64,128]{3,2,1,0:T(8,128)S(1)} %get-tuple-element.27), channel_id=1, source_target_pairs={{0,1},{1,0},{2,3},{3,2},{4,5},{5,4},{6,7},{7,6},{8,9},{9,8},{10,11... | collective-permute-start | bytes 1376264 | tf_op jit(solution)/shard_map/ppermute | solution.py:337
  4.7 0.0 collective-permute-start
  4.7 4.2 %shard_map.46 = (f32[2,9,64,128]{3,2,1,0:T(8,128)S(1)}, f32[2,14,64,128]{3,2,1,0:T(8,128)S(1)}, f32[64,128]{1,0:T(8,128)S(1)}, f32[64,128]{1,0:T(8,128)S(1)}, f3...) custom-call(f32[2,2,2,512,128]{4,3,2,1,0:T(8,128)} %bitcast.16, ...), custom_call_target="tpu_custom_call" | custom-call | flops 2000000000 | bytes 6291456 | tf_op jit(solution)/shard_map/pallas_call | solution.py:290
  8.9 1.5 %collective-permute-start.2 = (f32[64,128]{1,0:T(8,128)S(1)}, f32[64,128]{1,0:T(8,128)S(1)}, u32[]{:S(2)}, u32[]{:S(2)}) collective-permute-start(f32[64,128]{1,0:T(8,128)S(1)} %get-tuple-element.30), channel_id=1, source_target_pairs={{0,1},{1,0},{2,3},{3,2},{4,5},{5,4},{6,7},{7,6},{8,9},{9,8},{10,11... | collective-permute-start | bytes 98312 | tf_op jit(solution)/shard_map/ppermute | solution.py:360
  10.4 0.0 collective-permute-done.1.near_ref
  10.4 0.9 %shard_map.48 = (f32[7,64,128]{2,1,0:T(8,128)S(1)}, f32[64,128]{1,0:T(8,128)S(1)}) custom-call(f32[2,14,64,128]{3,2,1,0:T(8,128)S(1)} %get-tuple-element.22.part_ref, f32[2,7,64,128]{3,2,1,0:T(8,128)S(1)} %collective-permute-done.1.near_ref, f32[512,128]{1,0:T(8,128)S(1)} %get-tuple-element.24.taps_ref, bf16[768,256]{1,0:T(8,128)(2,1)S(1)} %get-tuple-element.25.table_ref, ...), custom_call_target="tpu_custom_call" | custom-call | flops 1000000000 | bytes 3145728 | tf_op jit(solution)/shard_map/pallas_call | solution.py:290
  11.3 0.0 collective-permute-done.2.other_ref
  11.4 1.5 %collective-permute-done.cross_ref = f32[2,7,64,128]{3,2,1,0:T(8,128)S(1)} collective-permute-done((f32[2,7,64,128]{3,2,1,0:T(8,128)S(1)}, f32[2,7,64,128]{3,2,1,0:T(8,128)S(1)}, u32[]{:S(2)}, u32[]{:S(2)}) %collective-permute-start) | collective-permute-done | bytes 458784 | tf_op jit(solution)/shard_map/ppermute | solution.py:338
  12.9 0.9 %shard_map.49 = (f32[7,64,128]{2,1,0:T(8,128)S(1)}, f32[7,64,128]{2,1,0:T(8,128)S(1)}, f32[64,128]{1,0:T(8,128)S(1)}) custom-call(f32[2,14,64,128]{3,2,1,0:T(8,128)S(1)} %get-tuple-element.22.part_ref, f32[2,7,64,128]{3,2,1,0:T(8,128)S(1)} %collective-permute-done.cross_ref, f32[512,128]{1,0:T(8,128)S(1)} %get-tuple-element.24.taps_ref, ...), custom_call_target="tpu_custom_call" | custom-call | tf_op jit(solution)/shard_map/pallas_call | solution.py:290
  13.9 0.5 %collective-permute-start.3 = (f32[64,128]{1,0:T(8,128)S(1)}, f32[64,128]{1,0:T(8,128)S(1)}, u32[]{:S(2)}, u32[]{:S(2)}) collective-permute-start(f32[64,128]{1,0:T(8,128)S(1)} %get-tuple-element.32), channel_id=1, source_target_pairs={{0,9},{1,8},{2,11},{3,10},{4,13},{5,12},{6,15},{7,14},{8,1},{9,0},... | collective-permute-start | bytes 98312 | tf_op jit(solution)/shard_map/ppermute | solution.py:321
  14.4 3.2 %collective-permute-done.3 = f32[64,128]{1,0:T(8,128)S(1)} collective-permute-done((f32[64,128]{1,0:T(8,128)S(1)}, f32[64,128]{1,0:T(8,128)S(1)}, u32[]{:S(2)}, u32[]{:S(2)}) %collective-permute-start.3) | collective-permute-done | bytes 32800 | tf_op jit(solution)/shard_map/ppermute | solution.py:321
  17.6 1.6 %collective-permute-start.5 = (f32[64,128]{1,0:T(8,128)S(1)}, f32[64,128]{1,0:T(8,128)S(1)}, u32[]{:S(2)}, u32[]{:S(2)}) collective-permute-start(f32[64,128]{1,0:T(8,128)S(1)} %add.21), channel_id=1, source_target_pairs={{0,25},{1,24},{2,27},{3,26},{4,29},{5,28},{6,31},{7,30},{8,17},{9,... | collective-permute-start | bytes 98312 | tf_op jit(solution)/shard_map/ppermute | solution.py:321
  19.2 0.0 collective-permute-start.4
  19.2 3.6 %collective-permute-done.5 = f32[64,128]{1,0:T(8,128)S(1)} collective-permute-done((f32[64,128]{1,0:T(8,128)S(1)}, f32[64,128]{1,0:T(8,128)S(1)}, u32[]{:S(2)}, u32[]{:S(2)}) %collective-permute-start.5) | collective-permute-done | bytes 32800 | tf_op jit(solution)/shard_map/ppermute | solution.py:321
  22.8 0.0 collective-permute-start.6
  22.8 2.8 %collective-permute-done.6 = f32[64,128]{1,0:T(8,128)S(1)} collective-permute-done((f32[64,128]{1,0:T(8,128)S(1)}, f32[64,128]{1,0:T(8,128)S(1)}, u32[]{:S(2)}, u32[]{:S(2)}) %collective-permute-start.6) | collective-permute-done | bytes 32800 | tf_op jit(solution)/shard_map/ppermute | solution.py:321
  25.6 1.0 %collective-permute-start.7 = (f32[64,128]{1,0:T(8,128)S(1)}, f32[64,128]{1,0:T(8,128)S(1)}, u32[]{:S(2)}, u32[]{:S(2)}) collective-permute-start(f32[64,128]{1,0:T(8,128)S(1)} %add.23), channel_id=1, source_target_pairs={{0,6},{1,7},{2,4},{3,5},{4,2},{5,3},{6,0},{7,1},{8,14},{9,15},{10,... | collective-permute-start | bytes 98312 | tf_op jit(solution)/shard_map/ppermute | solution.py:321
  26.5 3.0 %collective-permute-done.7 = f32[64,128]{1,0:T(8,128)S(1)} collective-permute-done((f32[64,128]{1,0:T(8,128)S(1)}, f32[64,128]{1,0:T(8,128)S(1)}, u32[]{:S(2)}, u32[]{:S(2)}) %collective-permute-start.7) | collective-permute-done | bytes 32800 | tf_op jit(solution)/shard_map/ppermute | solution.py:321
  29.6 3.1 %collective-permute-start.8 = (f32[64,128]{1,0:T(8,128)S(1)}, f32[64,128]{1,0:T(8,128)S(1)}, u32[]{:S(2)}, u32[]{:S(2)}) collective-permute-start(f32[64,128]{1,0:T(8,128)S(1)} %add.24), channel_id=1, source_target_pairs={{0,33},{1,32},{2,35},{3,34},{4,37},{5,36},{6,39},{7,38},{8,41},{9,... | collective-permute-start | bytes 98312 | tf_op jit(solution)/shard_map/ppermute | solution.py:321
  32.7 1.6 %collective-permute-done.8 = f32[64,128]{1,0:T(8,128)S(1)} collective-permute-done((f32[64,128]{1,0:T(8,128)S(1)}, f32[64,128]{1,0:T(8,128)S(1)}, u32[]{:S(2)}, u32[]{:S(2)}) %collective-permute-start.8) | collective-permute-done | bytes 32800 | tf_op jit(solution)/shard_map/ppermute | solution.py:321
  34.3 3.1 %collective-permute-start.9 = (f32[64,128]{1,0:T(8,128)S(1)}, f32[64,128]{1,0:T(8,128)S(1)}, u32[]{:S(2)}, u32[]{:S(2)}) collective-permute-start(f32[64,128]{1,0:T(8,128)S(1)} %add.25), channel_id=1, source_target_pairs={{0,65},{1,64},{2,67},{3,66},{4,69},{5,68},{6,71},{7,70},{8,73},{9,... | collective-permute-start | bytes 98312 | tf_op jit(solution)/shard_map/ppermute | solution.py:321
  37.4 2.0 %collective-permute-done.9 = f32[64,128]{1,0:T(8,128)S(1)} collective-permute-done((f32[64,128]{1,0:T(8,128)S(1)}, f32[64,128]{1,0:T(8,128)S(1)}, u32[]{:S(2)}, u32[]{:S(2)}) %collective-permute-start.9) | collective-permute-done | bytes 32800 | tf_op jit(solution)/shard_map/ppermute | solution.py:321
  39.4 5.5 %collective-permute-start.10 = (f32[64,128]{1,0:T(8,128)S(1)}, f32[64,128]{1,0:T(8,128)S(1)}, u32[]{:S(2)}, u32[]{:S(2)}) collective-permute-start(f32[64,128]{1,0:T(8,128)S(1)} %add.26), channel_id=1, source_target_pairs={{0,225},{1,224},{2,227},{3,226},{4,229},{5,228},{6,231},{7,230},{8... | collective-permute-start | bytes 98312 | tf_op jit(solution)/shard_map/ppermute | solution.py:321
  44.9 1.7 %collective-permute-done.10 = f32[64,128]{1,0:T(8,128)S(1)} collective-permute-done((f32[64,128]{1,0:T(8,128)S(1)}, f32[64,128]{1,0:T(8,128)S(1)}, u32[]{:S(2)}, u32[]{:S(2)}) %collective-permute-start.10) | collective-permute-done | bytes 32800 | tf_op jit(solution)/shard_map/ppermute | solution.py:321
  46.6 0.0 collective-permute-start.11
  46.6 0.9 %shard_map.50.refs_0_ = f32[2,2,512,128]{3,2,1,0:T(8,128)} custom-call(f32[2,9,64,128]{3,2,1,0:T(8,128)S(1)} %get-tuple-element.21.held_ref, f32[7,64,128]{2,1,0:T(8,128)S(1)} %get-tuple-element.36.rim_ref, f32[64,128]{1,0:T(8,128)S(1)} %add.27.sum_ref), custom_call_target="tpu_custom_call" | custom-call | flops 1000000 | bytes 2097152 | tf_op jit(solution)/shard_map/pallas_call | solution.py:274
  47.5 0.0 collective-permute-done.4.rim_ref
  47.6 0.3 collective-permute-done.11.sum_ref
  47.8 0.9 %shard_map.51 = f32[2,2,512,128]{3,2,1,0:T(8,128)} custom-call(f32[2,9,64,128]{3,2,1,0:T(8,128)S(1)} %get-tuple-element.21.held_ref, f32[7,64,128]{2,1,0:T(8,128)S(1)} %collective-permute-done.4.rim_ref, f32[64,128]{1,0:T(8,128)S(1)} %collective-permute-done.11.sum_ref, f32[2,2,512,128]{3,2,1,0:T(8,128)} %shard_map.50.refs_0_), custom_call_target="tpu_custom_call", output_to_operand_aliasing={{}: (3, {})} | custom-call | flops 1000000 | bytes 2097152 | tf_op jit(solution)/shard_map/pallas_call | solution.py:274
  (7 shorter events, 0.0 us)
Async XLA Ops:
  1.4 9.0 %collective-permute-start.1 = (f32[2,7,64,128]{3,2,1,0:T(8,128)S(1)}, f32[2,7,64,128]{3,2,1,0:T(8,128)S(1)}, u32[]{:S(2)}, u32[]{:S(2)}) collective-permute-start(f32[2,7,64,128]{3,2,1,0:T(8,128)S(1)} %get-tuple-element.27), channel_id=1, source_target_pairs={{0,1},{1,0},{2,3},{3,2},{4,5},{5,4},{6,7},{7,6},{8,9},{9,8},{10,11... | collective-permute-start | bytes 1376264 | tf_op jit(solution)/shard_map/ppermute | solution.py:337
  4.7 8.2 %collective-permute-start = (f32[2,7,64,128]{3,2,1,0:T(8,128)S(1)}, f32[2,7,64,128]{3,2,1,0:T(8,128)S(1)}, u32[]{:S(2)}, u32[]{:S(2)}) collective-permute-start(f32[2,7,64,128]{3,2,1,0:T(8,128)S(1)} %get-tuple-element.23), channel_id=1, source_target_pairs={{0,7},{1,2},{2,1},{3,4},{4,3},{5,6},{6,5},{7,0},{8,15},{9,10},{10,... | collective-permute-start | bytes 1376264 | tf_op jit(solution)/shard_map/ppermute | solution.py:338
  8.9 2.4 %collective-permute-start.2 = (f32[64,128]{1,0:T(8,128)S(1)}, f32[64,128]{1,0:T(8,128)S(1)}, u32[]{:S(2)}, u32[]{:S(2)}) collective-permute-start(f32[64,128]{1,0:T(8,128)S(1)} %get-tuple-element.30), channel_id=1, source_target_pairs={{0,1},{1,0},{2,3},{3,2},{4,5},{5,4},{6,7},{7,6},{8,9},{9,8},{10,11... | collective-permute-start | bytes 98312 | tf_op jit(solution)/shard_map/ppermute | solution.py:360
  13.9 3.8 %collective-permute-start.3 = (f32[64,128]{1,0:T(8,128)S(1)}, f32[64,128]{1,0:T(8,128)S(1)}, u32[]{:S(2)}, u32[]{:S(2)}) collective-permute-start(f32[64,128]{1,0:T(8,128)S(1)} %get-tuple-element.32), channel_id=1, source_target_pairs={{0,9},{1,8},{2,11},{3,10},{4,13},{5,12},{6,15},{7,14},{8,1},{9,0},... | collective-permute-start | bytes 98312 | tf_op jit(solution)/shard_map/ppermute | solution.py:321
  17.6 5.2 %collective-permute-start.5 = (f32[64,128]{1,0:T(8,128)S(1)}, f32[64,128]{1,0:T(8,128)S(1)}, u32[]{:S(2)}, u32[]{:S(2)}) collective-permute-start(f32[64,128]{1,0:T(8,128)S(1)} %add.21), channel_id=1, source_target_pairs={{0,25},{1,24},{2,27},{3,26},{4,29},{5,28},{6,31},{7,30},{8,17},{9,... | collective-permute-start | bytes 98312 | tf_op jit(solution)/shard_map/ppermute | solution.py:321
  19.2 28.4 %collective-permute-start.4 = (f32[7,64,128]{2,1,0:T(8,128)S(1)}, f32[7,64,128]{2,1,0:T(8,128)S(1)}, u32[]{:S(2)}, u32[]{:S(2)}) collective-permute-start(f32[7,64,128]{2,1,0:T(8,128)S(1)} %get-tuple-element.34), channel_id=1, source_target_pairs={{0,7},{1,0},{2,1},{3,2},{4,3},{5,4},{6,5},{7,6},{8,15},{9,8},{10,9... | collective-permute-start | bytes 688136 | tf_op jit(solution)/shard_map/ppermute | solution.py:320
  22.8 2.8 %collective-permute-start.6 = (f32[64,128]{1,0:T(8,128)S(1)}, f32[64,128]{1,0:T(8,128)S(1)}, u32[]{:S(2)}, u32[]{:S(2)}) collective-permute-start(f32[64,128]{1,0:T(8,128)S(1)} %add.22), channel_id=1, source_target_pairs={{0,2},{1,3},{2,0},{3,1},{4,6},{5,7},{6,4},{7,5},{8,10},{9,11},{10,... | collective-permute-start | bytes 98312 | tf_op jit(solution)/shard_map/ppermute | solution.py:321
  25.6 4.0 %collective-permute-start.7 = (f32[64,128]{1,0:T(8,128)S(1)}, f32[64,128]{1,0:T(8,128)S(1)}, u32[]{:S(2)}, u32[]{:S(2)}) collective-permute-start(f32[64,128]{1,0:T(8,128)S(1)} %add.23), channel_id=1, source_target_pairs={{0,6},{1,7},{2,4},{3,5},{4,2},{5,3},{6,0},{7,1},{8,14},{9,15},{10,... | collective-permute-start | bytes 98312 | tf_op jit(solution)/shard_map/ppermute | solution.py:321
  29.6 4.7 %collective-permute-start.8 = (f32[64,128]{1,0:T(8,128)S(1)}, f32[64,128]{1,0:T(8,128)S(1)}, u32[]{:S(2)}, u32[]{:S(2)}) collective-permute-start(f32[64,128]{1,0:T(8,128)S(1)} %add.24), channel_id=1, source_target_pairs={{0,33},{1,32},{2,35},{3,34},{4,37},{5,36},{6,39},{7,38},{8,41},{9,... | collective-permute-start | bytes 98312 | tf_op jit(solution)/shard_map/ppermute | solution.py:321
  34.3 5.1 %collective-permute-start.9 = (f32[64,128]{1,0:T(8,128)S(1)}, f32[64,128]{1,0:T(8,128)S(1)}, u32[]{:S(2)}, u32[]{:S(2)}) collective-permute-start(f32[64,128]{1,0:T(8,128)S(1)} %add.25), channel_id=1, source_target_pairs={{0,65},{1,64},{2,67},{3,66},{4,69},{5,68},{6,71},{7,70},{8,73},{9,... | collective-permute-start | bytes 98312 | tf_op jit(solution)/shard_map/ppermute | solution.py:321
  39.4 7.2 %collective-permute-start.10 = (f32[64,128]{1,0:T(8,128)S(1)}, f32[64,128]{1,0:T(8,128)S(1)}, u32[]{:S(2)}, u32[]{:S(2)}) collective-permute-start(f32[64,128]{1,0:T(8,128)S(1)} %add.26), channel_id=1, source_target_pairs={{0,225},{1,224},{2,227},{3,226},{4,229},{5,228},{6,231},{7,230},{8... | collective-permute-start | bytes 98312 | tf_op jit(solution)/shard_map/ppermute | solution.py:321
  46.6 1.2 %collective-permute-start.11 = (f32[64,128]{1,0:T(8,128)S(1)}, f32[64,128]{1,0:T(8,128)S(1)}, u32[]{:S(2)}, u32[]{:S(2)}) collective-permute-start(f32[64,128]{1,0:T(8,128)S(1)} %add.27.sum_ref), channel_id=1, source_target_pairs={{0,1},{1,0},{2,3},{3,2},{4,5},{5,4},{6,7},{7,6},{8,9},{9,8},{10,11... | collective-permute-start | bytes 98312 | tf_op jit(solution)/shard_map/ppermute | solution.py:322

commit v9 on v8

--- a/solution.py
+++ b/solution.py
@@ -21,8 +21,9 @@
 BOTH = ("beam", "tm")
 X, Y, Z = 4, 4, 8
 
-RING4 = ((1, 0, 3, 2), (3, 2, 1, 0))
-RING8 = ((1, 0, 3, 2, 5, 4, 7, 6), (2, 3, 0, 1, 6, 7, 4, 5), (7, 6, 5, 4, 3, 2, 1, 0))
+YS = ((3, 2, 1, 0), (1, 0, 3, 2))
+XS = ((1, 0, 3, 2), (2, 3, 0, 1))
+ZS = ((1, 0, 3, 2, 5, 4, 7, 6), (2, 3, 0, 1, 6, 7, 4, 5), (7, 6, 5, 4, 3, 2, 1, 0))
 
 
 def place(z, x, y, core):
@@ -45,8 +46,8 @@
 
 def kept_half():
     tm, beam = lax.axis_index("tm"), lax.axis_index("beam")
-    z = beam // X
-    return (tm + beam % X + z + z // 2 + z // 4) % 2
+    x, z = beam % X, beam // X
+    return (tm + x + x // 2 + z + z // 2 + z // 4) % 2
 
 
 def in_two(table):
@@ -313,7 +314,7 @@
 
 def total_over_all(sums, back):
     left = [(i, (i - 1) % (2 * Y)) for i in range(2 * Y)]
-    steps = [("x", r) for r in RING4] + [("y", r) for r in RING4] + [("z", r) for r in RING8]
+    steps = [("y", YS[0])] + [("x", r) for r in XS] + [("y", YS[1])] + [("z", r) for r in ZS]
     for n, (axis, partner) in enumerate(steps):
         if n == 1:
             sums, back = lax.optimization_barrier((sums, back))

time: 48.9 us -> 48.7 us (level)
  waiting for transfers between devices: 19.8 us -> 14.3 us
  starting transfers between devices: 19.5 us -> 24.8 us
    ppermute x7, waiting for transfers between devices: 18 us -> 12.5 us  [total_over_all(): sums = sums + lax.ppermute(sums, BOTH, swap_pairs(axis, partner))]
    ppermute x7, starting transfers between devices: 14.7 us -> 19.4 us  [total_over_all(): sums = sums + lax.ppermute(sums, BOTH, swap_pairs(axis, partner))]
    ppermute x1, starting transfers between devices: 0.01 us -> 0.59 us  [total_over_all(): back = lax.ppermute(back, 'tm', left)]
where the time goes in v9:
time: 48.7 us; the launch traced here: 48.5 us
  starting transfers between devices  24.8 us (51%)
  waiting for transfers between devices  14.3 us (29%)
  Pallas kernels  9.27 us (19%)
    ppermute x7, starting transfers between devices, total_over_all(): sums = sums + lax.ppermute(sums, BOTH, swap_pairs(axis, partner))  19.4 us
    ppermute x7, waiting for transfers between devices, total_over_all(): sums = sums + lax.ppermute(sums, BOTH, swap_pairs(axis, partner))  12.5 us
    pallas_call x4, Pallas kernels, on_core(): pl.pallas_call(kernel, out_shape=shapes, in_specs=[pl.BlockSpec(memory_sp...  7.45 us
    ppermute x1, starting transfers between devices, body(): near = lax.ppermute(near, 'tm', [(i, i ^ 1) for i in range(devices)])  3.33 us
    pallas_call x2, Pallas kernels, clean(): pl.pallas_call(functools.partial(clean_kernel, scale), out_shape=pltpu.HB...  1.82 us
    ppermute x1, waiting for transfers between devices, body(): lax.ppermute(cross, 'tm', [(i, (i + 1 if i % 2 else i - 1) % devices) for...  1.55 us
    ppermute x1, starting transfers between devices, body(): other = lax.ppermute(send, BOTH, CORES)  1.47 us
  transfers between devices with their start and end apart: 12, of which 9 were waited for; matrix products, arithmetic and copies ran while one was open for 0% of the time, Pallas kernels for 12%

profile of v9, /device:TPU:1, one launch (start us, length us, event | category | flops | bytes accessed | tf_op | source)
XLA Modules:
  0.0 48.5 jit_solution(2913180584472872314)
XLA Ops:
  0.0 1.4 %shard_map.47 = (f32[2,7,64,128]{3,2,1,0:T(8,128)S(1)}, f32[2,7,64,128]{3,2,1,0:T(8,128)S(1)}) custom-call(f32[2,2,2,64,8,128]{5,4,3,2,1,0:T(8,128)} %bitcast.15), custom_call_target="tpu_custom_call" | custom-call | flops 1000 | bytes 1000 | tf_op jit(solution)/shard_map/pallas_call | solution.py:291
  1.4 3.3 %collective-permute-start.1 = (f32[2,7,64,128]{3,2,1,0:T(8,128)S(1)}, f32[2,7,64,128]{3,2,1,0:T(8,128)S(1)}, u32[]{:S(2)}, u32[]{:S(2)}) collective-permute-start(f32[2,7,64,128]{3,2,1,0:T(8,128)S(1)} %get-tuple-element.27), channel_id=1, source_target_pairs={{0,1},{1,0},{2,3},{3,2},{4,5},{5,4},{6,7},{7,6},{8,9},{9,8},{10,11... | collective-permute-start | bytes 1376264 | tf_op jit(solution)/shard_map/ppermute | solution.py:338
  4.7 0.0 collective-permute-start
  4.7 4.2 %shard_map.46 = (f32[2,9,64,128]{3,2,1,0:T(8,128)S(1)}, f32[2,14,64,128]{3,2,1,0:T(8,128)S(1)}, f32[64,128]{1,0:T(8,128)S(1)}, f32[64,128]{1,0:T(8,128)S(1)}, f3...) custom-call(f32[2,2,2,512,128]{4,3,2,1,0:T(8,128)} %bitcast.16, ...), custom_call_target="tpu_custom_call" | custom-call | flops 2000000000 | bytes 6291456 | tf_op jit(solution)/shard_map/pallas_call | solution.py:291
  8.9 1.5 %collective-permute-start.2 = (f32[64,128]{1,0:T(8,128)S(1)}, f32[64,128]{1,0:T(8,128)S(1)}, u32[]{:S(2)}, u32[]{:S(2)}) collective-permute-start(f32[64,128]{1,0:T(8,128)S(1)} %get-tuple-element.30), channel_id=1, source_target_pairs={{0,1},{1,0},{2,3},{3,2},{4,5},{5,4},{6,7},{7,6},{8,9},{9,8},{10,11... | collective-permute-start | bytes 98312 | tf_op jit(solution)/shard_map/ppermute | solution.py:361
  10.4 0.0 collective-permute-done.1.near_ref
  10.4 0.9 %shard_map.48 = (f32[7,64,128]{2,1,0:T(8,128)S(1)}, f32[64,128]{1,0:T(8,128)S(1)}) custom-call(f32[2,14,64,128]{3,2,1,0:T(8,128)S(1)} %get-tuple-element.22.part_ref, f32[2,7,64,128]{3,2,1,0:T(8,128)S(1)} %collective-permute-done.1.near_ref, f32[512,128]{1,0:T(8,128)S(1)} %get-tuple-element.24.taps_ref, bf16[768,256]{1,0:T(8,128)(2,1)S(1)} %get-tuple-element.25.table_ref, ...), custom_call_target="tpu_custom_call" | custom-call | flops 1000000000 | bytes 3145728 | tf_op jit(solution)/shard_map/pallas_call | solution.py:291
  11.3 0.0 collective-permute-done.2.other_ref
  11.4 1.5 %collective-permute-done.cross_ref = f32[2,7,64,128]{3,2,1,0:T(8,128)S(1)} collective-permute-done((f32[2,7,64,128]{3,2,1,0:T(8,128)S(1)}, f32[2,7,64,128]{3,2,1,0:T(8,128)S(1)}, u32[]{:S(2)}, u32[]{:S(2)}) %collective-permute-start) | collective-permute-done | bytes 458784 | tf_op jit(solution)/shard_map/ppermute | solution.py:339
  12.9 0.9 %shard_map.49 = (f32[7,64,128]{2,1,0:T(8,128)S(1)}, f32[7,64,128]{2,1,0:T(8,128)S(1)}, f32[64,128]{1,0:T(8,128)S(1)}) custom-call(f32[2,14,64,128]{3,2,1,0:T(8,128)S(1)} %get-tuple-element.22.part_ref, f32[2,7,64,128]{3,2,1,0:T(8,128)S(1)} %collective-permute-done.cross_ref, f32[512,128]{1,0:T(8,128)S(1)} %get-tuple-element.24.taps_ref, ...), custom_call_target="tpu_custom_call" | custom-call | tf_op jit(solution)/shard_map/pallas_call | solution.py:291
  13.9 2.0 %collective-permute-start.3 = (f32[64,128]{1,0:T(8,128)S(1)}, f32[64,128]{1,0:T(8,128)S(1)}, u32[]{:S(2)}, u32[]{:S(2)}) collective-permute-start(f32[64,128]{1,0:T(8,128)S(1)} %get-tuple-element.32), channel_id=1, source_target_pairs={{0,6},{1,7},{2,4},{3,5},{4,2},{5,3},{6,0},{7,1},{8,14},{9,15},{10,... | collective-permute-start | bytes 98312 | tf_op jit(solution)/shard_map/ppermute | solution.py:322
  15.9 2.1 %collective-permute-done.3 = f32[64,128]{1,0:T(8,128)S(1)} collective-permute-done((f32[64,128]{1,0:T(8,128)S(1)}, f32[64,128]{1,0:T(8,128)S(1)}, u32[]{:S(2)}, u32[]{:S(2)}) %collective-permute-start.3) | collective-permute-done | bytes 32800 | tf_op jit(solution)/shard_map/ppermute | solution.py:322
  17.9 1.6 %collective-permute-start.5 = (f32[64,128]{1,0:T(8,128)S(1)}, f32[64,128]{1,0:T(8,128)S(1)}, u32[]{:S(2)}, u32[]{:S(2)}) collective-permute-start(f32[64,128]{1,0:T(8,128)S(1)} %add.21), channel_id=1, source_target_pairs={{0,9},{1,8},{2,11},{3,10},{4,13},{5,12},{6,15},{7,14},{8,1},{9,0},... | collective-permute-start | bytes 98312 | tf_op jit(solution)/shard_map/ppermute | solution.py:322
  19.5 0.6 %collective-permute-start.4 = (f32[7,64,128]{2,1,0:T(8,128)S(1)}, f32[7,64,128]{2,1,0:T(8,128)S(1)}, u32[]{:S(2)}, u32[]{:S(2)}) collective-permute-start(f32[7,64,128]{2,1,0:T(8,128)S(1)} %get-tuple-element.34), channel_id=1, source_target_pairs={{0,7},{1,0},{2,1},{3,2},{4,3},{5,4},{6,5},{7,6},{8,15},{9,8},{10,9... | collective-permute-start | bytes 688136 | tf_op jit(solution)/shard_map/ppermute | solution.py:321
  20.1 1.2 %collective-permute-done.5 = f32[64,128]{1,0:T(8,128)S(1)} collective-permute-done((f32[64,128]{1,0:T(8,128)S(1)}, f32[64,128]{1,0:T(8,128)S(1)}, u32[]{:S(2)}, u32[]{:S(2)}) %collective-permute-start.5) | collective-permute-done | bytes 32800 | tf_op jit(solution)/shard_map/ppermute | solution.py:322
  21.3 3.2 %collective-permute-start.6 = (f32[64,128]{1,0:T(8,128)S(1)}, f32[64,128]{1,0:T(8,128)S(1)}, u32[]{:S(2)}, u32[]{:S(2)}) collective-permute-start(f32[64,128]{1,0:T(8,128)S(1)} %add.22), channel_id=1, source_target_pairs={{0,17},{1,16},{2,19},{3,18},{4,21},{5,20},{6,23},{7,22},{8,25},{9,... | collective-permute-start | bytes 98312 | tf_op jit(solution)/shard_map/ppermute | solution.py:322
  24.5 1.6 %collective-permute-done.6 = f32[64,128]{1,0:T(8,128)S(1)} collective-permute-done((f32[64,128]{1,0:T(8,128)S(1)}, f32[64,128]{1,0:T(8,128)S(1)}, u32[]{:S(2)}, u32[]{:S(2)}) %collective-permute-start.6) | collective-permute-done | bytes 32800 | tf_op jit(solution)/shard_map/ppermute | solution.py:322
  26.1 0.0 collective-permute-start.7
  26.1 2.8 %collective-permute-done.7 = f32[64,128]{1,0:T(8,128)S(1)} collective-permute-done((f32[64,128]{1,0:T(8,128)S(1)}, f32[64,128]{1,0:T(8,128)S(1)}, u32[]{:S(2)}, u32[]{:S(2)}) %collective-permute-start.7) | collective-permute-done | bytes 32800 | tf_op jit(solution)/shard_map/ppermute | solution.py:322
  28.9 3.5 %collective-permute-start.8 = (f32[64,128]{1,0:T(8,128)S(1)}, f32[64,128]{1,0:T(8,128)S(1)}, u32[]{:S(2)}, u32[]{:S(2)}) collective-permute-start(f32[64,128]{1,0:T(8,128)S(1)} %add.24), channel_id=1, source_target_pairs={{0,33},{1,32},{2,35},{3,34},{4,37},{5,36},{6,39},{7,38},{8,41},{9,... | collective-permute-start | bytes 98312 | tf_op jit(solution)/shard_map/ppermute | solution.py:322
  32.4 1.6 %collective-permute-done.8 = f32[64,128]{1,0:T(8,128)S(1)} collective-permute-done((f32[64,128]{1,0:T(8,128)S(1)}, f32[64,128]{1,0:T(8,128)S(1)}, u32[]{:S(2)}, u32[]{:S(2)}) %collective-permute-start.8) | collective-permute-done | bytes 32800 | tf_op jit(solution)/shard_map/ppermute | solution.py:322
  34.0 3.1 %collective-permute-start.9 = (f32[64,128]{1,0:T(8,128)S(1)}, f32[64,128]{1,0:T(8,128)S(1)}, u32[]{:S(2)}, u32[]{:S(2)}) collective-permute-start(f32[64,128]{1,0:T(8,128)S(1)} %add.25), channel_id=1, source_target_pairs={{0,65},{1,64},{2,67},{3,66},{4,69},{5,68},{6,71},{7,70},{8,73},{9,... | collective-permute-start | bytes 98312 | tf_op jit(solution)/shard_map/ppermute | solution.py:322
  37.1 1.6 %collective-permute-done.9 = f32[64,128]{1,0:T(8,128)S(1)} collective-permute-done((f32[64,128]{1,0:T(8,128)S(1)}, f32[64,128]{1,0:T(8,128)S(1)}, u32[]{:S(2)}, u32[]{:S(2)}) %collective-permute-start.9) | collective-permute-done | bytes 32800 | tf_op jit(solution)/shard_map/ppermute | solution.py:322
  38.7 5.9 %collective-permute-start.10 = (f32[64,128]{1,0:T(8,128)S(1)}, f32[64,128]{1,0:T(8,128)S(1)}, u32[]{:S(2)}, u32[]{:S(2)}) collective-permute-start(f32[64,128]{1,0:T(8,128)S(1)} %add.26), channel_id=1, source_target_pairs={{0,225},{1,224},{2,227},{3,226},{4,229},{5,228},{6,231},{7,230},{8... | collective-permute-start | bytes 98312 | tf_op jit(solution)/shard_map/ppermute | solution.py:322
  44.6 1.7 %collective-permute-done.10 = f32[64,128]{1,0:T(8,128)S(1)} collective-permute-done((f32[64,128]{1,0:T(8,128)S(1)}, f32[64,128]{1,0:T(8,128)S(1)}, u32[]{:S(2)}, u32[]{:S(2)}) %collective-permute-start.10) | collective-permute-done | bytes 32800 | tf_op jit(solution)/shard_map/ppermute | solution.py:322
  46.4 0.0 collective-permute-start.11
  46.4 0.9 %shard_map.50.refs_0_ = f32[2,2,512,128]{3,2,1,0:T(8,128)} custom-call(f32[2,9,64,128]{3,2,1,0:T(8,128)S(1)} %get-tuple-element.21.held_ref, f32[7,64,128]{2,1,0:T(8,128)S(1)} %get-tuple-element.36.rim_ref, f32[64,128]{1,0:T(8,128)S(1)} %add.27.sum_ref), custom_call_target="tpu_custom_call" | custom-call | flops 1000000 | bytes 2097152 | tf_op jit(solution)/shard_map/pallas_call | solution.py:275
  47.3 0.0 collective-permute-done.4.rim_ref
  47.3 0.3 collective-permute-done.11.sum_ref
  47.6 0.9 %shard_map.51 = f32[2,2,512,128]{3,2,1,0:T(8,128)} custom-call(f32[2,9,64,128]{3,2,1,0:T(8,128)S(1)} %get-tuple-element.21.held_ref, f32[7,64,128]{2,1,0:T(8,128)S(1)} %collective-permute-done.4.rim_ref, f32[64,128]{1,0:T(8,128)S(1)} %collective-permute-done.11.sum_ref, f32[2,2,512,128]{3,2,1,0:T(8,128)} %shard_map.50.refs_0_), custom_call_target="tpu_custom_call", output_to_operand_aliasing={{}: (3, {})} | custom-call | flops 1000000 | bytes 2097152 | tf_op jit(solution)/shard_map/pallas_call | solution.py:275
  (7 shorter events, 0.0 us)
Async XLA Ops:
  1.4 9.0 %collective-permute-start.1 = (f32[2,7,64,128]{3,2,1,0:T(8,128)S(1)}, f32[2,7,64,128]{3,2,1,0:T(8,128)S(1)}, u32[]{:S(2)}, u32[]{:S(2)}) collective-permute-start(f32[2,7,64,128]{3,2,1,0:T(8,128)S(1)} %get-tuple-element.27), channel_id=1, source_target_pairs={{0,1},{1,0},{2,3},{3,2},{4,5},{5,4},{6,7},{7,6},{8,9},{9,8},{10,11... | collective-permute-start | bytes 1376264 | tf_op jit(solution)/shard_map/ppermute | solution.py:338
  4.7 8.2 %collective-permute-start = (f32[2,7,64,128]{3,2,1,0:T(8,128)S(1)}, f32[2,7,64,128]{3,2,1,0:T(8,128)S(1)}, u32[]{:S(2)}, u32[]{:S(2)}) collective-permute-start(f32[2,7,64,128]{3,2,1,0:T(8,128)S(1)} %get-tuple-element.23), channel_id=1, source_target_pairs={{0,7},{1,2},{2,1},{3,4},{4,3},{5,6},{6,5},{7,0},{8,15},{9,10},{10,... | collective-permute-start | bytes 1376264 | tf_op jit(solution)/shard_map/ppermute | solution.py:339
  8.9 2.4 %collective-permute-start.2 = (f32[64,128]{1,0:T(8,128)S(1)}, f32[64,128]{1,0:T(8,128)S(1)}, u32[]{:S(2)}, u32[]{:S(2)}) collective-permute-start(f32[64,128]{1,0:T(8,128)S(1)} %get-tuple-element.30), channel_id=1, source_target_pairs={{0,1},{1,0},{2,3},{3,2},{4,5},{5,4},{6,7},{7,6},{8,9},{9,8},{10,11... | collective-permute-start | bytes 98312 | tf_op jit(solution)/shard_map/ppermute | solution.py:361
  13.9 4.1 %collective-permute-start.3 = (f32[64,128]{1,0:T(8,128)S(1)}, f32[64,128]{1,0:T(8,128)S(1)}, u32[]{:S(2)}, u32[]{:S(2)}) collective-permute-start(f32[64,128]{1,0:T(8,128)S(1)} %get-tuple-element.32), channel_id=1, source_target_pairs={{0,6},{1,7},{2,4},{3,5},{4,2},{5,3},{6,0},{7,1},{8,14},{9,15},{10,... | collective-permute-start | bytes 98312 | tf_op jit(solution)/shard_map/ppermute | solution.py:322
  17.9 3.3 %collective-permute-start.5 = (f32[64,128]{1,0:T(8,128)S(1)}, f32[64,128]{1,0:T(8,128)S(1)}, u32[]{:S(2)}, u32[]{:S(2)}) collective-permute-start(f32[64,128]{1,0:T(8,128)S(1)} %add.21), channel_id=1, source_target_pairs={{0,9},{1,8},{2,11},{3,10},{4,13},{5,12},{6,15},{7,14},{8,1},{9,0},... | collective-permute-start | bytes 98312 | tf_op jit(solution)/shard_map/ppermute | solution.py:322
  19.5 27.8 %collective-permute-start.4 = (f32[7,64,128]{2,1,0:T(8,128)S(1)}, f32[7,64,128]{2,1,0:T(8,128)S(1)}, u32[]{:S(2)}, u32[]{:S(2)}) collective-permute-start(f32[7,64,128]{2,1,0:T(8,128)S(1)} %get-tuple-element.34), channel_id=1, source_target_pairs={{0,7},{1,0},{2,1},{3,2},{4,3},{5,4},{6,5},{7,6},{8,15},{9,8},{10,9... | collective-permute-start | bytes 688136 | tf_op jit(solution)/shard_map/ppermute | solution.py:321
  21.3 4.8 %collective-permute-start.6 = (f32[64,128]{1,0:T(8,128)S(1)}, f32[64,128]{1,0:T(8,128)S(1)}, u32[]{:S(2)}, u32[]{:S(2)}) collective-permute-start(f32[64,128]{1,0:T(8,128)S(1)} %add.22), channel_id=1, source_target_pairs={{0,17},{1,16},{2,19},{3,18},{4,21},{5,20},{6,23},{7,22},{8,25},{9,... | collective-permute-start | bytes 98312 | tf_op jit(solution)/shard_map/ppermute | solution.py:322
  26.1 2.8 %collective-permute-start.7 = (f32[64,128]{1,0:T(8,128)S(1)}, f32[64,128]{1,0:T(8,128)S(1)}, u32[]{:S(2)}, u32[]{:S(2)}) collective-permute-start(f32[64,128]{1,0:T(8,128)S(1)} %add.23), channel_id=1, source_target_pairs={{0,2},{1,3},{2,0},{3,1},{4,6},{5,7},{6,4},{7,5},{8,10},{9,11},{10,... | collective-permute-start | bytes 98312 | tf_op jit(solution)/shard_map/ppermute | solution.py:322
  28.9 5.1 %collective-permute-start.8 = (f32[64,128]{1,0:T(8,128)S(1)}, f32[64,128]{1,0:T(8,128)S(1)}, u32[]{:S(2)}, u32[]{:S(2)}) collective-permute-start(f32[64,128]{1,0:T(8,128)S(1)} %add.24), channel_id=1, source_target_pairs={{0,33},{1,32},{2,35},{3,34},{4,37},{5,36},{6,39},{7,38},{8,41},{9,... | collective-permute-start | bytes 98312 | tf_op jit(solution)/shard_map/ppermute | solution.py:322
  34.0 4.7 %collective-permute-start.9 = (f32[64,128]{1,0:T(8,128)S(1)}, f32[64,128]{1,0:T(8,128)S(1)}, u32[]{:S(2)}, u32[]{:S(2)}) collective-permute-start(f32[64,128]{1,0:T(8,128)S(1)} %add.25), channel_id=1, source_target_pairs={{0,65},{1,64},{2,67},{3,66},{4,69},{5,68},{6,71},{7,70},{8,73},{9,... | collective-permute-start | bytes 98312 | tf_op jit(solution)/shard_map/ppermute | solution.py:322
  38.7 7.6 %collective-permute-start.10 = (f32[64,128]{1,0:T(8,128)S(1)}, f32[64,128]{1,0:T(8,128)S(1)}, u32[]{:S(2)}, u32[]{:S(2)}) collective-permute-start(f32[64,128]{1,0:T(8,128)S(1)} %add.26), channel_id=1, source_target_pairs={{0,225},{1,224},{2,227},{3,226},{4,229},{5,228},{6,231},{7,230},{8... | collective-permute-start | bytes 98312 | tf_op jit(solution)/shard_map/ppermute | solution.py:322
  46.4 1.2 %collective-permute-start.11 = (f32[64,128]{1,0:T(8,128)S(1)}, f32[64,128]{1,0:T(8,128)S(1)}, u32[]{:S(2)}, u32[]{:S(2)}) collective-permute-start(f32[64,128]{1,0:T(8,128)S(1)} %add.27.sum_ref), channel_id=1, source_target_pairs={{0,1},{1,0},{2,3},{3,2},{4,5},{5,4},{6,7},{7,6},{8,9},{9,8},{10,11... | collective-permute-start | bytes 98312 | tf_op jit(solution)/shard_map/ppermute | solution.py:323

commit v10 on v9

--- a/solution.py
+++ b/solution.py
@@ -22,7 +22,7 @@
 X, Y, Z = 4, 4, 8
 
 YS = ((3, 2, 1, 0), (1, 0, 3, 2))
-XS = ((1, 0, 3, 2), (2, 3, 0, 1))
+XS = ((1, 0, 3, 2), (3, 2, 1, 0))
 ZS = ((1, 0, 3, 2, 5, 4, 7, 6), (2, 3, 0, 1, 6, 7, 4, 5), (7, 6, 5, 4, 3, 2, 1, 0))
 
 
@@ -47,7 +47,7 @@
 def kept_half():
     tm, beam = lax.axis_index("tm"), lax.axis_index("beam")
     x, z = beam % X, beam // X
-    return (tm + x + x // 2 + z + z // 2 + z // 4) % 2
+    return (tm + x + z + z // 2 + z // 4) % 2
 
 
 def in_two(table):

time: 48.7 us -> 48.4 us (level)
  transfers between devices with their start and end apart: 12 -> 12, of which waited for: 9 -> 9; matrix products, arithmetic and copies ran while one was open for 0% -> 0% of each run, Pallas kernels for 12% -> 13%
where the time goes in v10:
time: 48.4 us; the launch traced here: 48.2 us
  starting transfers between devices  24.4 us (50%)
  waiting for transfers between devices  14.4 us (30%)
  Pallas kernels  9.26 us (19%)
    ppermute x7, starting transfers between devices, total_over_all(): sums = sums + lax.ppermute(sums, BOTH, swap_pairs(axis, partner))  19 us
    ppermute x7, waiting for transfers between devices, total_over_all(): sums = sums + lax.ppermute(sums, BOTH, swap_pairs(axis, partner))  12.6 us
    pallas_call x4, Pallas kernels, on_core(): pl.pallas_call(kernel, out_shape=shapes, in_specs=[pl.BlockSpec(memory_sp...  7.45 us
    ppermute x1, starting transfers between devices, body(): near = lax.ppermute(near, 'tm', [(i, i ^ 1) for i in range(devices)])  3.33 us
    pallas_call x2, Pallas kernels, clean(): pl.pallas_call(functools.partial(clean_kernel, scale), out_shape=pltpu.HB...  1.81 us
    ppermute x1, waiting for transfers between devices, body(): lax.ppermute(cross, 'tm', [(i, (i + 1 if i % 2 else i - 1) % devices) for...  1.55 us
    ppermute x1, starting transfers between devices, body(): other = lax.ppermute(send, BOTH, CORES)  1.47 us
  transfers between devices with their start and end apart: 12, of which 9 were waited for; matrix products, arithmetic and copies ran while one was open for 0% of the time, Pallas kernels for 13%

profile of v10, /device:TPU:1, one launch (start us, length us, event | category | flops | bytes accessed | tf_op | source)
XLA Modules:
  0.0 48.2 jit_solution(4621318069007899389)
XLA Ops:
  0.0 1.4 %shard_map.47 = (f32[2,7,64,128]{3,2,1,0:T(8,128)S(1)}, f32[2,7,64,128]{3,2,1,0:T(8,128)S(1)}) custom-call(f32[2,2,2,64,8,128]{5,4,3,2,1,0:T(8,128)} %bitcast.15), custom_call_target="tpu_custom_call" | custom-call | flops 1000 | bytes 1000 | tf_op jit(solution)/shard_map/pallas_call | solution.py:291
  1.4 3.3 %collective-permute-start.1 = (f32[2,7,64,128]{3,2,1,0:T(8,128)S(1)}, f32[2,7,64,128]{3,2,1,0:T(8,128)S(1)}, u32[]{:S(2)}, u32[]{:S(2)}) collective-permute-start(f32[2,7,64,128]{3,2,1,0:T(8,128)S(1)} %get-tuple-element.27), channel_id=1, source_target_pairs={{0,1},{1,0},{2,3},{3,2},{4,5},{5,4},{6,7},{7,6},{8,9},{9,8},{10,11... | collective-permute-start | bytes 1376264 | tf_op jit(solution)/shard_map/ppermute | solution.py:338
  4.7 0.0 collective-permute-start
  4.7 4.2 %shard_map.46 = (f32[2,9,64,128]{3,2,1,0:T(8,128)S(1)}, f32[2,14,64,128]{3,2,1,0:T(8,128)S(1)}, f32[64,128]{1,0:T(8,128)S(1)}, f32[64,128]{1,0:T(8,128)S(1)}, f3...) custom-call(f32[2,2,2,512,128]{4,3,2,1,0:T(8,128)} %bitcast.16, ...), custom_call_target="tpu_custom_call" | custom-call | flops 2000000000 | bytes 6291456 | tf_op jit(solution)/shard_map/pallas_call | solution.py:291
  8.9 1.5 %collective-permute-start.2 = (f32[64,128]{1,0:T(8,128)S(1)}, f32[64,128]{1,0:T(8,128)S(1)}, u32[]{:S(2)}, u32[]{:S(2)}) collective-permute-start(f32[64,128]{1,0:T(8,128)S(1)} %get-tuple-element.30), channel_id=1, source_target_pairs={{0,1},{1,0},{2,3},{3,2},{4,5},{5,4},{6,7},{7,6},{8,9},{9,8},{10,11... | collective-permute-start | bytes 98312 | tf_op jit(solution)/shard_map/ppermute | solution.py:361
  10.4 0.0 collective-permute-done.1.near_ref
  10.4 0.9 %shard_map.48 = (f32[7,64,128]{2,1,0:T(8,128)S(1)}, f32[64,128]{1,0:T(8,128)S(1)}) custom-call(f32[2,14,64,128]{3,2,1,0:T(8,128)S(1)} %get-tuple-element.22.part_ref, f32[2,7,64,128]{3,2,1,0:T(8,128)S(1)} %collective-permute-done.1.near_ref, f32[512,128]{1,0:T(8,128)S(1)} %get-tuple-element.24.taps_ref, bf16[768,256]{1,0:T(8,128)(2,1)S(1)} %get-tuple-element.25.table_ref, ...), custom_call_target="tpu_custom_call" | custom-call | flops 1000000000 | bytes 3145728 | tf_op jit(solution)/shard_map/pallas_call | solution.py:291
  11.3 0.0 collective-permute-done.2.other_ref
  11.4 1.5 %collective-permute-done.cross_ref = f32[2,7,64,128]{3,2,1,0:T(8,128)S(1)} collective-permute-done((f32[2,7,64,128]{3,2,1,0:T(8,128)S(1)}, f32[2,7,64,128]{3,2,1,0:T(8,128)S(1)}, u32[]{:S(2)}, u32[]{:S(2)}) %collective-permute-start) | collective-permute-done | bytes 458784 | tf_op jit(solution)/shard_map/ppermute | solution.py:339
  12.9 0.9 %shard_map.49 = (f32[7,64,128]{2,1,0:T(8,128)S(1)}, f32[7,64,128]{2,1,0:T(8,128)S(1)}, f32[64,128]{1,0:T(8,128)S(1)}) custom-call(f32[2,14,64,128]{3,2,1,0:T(8,128)S(1)} %get-tuple-element.22.part_ref, f32[2,7,64,128]{3,2,1,0:T(8,128)S(1)} %collective-permute-done.cross_ref, f32[512,128]{1,0:T(8,128)S(1)} %get-tuple-element.24.taps_ref, ...), custom_call_target="tpu_custom_call" | custom-call | tf_op jit(solution)/shard_map/pallas_call | solution.py:291
  13.9 2.0 %collective-permute-start.3 = (f32[64,128]{1,0:T(8,128)S(1)}, f32[64,128]{1,0:T(8,128)S(1)}, u32[]{:S(2)}, u32[]{:S(2)}) collective-permute-start(f32[64,128]{1,0:T(8,128)S(1)} %get-tuple-element.32), channel_id=1, source_target_pairs={{0,6},{1,7},{2,4},{3,5},{4,2},{5,3},{6,0},{7,1},{8,14},{9,15},{10,... | collective-permute-start | bytes 98312 | tf_op jit(solution)/shard_map/ppermute | solution.py:322
  15.9 2.1 %collective-permute-done.3 = f32[64,128]{1,0:T(8,128)S(1)} collective-permute-done((f32[64,128]{1,0:T(8,128)S(1)}, f32[64,128]{1,0:T(8,128)S(1)}, u32[]{:S(2)}, u32[]{:S(2)}) %collective-permute-start.3) | collective-permute-done | bytes 32800 | tf_op jit(solution)/shard_map/ppermute | solution.py:322
  17.9 1.6 %collective-permute-start.5 = (f32[64,128]{1,0:T(8,128)S(1)}, f32[64,128]{1,0:T(8,128)S(1)}, u32[]{:S(2)}, u32[]{:S(2)}) collective-permute-start(f32[64,128]{1,0:T(8,128)S(1)} %add.21), channel_id=1, source_target_pairs={{0,9},{1,8},{2,11},{3,10},{4,13},{5,12},{6,15},{7,14},{8,1},{9,0},... | collective-permute-start | bytes 98312 | tf_op jit(solution)/shard_map/ppermute | solution.py:322
  19.5 0.6 %collective-permute-start.4 = (f32[7,64,128]{2,1,0:T(8,128)S(1)}, f32[7,64,128]{2,1,0:T(8,128)S(1)}, u32[]{:S(2)}, u32[]{:S(2)}) collective-permute-start(f32[7,64,128]{2,1,0:T(8,128)S(1)} %get-tuple-element.34), channel_id=1, source_target_pairs={{0,7},{1,0},{2,1},{3,2},{4,3},{5,4},{6,5},{7,6},{8,15},{9,8},{10,9... | collective-permute-start | bytes 688136 | tf_op jit(solution)/shard_map/ppermute | solution.py:321
  20.1 1.2 %collective-permute-done.5 = f32[64,128]{1,0:T(8,128)S(1)} collective-permute-done((f32[64,128]{1,0:T(8,128)S(1)}, f32[64,128]{1,0:T(8,128)S(1)}, u32[]{:S(2)}, u32[]{:S(2)}) %collective-permute-start.5) | collective-permute-done | bytes 32800 | tf_op jit(solution)/shard_map/ppermute | solution.py:322
  21.3 2.9 %collective-permute-start.6 = (f32[64,128]{1,0:T(8,128)S(1)}, f32[64,128]{1,0:T(8,128)S(1)}, u32[]{:S(2)}, u32[]{:S(2)}) collective-permute-start(f32[64,128]{1,0:T(8,128)S(1)} %add.22), channel_id=1, source_target_pairs={{0,25},{1,24},{2,27},{3,26},{4,29},{5,28},{6,31},{7,30},{8,17},{9,... | collective-permute-start | bytes 98312 | tf_op jit(solution)/shard_map/ppermute | solution.py:322
  24.1 1.7 %collective-permute-done.6 = f32[64,128]{1,0:T(8,128)S(1)} collective-permute-done((f32[64,128]{1,0:T(8,128)S(1)}, f32[64,128]{1,0:T(8,128)S(1)}, u32[]{:S(2)}, u32[]{:S(2)}) %collective-permute-start.6) | collective-permute-done | bytes 32800 | tf_op jit(solution)/shard_map/ppermute | solution.py:322
  25.8 0.0 collective-permute-start.7
  25.8 2.8 %collective-permute-done.7 = f32[64,128]{1,0:T(8,128)S(1)} collective-permute-done((f32[64,128]{1,0:T(8,128)S(1)}, f32[64,128]{1,0:T(8,128)S(1)}, u32[]{:S(2)}, u32[]{:S(2)}) %collective-permute-start.7) | collective-permute-done | bytes 32800 | tf_op jit(solution)/shard_map/ppermute | solution.py:322
  28.6 3.5 %collective-permute-start.8 = (f32[64,128]{1,0:T(8,128)S(1)}, f32[64,128]{1,0:T(8,128)S(1)}, u32[]{:S(2)}, u32[]{:S(2)}) collective-permute-start(f32[64,128]{1,0:T(8,128)S(1)} %add.24), channel_id=1, source_target_pairs={{0,33},{1,32},{2,35},{3,34},{4,37},{5,36},{6,39},{7,38},{8,41},{9,... | collective-permute-start | bytes 98312 | tf_op jit(solution)/shard_map/ppermute | solution.py:322
  32.1 1.6 %collective-permute-done.8 = f32[64,128]{1,0:T(8,128)S(1)} collective-permute-done((f32[64,128]{1,0:T(8,128)S(1)}, f32[64,128]{1,0:T(8,128)S(1)}, u32[]{:S(2)}, u32[]{:S(2)}) %collective-permute-start.8) | collective-permute-done | bytes 32800 | tf_op jit(solution)/shard_map/ppermute | solution.py:322
  33.7 3.1 %collective-permute-start.9 = (f32[64,128]{1,0:T(8,128)S(1)}, f32[64,128]{1,0:T(8,128)S(1)}, u32[]{:S(2)}, u32[]{:S(2)}) collective-permute-start(f32[64,128]{1,0:T(8,128)S(1)} %add.25), channel_id=1, source_target_pairs={{0,65},{1,64},{2,67},{3,66},{4,69},{5,68},{6,71},{7,70},{8,73},{9,... | collective-permute-start | bytes 98312 | tf_op jit(solution)/shard_map/ppermute | solution.py:322
  36.8 1.6 %collective-permute-done.9 = f32[64,128]{1,0:T(8,128)S(1)} collective-permute-done((f32[64,128]{1,0:T(8,128)S(1)}, f32[64,128]{1,0:T(8,128)S(1)}, u32[]{:S(2)}, u32[]{:S(2)}) %collective-permute-start.9) | collective-permute-done | bytes 32800 | tf_op jit(solution)/shard_map/ppermute | solution.py:322
  38.4 5.9 %collective-permute-start.10 = (f32[64,128]{1,0:T(8,128)S(1)}, f32[64,128]{1,0:T(8,128)S(1)}, u32[]{:S(2)}, u32[]{:S(2)}) collective-permute-start(f32[64,128]{1,0:T(8,128)S(1)} %add.26), channel_id=1, source_target_pairs={{0,225},{1,224},{2,227},{3,226},{4,229},{5,228},{6,231},{7,230},{8... | collective-permute-start | bytes 98312 | tf_op jit(solution)/shard_map/ppermute | solution.py:322
  44.4 1.7 %collective-permute-done.10 = f32[64,128]{1,0:T(8,128)S(1)} collective-permute-done((f32[64,128]{1,0:T(8,128)S(1)}, f32[64,128]{1,0:T(8,128)S(1)}, u32[]{:S(2)}, u32[]{:S(2)}) %collective-permute-start.10) | collective-permute-done | bytes 32800 | tf_op jit(solution)/shard_map/ppermute | solution.py:322
  46.1 0.0 collective-permute-start.11
  46.1 0.9 %shard_map.50.refs_0_ = f32[2,2,512,128]{3,2,1,0:T(8,128)} custom-call(f32[2,9,64,128]{3,2,1,0:T(8,128)S(1)} %get-tuple-element.21.held_ref, f32[7,64,128]{2,1,0:T(8,128)S(1)} %get-tuple-element.36.rim_ref, f32[64,128]{1,0:T(8,128)S(1)} %add.27.sum_ref), custom_call_target="tpu_custom_call" | custom-call | flops 1000000 | bytes 2097152 | tf_op jit(solution)/shard_map/pallas_call | solution.py:275
  47.0 0.0 collective-permute-done.4.rim_ref
  47.0 0.3 collective-permute-done.11.sum_ref
  47.3 0.9 %shard_map.51 = f32[2,2,512,128]{3,2,1,0:T(8,128)} custom-call(f32[2,9,64,128]{3,2,1,0:T(8,128)S(1)} %get-tuple-element.21.held_ref, f32[7,64,128]{2,1,0:T(8,128)S(1)} %collective-permute-done.4.rim_ref, f32[64,128]{1,0:T(8,128)S(1)} %collective-permute-done.11.sum_ref, f32[2,2,512,128]{3,2,1,0:T(8,128)} %shard_map.50.refs_0_), custom_call_target="tpu_custom_call", output_to_operand_aliasing={{}: (3, {})} | custom-call | flops 1000000 | bytes 2097152 | tf_op jit(solution)/shard_map/pallas_call | solution.py:275
  (7 shorter events, 0.0 us)
Async XLA Ops:
  1.4 9.0 %collective-permute-start.1 = (f32[2,7,64,128]{3,2,1,0:T(8,128)S(1)}, f32[2,7,64,128]{3,2,1,0:T(8,128)S(1)}, u32[]{:S(2)}, u32[]{:S(2)}) collective-permute-start(f32[2,7,64,128]{3,2,1,0:T(8,128)S(1)} %get-tuple-element.27), channel_id=1, source_target_pairs={{0,1},{1,0},{2,3},{3,2},{4,5},{5,4},{6,7},{7,6},{8,9},{9,8},{10,11... | collective-permute-start | bytes 1376264 | tf_op jit(solution)/shard_map/ppermute | solution.py:338
  4.7 8.2 %collective-permute-start = (f32[2,7,64,128]{3,2,1,0:T(8,128)S(1)}, f32[2,7,64,128]{3,2,1,0:T(8,128)S(1)}, u32[]{:S(2)}, u32[]{:S(2)}) collective-permute-start(f32[2,7,64,128]{3,2,1,0:T(8,128)S(1)} %get-tuple-element.23), channel_id=1, source_target_pairs={{0,7},{1,2},{2,1},{3,4},{4,3},{5,6},{6,5},{7,0},{8,15},{9,10},{10,... | collective-permute-start | bytes 1376264 | tf_op jit(solution)/shard_map/ppermute | solution.py:339
  8.9 2.4 %collective-permute-start.2 = (f32[64,128]{1,0:T(8,128)S(1)}, f32[64,128]{1,0:T(8,128)S(1)}, u32[]{:S(2)}, u32[]{:S(2)}) collective-permute-start(f32[64,128]{1,0:T(8,128)S(1)} %get-tuple-element.30), channel_id=1, source_target_pairs={{0,1},{1,0},{2,3},{3,2},{4,5},{5,4},{6,7},{7,6},{8,9},{9,8},{10,11... | collective-permute-start | bytes 98312 | tf_op jit(solution)/shard_map/ppermute | solution.py:361
  13.9 4.1 %collective-permute-start.3 = (f32[64,128]{1,0:T(8,128)S(1)}, f32[64,128]{1,0:T(8,128)S(1)}, u32[]{:S(2)}, u32[]{:S(2)}) collective-permute-start(f32[64,128]{1,0:T(8,128)S(1)} %get-tuple-element.32), channel_id=1, source_target_pairs={{0,6},{1,7},{2,4},{3,5},{4,2},{5,3},{6,0},{7,1},{8,14},{9,15},{10,... | collective-permute-start | bytes 98312 | tf_op jit(solution)/shard_map/ppermute | solution.py:322
  17.9 3.3 %collective-permute-start.5 = (f32[64,128]{1,0:T(8,128)S(1)}, f32[64,128]{1,0:T(8,128)S(1)}, u32[]{:S(2)}, u32[]{:S(2)}) collective-permute-start(f32[64,128]{1,0:T(8,128)S(1)} %add.21), channel_id=1, source_target_pairs={{0,9},{1,8},{2,11},{3,10},{4,13},{5,12},{6,15},{7,14},{8,1},{9,0},... | collective-permute-start | bytes 98312 | tf_op jit(solution)/shard_map/ppermute | solution.py:322
  19.5 27.5 %collective-permute-start.4 = (f32[7,64,128]{2,1,0:T(8,128)S(1)}, f32[7,64,128]{2,1,0:T(8,128)S(1)}, u32[]{:S(2)}, u32[]{:S(2)}) collective-permute-start(f32[7,64,128]{2,1,0:T(8,128)S(1)} %get-tuple-element.34), channel_id=1, source_target_pairs={{0,7},{1,0},{2,1},{3,2},{4,3},{5,4},{6,5},{7,6},{8,15},{9,8},{10,9... | collective-permute-start | bytes 688136 | tf_op jit(solution)/shard_map/ppermute | solution.py:321
  21.3 4.6 %collective-permute-start.6 = (f32[64,128]{1,0:T(8,128)S(1)}, f32[64,128]{1,0:T(8,128)S(1)}, u32[]{:S(2)}, u32[]{:S(2)}) collective-permute-start(f32[64,128]{1,0:T(8,128)S(1)} %add.22), channel_id=1, source_target_pairs={{0,25},{1,24},{2,27},{3,26},{4,29},{5,28},{6,31},{7,30},{8,17},{9,... | collective-permute-start | bytes 98312 | tf_op jit(solution)/shard_map/ppermute | solution.py:322
  25.8 2.8 %collective-permute-start.7 = (f32[64,128]{1,0:T(8,128)S(1)}, f32[64,128]{1,0:T(8,128)S(1)}, u32[]{:S(2)}, u32[]{:S(2)}) collective-permute-start(f32[64,128]{1,0:T(8,128)S(1)} %add.23), channel_id=1, source_target_pairs={{0,2},{1,3},{2,0},{3,1},{4,6},{5,7},{6,4},{7,5},{8,10},{9,11},{10,... | collective-permute-start | bytes 98312 | tf_op jit(solution)/shard_map/ppermute | solution.py:322
  28.6 5.1 %collective-permute-start.8 = (f32[64,128]{1,0:T(8,128)S(1)}, f32[64,128]{1,0:T(8,128)S(1)}, u32[]{:S(2)}, u32[]{:S(2)}) collective-permute-start(f32[64,128]{1,0:T(8,128)S(1)} %add.24), channel_id=1, source_target_pairs={{0,33},{1,32},{2,35},{3,34},{4,37},{5,36},{6,39},{7,38},{8,41},{9,... | collective-permute-start | bytes 98312 | tf_op jit(solution)/shard_map/ppermute | solution.py:322
  33.7 4.7 %collective-permute-start.9 = (f32[64,128]{1,0:T(8,128)S(1)}, f32[64,128]{1,0:T(8,128)S(1)}, u32[]{:S(2)}, u32[]{:S(2)}) collective-permute-start(f32[64,128]{1,0:T(8,128)S(1)} %add.25), channel_id=1, source_target_pairs={{0,65},{1,64},{2,67},{3,66},{4,69},{5,68},{6,71},{7,70},{8,73},{9,... | collective-permute-start | bytes 98312 | tf_op jit(solution)/shard_map/ppermute | solution.py:322
  38.4 7.6 %collective-permute-start.10 = (f32[64,128]{1,0:T(8,128)S(1)}, f32[64,128]{1,0:T(8,128)S(1)}, u32[]{:S(2)}, u32[]{:S(2)}) collective-permute-start(f32[64,128]{1,0:T(8,128)S(1)} %add.26), channel_id=1, source_target_pairs={{0,225},{1,224},{2,227},{3,226},{4,229},{5,228},{6,231},{7,230},{8... | collective-permute-start | bytes 98312 | tf_op jit(solution)/shard_map/ppermute | solution.py:322
  46.1 1.2 %collective-permute-start.11 = (f32[64,128]{1,0:T(8,128)S(1)}, f32[64,128]{1,0:T(8,128)S(1)}, u32[]{:S(2)}, u32[]{:S(2)}) collective-permute-start(f32[64,128]{1,0:T(8,128)S(1)} %add.27.sum_ref), channel_id=1, source_target_pairs={{0,1},{1,0},{2,3},{3,2},{4,5},{5,4},{6,7},{7,6},{8,9},{9,8},{10,11... | collective-permute-start | bytes 98312 | tf_op jit(solution)/shard_map/ppermute | solution.py:323

commit v11 on v10

--- a/solution.py
+++ b/solution.py
@@ -100,8 +100,8 @@
     across = (((1,), (1,)), ((), ()))
     table = table_ref[4 * ROWS :]
     both = lax.dot_general(table, high, across, preferred_element_type=jnp.float32)
-    both += lax.dot_general(table, low, across, preferred_element_type=jnp.float32)
-    spec = both[: 2 * LANES] + both[2 * LANES :]
+    rest = lax.dot_general(table[: 2 * LANES], low, across, preferred_element_type=jnp.float32)
+    spec = both[: 2 * LANES] + (both[2 * LANES :] + rest)
     re, im = spec[:LANES], spec[LANES:]
     powers = (re * re + im * im) * (1.0 / CHANNELS)
     left = lax.broadcasted_iota(jnp.int32, (ROWS, LANES), 1) < ROWS

time: 48.4 us -> 48.3 us (level)
  transfers between devices with their start and end apart: 12 -> 12, of which waited for: 9 -> 9; matrix products, arithmetic and copies ran while one was open for 0% -> 0% of each run, Pallas kernels for 13% -> 12%
where the time goes in v11:
time: 48.3 us; the launch traced here: 48.1 us
  starting transfers between devices  24.4 us (51%)
  waiting for transfers between devices  14.7 us (30%)
  Pallas kernels  8.94 us (19%)
    ppermute x7, starting transfers between devices, total_over_all(): sums = sums + lax.ppermute(sums, BOTH, swap_pairs(axis, partner))  19 us
    ppermute x7, waiting for transfers between devices, total_over_all(): sums = sums + lax.ppermute(sums, BOTH, swap_pairs(axis, partner))  12.6 us
    pallas_call x4, Pallas kernels, on_core(): pl.pallas_call(kernel, out_shape=shapes, in_specs=[pl.BlockSpec(memory_sp...  7.13 us
    ppermute x1, starting transfers between devices, body(): near = lax.ppermute(near, 'tm', [(i, i ^ 1) for i in range(devices)])  3.33 us
    pallas_call x2, Pallas kernels, clean(): pl.pallas_call(functools.partial(clean_kernel, scale), out_shape=pltpu.HB...  1.81 us
    ppermute x1, waiting for transfers between devices, body(): lax.ppermute(cross, 'tm', [(i, (i + 1 if i % 2 else i - 1) % devices) for...  1.79 us
    ppermute x1, starting transfers between devices, body(): other = lax.ppermute(send, BOTH, CORES)  1.48 us
  transfers between devices with their start and end apart: 12, of which 9 were waited for; matrix products, arithmetic and copies ran while one was open for 0% of the time, Pallas kernels for 12%

profile of v11, /device:TPU:1, one launch (start us, length us, event | category | flops | bytes accessed | tf_op | source)
XLA Modules:
  0.0 48.1 jit_solution(11298760114187192680)
XLA Ops:
  0.0 1.4 %shard_map.47 = (f32[2,7,64,128]{3,2,1,0:T(8,128)S(1)}, f32[2,7,64,128]{3,2,1,0:T(8,128)S(1)}) custom-call(f32[2,2,2,64,8,128]{5,4,3,2,1,0:T(8,128)} %bitcast.15), custom_call_target="tpu_custom_call" | custom-call | flops 1000 | bytes 1000 | tf_op jit(solution)/shard_map/pallas_call | solution.py:291
  1.4 3.3 %collective-permute-start.1 = (f32[2,7,64,128]{3,2,1,0:T(8,128)S(1)}, f32[2,7,64,128]{3,2,1,0:T(8,128)S(1)}, u32[]{:S(2)}, u32[]{:S(2)}) collective-permute-start(f32[2,7,64,128]{3,2,1,0:T(8,128)S(1)} %get-tuple-element.27), channel_id=1, source_target_pairs={{0,1},{1,0},{2,3},{3,2},{4,5},{5,4},{6,7},{7,6},{8,9},{9,8},{10,11... | collective-permute-start | bytes 1376264 | tf_op jit(solution)/shard_map/ppermute | solution.py:338
  4.7 0.0 collective-permute-start
  4.7 4.0 %shard_map.46 = (f32[2,9,64,128]{3,2,1,0:T(8,128)S(1)}, f32[2,14,64,128]{3,2,1,0:T(8,128)S(1)}, f32[64,128]{1,0:T(8,128)S(1)}, f32[64,128]{1,0:T(8,128)S(1)}, f3...) custom-call(f32[2,2,2,512,128]{4,3,2,1,0:T(8,128)} %bitcast.16, ...), custom_call_target="tpu_custom_call" | custom-call | flops 2000000000 | bytes 6291456 | tf_op jit(solution)/shard_map/pallas_call | solution.py:291
  8.8 1.5 %collective-permute-start.2 = (f32[64,128]{1,0:T(8,128)S(1)}, f32[64,128]{1,0:T(8,128)S(1)}, u32[]{:S(2)}, u32[]{:S(2)}) collective-permute-start(f32[64,128]{1,0:T(8,128)S(1)} %get-tuple-element.30), channel_id=1, source_target_pairs={{0,1},{1,0},{2,3},{3,2},{4,5},{5,4},{6,7},{7,6},{8,9},{9,8},{10,11... | collective-permute-start | bytes 98312 | tf_op jit(solution)/shard_map/ppermute | solution.py:361
  10.2 0.0 collective-permute-done.1.near_ref
  10.2 0.9 %shard_map.48 = (f32[7,64,128]{2,1,0:T(8,128)S(1)}, f32[64,128]{1,0:T(8,128)S(1)}) custom-call(f32[2,14,64,128]{3,2,1,0:T(8,128)S(1)} %get-tuple-element.22.part_ref, f32[2,7,64,128]{3,2,1,0:T(8,128)S(1)} %collective-permute-done.1.near_ref, f32[512,128]{1,0:T(8,128)S(1)} %get-tuple-element.24.taps_ref, bf16[768,256]{1,0:T(8,128)(2,1)S(1)} %get-tuple-element.25.table_ref, ...), custom_call_target="tpu_custom_call" | custom-call | flops 1000000000 | bytes 3145728 | tf_op jit(solution)/shard_map/pallas_call | solution.py:291
  11.1 0.0 collective-permute-done.2.other_ref
  11.1 1.8 %collective-permute-done.cross_ref = f32[2,7,64,128]{3,2,1,0:T(8,128)S(1)} collective-permute-done((f32[2,7,64,128]{3,2,1,0:T(8,128)S(1)}, f32[2,7,64,128]{3,2,1,0:T(8,128)S(1)}, u32[]{:S(2)}, u32[]{:S(2)}) %collective-permute-start) | collective-permute-done | bytes 458784 | tf_op jit(solution)/shard_map/ppermute | solution.py:339
  12.9 0.9 %shard_map.49 = (f32[7,64,128]{2,1,0:T(8,128)S(1)}, f32[7,64,128]{2,1,0:T(8,128)S(1)}, f32[64,128]{1,0:T(8,128)S(1)}) custom-call(f32[2,14,64,128]{3,2,1,0:T(8,128)S(1)} %get-tuple-element.22.part_ref, f32[2,7,64,128]{3,2,1,0:T(8,128)S(1)} %collective-permute-done.cross_ref, f32[512,128]{1,0:T(8,128)S(1)} %get-tuple-element.24.taps_ref, ...), custom_call_target="tpu_custom_call" | custom-call | tf_op jit(solution)/shard_map/pallas_call | solution.py:291
  13.8 2.0 %collective-permute-start.3 = (f32[64,128]{1,0:T(8,128)S(1)}, f32[64,128]{1,0:T(8,128)S(1)}, u32[]{:S(2)}, u32[]{:S(2)}) collective-permute-start(f32[64,128]{1,0:T(8,128)S(1)} %get-tuple-element.32), channel_id=1, source_target_pairs={{0,6},{1,7},{2,4},{3,5},{4,2},{5,3},{6,0},{7,1},{8,14},{9,15},{10,... | collective-permute-start | bytes 98312 | tf_op jit(solution)/shard_map/ppermute | solution.py:322
  15.8 2.1 %collective-permute-done.3 = f32[64,128]{1,0:T(8,128)S(1)} collective-permute-done((f32[64,128]{1,0:T(8,128)S(1)}, f32[64,128]{1,0:T(8,128)S(1)}, u32[]{:S(2)}, u32[]{:S(2)}) %collective-permute-start.3) | collective-permute-done | bytes 32800 | tf_op jit(solution)/shard_map/ppermute | solution.py:322
  17.9 1.6 %collective-permute-start.5 = (f32[64,128]{1,0:T(8,128)S(1)}, f32[64,128]{1,0:T(8,128)S(1)}, u32[]{:S(2)}, u32[]{:S(2)}) collective-permute-start(f32[64,128]{1,0:T(8,128)S(1)} %add.21), channel_id=1, source_target_pairs={{0,9},{1,8},{2,11},{3,10},{4,13},{5,12},{6,15},{7,14},{8,1},{9,0},... | collective-permute-start | bytes 98312 | tf_op jit(solution)/shard_map/ppermute | solution.py:322
  19.4 0.6 %collective-permute-start.4 = (f32[7,64,128]{2,1,0:T(8,128)S(1)}, f32[7,64,128]{2,1,0:T(8,128)S(1)}, u32[]{:S(2)}, u32[]{:S(2)}) collective-permute-start(f32[7,64,128]{2,1,0:T(8,128)S(1)} %get-tuple-element.34), channel_id=1, source_target_pairs={{0,7},{1,0},{2,1},{3,2},{4,3},{5,4},{6,5},{7,6},{8,15},{9,8},{10,9... | collective-permute-start | bytes 688136 | tf_op jit(solution)/shard_map/ppermute | solution.py:321
  20.0 1.2 %collective-permute-done.5 = f32[64,128]{1,0:T(8,128)S(1)} collective-permute-done((f32[64,128]{1,0:T(8,128)S(1)}, f32[64,128]{1,0:T(8,128)S(1)}, u32[]{:S(2)}, u32[]{:S(2)}) %collective-permute-start.5) | collective-permute-done | bytes 32800 | tf_op jit(solution)/shard_map/ppermute | solution.py:322
  21.2 2.8 %collective-permute-start.6 = (f32[64,128]{1,0:T(8,128)S(1)}, f32[64,128]{1,0:T(8,128)S(1)}, u32[]{:S(2)}, u32[]{:S(2)}) collective-permute-start(f32[64,128]{1,0:T(8,128)S(1)} %add.22), channel_id=1, source_target_pairs={{0,25},{1,24},{2,27},{3,26},{4,29},{5,28},{6,31},{7,30},{8,17},{9,... | collective-permute-start | bytes 98312 | tf_op jit(solution)/shard_map/ppermute | solution.py:322
  24.0 1.7 %collective-permute-done.6 = f32[64,128]{1,0:T(8,128)S(1)} collective-permute-done((f32[64,128]{1,0:T(8,128)S(1)}, f32[64,128]{1,0:T(8,128)S(1)}, u32[]{:S(2)}, u32[]{:S(2)}) %collective-permute-start.6) | collective-permute-done | bytes 32800 | tf_op jit(solution)/shard_map/ppermute | solution.py:322
  25.8 0.0 collective-permute-start.7
  25.8 2.8 %collective-permute-done.7 = f32[64,128]{1,0:T(8,128)S(1)} collective-permute-done((f32[64,128]{1,0:T(8,128)S(1)}, f32[64,128]{1,0:T(8,128)S(1)}, u32[]{:S(2)}, u32[]{:S(2)}) %collective-permute-start.7) | collective-permute-done | bytes 32800 | tf_op jit(solution)/shard_map/ppermute | solution.py:322
  28.5 3.5 %collective-permute-start.8 = (f32[64,128]{1,0:T(8,128)S(1)}, f32[64,128]{1,0:T(8,128)S(1)}, u32[]{:S(2)}, u32[]{:S(2)}) collective-permute-start(f32[64,128]{1,0:T(8,128)S(1)} %add.24), channel_id=1, source_target_pairs={{0,33},{1,32},{2,35},{3,34},{4,37},{5,36},{6,39},{7,38},{8,41},{9,... | collective-permute-start | bytes 98312 | tf_op jit(solution)/shard_map/ppermute | solution.py:322
  32.0 1.6 %collective-permute-done.8 = f32[64,128]{1,0:T(8,128)S(1)} collective-permute-done((f32[64,128]{1,0:T(8,128)S(1)}, f32[64,128]{1,0:T(8,128)S(1)}, u32[]{:S(2)}, u32[]{:S(2)}) %collective-permute-start.8) | collective-permute-done | bytes 32800 | tf_op jit(solution)/shard_map/ppermute | solution.py:322
  33.7 3.1 %collective-permute-start.9 = (f32[64,128]{1,0:T(8,128)S(1)}, f32[64,128]{1,0:T(8,128)S(1)}, u32[]{:S(2)}, u32[]{:S(2)}) collective-permute-start(f32[64,128]{1,0:T(8,128)S(1)} %add.25), channel_id=1, source_target_pairs={{0,65},{1,64},{2,67},{3,66},{4,69},{5,68},{6,71},{7,70},{8,73},{9,... | collective-permute-start | bytes 98312 | tf_op jit(solution)/shard_map/ppermute | solution.py:322
  36.7 1.6 %collective-permute-done.9 = f32[64,128]{1,0:T(8,128)S(1)} collective-permute-done((f32[64,128]{1,0:T(8,128)S(1)}, f32[64,128]{1,0:T(8,128)S(1)}, u32[]{:S(2)}, u32[]{:S(2)}) %collective-permute-start.9) | collective-permute-done | bytes 32800 | tf_op jit(solution)/shard_map/ppermute | solution.py:322
  38.3 5.9 %collective-permute-start.10 = (f32[64,128]{1,0:T(8,128)S(1)}, f32[64,128]{1,0:T(8,128)S(1)}, u32[]{:S(2)}, u32[]{:S(2)}) collective-permute-start(f32[64,128]{1,0:T(8,128)S(1)} %add.26), channel_id=1, source_target_pairs={{0,225},{1,224},{2,227},{3,226},{4,229},{5,228},{6,231},{7,230},{8... | collective-permute-start | bytes 98312 | tf_op jit(solution)/shard_map/ppermute | solution.py:322
  44.3 1.7 %collective-permute-done.10 = f32[64,128]{1,0:T(8,128)S(1)} collective-permute-done((f32[64,128]{1,0:T(8,128)S(1)}, f32[64,128]{1,0:T(8,128)S(1)}, u32[]{:S(2)}, u32[]{:S(2)}) %collective-permute-start.10) | collective-permute-done | bytes 32800 | tf_op jit(solution)/shard_map/ppermute | solution.py:322
  46.0 0.0 collective-permute-start.11
  46.0 0.9 %shard_map.50.refs_0_ = f32[2,2,512,128]{3,2,1,0:T(8,128)} custom-call(f32[2,9,64,128]{3,2,1,0:T(8,128)S(1)} %get-tuple-element.21.held_ref, f32[7,64,128]{2,1,0:T(8,128)S(1)} %get-tuple-element.36.rim_ref, f32[64,128]{1,0:T(8,128)S(1)} %add.27.sum_ref), custom_call_target="tpu_custom_call" | custom-call | flops 1000000 | bytes 2097152 | tf_op jit(solution)/shard_map/pallas_call | solution.py:275
  46.9 0.0 collective-permute-done.4.rim_ref
  46.9 0.3 collective-permute-done.11.sum_ref
  47.2 0.9 %shard_map.51 = f32[2,2,512,128]{3,2,1,0:T(8,128)} custom-call(f32[2,9,64,128]{3,2,1,0:T(8,128)S(1)} %get-tuple-element.21.held_ref, f32[7,64,128]{2,1,0:T(8,128)S(1)} %collective-permute-done.4.rim_ref, f32[64,128]{1,0:T(8,128)S(1)} %collective-permute-done.11.sum_ref, f32[2,2,512,128]{3,2,1,0:T(8,128)} %shard_map.50.refs_0_), custom_call_target="tpu_custom_call", output_to_operand_aliasing={{}: (3, {})} | custom-call | flops 1000000 | bytes 2097152 | tf_op jit(solution)/shard_map/pallas_call | solution.py:275
  (7 shorter events, 0.0 us)
Async XLA Ops:
  1.4 8.9 %collective-permute-start.1 = (f32[2,7,64,128]{3,2,1,0:T(8,128)S(1)}, f32[2,7,64,128]{3,2,1,0:T(8,128)S(1)}, u32[]{:S(2)}, u32[]{:S(2)}) collective-permute-start(f32[2,7,64,128]{3,2,1,0:T(8,128)S(1)} %get-tuple-element.27), channel_id=1, source_target_pairs={{0,1},{1,0},{2,3},{3,2},{4,5},{5,4},{6,7},{7,6},{8,9},{9,8},{10,11... | collective-permute-start | bytes 1376264 | tf_op jit(solution)/shard_map/ppermute | solution.py:338
  4.7 8.2 %collective-permute-start = (f32[2,7,64,128]{3,2,1,0:T(8,128)S(1)}, f32[2,7,64,128]{3,2,1,0:T(8,128)S(1)}, u32[]{:S(2)}, u32[]{:S(2)}) collective-permute-start(f32[2,7,64,128]{3,2,1,0:T(8,128)S(1)} %get-tuple-element.23), channel_id=1, source_target_pairs={{0,7},{1,2},{2,1},{3,4},{4,3},{5,6},{6,5},{7,0},{8,15},{9,10},{10,... | collective-permute-start | bytes 1376264 | tf_op jit(solution)/shard_map/ppermute | solution.py:339
  8.8 2.3 %collective-permute-start.2 = (f32[64,128]{1,0:T(8,128)S(1)}, f32[64,128]{1,0:T(8,128)S(1)}, u32[]{:S(2)}, u32[]{:S(2)}) collective-permute-start(f32[64,128]{1,0:T(8,128)S(1)} %get-tuple-element.30), channel_id=1, source_target_pairs={{0,1},{1,0},{2,3},{3,2},{4,5},{5,4},{6,7},{7,6},{8,9},{9,8},{10,11... | collective-permute-start | bytes 98312 | tf_op jit(solution)/shard_map/ppermute | solution.py:361
  13.8 4.1 %collective-permute-start.3 = (f32[64,128]{1,0:T(8,128)S(1)}, f32[64,128]{1,0:T(8,128)S(1)}, u32[]{:S(2)}, u32[]{:S(2)}) collective-permute-start(f32[64,128]{1,0:T(8,128)S(1)} %get-tuple-element.32), channel_id=1, source_target_pairs={{0,6},{1,7},{2,4},{3,5},{4,2},{5,3},{6,0},{7,1},{8,14},{9,15},{10,... | collective-permute-start | bytes 98312 | tf_op jit(solution)/shard_map/ppermute | solution.py:322
  17.9 3.3 %collective-permute-start.5 = (f32[64,128]{1,0:T(8,128)S(1)}, f32[64,128]{1,0:T(8,128)S(1)}, u32[]{:S(2)}, u32[]{:S(2)}) collective-permute-start(f32[64,128]{1,0:T(8,128)S(1)} %add.21), channel_id=1, source_target_pairs={{0,9},{1,8},{2,11},{3,10},{4,13},{5,12},{6,15},{7,14},{8,1},{9,0},... | collective-permute-start | bytes 98312 | tf_op jit(solution)/shard_map/ppermute | solution.py:322
  19.4 27.5 %collective-permute-start.4 = (f32[7,64,128]{2,1,0:T(8,128)S(1)}, f32[7,64,128]{2,1,0:T(8,128)S(1)}, u32[]{:S(2)}, u32[]{:S(2)}) collective-permute-start(f32[7,64,128]{2,1,0:T(8,128)S(1)} %get-tuple-element.34), channel_id=1, source_target_pairs={{0,7},{1,0},{2,1},{3,2},{4,3},{5,4},{6,5},{7,6},{8,15},{9,8},{10,9... | collective-permute-start | bytes 688136 | tf_op jit(solution)/shard_map/ppermute | solution.py:321
  21.2 4.6 %collective-permute-start.6 = (f32[64,128]{1,0:T(8,128)S(1)}, f32[64,128]{1,0:T(8,128)S(1)}, u32[]{:S(2)}, u32[]{:S(2)}) collective-permute-start(f32[64,128]{1,0:T(8,128)S(1)} %add.22), channel_id=1, source_target_pairs={{0,25},{1,24},{2,27},{3,26},{4,29},{5,28},{6,31},{7,30},{8,17},{9,... | collective-permute-start | bytes 98312 | tf_op jit(solution)/shard_map/ppermute | solution.py:322
  25.8 2.8 %collective-permute-start.7 = (f32[64,128]{1,0:T(8,128)S(1)}, f32[64,128]{1,0:T(8,128)S(1)}, u32[]{:S(2)}, u32[]{:S(2)}) collective-permute-start(f32[64,128]{1,0:T(8,128)S(1)} %add.23), channel_id=1, source_target_pairs={{0,2},{1,3},{2,0},{3,1},{4,6},{5,7},{6,4},{7,5},{8,10},{9,11},{10,... | collective-permute-start | bytes 98312 | tf_op jit(solution)/shard_map/ppermute | solution.py:322
  28.5 5.1 %collective-permute-start.8 = (f32[64,128]{1,0:T(8,128)S(1)}, f32[64,128]{1,0:T(8,128)S(1)}, u32[]{:S(2)}, u32[]{:S(2)}) collective-permute-start(f32[64,128]{1,0:T(8,128)S(1)} %add.24), channel_id=1, source_target_pairs={{0,33},{1,32},{2,35},{3,34},{4,37},{5,36},{6,39},{7,38},{8,41},{9,... | collective-permute-start | bytes 98312 | tf_op jit(solution)/shard_map/ppermute | solution.py:322
  33.7 4.7 %collective-permute-start.9 = (f32[64,128]{1,0:T(8,128)S(1)}, f32[64,128]{1,0:T(8,128)S(1)}, u32[]{:S(2)}, u32[]{:S(2)}) collective-permute-start(f32[64,128]{1,0:T(8,128)S(1)} %add.25), channel_id=1, source_target_pairs={{0,65},{1,64},{2,67},{3,66},{4,69},{5,68},{6,71},{7,70},{8,73},{9,... | collective-permute-start | bytes 98312 | tf_op jit(solution)/shard_map/ppermute | solution.py:322
  38.3 7.7 %collective-permute-start.10 = (f32[64,128]{1,0:T(8,128)S(1)}, f32[64,128]{1,0:T(8,128)S(1)}, u32[]{:S(2)}, u32[]{:S(2)}) collective-permute-start(f32[64,128]{1,0:T(8,128)S(1)} %add.26), channel_id=1, source_target_pairs={{0,225},{1,224},{2,227},{3,226},{4,229},{5,228},{6,231},{7,230},{8... | collective-permute-start | bytes 98312 | tf_op jit(solution)/shard_map/ppermute | solution.py:322
  46.0 1.2 %collective-permute-start.11 = (f32[64,128]{1,0:T(8,128)S(1)}, f32[64,128]{1,0:T(8,128)S(1)}, u32[]{:S(2)}, u32[]{:S(2)}) collective-permute-start(f32[64,128]{1,0:T(8,128)S(1)} %add.27.sum_ref), channel_id=1, source_target_pairs={{0,1},{1,0},{2,3},{3,2},{4,5},{5,4},{6,7},{7,6},{8,9},{9,8},{10,11... | collective-permute-start | bytes 98312 | tf_op jit(solution)/shard_map/ppermute | solution.py:323

commit v12 on v10

--- a/solution.py
+++ b/solution.py
@@ -30,7 +30,7 @@
     return ((z * X + x) * Y + y) * 2 + core
 
 
-def swap_pairs(axis, partner):
+def swap_pairs(axis, partner, crosswise=True):
     pairs = []
     for z in range(Z):
         for x in range(X):
@@ -40,7 +40,7 @@
                     "x": lambda: (z, partner[x], y),
                     "y": lambda: (z, x, partner[y]),
                 }[axis]()
-                pairs += [(place(z, x, y, c), place(*there, c if axis == "y" else 1 - c)) for c in range(2)]
+                pairs += [(place(z, x, y, c), place(*there, 1 - c if crosswise and axis != "y" else c)) for c in range(2)]
     return pairs
 
 
@@ -255,32 +255,30 @@
             kept_ref[...] = early_ref[...]
 
 
-def clean_kernel(scale, held_ref, rim_ref, sum_ref, *refs):
-    out_ref, tile_ref, sems = refs[-3:]
-    p = kept_half() if len(refs) == 3 else 1 - kept_half()
-    base = sum_ref[...] * scale
+def clean_kernel(scale, held_ref, ahead_ref, back_ref, mine_ref, other_ref, out_ref, tile_ref, sems):
     copies = []
-    for half in range(2):
-        for f in range(8 * half, 8 * half + 8):
-            power = held_ref[p, f] if f < HELD else rim_ref[f - HELD]
-            tile_ref[half, pl.ds(f % 8, ROWS, stride=8), :] = power - base
-        copies.append(pltpu.make_async_copy(tile_ref.at[half], out_ref.at[p, half], sems.at[half]))
-        copies[-1].start()
+    for n, (rim_ref, sum_ref) in enumerate(((ahead_ref, mine_ref), (back_ref, other_ref))):
+        p = 1 - kept_half() if n else kept_half()
+        base = sum_ref[...] * scale
+        for half in range(2):
+            for f in range(8 * half, 8 * half + 8):
+                power = held_ref[p, f] if f < HELD else rim_ref[f - HELD]
+                tile_ref[n, half, pl.ds(f % 8, ROWS, stride=8), :] = power - base
+            copies.append(pltpu.make_async_copy(tile_ref.at[n, half], out_ref.at[p, half], sems.at[n, half]))
+            copies[-1].start()
     for copy in copies:
         copy.wait()
 
 
 def clean(scale, *args):
-    far = [pl.BlockSpec(memory_space=pl.ANY)]
     return pl.pallas_call(
         functools.partial(clean_kernel, scale),
         out_shape=pltpu.HBM((2, 2, 8 * ROWS, LANES), jnp.float32),
-        in_specs=[pl.BlockSpec(memory_space=pltpu.VMEM)] * 3 + far * (len(args) - 3),
-        out_specs=far[0],
-        scratch_shapes=[pltpu.VMEM((2, 8 * ROWS, LANES), jnp.float32), pltpu.SemaphoreType.DMA((2,))],
-        input_output_aliases={3: 0} if len(args) == 4 else {},
+        in_specs=[pl.BlockSpec(memory_space=pltpu.VMEM)] * len(args),
+        out_specs=pl.BlockSpec(memory_space=pl.ANY),
+        scratch_shapes=[pltpu.VMEM((2, 2, 8 * ROWS, LANES), jnp.float32), pltpu.SemaphoreType.DMA((2, 2))],
         compiler_params=pltpu.CompilerParams(vmem_limit_bytes=16 << 20),
-        cost_estimate=pl.CostEstimate(flops=10**6, bytes_accessed=2 << 20, transcendentals=0),
+        cost_estimate=pl.CostEstimate(flops=10**6, bytes_accessed=4 << 20, transcendentals=0),
     )(*args)
 
 
@@ -316,11 +314,13 @@
     left = [(i, (i - 1) % (2 * Y)) for i in range(2 * Y)]
     steps = [("y", YS[0])] + [("x", r) for r in XS] + [("y", YS[1])] + [("z", r) for r in ZS]
     for n, (axis, partner) in enumerate(steps):
-        if n == 1:
-            sums, back = lax.optimization_barrier((sums, back))
+        if n == 0:
             back = lax.ppermute(back, "tm", left)
+        if n == len(steps) - 1:
+            there = lax.ppermute(sums, BOTH, swap_pairs(axis, partner, crosswise=False))
+            here = lax.ppermute(sums, BOTH, CORES)
         sums = sums + lax.ppermute(sums, BOTH, swap_pairs(axis, partner))
-    return sums, lax.ppermute(sums, BOTH, CORES), back
+    return sums, here + there, back
 
 
 def body(voltages, filter_taps):
@@ -370,8 +370,7 @@
     )(part, cross, taps, table, twist, had, other, early)
     mine, other, back = total_over_all(sums, back)
     scale = 1.0 / (FRAMES * devices * lax.axis_size("beam"))
-    out = clean(scale, held, ahead, mine)
-    out = clean(scale, held, back, other, out)
+    out = clean(scale, held, ahead, back, mine, other)
     out = jnp.swapaxes(out.reshape(2, 2, ROWS, 8, LANES), 2, 3)
     return out.reshape(1, 2, FRAMES, CHANNELS)
 

time: 48.4 us -> 50.4 us (1.041); the launches traced: 48.2 us -> 49.5 us
  waiting for transfers between devices: 14.4 us -> 16.5 us
  Pallas kernels: 9.26 us -> 8.55 us
    ppermute x1 -> x2, waiting for transfers between devices: 0.27 us -> 2.26 us  [the longest x1 2.26 us: total_over_all(): there = lax.ppermute(sums, BOTH, swap_pairs(axis, partner, crosswise=False))]
    pallas_call x2 -> x1, Pallas kernels: 1.81 us -> 1.1 us  [clean(): pl.pallas_call(functools.partial(clean_kernel, scale), out_shape=pltpu.HB...]
    ppermute x1, starting transfers between devices: 0.59 us -> 0.01 us  [total_over_all(): back = lax.ppermute(back, 'tm', left)]
  transfers between devices with their start and end apart: 12 -> 13, of which waited for: 9 -> 9; matrix products, arithmetic and copies ran while one was open for 0% -> 0% of each run, Pallas kernels for 13% -> 10%
where the time goes in v12:
time: 50.4 us; the launch traced here: 49.5 us
  starting transfers between devices  24.3 us (48%)
  waiting for transfers between devices  16.5 us (33%)
  Pallas kernels  8.55 us (17%)
    ppermute x7, starting transfers between devices, total_over_all(): sums = sums + lax.ppermute(sums, BOTH, swap_pairs(axis, partner))  19 us
    ppermute x7, waiting for transfers between devices, total_over_all(): sums = sums + lax.ppermute(sums, BOTH, swap_pairs(axis, partner))  12.7 us
    pallas_call x4, Pallas kernels, on_core(): pl.pallas_call(kernel, out_shape=shapes, in_specs=[pl.BlockSpec(memory_sp...  7.45 us
    ppermute x1, starting transfers between devices, body(): near = lax.ppermute(near, 'tm', [(i, i ^ 1) for i in range(devices)])  3.33 us
    ppermute x1, waiting for transfers between devices, total_over_all(): there = lax.ppermute(sums, BOTH, swap_pairs(axis, partner, crosswise=False))  2.26 us
    ppermute x1, waiting for transfers between devices, body(): lax.ppermute(cross, 'tm', [(i, (i + 1 if i % 2 else i - 1) % devices) for...  1.55 us
    ppermute x1, starting transfers between devices, body(): other = lax.ppermute(send, BOTH, CORES)  1.47 us
    pallas_call x1, Pallas kernels, clean(): pl.pallas_call(functools.partial(clean_kernel, scale), out_shape=pltpu.HB...  1.1 us
  transfers between devices with their start and end apart: 13, of which 9 were waited for; matrix products, arithmetic and copies ran while one was open for 0% of the time, Pallas kernels for 10%

profile of v12, /device:TPU:1, one launch (start us, length us, event | category | flops | bytes accessed | tf_op | source)
XLA Modules:
  0.0 49.5 jit_solution(10514529218426884627)
XLA Ops:
  0.0 1.4 %shard_map.47 = (f32[2,7,64,128]{3,2,1,0:T(8,128)S(1)}, f32[2,7,64,128]{3,2,1,0:T(8,128)S(1)}) custom-call(f32[2,2,2,64,8,128]{5,4,3,2,1,0:T(8,128)} %bitcast.15), custom_call_target="tpu_custom_call" | custom-call | flops 1000 | bytes 1000 | tf_op jit(solution)/shard_map/pallas_call | solution.py:289
  1.4 3.3 %collective-permute-start.1 = (f32[2,7,64,128]{3,2,1,0:T(8,128)S(1)}, f32[2,7,64,128]{3,2,1,0:T(8,128)S(1)}, u32[]{:S(2)}, u32[]{:S(2)}) collective-permute-start(f32[2,7,64,128]{3,2,1,0:T(8,128)S(1)} %get-tuple-element.25), channel_id=1, source_target_pairs={{0,1},{1,0},{2,3},{3,2},{4,5},{5,4},{6,7},{7,6},{8,9},{9,8},{10,11... | collective-permute-start | bytes 1376264 | tf_op jit(solution)/shard_map/ppermute | solution.py:338
  4.7 0.0 collective-permute-start
  4.7 4.2 %shard_map.46 = (f32[2,9,64,128]{3,2,1,0:T(8,128)S(1)}, f32[2,14,64,128]{3,2,1,0:T(8,128)S(1)}, f32[64,128]{1,0:T(8,128)S(1)}, f32[64,128]{1,0:T(8,128)S(1)}, f3...) custom-call(f32[2,2,2,512,128]{4,3,2,1,0:T(8,128)} %bitcast.16, ...), custom_call_target="tpu_custom_call" | custom-call | flops 2000000000 | bytes 6291456 | tf_op jit(solution)/shard_map/pallas_call | solution.py:289
  8.9 1.5 %collective-permute-start.2 = (f32[64,128]{1,0:T(8,128)S(1)}, f32[64,128]{1,0:T(8,128)S(1)}, u32[]{:S(2)}, u32[]{:S(2)}) collective-permute-start(f32[64,128]{1,0:T(8,128)S(1)} %get-tuple-element.28), channel_id=1, source_target_pairs={{0,1},{1,0},{2,3},{3,2},{4,5},{5,4},{6,7},{7,6},{8,9},{9,8},{10,11... | collective-permute-start | bytes 98312 | tf_op jit(solution)/shard_map/ppermute | solution.py:361
  10.4 0.0 collective-permute-done.1.near_ref
  10.4 0.9 %shard_map.48 = (f32[7,64,128]{2,1,0:T(8,128)S(1)}, f32[64,128]{1,0:T(8,128)S(1)}) custom-call(f32[2,14,64,128]{3,2,1,0:T(8,128)S(1)} %get-tuple-element.20.part_ref, f32[2,7,64,128]{3,2,1,0:T(8,128)S(1)} %collective-permute-done.1.near_ref, f32[512,128]{1,0:T(8,128)S(1)} %get-tuple-element.22.taps_ref, bf16[768,256]{1,0:T(8,128)(2,1)S(1)} %get-tuple-element.23.table_ref, ...), custom_call_target="tpu_custom_call" | custom-call | flops 1000000000 | bytes 3145728 | tf_op jit(solution)/shard_map/pallas_call | solution.py:289
  11.3 0.0 collective-permute-done.2.other_ref
  11.4 1.5 %collective-permute-done.cross_ref = f32[2,7,64,128]{3,2,1,0:T(8,128)S(1)} collective-permute-done((f32[2,7,64,128]{3,2,1,0:T(8,128)S(1)}, f32[2,7,64,128]{3,2,1,0:T(8,128)S(1)}, u32[]{:S(2)}, u32[]{:S(2)}) %collective-permute-start) | collective-permute-done | bytes 458784 | tf_op jit(solution)/shard_map/ppermute | solution.py:339
  12.9 0.9 %shard_map.49 = (f32[7,64,128]{2,1,0:T(8,128)S(1)}, f32[7,64,128]{2,1,0:T(8,128)S(1)}, f32[64,128]{1,0:T(8,128)S(1)}) custom-call(f32[2,14,64,128]{3,2,1,0:T(8,128)S(1)} %get-tuple-element.20.part_ref, f32[2,7,64,128]{3,2,1,0:T(8,128)S(1)} %collective-permute-done.cross_ref, f32[512,128]{1,0:T(8,128)S(1)} %get-tuple-element.22.taps_ref, ...), custom_call_target="tpu_custom_call" | custom-call | tf_op jit(solution)/shard_map/pallas_call | solution.py:289
  13.9 2.0 %collective-permute-start.4 = (f32[64,128]{1,0:T(8,128)S(1)}, f32[64,128]{1,0:T(8,128)S(1)}, u32[]{:S(2)}, u32[]{:S(2)}) collective-permute-start(f32[64,128]{1,0:T(8,128)S(1)} %get-tuple-element.32), channel_id=1, source_target_pairs={{0,6},{1,7},{2,4},{3,5},{4,2},{5,3},{6,0},{7,1},{8,14},{9,15},{10,... | collective-permute-start | bytes 98312 | tf_op jit(solution)/shard_map/ppermute | solution.py:322
  15.9 0.0 collective-permute-start.3
  15.9 2.1 %collective-permute-done.4 = f32[64,128]{1,0:T(8,128)S(1)} collective-permute-done((f32[64,128]{1,0:T(8,128)S(1)}, f32[64,128]{1,0:T(8,128)S(1)}, u32[]{:S(2)}, u32[]{:S(2)}) %collective-permute-start.4) | collective-permute-done | bytes 32800 | tf_op jit(solution)/shard_map/ppermute | solution.py:322
  17.9 1.6 %collective-permute-start.5 = (f32[64,128]{1,0:T(8,128)S(1)}, f32[64,128]{1,0:T(8,128)S(1)}, u32[]{:S(2)}, u32[]{:S(2)}) collective-permute-start(f32[64,128]{1,0:T(8,128)S(1)} %add.24), channel_id=1, source_target_pairs={{0,9},{1,8},{2,11},{3,10},{4,13},{5,12},{6,15},{7,14},{8,1},{9,0},... | collective-permute-start | bytes 98312 | tf_op jit(solution)/shard_map/ppermute | solution.py:322
  19.5 1.8 %collective-permute-done.5 = f32[64,128]{1,0:T(8,128)S(1)} collective-permute-done((f32[64,128]{1,0:T(8,128)S(1)}, f32[64,128]{1,0:T(8,128)S(1)}, u32[]{:S(2)}, u32[]{:S(2)}) %collective-permute-start.5) | collective-permute-done | bytes 32800 | tf_op jit(solution)/shard_map/ppermute | solution.py:322
  21.3 2.9 %collective-permute-start.6 = (f32[64,128]{1,0:T(8,128)S(1)}, f32[64,128]{1,0:T(8,128)S(1)}, u32[]{:S(2)}, u32[]{:S(2)}) collective-permute-start(f32[64,128]{1,0:T(8,128)S(1)} %add.25), channel_id=1, source_target_pairs={{0,25},{1,24},{2,27},{3,26},{4,29},{5,28},{6,31},{7,30},{8,17},{9,... | collective-permute-start | bytes 98312 | tf_op jit(solution)/shard_map/ppermute | solution.py:322
  24.1 1.7 %collective-permute-done.6 = f32[64,128]{1,0:T(8,128)S(1)} collective-permute-done((f32[64,128]{1,0:T(8,128)S(1)}, f32[64,128]{1,0:T(8,128)S(1)}, u32[]{:S(2)}, u32[]{:S(2)}) %collective-permute-start.6) | collective-permute-done | bytes 32800 | tf_op jit(solution)/shard_map/ppermute | solution.py:322
  25.8 0.0 collective-permute-start.7
  25.8 2.8 %collective-permute-done.7 = f32[64,128]{1,0:T(8,128)S(1)} collective-permute-done((f32[64,128]{1,0:T(8,128)S(1)}, f32[64,128]{1,0:T(8,128)S(1)}, u32[]{:S(2)}, u32[]{:S(2)}) %collective-permute-start.7) | collective-permute-done | bytes 32800 | tf_op jit(solution)/shard_map/ppermute | solution.py:322
  28.6 3.5 %collective-permute-start.8 = (f32[64,128]{1,0:T(8,128)S(1)}, f32[64,128]{1,0:T(8,128)S(1)}, u32[]{:S(2)}, u32[]{:S(2)}) collective-permute-start(f32[64,128]{1,0:T(8,128)S(1)} %add.27), channel_id=1, source_target_pairs={{0,33},{1,32},{2,35},{3,34},{4,37},{5,36},{6,39},{7,38},{8,41},{9,... | collective-permute-start | bytes 98312 | tf_op jit(solution)/shard_map/ppermute | solution.py:322
  32.1 1.6 %collective-permute-done.8 = f32[64,128]{1,0:T(8,128)S(1)} collective-permute-done((f32[64,128]{1,0:T(8,128)S(1)}, f32[64,128]{1,0:T(8,128)S(1)}, u32[]{:S(2)}, u32[]{:S(2)}) %collective-permute-start.8) | collective-permute-done | bytes 32800 | tf_op jit(solution)/shard_map/ppermute | solution.py:322
  33.7 3.1 %collective-permute-start.9 = (f32[64,128]{1,0:T(8,128)S(1)}, f32[64,128]{1,0:T(8,128)S(1)}, u32[]{:S(2)}, u32[]{:S(2)}) collective-permute-start(f32[64,128]{1,0:T(8,128)S(1)} %add.28), channel_id=1, source_target_pairs={{0,65},{1,64},{2,67},{3,66},{4,69},{5,68},{6,71},{7,70},{8,73},{9,... | collective-permute-start | bytes 98312 | tf_op jit(solution)/shard_map/ppermute | solution.py:322
  36.8 1.6 %collective-permute-done.9 = f32[64,128]{1,0:T(8,128)S(1)} collective-permute-done((f32[64,128]{1,0:T(8,128)S(1)}, f32[64,128]{1,0:T(8,128)S(1)}, u32[]{:S(2)}, u32[]{:S(2)}) %collective-permute-start.9) | collective-permute-done | bytes 32800 | tf_op jit(solution)/shard_map/ppermute | solution.py:322
  38.4 5.9 %collective-permute-start.10 = (f32[64,128]{1,0:T(8,128)S(1)}, f32[64,128]{1,0:T(8,128)S(1)}, u32[]{:S(2)}, u32[]{:S(2)}) collective-permute-start(f32[64,128]{1,0:T(8,128)S(1)} %add.29), channel_id=1, source_target_pairs={{0,225},{1,224},{2,227},{3,226},{4,229},{5,228},{6,231},{7,230},{8... | collective-permute-start | bytes 98312 | tf_op jit(solution)/shard_map/ppermute | solution.py:322
  44.4 0.0 collective-permute-start.12
  44.4 0.5 collective-permute-start.11
  44.8 1.2 %collective-permute-done.10 = f32[64,128]{1,0:T(8,128)S(1)} collective-permute-done((f32[64,128]{1,0:T(8,128)S(1)}, f32[64,128]{1,0:T(8,128)S(1)}, u32[]{:S(2)}, u32[]{:S(2)}) %collective-permute-start.10) | collective-permute-done | bytes 32800 | tf_op jit(solution)/shard_map/ppermute | solution.py:322
  46.1 2.3 %collective-permute-done.12 = f32[64,128]{1,0:T(8,128)S(1)} collective-permute-done((f32[64,128]{1,0:T(8,128)S(1)}, f32[64,128]{1,0:T(8,128)S(1)}, u32[]{:S(2)}, u32[]{:S(2)}) %collective-permute-start.12) | collective-permute-done | bytes 32800 | tf_op jit(solution)/shard_map/ppermute | solution.py:320
  48.3 0.0 collective-permute-done.11
  48.3 0.0 collective-permute-done.3.back_ref
  48.4 1.1 %shard_map.50 = f32[2,2,512,128]{3,2,1,0:T(8,128)} custom-call(f32[2,9,64,128]{3,2,1,0:T(8,128)S(1)} %get-tuple-element.19.held_ref, f32[7,64,128]{2,1,0:T(8,128)S(1)} %get-tuple-element.30.ahead_ref, f32[7,64,128]{2,1,0:T(8,128)S(1)} %collective-permute-done.3.back_ref, f32[64,128]{1,0:T(8,128)S(1)} %add.30.mine_ref, f32[64,128]{1,0:T(8,128)S(1)} %add.31.other_ref), custom_call_target="tpu_custom_call" | custom-call | flops 1000000 | bytes 4194304 | tf_op jit(solution)/shard_map/pallas_call | solution.py:274
  (8 shorter events, 0.0 us)
Async XLA Ops:
  1.4 9.0 %collective-permute-start.1 = (f32[2,7,64,128]{3,2,1,0:T(8,128)S(1)}, f32[2,7,64,128]{3,2,1,0:T(8,128)S(1)}, u32[]{:S(2)}, u32[]{:S(2)}) collective-permute-start(f32[2,7,64,128]{3,2,1,0:T(8,128)S(1)} %get-tuple-element.25), channel_id=1, source_target_pairs={{0,1},{1,0},{2,3},{3,2},{4,5},{5,4},{6,7},{7,6},{8,9},{9,8},{10,11... | collective-permute-start | bytes 1376264 | tf_op jit(solution)/shard_map/ppermute | solution.py:338
  4.7 8.2 %collective-permute-start = (f32[2,7,64,128]{3,2,1,0:T(8,128)S(1)}, f32[2,7,64,128]{3,2,1,0:T(8,128)S(1)}, u32[]{:S(2)}, u32[]{:S(2)}) collective-permute-start(f32[2,7,64,128]{3,2,1,0:T(8,128)S(1)} %get-tuple-element.21), channel_id=1, source_target_pairs={{0,7},{1,2},{2,1},{3,4},{4,3},{5,6},{6,5},{7,0},{8,15},{9,10},{10,... | collective-permute-start | bytes 1376264 | tf_op jit(solution)/shard_map/ppermute | solution.py:339
  8.9 2.4 %collective-permute-start.2 = (f32[64,128]{1,0:T(8,128)S(1)}, f32[64,128]{1,0:T(8,128)S(1)}, u32[]{:S(2)}, u32[]{:S(2)}) collective-permute-start(f32[64,128]{1,0:T(8,128)S(1)} %get-tuple-element.28), channel_id=1, source_target_pairs={{0,1},{1,0},{2,3},{3,2},{4,5},{5,4},{6,7},{7,6},{8,9},{9,8},{10,11... | collective-permute-start | bytes 98312 | tf_op jit(solution)/shard_map/ppermute | solution.py:361
  13.9 4.1 %collective-permute-start.4 = (f32[64,128]{1,0:T(8,128)S(1)}, f32[64,128]{1,0:T(8,128)S(1)}, u32[]{:S(2)}, u32[]{:S(2)}) collective-permute-start(f32[64,128]{1,0:T(8,128)S(1)} %get-tuple-element.32), channel_id=1, source_target_pairs={{0,6},{1,7},{2,4},{3,5},{4,2},{5,3},{6,0},{7,1},{8,14},{9,15},{10,... | collective-permute-start | bytes 98312 | tf_op jit(solution)/shard_map/ppermute | solution.py:322
  15.9 32.5 %collective-permute-start.3 = (f32[7,64,128]{2,1,0:T(8,128)S(1)}, f32[7,64,128]{2,1,0:T(8,128)S(1)}, u32[]{:S(2)}, u32[]{:S(2)}) collective-permute-start(f32[7,64,128]{2,1,0:T(8,128)S(1)} %get-tuple-element.31), channel_id=1, source_target_pairs={{0,7},{1,0},{2,1},{3,2},{4,3},{5,4},{6,5},{7,6},{8,15},{9,8},{10,9... | collective-permute-start | bytes 688136 | tf_op jit(solution)/shard_map/ppermute | solution.py:318
  17.9 3.3 %collective-permute-start.5 = (f32[64,128]{1,0:T(8,128)S(1)}, f32[64,128]{1,0:T(8,128)S(1)}, u32[]{:S(2)}, u32[]{:S(2)}) collective-permute-start(f32[64,128]{1,0:T(8,128)S(1)} %add.24), channel_id=1, source_target_pairs={{0,9},{1,8},{2,11},{3,10},{4,13},{5,12},{6,15},{7,14},{8,1},{9,0},... | collective-permute-start | bytes 98312 | tf_op jit(solution)/shard_map/ppermute | solution.py:322
  21.3 4.6 %collective-permute-start.6 = (f32[64,128]{1,0:T(8,128)S(1)}, f32[64,128]{1,0:T(8,128)S(1)}, u32[]{:S(2)}, u32[]{:S(2)}) collective-permute-start(f32[64,128]{1,0:T(8,128)S(1)} %add.25), channel_id=1, source_target_pairs={{0,25},{1,24},{2,27},{3,26},{4,29},{5,28},{6,31},{7,30},{8,17},{9,... | collective-permute-start | bytes 98312 | tf_op jit(solution)/shard_map/ppermute | solution.py:322
  25.8 2.8 %collective-permute-start.7 = (f32[64,128]{1,0:T(8,128)S(1)}, f32[64,128]{1,0:T(8,128)S(1)}, u32[]{:S(2)}, u32[]{:S(2)}) collective-permute-start(f32[64,128]{1,0:T(8,128)S(1)} %add.26), channel_id=1, source_target_pairs={{0,2},{1,3},{2,0},{3,1},{4,6},{5,7},{6,4},{7,5},{8,10},{9,11},{10,... | collective-permute-start | bytes 98312 | tf_op jit(solution)/shard_map/ppermute | solution.py:322
  28.6 5.1 %collective-permute-start.8 = (f32[64,128]{1,0:T(8,128)S(1)}, f32[64,128]{1,0:T(8,128)S(1)}, u32[]{:S(2)}, u32[]{:S(2)}) collective-permute-start(f32[64,128]{1,0:T(8,128)S(1)} %add.27), channel_id=1, source_target_pairs={{0,33},{1,32},{2,35},{3,34},{4,37},{5,36},{6,39},{7,38},{8,41},{9,... | collective-permute-start | bytes 98312 | tf_op jit(solution)/shard_map/ppermute | solution.py:322
  33.7 4.7 %collective-permute-start.9 = (f32[64,128]{1,0:T(8,128)S(1)}, f32[64,128]{1,0:T(8,128)S(1)}, u32[]{:S(2)}, u32[]{:S(2)}) collective-permute-start(f32[64,128]{1,0:T(8,128)S(1)} %add.28), channel_id=1, source_target_pairs={{0,65},{1,64},{2,67},{3,66},{4,69},{5,68},{6,71},{7,70},{8,73},{9,... | collective-permute-start | bytes 98312 | tf_op jit(solution)/shard_map/ppermute | solution.py:322
  38.4 7.6 %collective-permute-start.10 = (f32[64,128]{1,0:T(8,128)S(1)}, f32[64,128]{1,0:T(8,128)S(1)}, u32[]{:S(2)}, u32[]{:S(2)}) collective-permute-start(f32[64,128]{1,0:T(8,128)S(1)} %add.29), channel_id=1, source_target_pairs={{0,225},{1,224},{2,227},{3,226},{4,229},{5,228},{6,231},{7,230},{8... | collective-permute-start | bytes 98312 | tf_op jit(solution)/shard_map/ppermute | solution.py:322
  44.4 4.0 %collective-permute-start.12 = (f32[64,128]{1,0:T(8,128)S(1)}, f32[64,128]{1,0:T(8,128)S(1)}, u32[]{:S(2)}, u32[]{:S(2)}) collective-permute-start(f32[64,128]{1,0:T(8,128)S(1)} %add.29), channel_id=1, source_target_pairs={{0,224},{1,225},{2,226},{3,227},{4,228},{5,229},{6,230},{7,231},{8... | collective-permute-start | bytes 98312 | tf_op jit(solution)/shard_map/ppermute | solution.py:320
  44.4 4.0 %collective-permute-start.11 = (f32[64,128]{1,0:T(8,128)S(1)}, f32[64,128]{1,0:T(8,128)S(1)}, u32[]{:S(2)}, u32[]{:S(2)}) collective-permute-start(f32[64,128]{1,0:T(8,128)S(1)} %add.29), channel_id=1, source_target_pairs={{0,1},{1,0},{2,3},{3,2},{4,5},{5,4},{6,7},{7,6},{8,9},{9,8},{10,11... | collective-permute-start | bytes 98312 | tf_op jit(solution)/shard_map/ppermute | solution.py:321

commit v13 on v10

--- a/solution.py
+++ b/solution.py
@@ -17,6 +17,7 @@
 FRAMES = 16
 HELD = 9
 RIM = FRAMES - HELD
+PIECES = 4
 SHORT = pl.CostEstimate(flops=1000, bytes_accessed=1000, transcendentals=0)
 BOTH = ("beam", "tm")
 X, Y, Z = 4, 4, 8
@@ -258,13 +259,16 @@
 def clean_kernel(scale, held_ref, rim_ref, sum_ref, *refs):
     out_ref, tile_ref, sems = refs[-3:]
     p = kept_half() if len(refs) == 3 else 1 - kept_half()
-    base = sum_ref[...] * scale
     copies = []
-    for half in range(2):
+    for n in range(2 * PIECES):
+        half, at = n % 2, n // 2 * (ROWS // PIECES)
+        rows = pl.ds(at, ROWS // PIECES)
+        base = sum_ref[rows, :] * scale
         for f in range(8 * half, 8 * half + 8):
-            power = held_ref[p, f] if f < HELD else rim_ref[f - HELD]
-            tile_ref[half, pl.ds(f % 8, ROWS, stride=8), :] = power - base
-        copies.append(pltpu.make_async_copy(tile_ref.at[half], out_ref.at[p, half], sems.at[half]))
+            power = held_ref[p, f, rows, :] if f < HELD else rim_ref[f - HELD, rows, :]
+            tile_ref[half, pl.ds(8 * at + f % 8, ROWS // PIECES, stride=8), :] = power - base
+        piece = pl.ds(8 * at, 8 * ROWS // PIECES)
+        copies.append(pltpu.make_async_copy(tile_ref.at[half, piece, :], out_ref.at[p, half, piece, :], sems.at[n]))
         copies[-1].start()
     for copy in copies:
         copy.wait()
@@ -277,7 +281,7 @@
         out_shape=pltpu.HBM((2, 2, 8 * ROWS, LANES), jnp.float32),
         in_specs=[pl.BlockSpec(memory_space=pltpu.VMEM)] * 3 + far * (len(args) - 3),
         out_specs=far[0],
-        scratch_shapes=[pltpu.VMEM((2, 8 * ROWS, LANES), jnp.float32), pltpu.SemaphoreType.DMA((2,))],
+        scratch_shapes=[pltpu.VMEM((2, 8 * ROWS, LANES), jnp.float32), pltpu.SemaphoreType.DMA((2 * PIECES,))],
         input_output_aliases={3: 0} if len(args) == 4 else {},
         compiler_params=pltpu.CompilerParams(vmem_limit_bytes=16 << 20),
         cost_estimate=pl.CostEstimate(flops=10**6, bytes_accessed=2 << 20, transcendentals=0),

time: 48.4 us -> 48.4 us (level)
  no operation moved by 1% of the time
where the time goes in v13:
time: 48.4 us; the launch traced here: 48.2 us
  starting transfers between devices  24.4 us (50%)
  waiting for transfers between devices  14.4 us (30%)
  Pallas kernels  9.23 us (19%)
    ppermute x7, starting transfers between devices, total_over_all(): sums = sums + lax.ppermute(sums, BOTH, swap_pairs(axis, partner))  19 us
    ppermute x7, waiting for transfers between devices, total_over_all(): sums = sums + lax.ppermute(sums, BOTH, swap_pairs(axis, partner))  12.6 us
    pallas_call x4, Pallas kernels, on_core(): pl.pallas_call(kernel, out_shape=shapes, in_specs=[pl.BlockSpec(memory_sp...  7.45 us
    ppermute x1, starting transfers between devices, body(): near = lax.ppermute(near, 'tm', [(i, i ^ 1) for i in range(devices)])  3.33 us
    pallas_call x2, Pallas kernels, clean(): pl.pallas_call(functools.partial(clean_kernel, scale), out_shape=pltpu.HB...  1.78 us
    ppermute x1, waiting for transfers between devices, body(): lax.ppermute(cross, 'tm', [(i, (i + 1 if i % 2 else i - 1) % devices) for...  1.55 us
    ppermute x1, starting transfers between devices, body(): other = lax.ppermute(send, BOTH, CORES)  1.47 us
  transfers between devices with their start and end apart: 12, of which 9 were waited for; matrix products, arithmetic and copies ran while one was open for 0% of the time, Pallas kernels for 13%

profile of v13, /device:TPU:1, one launch (start us, length us, event | category | flops | bytes accessed | tf_op | source)
XLA Modules:
  0.0 48.2 jit_solution(8040928517798698885)
XLA Ops:
  0.0 1.4 %shard_map.47 = (f32[2,7,64,128]{3,2,1,0:T(8,128)S(1)}, f32[2,7,64,128]{3,2,1,0:T(8,128)S(1)}) custom-call(f32[2,2,2,64,8,128]{5,4,3,2,1,0:T(8,128)} %bitcast.15), custom_call_target="tpu_custom_call" | custom-call | flops 1000 | bytes 1000 | tf_op jit(solution)/shard_map/pallas_call | solution.py:295
  1.4 3.3 %collective-permute-start.1 = (f32[2,7,64,128]{3,2,1,0:T(8,128)S(1)}, f32[2,7,64,128]{3,2,1,0:T(8,128)S(1)}, u32[]{:S(2)}, u32[]{:S(2)}) collective-permute-start(f32[2,7,64,128]{3,2,1,0:T(8,128)S(1)} %get-tuple-element.27), channel_id=1, source_target_pairs={{0,1},{1,0},{2,3},{3,2},{4,5},{5,4},{6,7},{7,6},{8,9},{9,8},{10,11... | collective-permute-start | bytes 1376264 | tf_op jit(solution)/shard_map/ppermute | solution.py:342
  4.7 0.0 collective-permute-start
  4.7 4.2 %shard_map.46 = (f32[2,9,64,128]{3,2,1,0:T(8,128)S(1)}, f32[2,14,64,128]{3,2,1,0:T(8,128)S(1)}, f32[64,128]{1,0:T(8,128)S(1)}, f32[64,128]{1,0:T(8,128)S(1)}, f3...) custom-call(f32[2,2,2,512,128]{4,3,2,1,0:T(8,128)} %bitcast.16, ...), custom_call_target="tpu_custom_call" | custom-call | flops 2000000000 | bytes 6291456 | tf_op jit(solution)/shard_map/pallas_call | solution.py:295
  8.9 1.5 %collective-permute-start.2 = (f32[64,128]{1,0:T(8,128)S(1)}, f32[64,128]{1,0:T(8,128)S(1)}, u32[]{:S(2)}, u32[]{:S(2)}) collective-permute-start(f32[64,128]{1,0:T(8,128)S(1)} %get-tuple-element.30), channel_id=1, source_target_pairs={{0,1},{1,0},{2,3},{3,2},{4,5},{5,4},{6,7},{7,6},{8,9},{9,8},{10,11... | collective-permute-start | bytes 98312 | tf_op jit(solution)/shard_map/ppermute | solution.py:365
  10.4 0.0 collective-permute-done.1.near_ref
  10.4 0.9 %shard_map.48 = (f32[7,64,128]{2,1,0:T(8,128)S(1)}, f32[64,128]{1,0:T(8,128)S(1)}) custom-call(f32[2,14,64,128]{3,2,1,0:T(8,128)S(1)} %get-tuple-element.22.part_ref, f32[2,7,64,128]{3,2,1,0:T(8,128)S(1)} %collective-permute-done.1.near_ref, f32[512,128]{1,0:T(8,128)S(1)} %get-tuple-element.24.taps_ref, bf16[768,256]{1,0:T(8,128)(2,1)S(1)} %get-tuple-element.25.table_ref, ...), custom_call_target="tpu_custom_call" | custom-call | flops 1000000000 | bytes 3145728 | tf_op jit(solution)/shard_map/pallas_call | solution.py:295
  11.3 0.0 collective-permute-done.2.other_ref
  11.4 1.5 %collective-permute-done.cross_ref = f32[2,7,64,128]{3,2,1,0:T(8,128)S(1)} collective-permute-done((f32[2,7,64,128]{3,2,1,0:T(8,128)S(1)}, f32[2,7,64,128]{3,2,1,0:T(8,128)S(1)}, u32[]{:S(2)}, u32[]{:S(2)}) %collective-permute-start) | collective-permute-done | bytes 458784 | tf_op jit(solution)/shard_map/ppermute | solution.py:343
  12.9 0.9 %shard_map.49 = (f32[7,64,128]{2,1,0:T(8,128)S(1)}, f32[7,64,128]{2,1,0:T(8,128)S(1)}, f32[64,128]{1,0:T(8,128)S(1)}) custom-call(f32[2,14,64,128]{3,2,1,0:T(8,128)S(1)} %get-tuple-element.22.part_ref, f32[2,7,64,128]{3,2,1,0:T(8,128)S(1)} %collective-permute-done.cross_ref, f32[512,128]{1,0:T(8,128)S(1)} %get-tuple-element.24.taps_ref, ...), custom_call_target="tpu_custom_call" | custom-call | tf_op jit(solution)/shard_map/pallas_call | solution.py:295
  13.9 2.0 %collective-permute-start.3 = (f32[64,128]{1,0:T(8,128)S(1)}, f32[64,128]{1,0:T(8,128)S(1)}, u32[]{:S(2)}, u32[]{:S(2)}) collective-permute-start(f32[64,128]{1,0:T(8,128)S(1)} %get-tuple-element.32), channel_id=1, source_target_pairs={{0,6},{1,7},{2,4},{3,5},{4,2},{5,3},{6,0},{7,1},{8,14},{9,15},{10,... | collective-permute-start | bytes 98312 | tf_op jit(solution)/shard_map/ppermute | solution.py:326
  15.9 2.1 %collective-permute-done.3 = f32[64,128]{1,0:T(8,128)S(1)} collective-permute-done((f32[64,128]{1,0:T(8,128)S(1)}, f32[64,128]{1,0:T(8,128)S(1)}, u32[]{:S(2)}, u32[]{:S(2)}) %collective-permute-start.3) | collective-permute-done | bytes 32800 | tf_op jit(solution)/shard_map/ppermute | solution.py:326
  17.9 1.6 %collective-permute-start.5 = (f32[64,128]{1,0:T(8,128)S(1)}, f32[64,128]{1,0:T(8,128)S(1)}, u32[]{:S(2)}, u32[]{:S(2)}) collective-permute-start(f32[64,128]{1,0:T(8,128)S(1)} %add.21), channel_id=1, source_target_pairs={{0,9},{1,8},{2,11},{3,10},{4,13},{5,12},{6,15},{7,14},{8,1},{9,0},... | collective-permute-start | bytes 98312 | tf_op jit(solution)/shard_map/ppermute | solution.py:326
  19.5 0.6 %collective-permute-start.4 = (f32[7,64,128]{2,1,0:T(8,128)S(1)}, f32[7,64,128]{2,1,0:T(8,128)S(1)}, u32[]{:S(2)}, u32[]{:S(2)}) collective-permute-start(f32[7,64,128]{2,1,0:T(8,128)S(1)} %get-tuple-element.34), channel_id=1, source_target_pairs={{0,7},{1,0},{2,1},{3,2},{4,3},{5,4},{6,5},{7,6},{8,15},{9,8},{10,9... | collective-permute-start | bytes 688136 | tf_op jit(solution)/shard_map/ppermute | solution.py:325
  20.1 1.2 %collective-permute-done.5 = f32[64,128]{1,0:T(8,128)S(1)} collective-permute-done((f32[64,128]{1,0:T(8,128)S(1)}, f32[64,128]{1,0:T(8,128)S(1)}, u32[]{:S(2)}, u32[]{:S(2)}) %collective-permute-start.5) | collective-permute-done | bytes 32800 | tf_op jit(solution)/shard_map/ppermute | solution.py:326
  21.3 2.9 %collective-permute-start.6 = (f32[64,128]{1,0:T(8,128)S(1)}, f32[64,128]{1,0:T(8,128)S(1)}, u32[]{:S(2)}, u32[]{:S(2)}) collective-permute-start(f32[64,128]{1,0:T(8,128)S(1)} %add.22), channel_id=1, source_target_pairs={{0,25},{1,24},{2,27},{3,26},{4,29},{5,28},{6,31},{7,30},{8,17},{9,... | collective-permute-start | bytes 98312 | tf_op jit(solution)/shard_map/ppermute | solution.py:326
  24.1 1.7 %collective-permute-done.6 = f32[64,128]{1,0:T(8,128)S(1)} collective-permute-done((f32[64,128]{1,0:T(8,128)S(1)}, f32[64,128]{1,0:T(8,128)S(1)}, u32[]{:S(2)}, u32[]{:S(2)}) %collective-permute-start.6) | collective-permute-done | bytes 32800 | tf_op jit(solution)/shard_map/ppermute | solution.py:326
  25.8 0.0 collective-permute-start.7
  25.8 2.8 %collective-permute-done.7 = f32[64,128]{1,0:T(8,128)S(1)} collective-permute-done((f32[64,128]{1,0:T(8,128)S(1)}, f32[64,128]{1,0:T(8,128)S(1)}, u32[]{:S(2)}, u32[]{:S(2)}) %collective-permute-start.7) | collective-permute-done | bytes 32800 | tf_op jit(solution)/shard_map/ppermute | solution.py:326
  28.6 3.5 %collective-permute-start.8 = (f32[64,128]{1,0:T(8,128)S(1)}, f32[64,128]{1,0:T(8,128)S(1)}, u32[]{:S(2)}, u32[]{:S(2)}) collective-permute-start(f32[64,128]{1,0:T(8,128)S(1)} %add.24), channel_id=1, source_target_pairs={{0,33},{1,32},{2,35},{3,34},{4,37},{5,36},{6,39},{7,38},{8,41},{9,... | collective-permute-start | bytes 98312 | tf_op jit(solution)/shard_map/ppermute | solution.py:326
  32.1 1.6 %collective-permute-done.8 = f32[64,128]{1,0:T(8,128)S(1)} collective-permute-done((f32[64,128]{1,0:T(8,128)S(1)}, f32[64,128]{1,0:T(8,128)S(1)}, u32[]{:S(2)}, u32[]{:S(2)}) %collective-permute-start.8) | collective-permute-done | bytes 32800 | tf_op jit(solution)/shard_map/ppermute | solution.py:326
  33.7 3.1 %collective-permute-start.9 = (f32[64,128]{1,0:T(8,128)S(1)}, f32[64,128]{1,0:T(8,128)S(1)}, u32[]{:S(2)}, u32[]{:S(2)}) collective-permute-start(f32[64,128]{1,0:T(8,128)S(1)} %add.25), channel_id=1, source_target_pairs={{0,65},{1,64},{2,67},{3,66},{4,69},{5,68},{6,71},{7,70},{8,73},{9,... | collective-permute-start | bytes 98312 | tf_op jit(solution)/shard_map/ppermute | solution.py:326
  36.8 1.6 %collective-permute-done.9 = f32[64,128]{1,0:T(8,128)S(1)} collective-permute-done((f32[64,128]{1,0:T(8,128)S(1)}, f32[64,128]{1,0:T(8,128)S(1)}, u32[]{:S(2)}, u32[]{:S(2)}) %collective-permute-start.9) | collective-permute-done | bytes 32800 | tf_op jit(solution)/shard_map/ppermute | solution.py:326
  38.4 5.9 %collective-permute-start.10 = (f32[64,128]{1,0:T(8,128)S(1)}, f32[64,128]{1,0:T(8,128)S(1)}, u32[]{:S(2)}, u32[]{:S(2)}) collective-permute-start(f32[64,128]{1,0:T(8,128)S(1)} %add.26), channel_id=1, source_target_pairs={{0,225},{1,224},{2,227},{3,226},{4,229},{5,228},{6,231},{7,230},{8... | collective-permute-start | bytes 98312 | tf_op jit(solution)/shard_map/ppermute | solution.py:326
  44.4 1.7 %collective-permute-done.10 = f32[64,128]{1,0:T(8,128)S(1)} collective-permute-done((f32[64,128]{1,0:T(8,128)S(1)}, f32[64,128]{1,0:T(8,128)S(1)}, u32[]{:S(2)}, u32[]{:S(2)}) %collective-permute-start.10) | collective-permute-done | bytes 32800 | tf_op jit(solution)/shard_map/ppermute | solution.py:326
  46.1 0.0 collective-permute-start.11
  46.1 0.9 %shard_map.50.refs_0_ = f32[2,2,512,128]{3,2,1,0:T(8,128)} custom-call(f32[2,9,64,128]{3,2,1,0:T(8,128)S(1)} %get-tuple-element.21.held_ref, f32[7,64,128]{2,1,0:T(8,128)S(1)} %get-tuple-element.36.rim_ref, f32[64,128]{1,0:T(8,128)S(1)} %add.27.sum_ref), custom_call_target="tpu_custom_call" | custom-call | flops 1000000 | bytes 2097152 | tf_op jit(solution)/shard_map/pallas_call | solution.py:279
  47.0 0.0 collective-permute-done.4.rim_ref
  47.0 0.3 collective-permute-done.11.sum_ref
  47.3 0.9 %shard_map.51 = f32[2,2,512,128]{3,2,1,0:T(8,128)} custom-call(f32[2,9,64,128]{3,2,1,0:T(8,128)S(1)} %get-tuple-element.21.held_ref, f32[7,64,128]{2,1,0:T(8,128)S(1)} %collective-permute-done.4.rim_ref, f32[64,128]{1,0:T(8,128)S(1)} %collective-permute-done.11.sum_ref, f32[2,2,512,128]{3,2,1,0:T(8,128)} %shard_map.50.refs_0_), custom_call_target="tpu_custom_call", output_to_operand_aliasing={{}: (3, {})} | custom-call | flops 1000000 | bytes 2097152 | tf_op jit(solution)/shard_map/pallas_call | solution.py:279
  (7 shorter events, 0.0 us)
Async XLA Ops:
  1.4 9.0 %collective-permute-start.1 = (f32[2,7,64,128]{3,2,1,0:T(8,128)S(1)}, f32[2,7,64,128]{3,2,1,0:T(8,128)S(1)}, u32[]{:S(2)}, u32[]{:S(2)}) collective-permute-start(f32[2,7,64,128]{3,2,1,0:T(8,128)S(1)} %get-tuple-element.27), channel_id=1, source_target_pairs={{0,1},{1,0},{2,3},{3,2},{4,5},{5,4},{6,7},{7,6},{8,9},{9,8},{10,11... | collective-permute-start | bytes 1376264 | tf_op jit(solution)/shard_map/ppermute | solution.py:342
  4.7 8.2 %collective-permute-start = (f32[2,7,64,128]{3,2,1,0:T(8,128)S(1)}, f32[2,7,64,128]{3,2,1,0:T(8,128)S(1)}, u32[]{:S(2)}, u32[]{:S(2)}) collective-permute-start(f32[2,7,64,128]{3,2,1,0:T(8,128)S(1)} %get-tuple-element.23), channel_id=1, source_target_pairs={{0,7},{1,2},{2,1},{3,4},{4,3},{5,6},{6,5},{7,0},{8,15},{9,10},{10,... | collective-permute-start | bytes 1376264 | tf_op jit(solution)/shard_map/ppermute | solution.py:343
  8.9 2.4 %collective-permute-start.2 = (f32[64,128]{1,0:T(8,128)S(1)}, f32[64,128]{1,0:T(8,128)S(1)}, u32[]{:S(2)}, u32[]{:S(2)}) collective-permute-start(f32[64,128]{1,0:T(8,128)S(1)} %get-tuple-element.30), channel_id=1, source_target_pairs={{0,1},{1,0},{2,3},{3,2},{4,5},{5,4},{6,7},{7,6},{8,9},{9,8},{10,11... | collective-permute-start | bytes 98312 | tf_op jit(solution)/shard_map/ppermute | solution.py:365
  13.9 4.1 %collective-permute-start.3 = (f32[64,128]{1,0:T(8,128)S(1)}, f32[64,128]{1,0:T(8,128)S(1)}, u32[]{:S(2)}, u32[]{:S(2)}) collective-permute-start(f32[64,128]{1,0:T(8,128)S(1)} %get-tuple-element.32), channel_id=1, source_target_pairs={{0,6},{1,7},{2,4},{3,5},{4,2},{5,3},{6,0},{7,1},{8,14},{9,15},{10,... | collective-permute-start | bytes 98312 | tf_op jit(solution)/shard_map/ppermute | solution.py:326
  17.9 3.3 %collective-permute-start.5 = (f32[64,128]{1,0:T(8,128)S(1)}, f32[64,128]{1,0:T(8,128)S(1)}, u32[]{:S(2)}, u32[]{:S(2)}) collective-permute-start(f32[64,128]{1,0:T(8,128)S(1)} %add.21), channel_id=1, source_target_pairs={{0,9},{1,8},{2,11},{3,10},{4,13},{5,12},{6,15},{7,14},{8,1},{9,0},... | collective-permute-start | bytes 98312 | tf_op jit(solution)/shard_map/ppermute | solution.py:326
  19.5 27.5 %collective-permute-start.4 = (f32[7,64,128]{2,1,0:T(8,128)S(1)}, f32[7,64,128]{2,1,0:T(8,128)S(1)}, u32[]{:S(2)}, u32[]{:S(2)}) collective-permute-start(f32[7,64,128]{2,1,0:T(8,128)S(1)} %get-tuple-element.34), channel_id=1, source_target_pairs={{0,7},{1,0},{2,1},{3,2},{4,3},{5,4},{6,5},{7,6},{8,15},{9,8},{10,9... | collective-permute-start | bytes 688136 | tf_op jit(solution)/shard_map/ppermute | solution.py:325
  21.3 4.6 %collective-permute-start.6 = (f32[64,128]{1,0:T(8,128)S(1)}, f32[64,128]{1,0:T(8,128)S(1)}, u32[]{:S(2)}, u32[]{:S(2)}) collective-permute-start(f32[64,128]{1,0:T(8,128)S(1)} %add.22), channel_id=1, source_target_pairs={{0,25},{1,24},{2,27},{3,26},{4,29},{5,28},{6,31},{7,30},{8,17},{9,... | collective-permute-start | bytes 98312 | tf_op jit(solution)/shard_map/ppermute | solution.py:326
  25.8 2.8 %collective-permute-start.7 = (f32[64,128]{1,0:T(8,128)S(1)}, f32[64,128]{1,0:T(8,128)S(1)}, u32[]{:S(2)}, u32[]{:S(2)}) collective-permute-start(f32[64,128]{1,0:T(8,128)S(1)} %add.23), channel_id=1, source_target_pairs={{0,2},{1,3},{2,0},{3,1},{4,6},{5,7},{6,4},{7,5},{8,10},{9,11},{10,... | collective-permute-start | bytes 98312 | tf_op jit(solution)/shard_map/ppermute | solution.py:326
  28.6 5.1 %collective-permute-start.8 = (f32[64,128]{1,0:T(8,128)S(1)}, f32[64,128]{1,0:T(8,128)S(1)}, u32[]{:S(2)}, u32[]{:S(2)}) collective-permute-start(f32[64,128]{1,0:T(8,128)S(1)} %add.24), channel_id=1, source_target_pairs={{0,33},{1,32},{2,35},{3,34},{4,37},{5,36},{6,39},{7,38},{8,41},{9,... | collective-permute-start | bytes 98312 | tf_op jit(solution)/shard_map/ppermute | solution.py:326
  33.7 4.7 %collective-permute-start.9 = (f32[64,128]{1,0:T(8,128)S(1)}, f32[64,128]{1,0:T(8,128)S(1)}, u32[]{:S(2)}, u32[]{:S(2)}) collective-permute-start(f32[64,128]{1,0:T(8,128)S(1)} %add.25), channel_id=1, source_target_pairs={{0,65},{1,64},{2,67},{3,66},{4,69},{5,68},{6,71},{7,70},{8,73},{9,... | collective-permute-start | bytes 98312 | tf_op jit(solution)/shard_map/ppermute | solution.py:326
  38.4 7.6 %collective-permute-start.10 = (f32[64,128]{1,0:T(8,128)S(1)}, f32[64,128]{1,0:T(8,128)S(1)}, u32[]{:S(2)}, u32[]{:S(2)}) collective-permute-start(f32[64,128]{1,0:T(8,128)S(1)} %add.26), channel_id=1, source_target_pairs={{0,225},{1,224},{2,227},{3,226},{4,229},{5,228},{6,231},{7,230},{8... | collective-permute-start | bytes 98312 | tf_op jit(solution)/shard_map/ppermute | solution.py:326
  46.1 1.2 %collective-permute-start.11 = (f32[64,128]{1,0:T(8,128)S(1)}, f32[64,128]{1,0:T(8,128)S(1)}, u32[]{:S(2)}, u32[]{:S(2)}) collective-permute-start(f32[64,128]{1,0:T(8,128)S(1)} %add.27.sum_ref), channel_id=1, source_target_pairs={{0,1},{1,0},{2,3},{3,2},{4,5},{5,4},{6,7},{7,6},{8,9},{9,8},{10,11... | collective-permute-start | bytes 98312 | tf_op jit(solution)/shard_map/ppermute | solution.py:327

commit v14 on v10

--- a/solution.py
+++ b/solution.py
@@ -314,7 +314,7 @@
 
 def total_over_all(sums, back):
     left = [(i, (i - 1) % (2 * Y)) for i in range(2 * Y)]
-    steps = [("y", YS[0])] + [("x", r) for r in XS] + [("y", YS[1])] + [("z", r) for r in ZS]
+    steps = [("y", YS[0])] + [("x", r) for r in XS] + [("z", ZS[0]), ("y", YS[1])] + [("z", r) for r in ZS[1:]]
     for n, (axis, partner) in enumerate(steps):
         if n == 1:
             sums, back = lax.optimization_barrier((sums, back))

time: 48.4 us -> 47.6 us (0.983)
  starting transfers between devices: 24.4 us -> 23.7 us
    ppermute x7, starting transfers between devices: 19 us -> 18.3 us  [total_over_all(): sums = sums + lax.ppermute(sums, BOTH, swap_pairs(axis, partner))]
where the time goes in v14:
time: 47.6 us; the launch traced here: 47.4 us
  starting transfers between devices  23.7 us (50%)
  waiting for transfers between devices  14.3 us (30%)
  Pallas kernels  9.26 us (19%)
    ppermute x7, starting transfers between devices, total_over_all(): sums = sums + lax.ppermute(sums, BOTH, swap_pairs(axis, partner))  18.3 us
    ppermute x7, waiting for transfers between devices, total_over_all(): sums = sums + lax.ppermute(sums, BOTH, swap_pairs(axis, partner))  12.5 us
    pallas_call x4, Pallas kernels, on_core(): pl.pallas_call(kernel, out_shape=shapes, in_specs=[pl.BlockSpec(memory_sp...  7.45 us
    ppermute x1, starting transfers between devices, body(): near = lax.ppermute(near, 'tm', [(i, i ^ 1) for i in range(devices)])  3.33 us
    pallas_call x2, Pallas kernels, clean(): pl.pallas_call(functools.partial(clean_kernel, scale), out_shape=pltpu.HB...  1.81 us
    ppermute x1, waiting for transfers between devices, body(): lax.ppermute(cross, 'tm', [(i, (i + 1 if i % 2 else i - 1) % devices) for...  1.55 us
    ppermute x1, starting transfers between devices, body(): other = lax.ppermute(send, BOTH, CORES)  1.47 us
  transfers between devices with their start and end apart: 12, of which 9 were waited for; matrix products, arithmetic and copies ran while one was open for 0% of the time, Pallas kernels for 13%

profile of v14, /device:TPU:1, one launch (start us, length us, event | category | flops | bytes accessed | tf_op | source)
XLA Modules:
  0.0 47.4 jit_solution(12235516259721735349)
XLA Ops:
  0.0 1.4 %shard_map.47 = (f32[2,7,64,128]{3,2,1,0:T(8,128)S(1)}, f32[2,7,64,128]{3,2,1,0:T(8,128)S(1)}) custom-call(f32[2,2,2,64,8,128]{5,4,3,2,1,0:T(8,128)} %bitcast.15), custom_call_target="tpu_custom_call" | custom-call | flops 1000 | bytes 1000 | tf_op jit(solution)/shard_map/pallas_call | solution.py:291
  1.4 3.3 %collective-permute-start.1 = (f32[2,7,64,128]{3,2,1,0:T(8,128)S(1)}, f32[2,7,64,128]{3,2,1,0:T(8,128)S(1)}, u32[]{:S(2)}, u32[]{:S(2)}) collective-permute-start(f32[2,7,64,128]{3,2,1,0:T(8,128)S(1)} %get-tuple-element.27), channel_id=1, source_target_pairs={{0,1},{1,0},{2,3},{3,2},{4,5},{5,4},{6,7},{7,6},{8,9},{9,8},{10,11... | collective-permute-start | bytes 1376264 | tf_op jit(solution)/shard_map/ppermute | solution.py:338
  4.7 0.0 collective-permute-start
  4.7 4.2 %shard_map.46 = (f32[2,9,64,128]{3,2,1,0:T(8,128)S(1)}, f32[2,14,64,128]{3,2,1,0:T(8,128)S(1)}, f32[64,128]{1,0:T(8,128)S(1)}, f32[64,128]{1,0:T(8,128)S(1)}, f3...) custom-call(f32[2,2,2,512,128]{4,3,2,1,0:T(8,128)} %bitcast.16, ...), custom_call_target="tpu_custom_call" | custom-call | flops 2000000000 | bytes 6291456 | tf_op jit(solution)/shard_map/pallas_call | solution.py:291
  8.9 1.5 %collective-permute-start.2 = (f32[64,128]{1,0:T(8,128)S(1)}, f32[64,128]{1,0:T(8,128)S(1)}, u32[]{:S(2)}, u32[]{:S(2)}) collective-permute-start(f32[64,128]{1,0:T(8,128)S(1)} %get-tuple-element.30), channel_id=1, source_target_pairs={{0,1},{1,0},{2,3},{3,2},{4,5},{5,4},{6,7},{7,6},{8,9},{9,8},{10,11... | collective-permute-start | bytes 98312 | tf_op jit(solution)/shard_map/ppermute | solution.py:361
  10.4 0.0 collective-permute-done.1.near_ref
  10.4 0.9 %shard_map.48 = (f32[7,64,128]{2,1,0:T(8,128)S(1)}, f32[64,128]{1,0:T(8,128)S(1)}) custom-call(f32[2,14,64,128]{3,2,1,0:T(8,128)S(1)} %get-tuple-element.22.part_ref, f32[2,7,64,128]{3,2,1,0:T(8,128)S(1)} %collective-permute-done.1.near_ref, f32[512,128]{1,0:T(8,128)S(1)} %get-tuple-element.24.taps_ref, bf16[768,256]{1,0:T(8,128)(2,1)S(1)} %get-tuple-element.25.table_ref, ...), custom_call_target="tpu_custom_call" | custom-call | flops 1000000000 | bytes 3145728 | tf_op jit(solution)/shard_map/pallas_call | solution.py:291
  11.3 0.0 collective-permute-done.2.other_ref
  11.4 1.5 %collective-permute-done.cross_ref = f32[2,7,64,128]{3,2,1,0:T(8,128)S(1)} collective-permute-done((f32[2,7,64,128]{3,2,1,0:T(8,128)S(1)}, f32[2,7,64,128]{3,2,1,0:T(8,128)S(1)}, u32[]{:S(2)}, u32[]{:S(2)}) %collective-permute-start) | collective-permute-done | bytes 458784 | tf_op jit(solution)/shard_map/ppermute | solution.py:339
  12.9 0.9 %shard_map.49 = (f32[7,64,128]{2,1,0:T(8,128)S(1)}, f32[7,64,128]{2,1,0:T(8,128)S(1)}, f32[64,128]{1,0:T(8,128)S(1)}) custom-call(f32[2,14,64,128]{3,2,1,0:T(8,128)S(1)} %get-tuple-element.22.part_ref, f32[2,7,64,128]{3,2,1,0:T(8,128)S(1)} %collective-permute-done.cross_ref, f32[512,128]{1,0:T(8,128)S(1)} %get-tuple-element.24.taps_ref, ...), custom_call_target="tpu_custom_call" | custom-call | tf_op jit(solution)/shard_map/pallas_call | solution.py:291
  13.9 2.0 %collective-permute-start.3 = (f32[64,128]{1,0:T(8,128)S(1)}, f32[64,128]{1,0:T(8,128)S(1)}, u32[]{:S(2)}, u32[]{:S(2)}) collective-permute-start(f32[64,128]{1,0:T(8,128)S(1)} %get-tuple-element.32), channel_id=1, source_target_pairs={{0,6},{1,7},{2,4},{3,5},{4,2},{5,3},{6,0},{7,1},{8,14},{9,15},{10,... | collective-permute-start | bytes 98312 | tf_op jit(solution)/shard_map/ppermute | solution.py:322
  15.9 2.1 %collective-permute-done.3 = f32[64,128]{1,0:T(8,128)S(1)} collective-permute-done((f32[64,128]{1,0:T(8,128)S(1)}, f32[64,128]{1,0:T(8,128)S(1)}, u32[]{:S(2)}, u32[]{:S(2)}) %collective-permute-start.3) | collective-permute-done | bytes 32800 | tf_op jit(solution)/shard_map/ppermute | solution.py:322
  17.9 1.6 %collective-permute-start.5 = (f32[64,128]{1,0:T(8,128)S(1)}, f32[64,128]{1,0:T(8,128)S(1)}, u32[]{:S(2)}, u32[]{:S(2)}) collective-permute-start(f32[64,128]{1,0:T(8,128)S(1)} %add.21), channel_id=1, source_target_pairs={{0,9},{1,8},{2,11},{3,10},{4,13},{5,12},{6,15},{7,14},{8,1},{9,0},... | collective-permute-start | bytes 98312 | tf_op jit(solution)/shard_map/ppermute | solution.py:322
  19.5 0.6 %collective-permute-start.4 = (f32[7,64,128]{2,1,0:T(8,128)S(1)}, f32[7,64,128]{2,1,0:T(8,128)S(1)}, u32[]{:S(2)}, u32[]{:S(2)}) collective-permute-start(f32[7,64,128]{2,1,0:T(8,128)S(1)} %get-tuple-element.34), channel_id=1, source_target_pairs={{0,7},{1,0},{2,1},{3,2},{4,3},{5,4},{6,5},{7,6},{8,15},{9,8},{10,9... | collective-permute-start | bytes 688136 | tf_op jit(solution)/shard_map/ppermute | solution.py:321
  20.1 1.2 %collective-permute-done.5 = f32[64,128]{1,0:T(8,128)S(1)} collective-permute-done((f32[64,128]{1,0:T(8,128)S(1)}, f32[64,128]{1,0:T(8,128)S(1)}, u32[]{:S(2)}, u32[]{:S(2)}) %collective-permute-start.5) | collective-permute-done | bytes 32800 | tf_op jit(solution)/shard_map/ppermute | solution.py:322
  21.3 2.9 %collective-permute-start.6 = (f32[64,128]{1,0:T(8,128)S(1)}, f32[64,128]{1,0:T(8,128)S(1)}, u32[]{:S(2)}, u32[]{:S(2)}) collective-permute-start(f32[64,128]{1,0:T(8,128)S(1)} %add.22), channel_id=1, source_target_pairs={{0,25},{1,24},{2,27},{3,26},{4,29},{5,28},{6,31},{7,30},{8,17},{9,... | collective-permute-start | bytes 98312 | tf_op jit(solution)/shard_map/ppermute | solution.py:322
  24.1 1.7 %collective-permute-done.6 = f32[64,128]{1,0:T(8,128)S(1)} collective-permute-done((f32[64,128]{1,0:T(8,128)S(1)}, f32[64,128]{1,0:T(8,128)S(1)}, u32[]{:S(2)}, u32[]{:S(2)}) %collective-permute-start.6) | collective-permute-done | bytes 32800 | tf_op jit(solution)/shard_map/ppermute | solution.py:322
  25.8 2.4 %collective-permute-start.7 = (f32[64,128]{1,0:T(8,128)S(1)}, f32[64,128]{1,0:T(8,128)S(1)}, u32[]{:S(2)}, u32[]{:S(2)}) collective-permute-start(f32[64,128]{1,0:T(8,128)S(1)} %add.23), channel_id=1, source_target_pairs={{0,33},{1,32},{2,35},{3,34},{4,37},{5,36},{6,39},{7,38},{8,41},{9,... | collective-permute-start | bytes 98312 | tf_op jit(solution)/shard_map/ppermute | solution.py:322
  28.2 1.6 %collective-permute-done.7 = f32[64,128]{1,0:T(8,128)S(1)} collective-permute-done((f32[64,128]{1,0:T(8,128)S(1)}, f32[64,128]{1,0:T(8,128)S(1)}, u32[]{:S(2)}, u32[]{:S(2)}) %collective-permute-start.7) | collective-permute-done | bytes 32800 | tf_op jit(solution)/shard_map/ppermute | solution.py:322
  29.8 0.0 collective-permute-start.8
  29.8 2.8 %collective-permute-done.8 = f32[64,128]{1,0:T(8,128)S(1)} collective-permute-done((f32[64,128]{1,0:T(8,128)S(1)}, f32[64,128]{1,0:T(8,128)S(1)}, u32[]{:S(2)}, u32[]{:S(2)}) %collective-permute-start.8) | collective-permute-done | bytes 32800 | tf_op jit(solution)/shard_map/ppermute | solution.py:322
  32.6 4.3 %collective-permute-start.9 = (f32[64,128]{1,0:T(8,128)S(1)}, f32[64,128]{1,0:T(8,128)S(1)}, u32[]{:S(2)}, u32[]{:S(2)}) collective-permute-start(f32[64,128]{1,0:T(8,128)S(1)} %add.25), channel_id=1, source_target_pairs={{0,65},{1,64},{2,67},{3,66},{4,69},{5,68},{6,71},{7,70},{8,73},{9,... | collective-permute-start | bytes 98312 | tf_op jit(solution)/shard_map/ppermute | solution.py:322
  36.8 1.6 %collective-permute-done.9 = f32[64,128]{1,0:T(8,128)S(1)} collective-permute-done((f32[64,128]{1,0:T(8,128)S(1)}, f32[64,128]{1,0:T(8,128)S(1)}, u32[]{:S(2)}, u32[]{:S(2)}) %collective-permute-start.9) | collective-permute-done | bytes 32800 | tf_op jit(solution)/shard_map/ppermute | solution.py:322
  38.4 5.3 %collective-permute-start.10 = (f32[64,128]{1,0:T(8,128)S(1)}, f32[64,128]{1,0:T(8,128)S(1)}, u32[]{:S(2)}, u32[]{:S(2)}) collective-permute-start(f32[64,128]{1,0:T(8,128)S(1)} %add.26), channel_id=1, source_target_pairs={{0,225},{1,224},{2,227},{3,226},{4,229},{5,228},{6,231},{7,230},{8... | collective-permute-start | bytes 98312 | tf_op jit(solution)/shard_map/ppermute | solution.py:322
  43.7 1.6 %collective-permute-done.10 = f32[64,128]{1,0:T(8,128)S(1)} collective-permute-done((f32[64,128]{1,0:T(8,128)S(1)}, f32[64,128]{1,0:T(8,128)S(1)}, u32[]{:S(2)}, u32[]{:S(2)}) %collective-permute-start.10) | collective-permute-done | bytes 32800 | tf_op jit(solution)/shard_map/ppermute | solution.py:322
  45.3 0.0 collective-permute-start.11
  45.3 0.9 %shard_map.50.refs_0_ = f32[2,2,512,128]{3,2,1,0:T(8,128)} custom-call(f32[2,9,64,128]{3,2,1,0:T(8,128)S(1)} %get-tuple-element.21.held_ref, f32[7,64,128]{2,1,0:T(8,128)S(1)} %get-tuple-element.36.rim_ref, f32[64,128]{1,0:T(8,128)S(1)} %add.27.sum_ref), custom_call_target="tpu_custom_call" | custom-call | flops 1000000 | bytes 2097152 | tf_op jit(solution)/shard_map/pallas_call | solution.py:275
  46.2 0.0 collective-permute-done.4.rim_ref
  46.2 0.3 collective-permute-done.11.sum_ref
  46.5 0.9 %shard_map.51 = f32[2,2,512,128]{3,2,1,0:T(8,128)} custom-call(f32[2,9,64,128]{3,2,1,0:T(8,128)S(1)} %get-tuple-element.21.held_ref, f32[7,64,128]{2,1,0:T(8,128)S(1)} %collective-permute-done.4.rim_ref, f32[64,128]{1,0:T(8,128)S(1)} %collective-permute-done.11.sum_ref, f32[2,2,512,128]{3,2,1,0:T(8,128)} %shard_map.50.refs_0_), custom_call_target="tpu_custom_call", output_to_operand_aliasing={{}: (3, {})} | custom-call | flops 1000000 | bytes 2097152 | tf_op jit(solution)/shard_map/pallas_call | solution.py:275
  (7 shorter events, 0.0 us)
Async XLA Ops:
  1.4 9.0 %collective-permute-start.1 = (f32[2,7,64,128]{3,2,1,0:T(8,128)S(1)}, f32[2,7,64,128]{3,2,1,0:T(8,128)S(1)}, u32[]{:S(2)}, u32[]{:S(2)}) collective-permute-start(f32[2,7,64,128]{3,2,1,0:T(8,128)S(1)} %get-tuple-element.27), channel_id=1, source_target_pairs={{0,1},{1,0},{2,3},{3,2},{4,5},{5,4},{6,7},{7,6},{8,9},{9,8},{10,11... | collective-permute-start | bytes 1376264 | tf_op jit(solution)/shard_map/ppermute | solution.py:338
  4.7 8.2 %collective-permute-start = (f32[2,7,64,128]{3,2,1,0:T(8,128)S(1)}, f32[2,7,64,128]{3,2,1,0:T(8,128)S(1)}, u32[]{:S(2)}, u32[]{:S(2)}) collective-permute-start(f32[2,7,64,128]{3,2,1,0:T(8,128)S(1)} %get-tuple-element.23), channel_id=1, source_target_pairs={{0,7},{1,2},{2,1},{3,4},{4,3},{5,6},{6,5},{7,0},{8,15},{9,10},{10,... | collective-permute-start | bytes 1376264 | tf_op jit(solution)/shard_map/ppermute | solution.py:339
  8.9 2.4 %collective-permute-start.2 = (f32[64,128]{1,0:T(8,128)S(1)}, f32[64,128]{1,0:T(8,128)S(1)}, u32[]{:S(2)}, u32[]{:S(2)}) collective-permute-start(f32[64,128]{1,0:T(8,128)S(1)} %get-tuple-element.30), channel_id=1, source_target_pairs={{0,1},{1,0},{2,3},{3,2},{4,5},{5,4},{6,7},{7,6},{8,9},{9,8},{10,11... | collective-permute-start | bytes 98312 | tf_op jit(solution)/shard_map/ppermute | solution.py:361
  13.9 4.1 %collective-permute-start.3 = (f32[64,128]{1,0:T(8,128)S(1)}, f32[64,128]{1,0:T(8,128)S(1)}, u32[]{:S(2)}, u32[]{:S(2)}) collective-permute-start(f32[64,128]{1,0:T(8,128)S(1)} %get-tuple-element.32), channel_id=1, source_target_pairs={{0,6},{1,7},{2,4},{3,5},{4,2},{5,3},{6,0},{7,1},{8,14},{9,15},{10,... | collective-permute-start | bytes 98312 | tf_op jit(solution)/shard_map/ppermute | solution.py:322
  17.9 3.3 %collective-permute-start.5 = (f32[64,128]{1,0:T(8,128)S(1)}, f32[64,128]{1,0:T(8,128)S(1)}, u32[]{:S(2)}, u32[]{:S(2)}) collective-permute-start(f32[64,128]{1,0:T(8,128)S(1)} %add.21), channel_id=1, source_target_pairs={{0,9},{1,8},{2,11},{3,10},{4,13},{5,12},{6,15},{7,14},{8,1},{9,0},... | collective-permute-start | bytes 98312 | tf_op jit(solution)/shard_map/ppermute | solution.py:322
  19.5 26.7 %collective-permute-start.4 = (f32[7,64,128]{2,1,0:T(8,128)S(1)}, f32[7,64,128]{2,1,0:T(8,128)S(1)}, u32[]{:S(2)}, u32[]{:S(2)}) collective-permute-start(f32[7,64,128]{2,1,0:T(8,128)S(1)} %get-tuple-element.34), channel_id=1, source_target_pairs={{0,7},{1,0},{2,1},{3,2},{4,3},{5,4},{6,5},{7,6},{8,15},{9,8},{10,9... | collective-permute-start | bytes 688136 | tf_op jit(solution)/shard_map/ppermute | solution.py:321
  21.3 4.6 %collective-permute-start.6 = (f32[64,128]{1,0:T(8,128)S(1)}, f32[64,128]{1,0:T(8,128)S(1)}, u32[]{:S(2)}, u32[]{:S(2)}) collective-permute-start(f32[64,128]{1,0:T(8,128)S(1)} %add.22), channel_id=1, source_target_pairs={{0,25},{1,24},{2,27},{3,26},{4,29},{5,28},{6,31},{7,30},{8,17},{9,... | collective-permute-start | bytes 98312 | tf_op jit(solution)/shard_map/ppermute | solution.py:322
  25.8 4.0 %collective-permute-start.7 = (f32[64,128]{1,0:T(8,128)S(1)}, f32[64,128]{1,0:T(8,128)S(1)}, u32[]{:S(2)}, u32[]{:S(2)}) collective-permute-start(f32[64,128]{1,0:T(8,128)S(1)} %add.23), channel_id=1, source_target_pairs={{0,33},{1,32},{2,35},{3,34},{4,37},{5,36},{6,39},{7,38},{8,41},{9,... | collective-permute-start | bytes 98312 | tf_op jit(solution)/shard_map/ppermute | solution.py:322
  29.8 2.8 %collective-permute-start.8 = (f32[64,128]{1,0:T(8,128)S(1)}, f32[64,128]{1,0:T(8,128)S(1)}, u32[]{:S(2)}, u32[]{:S(2)}) collective-permute-start(f32[64,128]{1,0:T(8,128)S(1)} %add.24), channel_id=1, source_target_pairs={{0,2},{1,3},{2,0},{3,1},{4,6},{5,7},{6,4},{7,5},{8,10},{9,11},{10,... | collective-permute-start | bytes 98312 | tf_op jit(solution)/shard_map/ppermute | solution.py:322
  32.6 5.8 %collective-permute-start.9 = (f32[64,128]{1,0:T(8,128)S(1)}, f32[64,128]{1,0:T(8,128)S(1)}, u32[]{:S(2)}, u32[]{:S(2)}) collective-permute-start(f32[64,128]{1,0:T(8,128)S(1)} %add.25), channel_id=1, source_target_pairs={{0,65},{1,64},{2,67},{3,66},{4,69},{5,68},{6,71},{7,70},{8,73},{9,... | collective-permute-start | bytes 98312 | tf_op jit(solution)/shard_map/ppermute | solution.py:322
  38.4 6.9 %collective-permute-start.10 = (f32[64,128]{1,0:T(8,128)S(1)}, f32[64,128]{1,0:T(8,128)S(1)}, u32[]{:S(2)}, u32[]{:S(2)}) collective-permute-start(f32[64,128]{1,0:T(8,128)S(1)} %add.26), channel_id=1, source_target_pairs={{0,225},{1,224},{2,227},{3,226},{4,229},{5,228},{6,231},{7,230},{8... | collective-permute-start | bytes 98312 | tf_op jit(solution)/shard_map/ppermute | solution.py:322
  45.3 1.2 %collective-permute-start.11 = (f32[64,128]{1,0:T(8,128)S(1)}, f32[64,128]{1,0:T(8,128)S(1)}, u32[]{:S(2)}, u32[]{:S(2)}) collective-permute-start(f32[64,128]{1,0:T(8,128)S(1)} %add.27.sum_ref), channel_id=1, source_target_pairs={{0,1},{1,0},{2,3},{3,2},{4,5},{5,4},{6,7},{7,6},{8,9},{9,8},{10,11... | collective-permute-start | bytes 98312 | tf_op jit(solution)/shard_map/ppermute | solution.py:323
